TPU v7x, 32 devices: a whole 2x2x4 slice. The times are simulated.
32 devices in a mesh: gx: 2 (over y), gy: 4 (over x, core), gz: 4 (over z).
Axes of the slice: x: 2, y: 2, z: 4, core: 2. Of those that a mesh axis runs over, the one named last changes fastest.
Arguments:
- old_fields: float32 [2048, 4, 512], P(('gx', 'gy', 'gz')), may hold values from 0.5 to 2.5
- new_owner: int32 [2048], P(('gx', 'gy', 'gz')), may hold values from 0 to 7, as said below
- old_owner: int32 [2048], P(('gx', 'gy', 'gz')), may hold values from 0 to 7, as said below
Outputs:
- flame_fields: float32 [4, 32, 64, 512], P(None, 'gx', 'gy', 'gz')
Inputs may be any that keep to these rules, and one draw needn't show every extreme that they name: A box keeps its gy index; new_owner is the group index of the device of its gx+gz group that holds it after the move. A device sends at most 16 boxes to one device of its group, reaches that number for some device, and every device receives exactly 64 boxes. `old_owner`: agrees with new_owner: the positions of a device naming s are exactly as many as the boxes that device s of the same group and gy sends to it.
All inputs are finite; a program needn't handle non-finite values.
Results may differ from a plain program's by a relative error of at most 0.00002.
Values sent between devices are 32-bit elements; how exact they have to be, the bound alone decides.
No kernel may reach another device: no remote copies, remote signals or barrier semaphores. Data moves between devices by JAX's collectives and lax.ppermute only.
A program may use at most 64 MiB of HBM per device.

v0:
```python
import jax
import jax.numpy as jnp
from jax import lax
from jax.sharding import PartitionSpec as P

EDGE = 8
FIELDS = 4
BRICK_X = 2
BRICK_Y = 2
BRICK_Z = 16


DIFFUSION = (1.0, 3.3, 0.9, 1.2)
TIME_STEP = 0.012


def padded(cells, sides, width):
    for axis, dim in sides:
        count = lax.axis_size(axis)
        head = lax.slice_in_dim(cells, 0, width, axis=dim)
        tail = lax.slice_in_dim(cells, cells.shape[dim] - width, cells.shape[dim], axis=dim)
        cells = jnp.concatenate(
            [
                lax.ppermute(tail, axis, [(i, (i + 1) % count) for i in range(count)]),
                cells,
                lax.ppermute(head, axis, [((i + 1) % count, i) for i in range(count)]),
            ],
            axis=dim,
        )
    return cells


def window(array, direction, offset):
    pieces = [slice(None), slice(1, -1), slice(1, -1), slice(1, -1)]
    length = array.shape[direction]
    pieces[direction] = slice(1 + offset, length - 1 + offset)
    return array[tuple(pieces)]


def rates_inside(bordered_fields):
    thermal_field = bordered_fields[0]
    stepping_factors = jnp.array(DIFFUSION, jnp.float32)
    diffusion_coefficient = (
        stepping_factors[:, None, None, None] * (thermal_field * jnp.sqrt(thermal_field))[None]
    )
    centre = bordered_fields[:, 1:-1, 1:-1, 1:-1]
    centre_diffusivity = diffusion_coefficient[:, 1:-1, 1:-1, 1:-1]
    summed = jnp.zeros_like(centre)
    for direction in (1, 2, 3):
        for offset in (1, -1):
            beside = window(bordered_fields, direction, offset)
            beside_diffusivity = window(diffusion_coefficient, direction, offset)
            summed = summed + 0.5 * (centre_diffusivity + beside_diffusivity) * (beside - centre)
    return summed


def with_faces(present_state):
    return padded(present_state, (("gx", 1), ("gy", 2), ("gz", 3)), 1)


def body(old_fields, new_owner, old_owner):
    group_size = lax.axis_size("gx") * lax.axis_size("gz")
    box_count = new_owner.shape[0]
    capacity = 2 * (box_count // group_size)
    positions = jnp.arange(box_count, dtype=jnp.int32)
    earlier = positions[None, :] < positions[:, None]
    sent_rank = jnp.sum(
        ((new_owner[None, :] == new_owner[:, None]) & earlier).astype(jnp.int32), axis=1
    )
    slot_index = new_owner * capacity + sent_rank
    filler = jnp.zeros((group_size * capacity,), jnp.int32).at[slot_index].set(positions)
    departing_boxes = jnp.take(old_fields, filler, axis=0)
    arrived = lax.all_to_all(departing_boxes, ("gx", "gz"), split_axis=0, concat_axis=0, tiled=True)
    holder_position = jnp.sum(
        ((old_owner[None, :] == old_owner[:, None]) & earlier).astype(jnp.int32), axis=1
    )
    box_rows = jnp.take(arrived, old_owner * capacity + holder_position, axis=0)
    present_state = box_rows.reshape(BRICK_X, BRICK_Y, BRICK_Z, FIELDS, EDGE, EDGE, EDGE)
    present_state = present_state.transpose(3, 0, 4, 1, 5, 2, 6).reshape(
        FIELDS, BRICK_X * EDGE, BRICK_Y * EDGE, BRICK_Z * EDGE
    )
    first_section = present_state + TIME_STEP * rates_inside(with_faces(present_state))
    result_fields = 0.5 * present_state + 0.5 * (
        first_section + TIME_STEP * rates_inside(with_faces(first_section))
    )
    return result_fields


def solution(mesh):
    return jax.shard_map(
        body,
        mesh=mesh,
        in_specs=(P(("gx", "gy", "gz"), None, None), P(("gx", "gy", "gz")), P(("gx", "gy", "gz"))),
        out_specs=P(None, "gx", "gy", "gz"),
        check_vma=False,
    )
```

profile of v0, /device:TPU:0, one launch (start us, length us, event | category | flops | bytes accessed | tf_op | source)
XLA Modules:
  0.0 107.5 jit_solution(5839446029853638111)
XLA Ops:
  0.0 0.0 copy-start
  0.0 0.9 convert_reduce_fusion
  0.9 0.7 compare_select_fusion.1
  1.6 0.8 scatter_custom_fusion
  2.4 0.0 copy-done
  2.4 1.2 %gather_fusion = f32[128,4,512]{2,1,0:T(4,128)S(1)} fusion(f32[64,4,512]{2,1,0:T(4,128)S(1)} %copy-done, s32[1024]{0:T(1024)S(1)} %pad_clamp_fusion.1), kind=kCustom, calls=%fused_computation | custom fusion | bytes 2097664 | tf_op jit(solution)/shard_map/jit(_take)/gather | solution.py:72
  3.6 0.0 copy-start.5
  3.6 1.3 %broadcast_select_fusion = f32[128,4,512]{2,1,0:T(4,128)} fusion(f32[128,4,512]{2,1,0:T(4,128)S(1)} %gather_fusion, pred[128]{0:T(512)(128)(4,1)S(1)} %compare_and_fusion), kind=kLoop, calls=%fused_computation.102 | loop fusion | flops 262144 | bytes 2097280 | tf_op jit(solution)/shard_map/jit(_take)/select_n | solution.py:72
  4.9 7.3 %all-to-all-start = ((f32[128,4,512]{2,1,0:T(4,128)}), f32[128,4,512]{2,1,0:T(4,128)S(1)}, u32[]{:S(2)}, u32[]{:S(2)}) async-start(f32[128,4,512]{2,1,0:T(4,128)} %broadcast_select_fusion), calls=%async_computation | async-start | bytes 2097152 | tf_op jit(solution)/shard_map/all_to_all | solution.py:73
  12.2 0.2 convert_reduce_fusion.1
  12.4 0.1 broadcast_in_dim.42
  12.5 26.3 %all-to-all-done = f32[128,4,512]{2,1,0:T(4,128)S(1)} async-done(((f32[128,4,512]{2,1,0:T(4,128)}), f32[128,4,512]{2,1,0:T(4,128)S(1)}, u32[]{:S(2)}, u32[]{:S(2)}) %all-to-all-start) | async-done | bytes 1048608 | tf_op jit(solution)/shard_map/all_to_all | solution.py:73
  38.8 0.9 gather_fusion.1
  39.7 0.4 copy.23
  40.0 4.7 %gather.12 = f32[2,2,16,4,8,8,8]{2,1,0,6,5,4,3:T(2,128)} reshape(f32[64,4,512]{0,2,1:T(8,128)S(1)} %copy.23) | data formatting | bytes 1048576 | tf_op jit(solution)/shard_map/jit(_take)/gather | solution.py:77
  44.7 7.6 %select_bitcast_fusion = f32[4,2,8,2,8,16,8]{5,3,1,6,4,2,0:T(2,128)} fusion(f32[2,2,16,4,8,8,8]{2,1,0,6,5,4,3:T(2,128)} %gather.12, pred[2,2,16]{2,1,0:T(4,128)(4,1)S(1)} %broadcast_in_dim.42), kind=kLoop, calls=%fused_computation.3 | loop fusion | flops 131072 | bytes 1048640 | tf_op jit(solution)/shard_map/transpose | solution.py:79
  52.3 8.5 %copy.24 = f32[4,2,8,2,8,16,8]{6,5,4,3,2,1,0:T(8,128)} copy(f32[4,2,8,2,8,16,8]{5,3,1,6,4,2,0:T(2,128)} %select_bitcast_fusion) | data formatting | bytes 1048576 | tf_op jit(solution)/shard_map/transpose | solution.py:79
  60.8 6.4 %reshape.23 = f32[4,16,16,128]{3,2,1,0:T(8,128)S(1)} reshape(f32[4,2,8,2,8,16,8]{6,5,4,3,2,1,0:T(8,128)} %copy.24) | data formatting | bytes 1048576 | tf_op jit(solution)/shard_map/reshape | solution.py:79
  67.2 0.6 collective-permute-start
  67.8 1.5 %collective-permute-start.1 = (f32[4,1,16,128]{3,2,1,0:T(8,128)S(1)}, f32[4,1,16,128]{3,2,1,0:T(8,128)S(1)}, u32[]{:S(2)}, u32[]{:S(2)}) collective-permute-start(f32[4,1,16,128]{3,2,1,0:T(8,128)S(1)} %get-tuple-element.17), channel_id=1, source_target_pairs={{16,0},{0,16},{17,1},{1,17},{18,2},{2,18},{19,3},{3,19},{20,4},{4,... | collective-permute-start | bytes 98312 | tf_op jit(solution)/shard_map/ppermute | solution.py:26
  69.3 1.9 %collective-permute-done = f32[4,1,16,128]{3,2,1,0:T(8,128)S(1)} collective-permute-done((f32[4,1,16,128]{3,2,1,0:T(8,128)S(1)}, f32[4,1,16,128]{3,2,1,0:T(8,128)S(1)}, u32[]{:S(2)}, u32[]{:S(2)}) %collective-permute-start) | collective-permute-done | bytes 32800 | tf_op jit(solution)/shard_map/ppermute | solution.py:24
  71.2 0.5 collective-permute-done.1
  71.8 0.1 fusion.60
  71.8 0.1 collective-permute-start.2
  71.9 1.7 %collective-permute-start.3 = (f32[4,18,1,128]{3,2,1,0:T(1,128)S(1)}, f32[4,18,1,128]{3,2,1,0:T(1,128)S(1)}, u32[]{:S(2)}, u32[]{:S(2)}) collective-permute-start(f32[4,18,1,128]{3,2,1,0:T(1,128)S(1)} %get-tuple-element.14), channel_id=1, source_target_pairs={{4,0},{8,4},{12,8},{0,12},{5,1},{9,5},{13,9},{1,13},{6,2},{10,6},{... | collective-permute-start | bytes 110600 | tf_op jit(solution)/shard_map/ppermute | solution.py:26
  73.6 1.6 %collective-permute-done.2 = f32[4,18,1,128]{3,2,1,0:T(1,128)S(1)} collective-permute-done((f32[4,18,1,128]{3,2,1,0:T(1,128)S(1)}, f32[4,18,1,128]{3,2,1,0:T(1,128)S(1)}, u32[]{:S(2)}, u32[]{:S(2)}) %collective-permute-start.2) | collective-permute-done | bytes 36896 | tf_op jit(solution)/shard_map/ppermute | solution.py:24
  75.3 0.0 collective-permute-done.3
  75.3 0.1 pad_maximum_fusion
  75.4 0.3 fusion.59
  75.7 0.5 copy.26
  76.2 0.0 collective-permute-start.5
  76.3 0.5 copy.25
  76.8 2.2 %collective-permute-start.4 = (f32[4,18,18,1]{2,0,3,1:T(4,128)S(1)}, f32[4,18,18,1]{2,0,3,1:T(4,128)S(1)}, u32[]{:S(2)}, u32[]{:S(2)}) collective-permute-start(f32[4,18,18,1]{2,0,3,1:T(4,128)S(1)} %copy.25), channel_id=1, source_target_pairs={{0,1},{1,2},{2,3},{3,0},{4,5},{5,6},{6,7},{7,4},{8,9},{9,10},{10,1... | collective-permute-start | bytes 15560 | tf_op jit(solution)/shard_map/ppermute | solution.py:24
  79.0 1.2 %collective-permute-done.5 = f32[4,18,18,1]{2,0,3,1:T(4,128)S(1)} collective-permute-done((f32[4,18,18,1]{2,0,3,1:T(4,128)S(1)}, f32[4,18,18,1]{2,0,3,1:T(4,128)S(1)}, u32[]{:S(2)}, u32[]{:S(2)}) %collective-permute-start.5) | collective-permute-done | bytes 5216 | tf_op jit(solution)/shard_map/ppermute | solution.py:26
  80.2 0.6 copy.28
  80.8 2.0 %collective-permute-done.4 = f32[4,18,18,1]{2,0,3,1:T(4,128)S(1)} collective-permute-done((f32[4,18,18,1]{2,0,3,1:T(4,128)S(1)}, f32[4,18,18,1]{2,0,3,1:T(4,128)S(1)}, u32[]{:S(2)}, u32[]{:S(2)}) %collective-permute-start.4) | collective-permute-done | bytes 5216 | tf_op jit(solution)/shard_map/ppermute | solution.py:24
  82.8 0.6 copy.27
  83.3 1.2 %fusion.52 = f32[18,18,130]{2,1,0:T(8,128)S(1)} fusion(f32[4,18,18,1]{3,2,1,0:T(8,128)S(1)} %copy.28, f32[4,18,18,1]{3,2,1,0:T(8,128)S(1)} %copy.27, f32[4,18,1,128]{3,2,1,0:T(1,128)S(1)} %collective-permute-done.3, f32[4,18,16,128]{3,2,1,0:T(8,128)} %copy-done.1, f32[4,18,1,128]{3,2,1,0:T(1,128)S(1)} %collective-permute-done.2), kind=kLoop, calls=%fused_computation.103 | loop fusion | flops 210600 | bytes 842400 | tf_op jit(solution)/shard_map/mul | solution.py:44
  84.6 0.2 broadcast_multiply_fusion.1
  84.8 0.8 copy-done.2
  85.7 1.7 %fusion.31 = f32[4,16,16,128]{3,2,1,0:T(8,128)S(1)} fusion(f32[4,16,16,128]{3,2,1,0:T(8,128)S(1)} %reshape.23, f32[4,18,18,1]{3,2,1,0:T(8,128)S(1)} %copy.27, f32[4,18,1,128]{3,2,1,0:T(1,128)S(1)} %collective-permute-done.3, f32[4,18,16,128]{3,2,1,0:T(8,128)S(1)} %copy-done.2, f32[4,18,1,128]{3,2,1,0:T(1,128)S(1)} %collective-permute-done.2, ...), kind=kLoop, calls=%fused_computation.66 | loop fusion | flops 5373952 | bytes 5458048 | tf_op jit(solution)/shard_map/add | solution.py:82
  87.4 1.5 %collective-permute-start.6 = (f32[4,1,16,128]{3,2,1,0:T(8,128)S(1)}, f32[4,1,16,128]{3,2,1,0:T(8,128)S(1)}, u32[]{:S(2)}, u32[]{:S(2)}) collective-permute-start(f32[4,1,16,128]{3,2,1,0:T(8,128)S(1)} %get-tuple-element.15), channel_id=1, source_target_pairs={{0,16},{16,0},{1,17},{17,1},{2,18},{18,2},{3,19},{19,3},{4,20},{20... | collective-permute-start | bytes 98312 | tf_op jit(solution)/shard_map/ppermute | solution.py:24
  88.9 0.6 collective-permute-start.7
  89.5 1.9 %collective-permute-done.6 = f32[4,1,16,128]{3,2,1,0:T(8,128)S(1)} collective-permute-done((f32[4,1,16,128]{3,2,1,0:T(8,128)S(1)}, f32[4,1,16,128]{3,2,1,0:T(8,128)S(1)}, u32[]{:S(2)}, u32[]{:S(2)}) %collective-permute-start.6) | collective-permute-done | bytes 32800 | tf_op jit(solution)/shard_map/ppermute | solution.py:24
  91.4 1.5 %collective-permute-done.7 = f32[4,1,16,128]{3,2,1,0:T(8,128)S(1)} collective-permute-done((f32[4,1,16,128]{3,2,1,0:T(8,128)S(1)}, f32[4,1,16,128]{3,2,1,0:T(8,128)S(1)}, u32[]{:S(2)}, u32[]{:S(2)}) %collective-permute-start.7) | collective-permute-done | bytes 32800 | tf_op jit(solution)/shard_map/ppermute | solution.py:26
  92.8 0.1 pad_maximum_fusion.42
  92.9 0.1 collective-permute-start.8
  93.0 1.7 %collective-permute-start.9 = (f32[4,18,1,128]{3,2,1,0:T(1,128)S(1)}, f32[4,18,1,128]{3,2,1,0:T(1,128)S(1)}, u32[]{:S(2)}, u32[]{:S(2)}) collective-permute-start(f32[4,18,1,128]{3,2,1,0:T(1,128)S(1)} %get-tuple-element.12), channel_id=1, source_target_pairs={{4,0},{8,4},{12,8},{0,12},{5,1},{9,5},{13,9},{1,13},{6,2},{10,6},{... | collective-permute-start | bytes 110600 | tf_op jit(solution)/shard_map/ppermute | solution.py:26
  94.7 1.6 %collective-permute-done.8 = f32[4,18,1,128]{3,2,1,0:T(1,128)S(1)} collective-permute-done((f32[4,18,1,128]{3,2,1,0:T(1,128)S(1)}, f32[4,18,1,128]{3,2,1,0:T(1,128)S(1)}, u32[]{:S(2)}, u32[]{:S(2)}) %collective-permute-start.8) | collective-permute-done | bytes 36896 | tf_op jit(solution)/shard_map/ppermute | solution.py:24
  96.3 0.0 collective-permute-done.9
  96.3 0.1 pad_maximum_fusion.1
  96.5 0.3 fusion.58
  96.8 0.5 copy.32
  97.3 0.1 collective-permute-start.11
  97.4 0.5 copy.31
  97.9 2.0 %collective-permute-start.10 = (f32[4,18,18,1]{2,0,3,1:T(4,128)S(1)}, f32[4,18,18,1]{2,0,3,1:T(4,128)S(1)}, u32[]{:S(2)}, u32[]{:S(2)}) collective-permute-start(f32[4,18,18,1]{2,0,3,1:T(4,128)S(1)} %copy.31), channel_id=1, source_target_pairs={{0,1},{1,2},{2,3},{3,0},{4,5},{5,6},{6,7},{7,4},{8,9},{9,10},{10,1... | collective-permute-start | bytes 15560 | tf_op jit(solution)/shard_map/ppermute | solution.py:24
  99.9 1.4 %collective-permute-done.11 = f32[4,18,18,1]{2,0,3,1:T(4,128)S(1)} collective-permute-done((f32[4,18,18,1]{2,0,3,1:T(4,128)S(1)}, f32[4,18,18,1]{2,0,3,1:T(4,128)S(1)}, u32[]{:S(2)}, u32[]{:S(2)}) %collective-permute-start.11) | collective-permute-done | bytes 5216 | tf_op jit(solution)/shard_map/ppermute | solution.py:26
  101.3 0.6 copy.34
  101.9 1.9 %collective-permute-done.10 = f32[4,18,18,1]{2,0,3,1:T(4,128)S(1)} collective-permute-done((f32[4,18,18,1]{2,0,3,1:T(4,128)S(1)}, f32[4,18,18,1]{2,0,3,1:T(4,128)S(1)}, u32[]{:S(2)}, u32[]{:S(2)}) %collective-permute-start.10) | collective-permute-done | bytes 5216 | tf_op jit(solution)/shard_map/ppermute | solution.py:24
  103.7 0.6 copy.33
  104.3 0.3 fusion.53
  104.6 0.0 copy-done.4
  104.6 0.2 broadcast_multiply_fusion
  104.8 2.7 %fusion.6 = f32[4,16,16,128]{3,2,1,0:T(8,128)} fusion(f32[4,16,16,128]{3,2,1,0:T(8,128)S(1)} %reshape.23, f32[4,16,16,128]{3,2,1,0:T(8,128)S(1)} %fusion.31, f32[4,18,18,1]{3,2,1,0:T(8,128)S(1)} %copy.33, f32[4,18,1,128]{3,2,1,0:T(1,128)S(1)} %collective-permute-done.9, f32[4,18,1,128]{3,2,1,0:T(1,128)S(1)} %collective-permute-done.8, ...), kind=kLoop, calls=%fused_computation.17 | loop fusion | flops 6684672 | bytes 5392512 | tf_op jit(solution)/shard_map/add | solution.py:83
  (18 shorter events, 0.1 us)
Async XLA Ops:
  0.0 2.4 %copy-start = (f32[64,4,512]{2,1,0:T(4,128)S(1)}, f32[64,4,512]{2,1,0:T(4,128)}, u32[]{:S(2)}) copy-start(f32[64,4,512]{2,1,0:T(4,128)} %param.5) | copy-start | bytes 1572868
  3.6 8.6 %copy-start.5 = (s32[64]{0:T(128)S(1)}, s32[64]{0:T(128)}, u32[]{:S(2)}) copy-start(s32[64]{0:T(128)} %param.7) | copy-start | bytes 772
  4.9 33.9 %all-to-all-start = ((f32[128,4,512]{2,1,0:T(4,128)}), f32[128,4,512]{2,1,0:T(4,128)S(1)}, u32[]{:S(2)}, u32[]{:S(2)}) async-start(f32[128,4,512]{2,1,0:T(4,128)} %broadcast_select_fusion), calls=%async_computation | async-start | bytes 2097152 | tf_op jit(solution)/shard_map/all_to_all | solution.py:73
  67.2 4.0 %collective-permute-start = (f32[4,1,16,128]{3,2,1,0:T(8,128)S(1)}, f32[4,1,16,128]{3,2,1,0:T(8,128)S(1)}, u32[]{:S(2)}, u32[]{:S(2)}) collective-permute-start(f32[4,1,16,128]{3,2,1,0:T(8,128)S(1)} %get-tuple-element.18), channel_id=1, source_target_pairs={{0,16},{16,0},{1,17},{17,1},{2,18},{18,2},{3,19},{19,3},{4,20},{20... | collective-permute-start | bytes 98312 | tf_op jit(solution)/shard_map/ppermute | solution.py:24
  67.8 3.9 %collective-permute-start.1 = (f32[4,1,16,128]{3,2,1,0:T(8,128)S(1)}, f32[4,1,16,128]{3,2,1,0:T(8,128)S(1)}, u32[]{:S(2)}, u32[]{:S(2)}) collective-permute-start(f32[4,1,16,128]{3,2,1,0:T(8,128)S(1)} %get-tuple-element.17), channel_id=1, source_target_pairs={{16,0},{0,16},{17,1},{1,17},{18,2},{2,18},{19,3},{3,19},{20,4},{4,... | collective-permute-start | bytes 98312 | tf_op jit(solution)/shard_map/ppermute | solution.py:26
  71.8 3.5 %copy-start.1 = (f32[4,18,16,128]{3,2,1,0:T(8,128)}, f32[4,18,16,128]{3,2,1,0:T(8,128)S(1)}, u32[]{:S(2)}) copy-start(f32[4,18,16,128]{3,2,1,0:T(8,128)S(1)} %constant_dynamic-update-slice_fusion) | copy-start | bytes 1769476
  71.8 3.4 %collective-permute-start.2 = (f32[4,18,1,128]{3,2,1,0:T(1,128)S(1)}, f32[4,18,1,128]{3,2,1,0:T(1,128)S(1)}, u32[]{:S(2)}, u32[]{:S(2)}) collective-permute-start(f32[4,18,1,128]{3,2,1,0:T(1,128)S(1)} %get-tuple-element.13), channel_id=1, source_target_pairs={{0,4},{4,8},{8,12},{12,0},{1,5},{5,9},{9,13},{13,1},{2,6},{6,10},{... | collective-permute-start | bytes 110600 | tf_op jit(solution)/shard_map/ppermute | solution.py:24
  71.9 3.4 %collective-permute-start.3 = (f32[4,18,1,128]{3,2,1,0:T(1,128)S(1)}, f32[4,18,1,128]{3,2,1,0:T(1,128)S(1)}, u32[]{:S(2)}, u32[]{:S(2)}) collective-permute-start(f32[4,18,1,128]{3,2,1,0:T(1,128)S(1)} %get-tuple-element.14), channel_id=1, source_target_pairs={{4,0},{8,4},{12,8},{0,12},{5,1},{9,5},{13,9},{1,13},{6,2},{10,6},{... | collective-permute-start | bytes 110600 | tf_op jit(solution)/shard_map/ppermute | solution.py:26
  76.2 4.0 %collective-permute-start.5 = (f32[4,18,18,1]{2,0,3,1:T(4,128)S(1)}, f32[4,18,18,1]{2,0,3,1:T(4,128)S(1)}, u32[]{:S(2)}, u32[]{:S(2)}) collective-permute-start(f32[4,18,18,1]{2,0,3,1:T(4,128)S(1)} %copy.26), channel_id=1, source_target_pairs={{1,0},{2,1},{3,2},{0,3},{5,4},{6,5},{7,6},{4,7},{9,8},{10,9},{11,1... | collective-permute-start | bytes 15560 | tf_op jit(solution)/shard_map/ppermute | solution.py:26
  76.8 6.0 %collective-permute-start.4 = (f32[4,18,18,1]{2,0,3,1:T(4,128)S(1)}, f32[4,18,18,1]{2,0,3,1:T(4,128)S(1)}, u32[]{:S(2)}, u32[]{:S(2)}) collective-permute-start(f32[4,18,18,1]{2,0,3,1:T(4,128)S(1)} %copy.25), channel_id=1, source_target_pairs={{0,1},{1,2},{2,3},{3,0},{4,5},{5,6},{6,7},{7,4},{8,9},{9,10},{10,1... | collective-permute-start | bytes 15560 | tf_op jit(solution)/shard_map/ppermute | solution.py:24
  80.8 3.8 %copy-start.3 = (f32[4]{0:T(128)S(1)}, f32[4]{0:T(128)}, u32[]{:S(2)}) copy-start(f32[4]{0:T(128)} %constant.42.clone) | copy-start | bytes 52
  84.6 1.1 copy-start.2
  87.4 4.0 %collective-permute-start.6 = (f32[4,1,16,128]{3,2,1,0:T(8,128)S(1)}, f32[4,1,16,128]{3,2,1,0:T(8,128)S(1)}, u32[]{:S(2)}, u32[]{:S(2)}) collective-permute-start(f32[4,1,16,128]{3,2,1,0:T(8,128)S(1)} %get-tuple-element.15), channel_id=1, source_target_pairs={{0,16},{16,0},{1,17},{17,1},{2,18},{18,2},{3,19},{19,3},{4,20},{20... | collective-permute-start | bytes 98312 | tf_op jit(solution)/shard_map/ppermute | solution.py:24
  88.9 3.9 %collective-permute-start.7 = (f32[4,1,16,128]{3,2,1,0:T(8,128)S(1)}, f32[4,1,16,128]{3,2,1,0:T(8,128)S(1)}, u32[]{:S(2)}, u32[]{:S(2)}) collective-permute-start(f32[4,1,16,128]{3,2,1,0:T(8,128)S(1)} %get-tuple-element.16), channel_id=1, source_target_pairs={{16,0},{0,16},{17,1},{1,17},{18,2},{2,18},{19,3},{3,19},{20,4},{4,... | collective-permute-start | bytes 98312 | tf_op jit(solution)/shard_map/ppermute | solution.py:26
  92.9 3.4 %collective-permute-start.8 = (f32[4,18,1,128]{3,2,1,0:T(1,128)S(1)}, f32[4,18,1,128]{3,2,1,0:T(1,128)S(1)}, u32[]{:S(2)}, u32[]{:S(2)}) collective-permute-start(f32[4,18,1,128]{3,2,1,0:T(1,128)S(1)} %get-tuple-element.11), channel_id=1, source_target_pairs={{0,4},{4,8},{8,12},{12,0},{1,5},{5,9},{9,13},{13,1},{2,6},{6,10},{... | collective-permute-start | bytes 110600 | tf_op jit(solution)/shard_map/ppermute | solution.py:24
  93.0 3.4 %collective-permute-start.9 = (f32[4,18,1,128]{3,2,1,0:T(1,128)S(1)}, f32[4,18,1,128]{3,2,1,0:T(1,128)S(1)}, u32[]{:S(2)}, u32[]{:S(2)}) collective-permute-start(f32[4,18,1,128]{3,2,1,0:T(1,128)S(1)} %get-tuple-element.12), channel_id=1, source_target_pairs={{4,0},{8,4},{12,8},{0,12},{5,1},{9,5},{13,9},{1,13},{6,2},{10,6},{... | collective-permute-start | bytes 110600 | tf_op jit(solution)/shard_map/ppermute | solution.py:26
  97.3 4.0 %collective-permute-start.11 = (f32[4,18,18,1]{2,0,3,1:T(4,128)S(1)}, f32[4,18,18,1]{2,0,3,1:T(4,128)S(1)}, u32[]{:S(2)}, u32[]{:S(2)}) collective-permute-start(f32[4,18,18,1]{2,0,3,1:T(4,128)S(1)} %copy.32), channel_id=1, source_target_pairs={{1,0},{2,1},{3,2},{0,3},{5,4},{6,5},{7,6},{4,7},{9,8},{10,9},{11,1... | collective-permute-start | bytes 15560 | tf_op jit(solution)/shard_map/ppermute | solution.py:26
  97.9 5.8 %collective-permute-start.10 = (f32[4,18,18,1]{2,0,3,1:T(4,128)S(1)}, f32[4,18,18,1]{2,0,3,1:T(4,128)S(1)}, u32[]{:S(2)}, u32[]{:S(2)}) collective-permute-start(f32[4,18,18,1]{2,0,3,1:T(4,128)S(1)} %copy.31), channel_id=1, source_target_pairs={{0,1},{1,2},{2,3},{3,0},{4,5},{5,6},{6,7},{7,4},{8,9},{9,10},{10,1... | collective-permute-start | bytes 15560 | tf_op jit(solution)/shard_map/ppermute | solution.py:24
  101.8 2.8 %copy-start.4 = (f32[4]{0:T(128)S(1)}, f32[4]{0:T(128)}, u32[]{:S(2)}) copy-start(f32[4]{0:T(128)} %constant.42.clone) | copy-start | bytes 52
where the time goes:
time: 108 us
  waiting for transfers between devices  41.8 us (39%)
  local copies, waits for them, and re-layouts  28.8 us (27%)
  starting transfers between devices  19.4 us (18%)
  other arithmetic  17.4 us (16%)
    all_to_all x1, waiting for transfers between devices, body(): lax.all_to_all(departing_boxes, ('gx', 'gz'), split_axis=0, concat_axis=0...  26.3 us
    ppermute x6, waiting for transfers between devices, padded(): lax.ppermute(tail, axis, [(i, (i + 1) % count) for i in range(count)])  10.9 us
    transpose x1, local copies, waits for them, and re-layouts, body(): present_state.transpose(3, 0, 4, 1, 5, 2, 6)  8.52 us
    transpose x1, other arithmetic, body(): present_state.transpose(3, 0, 4, 1, 5, 2, 6)  7.6 us
    all_to_all x1, starting transfers between devices, body(): lax.all_to_all(departing_boxes, ('gx', 'gz'), split_axis=0, concat_axis=0...  7.28 us
    ppermute x6, starting transfers between devices, padded(): lax.ppermute(tail, axis, [(i, (i + 1) % count) for i in range(count)])  6.47 us
    reshape x1, local copies, waits for them, and re-layouts, body(): present_state.transpose(3, 0, 4, 1, 5, 2, 6)  6.37 us
    gather x3, local copies, waits for them, and re-layouts, body(): box_rows = jnp.take(arrived, old_owner * capacity + holder_position, axis=0)  5.88 us
  transfers between devices with their start and end apart: 13, of which 11 were waited for; matrix products, arithmetic and copies ran while one was open for 2% of the time, Pallas kernels for 0%

commit v1 on v0

--- a/solution.py
+++ b/solution.py
@@ -1,6 +1,8 @@
 import jax
 import jax.numpy as jnp
 from jax import lax
+from jax.experimental import pallas as pl
+from jax.experimental.pallas import tpu as pltpu
 from jax.sharding import PartitionSpec as P
 
 EDGE = 8
@@ -8,10 +10,16 @@
 BRICK_X = 2
 BRICK_Y = 2
 BRICK_Z = 16
+CELLS = EDGE**3
+LANES = 128
+TILES = CELLS // LANES
 
 
 DIFFUSION = (1.0, 3.3, 0.9, 1.2)
 TIME_STEP = 0.012
+
+VMEM = pl.BlockSpec(memory_space=pltpu.VMEM)
+SMEM = pl.BlockSpec(memory_space=pltpu.SMEM)
 
 
 def padded(cells, sides, width):
@@ -58,27 +66,141 @@
     return padded(present_state, (("gx", 1), ("gy", 2), ("gz", 3)), 1)
 
 
+def rank_table(owner, table, counts, group, capacity, boxes, empty):
+    def clear(i, carry):
+        table[i] = empty
+        return carry
+
+    lax.fori_loop(0, group * capacity, clear, 0)
+    for g in range(group):
+        counts[g] = g * capacity
+
+    def place(b, carry):
+        o = owner[b]
+        slot = counts[o]
+        table[slot] = b
+        counts[o] = slot + 1
+        return carry
+
+    lax.fori_loop(0, boxes, place, 0, unroll=8)
+
+
+def pack_boxes(old_fields, new_owner, me, group, capacity, split):
+    boxes = new_owner.shape[0]
+    pieces = group if split else 1
+    rows = group * capacity // pieces
+
+    def kernel(me_ref, owner, fields, *refs):
+        outs, (table, counts) = refs[:pieces], refs[pieces:]
+        rank_table(owner, table, counts, group, capacity, boxes, 0)
+        for k, out in enumerate(outs):
+            base = (me_ref[0] ^ k) * capacity if split else 0
+
+            def copy(r, carry, out=out, base=base):
+                out[r] = fields[table[base + r]]
+                return carry
+
+            lax.fori_loop(0, rows, copy, 0, unroll=8)
+
+    return pl.pallas_call(
+        kernel,
+        out_shape=[jax.ShapeDtypeStruct((rows,) + old_fields.shape[1:], jnp.float32)] * pieces,
+        in_specs=[SMEM, SMEM, VMEM],
+        out_specs=[VMEM] * pieces,
+        scratch_shapes=[
+            pltpu.SMEM((group * capacity,), jnp.int32),
+            pltpu.SMEM((group,), jnp.int32),
+        ],
+        name="pack_boxes",
+    )(me, new_owner, old_fields)
+
+
+def swap_boxes(columns):
+    lane = lax.broadcasted_iota(jnp.int32, columns[0].shape, 1)
+    for bit in range(4):
+        width = EDGE << bit
+        upper = (lane & width) != 0
+        fresh = list(columns)
+        for low in range(16):
+            if low >> bit & 1:
+                continue
+            high = low | 1 << bit
+            a, b = columns[low], columns[high]
+            fresh[low] = jnp.where(upper, pltpu.roll(b, width, 1), a)
+            fresh[high] = jnp.where(upper, b, pltpu.roll(a, LANES - width, 1))
+        columns = fresh
+    return columns
+
+
+def grid_from_boxes(arrived, old_owner, me, group, capacity, split):
+    boxes = old_owner.shape[0]
+    pieces = len(arrived)
+    rows = group * capacity // pieces
+
+    def kernel(me_ref, owner, *refs):
+        ins, (out, table, counts, held, turned) = refs[:pieces], refs[pieces:]
+        rank_table(owner, table, counts, group, capacity, boxes, boxes)
+        for k, rows_in in enumerate(ins):
+            base = (me_ref[0] ^ k) * capacity if split else 0
+
+            def scatter(r, carry, rows_in=rows_in, base=base):
+                p = table[base + r]
+                for t in range(TILES):
+                    held[p, t // 2, pl.ds(t % 2 * FIELDS, FIELDS), :] = rows_in[
+                        r, :, pl.ds(t * LANES, LANES)
+                    ]
+                return carry
+
+            lax.fori_loop(0, rows, scatter, 0, unroll=4)
+        for bx in range(BRICK_X):
+            for by in range(BRICK_Y):
+                first = (bx * BRICK_Y + by) * BRICK_Z
+                for half in range(TILES // 2):
+                    columns = swap_boxes([held[first + bz, half] for bz in range(BRICK_Z)])
+                    for r in range(16):
+                        turned[pl.ds(r * 8, 8), :] = columns[r]
+                    for t in range(2):
+                        for i in range(2):
+                            x = bx * EDGE + half * 4 + t * 2 + i
+                            for f in range(FIELDS):
+                                out[f, x, pl.ds(by * EDGE, EDGE), :] = turned[
+                                    pl.ds(i * 64 + t * FIELDS + f, 8, stride=8), :
+                                ]
+
+    return pl.pallas_call(
+        kernel,
+        out_shape=jax.ShapeDtypeStruct(
+            (FIELDS, BRICK_X * EDGE, BRICK_Y * EDGE, BRICK_Z * EDGE), jnp.float32
+        ),
+        in_specs=[SMEM, SMEM] + [VMEM] * pieces,
+        out_specs=VMEM,
+        scratch_shapes=[
+            pltpu.SMEM((group * capacity,), jnp.int32),
+            pltpu.SMEM((group,), jnp.int32),
+            pltpu.VMEM((boxes + 1, TILES // 2, 2 * FIELDS, LANES), jnp.float32),
+            pltpu.VMEM((LANES, LANES), jnp.float32),
+        ],
+        name="grid_from_boxes",
+    )(me, old_owner, *arrived)
+
+
 def body(old_fields, new_owner, old_owner):
     group_size = lax.axis_size("gx") * lax.axis_size("gz")
     box_count = new_owner.shape[0]
     capacity = 2 * (box_count // group_size)
-    positions = jnp.arange(box_count, dtype=jnp.int32)
-    earlier = positions[None, :] < positions[:, None]
-    sent_rank = jnp.sum(
-        ((new_owner[None, :] == new_owner[:, None]) & earlier).astype(jnp.int32), axis=1
-    )
-    slot_index = new_owner * capacity + sent_rank
-    filler = jnp.zeros((group_size * capacity,), jnp.int32).at[slot_index].set(positions)
-    departing_boxes = jnp.take(old_fields, filler, axis=0)
-    arrived = lax.all_to_all(departing_boxes, ("gx", "gz"), split_axis=0, concat_axis=0, tiled=True)
-    holder_position = jnp.sum(
-        ((old_owner[None, :] == old_owner[:, None]) & earlier).astype(jnp.int32), axis=1
-    )
-    box_rows = jnp.take(arrived, old_owner * capacity + holder_position, axis=0)
-    present_state = box_rows.reshape(BRICK_X, BRICK_Y, BRICK_Z, FIELDS, EDGE, EDGE, EDGE)
-    present_state = present_state.transpose(3, 0, 4, 1, 5, 2, 6).reshape(
-        FIELDS, BRICK_X * EDGE, BRICK_Y * EDGE, BRICK_Z * EDGE
-    )
+    split = group_size <= 8
+    me = (lax.axis_index("gx") * lax.axis_size("gz") + lax.axis_index("gz")).reshape(1)
+    departing = pack_boxes(old_fields, new_owner, me, group_size, capacity, split)
+    if split:
+        arrived = [departing[0]] + [
+            lax.ppermute(departing[k], ("gx", "gz"), [(i, i ^ k) for i in range(group_size)])
+            for k in range(1, group_size)
+        ]
+    else:
+        arrived = [
+            lax.all_to_all(departing[0], ("gx", "gz"), split_axis=0, concat_axis=0, tiled=True)
+        ]
+    present_state = grid_from_boxes(arrived, old_owner, me, group_size, capacity, split)
     first_section = present_state + TIME_STEP * rates_inside(with_faces(present_state))
     result_fields = 0.5 * present_state + 0.5 * (
         first_section + TIME_STEP * rates_inside(with_faces(first_section))

time: 108 us -> 82.4 us (0.76)
  local copies, waits for them, and re-layouts: 28.8 us -> 6.46 us
  waiting for transfers between devices: 41.8 us -> 30.7 us
  other arithmetic: 17.4 us -> 8.17 us
  starting transfers between devices: 19.4 us -> 28.3 us
  Pallas kernels: 0 us -> 8.33 us
    all_to_all x1 -> x0, waiting for transfers between devices: 26.3 us -> none  [body(): lax.all_to_all(departing_boxes, ('gx', 'gz'), split_axis=0, concat_axis=0...]
    ppermute x0 -> x7, starting transfers between devices: none -> 16.1 us  [body(): lax.ppermute(departing[k], ('gx', 'gz'), [(i, i ^ k) for i in range(group...]
    ppermute x0 -> x7, waiting for transfers between devices: none -> 12.2 us  [body(): lax.ppermute(departing[k], ('gx', 'gz'), [(i, i ^ k) for i in range(group...]
    transpose x1 -> x0, local copies, waits for them, and re-layouts: 8.52 us -> none  [body(): present_state.transpose(3, 0, 4, 1, 5, 2, 6)]
    pallas_call x0 -> x2, Pallas kernels: none -> 8.33 us  [the longest x1 4.93 us: grid_from_boxes(): pl.pallas_call(kernel, out_shape=jax.ShapeDtypeStruct((FIELDS, BRICK_X *...]
    transpose x1 -> x0, other arithmetic: 7.6 us -> none  [body(): present_state.transpose(3, 0, 4, 1, 5, 2, 6)]
    all_to_all x1 -> x0, starting transfers between devices: 7.28 us -> none  [body(): lax.all_to_all(departing_boxes, ('gx', 'gz'), split_axis=0, concat_axis=0...]
    gather x4 -> x0, local copies, waits for them, and re-layouts: 7.07 us -> none  [the longest x3 5.88 us: body(): box_rows = jnp.take(arrived, old_owner * capacity + holder_position, axis=0)]
  transfers between devices with their start and end apart: 13 -> 19, of which waited for: 11 -> 13; matrix products, arithmetic and copies ran while one was open for 2% -> 3% of each run, Pallas kernels for 0% -> 0%
where the time goes in v1:
time: 82.4 us; the launch traced here: 82.1 us
  waiting for transfers between devices  30.7 us (37%)
  starting transfers between devices  28.3 us (34%)
  Pallas kernels  8.33 us (10%)
  other arithmetic  8.17 us (10%)
  local copies, waits for them, and re-layouts  6.46 us (8%)
    ppermute x7, starting transfers between devices, body(): lax.ppermute(departing[k], ('gx', 'gz'), [(i, i ^ k) for i in range(group...  16.1 us
    ppermute x6, waiting for transfers between devices, padded(): lax.ppermute(tail, axis, [(i, (i + 1) % count) for i in range(count)])  14 us
    ppermute x7, waiting for transfers between devices, body(): lax.ppermute(departing[k], ('gx', 'gz'), [(i, i ^ k) for i in range(group...  12.2 us
    ppermute x6, starting transfers between devices, padded(): lax.ppermute(head, axis, [((i + 1) % count, i) for i in range(count)])  8.54 us
    pallas_call x1, Pallas kernels, grid_from_boxes(): pl.pallas_call(kernel, out_shape=jax.ShapeDtypeStruct((FIELDS, BRICK_X *...  4.93 us
    ppermute x6, waiting for transfers between devices, padded(): lax.ppermute(head, axis, [((i + 1) % count, i) for i in range(count)])  4.47 us
    ppermute x6, starting transfers between devices, padded(): lax.ppermute(tail, axis, [(i, (i + 1) % count) for i in range(count)])  3.63 us
    pallas_call x1, Pallas kernels, pack_boxes(): pl.pallas_call(kernel, out_shape=[jax.ShapeDtypeStruct((rows,) + old_fiel...  3.4 us
  transfers between devices with their start and end apart: 19, of which 13 were waited for; matrix products, arithmetic and copies ran while one was open for 3% of the time, Pallas kernels for 0%

profile of v1, /device:TPU:0, one launch (start us, length us, event | category | flops | bytes accessed | tf_op | source)
XLA Modules:
  0.0 82.1 jit_solution(14415015413546998102)
XLA Ops:
  0.0 3.4 %pack_boxes.1 = (f32[16,4,512]{2,1,0:T(4,128)}, f32[16,4,512]{2,1,0:T(4,128)}, f32[16,4,512]{2,1,0:T(4,128)}, f32[16,4,512]{2,1,0:T(4,128)}, f32[16,4,512]{2,1,0...) custom-call(s32[1]{0:T(128)} %bitcast.me_ref, s32[64]{0:T(128)} %owner.2, ...), custom_call_target="tpu_custom_call" | custom-call | tf_op jit(solution)/shard_map/pack_boxes/pallas_call | solution.py:105
  3.4 3.0 %collective-permute-start = (f32[16,4,512]{2,1,0:T(4,128)}, f32[16,4,512]{2,1,0:T(4,128)S(1)}, u32[]{:S(2)}, u32[]{:S(2)}) collective-permute-start(f32[16,4,512]{2,1,0:T(4,128)} %get-tuple-element.14), channel_id=1, source_target_pairs={{0,1},{1,0},{2,3},{3,2},{16,17},{17,16},{18,19},{19,18},{4,5},{5,4... | collective-permute-start | bytes 393224 | tf_op jit(solution)/shard_map/ppermute | solution.py:196
  6.4 2.6 %collective-permute-start.1 = (f32[16,4,512]{2,1,0:T(4,128)}, f32[16,4,512]{2,1,0:T(4,128)S(1)}, u32[]{:S(2)}, u32[]{:S(2)}) collective-permute-start(f32[16,4,512]{2,1,0:T(4,128)} %get-tuple-element.15), channel_id=1, source_target_pairs={{0,2},{1,3},{2,0},{3,1},{16,18},{17,19},{18,16},{19,17},{4,6},{5,7... | collective-permute-start | bytes 393224 | tf_op jit(solution)/shard_map/ppermute | solution.py:196
  9.0 0.0 collective-permute-start.2
  9.0 1.7 %collective-permute-start.3 = (f32[16,4,512]{2,1,0:T(4,128)}, f32[16,4,512]{2,1,0:T(4,128)S(1)}, u32[]{:S(2)}, u32[]{:S(2)}) collective-permute-start(f32[16,4,512]{2,1,0:T(4,128)} %get-tuple-element.17), channel_id=1, source_target_pairs={{0,16},{1,17},{2,18},{3,19},{16,0},{17,1},{18,2},{19,3},{4,20},{5,... | collective-permute-start | bytes 393224 | tf_op jit(solution)/shard_map/ppermute | solution.py:196
  10.8 0.6 collective-permute-start.4
  11.4 0.3 collective-permute-done.refs_1_
  11.7 4.2 %collective-permute-start.5 = (f32[16,4,512]{2,1,0:T(4,128)}, f32[16,4,512]{2,1,0:T(4,128)S(1)}, u32[]{:S(2)}, u32[]{:S(2)}) collective-permute-start(f32[16,4,512]{2,1,0:T(4,128)} %get-tuple-element.19), channel_id=1, source_target_pairs={{0,18},{1,19},{2,16},{3,17},{16,2},{17,3},{18,0},{19,1},{4,22},{5,... | collective-permute-start | bytes 393224 | tf_op jit(solution)/shard_map/ppermute | solution.py:196
  15.8 3.7 %collective-permute-done.1.refs_2_ = f32[16,4,512]{2,1,0:T(4,128)S(1)} collective-permute-done((f32[16,4,512]{2,1,0:T(4,128)}, f32[16,4,512]{2,1,0:T(4,128)S(1)}, u32[]{:S(2)}, u32[]{:S(2)}) %collective-permute-start.1) | collective-permute-done | bytes 131104 | tf_op jit(solution)/shard_map/ppermute | solution.py:196
  19.6 4.0 %collective-permute-start.6 = (f32[16,4,512]{2,1,0:T(4,128)}, f32[16,4,512]{2,1,0:T(4,128)S(1)}, u32[]{:S(2)}, u32[]{:S(2)}) collective-permute-start(f32[16,4,512]{2,1,0:T(4,128)} %get-tuple-element.20), channel_id=1, source_target_pairs={{0,19},{1,18},{2,17},{3,16},{16,3},{17,2},{18,1},{19,0},{4,23},{5,... | collective-permute-start | bytes 393224 | tf_op jit(solution)/shard_map/ppermute | solution.py:196
  23.6 0.0 collective-permute-done.2.refs_3_
  23.6 0.0 collective-permute-done.3.refs_4_
  23.6 0.0 collective-permute-done.4.refs_5_
  23.6 8.1 %collective-permute-done.5.refs_6_ = f32[16,4,512]{2,1,0:T(4,128)S(1)} collective-permute-done((f32[16,4,512]{2,1,0:T(4,128)}, f32[16,4,512]{2,1,0:T(4,128)S(1)}, u32[]{:S(2)}, u32[]{:S(2)}) %collective-permute-start.5) | collective-permute-done | bytes 131104 | tf_op jit(solution)/shard_map/ppermute | solution.py:196
  31.8 0.0 collective-permute-done.6.refs_7_
  31.8 0.0 copy-done.2
  31.8 0.6 copy-done.6
  32.4 0.1 copy-done.7
  32.5 4.9 %grid_from_boxes.1 = f32[4,16,16,128]{3,2,1,0:T(8,128)} custom-call(s32[1]{0:T(128)} %bitcast.me_ref, s32[64]{0:T(128)} %owner.3, f32[16,4,512]{2,1,0:T(4,128)} %get-tuple-element.13.refs_0_, f32[16,4,512]{2,1,0:T(4,128)} %copy-done.1, f32[16,4,512]{2,1,0:T(4,128)} %copy-done.2, f32[16,4,512]{2,1,0:T(4,128)} %copy-done.3, f32[16,4,512]{2,1,0:T(4,128)} %copy-done.4, ...), custom_call_target="tpu_custom_call" | custom-call | tf_op jit(solution)/shard_map/grid_from_boxes/pallas_call | solution.py:170
  37.4 0.8 fusion.57
  38.2 0.5 collective-permute-start.7
  38.7 1.5 %collective-permute-start.8 = (f32[4,1,16,128]{3,2,1,0:T(8,128)S(1)}, f32[4,1,16,128]{3,2,1,0:T(8,128)S(1)}, u32[]{:S(2)}, u32[]{:S(2)}) collective-permute-start(f32[4,1,16,128]{3,2,1,0:T(8,128)S(1)} %get-tuple-element.32), channel_id=1, source_target_pairs={{16,0},{0,16},{17,1},{1,17},{18,2},{2,18},{19,3},{3,19},{20,4},{4,... | collective-permute-start | bytes 98312 | tf_op jit(solution)/shard_map/ppermute | solution.py:34
  40.2 1.9 %collective-permute-done.7 = f32[4,1,16,128]{3,2,1,0:T(8,128)S(1)} collective-permute-done((f32[4,1,16,128]{3,2,1,0:T(8,128)S(1)}, f32[4,1,16,128]{3,2,1,0:T(8,128)S(1)}, u32[]{:S(2)}, u32[]{:S(2)}) %collective-permute-start.7) | collective-permute-done | bytes 32800 | tf_op jit(solution)/shard_map/ppermute | solution.py:32
  42.1 0.5 collective-permute-done.8
  42.6 1.1 %pad_maximum_fusion.55 = (f32[4,18,1,128]{3,2,1,0:T(1,128)S(1)}, f32[4,18,1,128]{3,2,1,0:T(1,128)S(1)}) fusion(f32[4,1,16,128]{3,2,1,0:T(8,128)S(1)} %collective-permute-done.8, f32[4,16,16,128]{3,2,1,0:T(8,128)} %grid_from_boxes.1, f32[4,1,16,128]{3,2,1,0:T(8,128)S(1)} %collective-permute-done.7), kind=kLoop, calls=%fused_computation.125 | loop fusion | flops 36864 | bytes 663552 | tf_op jit(solution)/shard_map/slice | solution.py:29
  43.7 0.1 collective-permute-start.9
  43.8 1.7 %collective-permute-start.10 = (f32[4,18,1,128]{3,2,1,0:T(1,128)S(1)}, f32[4,18,1,128]{3,2,1,0:T(1,128)S(1)}, u32[]{:S(2)}, u32[]{:S(2)}) collective-permute-start(f32[4,18,1,128]{3,2,1,0:T(1,128)S(1)} %get-tuple-element.28), channel_id=1, source_target_pairs={{4,0},{8,4},{12,8},{0,12},{5,1},{9,5},{13,9},{1,13},{6,2},{10,6},{... | collective-permute-start | bytes 110600 | tf_op jit(solution)/shard_map/ppermute | solution.py:34
  45.5 1.6 %collective-permute-done.9 = f32[4,18,1,128]{3,2,1,0:T(1,128)S(1)} collective-permute-done((f32[4,18,1,128]{3,2,1,0:T(1,128)S(1)}, f32[4,18,1,128]{3,2,1,0:T(1,128)S(1)}, u32[]{:S(2)}, u32[]{:S(2)}) %collective-permute-start.9) | collective-permute-done | bytes 36896 | tf_op jit(solution)/shard_map/ppermute | solution.py:32
  47.1 0.0 collective-permute-done.10
  47.1 1.2 %pad_maximum_fusion = f32[4,18,18,128]{3,2,1,0:T(8,128)S(1)} fusion(f32[4,18,1,128]{3,2,1,0:T(1,128)S(1)} %collective-permute-done.10, f32[4,1,16,128]{3,2,1,0:T(8,128)S(1)} %collective-permute-done.8, f32[4,16,16,128]{3,2,1,0:T(8,128)} %grid_from_boxes.1, f32[4,1,16,128]{3,2,1,0:T(8,128)S(1)} %collective-permute-done.7, ...), kind=kLoop, calls=%fused_computation | loop fusion | flops 663552 | bytes 1327104 | tf_op jit(solution)/shard_map/concatenate | solution.py:30
  48.3 0.3 fusion.55
  48.6 0.5 copy.7
  49.2 2.4 %collective-permute-start.12 = (f32[4,18,18,1]{2,0,3,1:T(4,128)S(1)}, f32[4,18,18,1]{2,0,3,1:T(4,128)S(1)}, u32[]{:S(2)}, u32[]{:S(2)}) collective-permute-start(f32[4,18,18,1]{2,0,3,1:T(4,128)S(1)} %copy.7), channel_id=1, source_target_pairs={{1,0},{2,1},{3,2},{0,3},{5,4},{6,5},{7,6},{4,7},{9,8},{10,9},{11,1... | collective-permute-start | bytes 15560 | tf_op jit(solution)/shard_map/ppermute | solution.py:34
  51.5 0.5 copy.6
  52.1 0.0 collective-permute-start.11
  52.1 1.1 %collective-permute-done.12 = f32[4,18,18,1]{2,0,3,1:T(4,128)S(1)} collective-permute-done((f32[4,18,18,1]{2,0,3,1:T(4,128)S(1)}, f32[4,18,18,1]{2,0,3,1:T(4,128)S(1)}, u32[]{:S(2)}, u32[]{:S(2)}) %collective-permute-start.12) | collective-permute-done | bytes 5216 | tf_op jit(solution)/shard_map/ppermute | solution.py:34
  53.2 0.6 copy.9
  53.7 4.2 %collective-permute-done.11 = f32[4,18,18,1]{2,0,3,1:T(4,128)S(1)} collective-permute-done((f32[4,18,18,1]{2,0,3,1:T(4,128)S(1)}, f32[4,18,18,1]{2,0,3,1:T(4,128)S(1)}, u32[]{:S(2)}, u32[]{:S(2)}) %collective-permute-start.11) | collective-permute-done | bytes 5216 | tf_op jit(solution)/shard_map/ppermute | solution.py:32
  58.0 0.6 copy.8
  58.5 0.3 fusion.52
  58.9 0.2 broadcast_multiply_fusion.1
  59.1 2.0 %fusion.31 = f32[4,16,16,128]{3,2,1,0:T(8,128)S(1)} fusion(f32[4,16,16,128]{3,2,1,0:T(8,128)S(1)} %copy-done, f32[4,18,18,1]{3,2,1,0:T(8,128)S(1)} %copy.8, f32[4,18,1,128]{3,2,1,0:T(1,128)S(1)} %collective-permute-done.10, f32[4,18,1,128]{3,2,1,0:T(1,128)S(1)} %collective-permute-done.9, f32[4,1,16,128]{3,2,1,0:T(8,128)S(1)} %collective-permute-done.8, ...), kind=kLoop, calls=%fused_computation.62 | loop fusion | flops 6422528 | bytes 4868224 | tf_op jit(solution)/shard_map/add | solution.py:204
  61.1 1.6 %collective-permute-start.13 = (f32[4,1,16,128]{3,2,1,0:T(8,128)S(1)}, f32[4,1,16,128]{3,2,1,0:T(8,128)S(1)}, u32[]{:S(2)}, u32[]{:S(2)}) collective-permute-start(f32[4,1,16,128]{3,2,1,0:T(8,128)S(1)} %get-tuple-element.29), channel_id=1, source_target_pairs={{0,16},{16,0},{1,17},{17,1},{2,18},{18,2},{3,19},{19,3},{4,20},{20... | collective-permute-start | bytes 98312 | tf_op jit(solution)/shard_map/ppermute | solution.py:32
  62.7 0.5 collective-permute-start.14
  63.2 1.9 %collective-permute-done.13 = f32[4,1,16,128]{3,2,1,0:T(8,128)S(1)} collective-permute-done((f32[4,1,16,128]{3,2,1,0:T(8,128)S(1)}, f32[4,1,16,128]{3,2,1,0:T(8,128)S(1)}, u32[]{:S(2)}, u32[]{:S(2)}) %collective-permute-start.13) | collective-permute-done | bytes 32800 | tf_op jit(solution)/shard_map/ppermute | solution.py:32
  65.1 1.5 %collective-permute-done.14 = f32[4,1,16,128]{3,2,1,0:T(8,128)S(1)} collective-permute-done((f32[4,1,16,128]{3,2,1,0:T(8,128)S(1)}, f32[4,1,16,128]{3,2,1,0:T(8,128)S(1)}, u32[]{:S(2)}, u32[]{:S(2)}) %collective-permute-start.14) | collective-permute-done | bytes 32800 | tf_op jit(solution)/shard_map/ppermute | solution.py:34
  66.6 0.1 pad_maximum_fusion.52
  66.6 0.1 collective-permute-start.15
  66.7 1.7 %collective-permute-start.16 = (f32[4,18,1,128]{3,2,1,0:T(1,128)S(1)}, f32[4,18,1,128]{3,2,1,0:T(1,128)S(1)}, u32[]{:S(2)}, u32[]{:S(2)}) collective-permute-start(f32[4,18,1,128]{3,2,1,0:T(1,128)S(1)} %get-tuple-element.26), channel_id=1, source_target_pairs={{4,0},{8,4},{12,8},{0,12},{5,1},{9,5},{13,9},{1,13},{6,2},{10,6},{... | collective-permute-start | bytes 110600 | tf_op jit(solution)/shard_map/ppermute | solution.py:34
  68.4 1.6 %collective-permute-done.15 = f32[4,18,1,128]{3,2,1,0:T(1,128)S(1)} collective-permute-done((f32[4,18,1,128]{3,2,1,0:T(1,128)S(1)}, f32[4,18,1,128]{3,2,1,0:T(1,128)S(1)}, u32[]{:S(2)}, u32[]{:S(2)}) %collective-permute-start.15) | collective-permute-done | bytes 36896 | tf_op jit(solution)/shard_map/ppermute | solution.py:32
  70.1 0.0 collective-permute-done.16
  70.1 0.1 pad_maximum_fusion.1
  70.2 0.3 fusion.54
  70.5 0.5 copy.13
  71.0 0.7 collective-permute-start.18
  71.7 0.5 copy.12
  72.3 1.4 %collective-permute-start.17 = (f32[4,18,18,1]{2,0,3,1:T(4,128)S(1)}, f32[4,18,18,1]{2,0,3,1:T(4,128)S(1)}, u32[]{:S(2)}, u32[]{:S(2)}) collective-permute-start(f32[4,18,18,1]{2,0,3,1:T(4,128)S(1)} %copy.12), channel_id=1, source_target_pairs={{0,1},{1,2},{2,3},{3,0},{4,5},{5,6},{6,7},{7,4},{8,9},{9,10},{10,1... | collective-permute-start | bytes 15560 | tf_op jit(solution)/shard_map/ppermute | solution.py:32
  73.7 1.4 %collective-permute-done.18 = f32[4,18,18,1]{2,0,3,1:T(4,128)S(1)} collective-permute-done((f32[4,18,18,1]{2,0,3,1:T(4,128)S(1)}, f32[4,18,18,1]{2,0,3,1:T(4,128)S(1)}, u32[]{:S(2)}, u32[]{:S(2)}) %collective-permute-start.18) | collective-permute-done | bytes 5216 | tf_op jit(solution)/shard_map/ppermute | solution.py:34
  75.0 0.6 copy.15
  75.6 2.7 %collective-permute-done.17 = f32[4,18,18,1]{2,0,3,1:T(4,128)S(1)} collective-permute-done((f32[4,18,18,1]{2,0,3,1:T(4,128)S(1)}, f32[4,18,18,1]{2,0,3,1:T(4,128)S(1)}, u32[]{:S(2)}, u32[]{:S(2)}) %collective-permute-start.17) | collective-permute-done | bytes 5216 | tf_op jit(solution)/shard_map/ppermute | solution.py:32
  78.3 0.6 copy.14
  78.9 0.3 fusion.53
  79.2 0.2 broadcast_multiply_fusion
  79.4 2.7 %fusion.6 = f32[4,16,16,128]{3,2,1,0:T(8,128)} fusion(f32[4,16,16,128]{3,2,1,0:T(8,128)S(1)} %copy-done, f32[4,16,16,128]{3,2,1,0:T(8,128)S(1)} %fusion.31, f32[4,18,18,1]{3,2,1,0:T(8,128)S(1)} %copy.14, f32[4,18,1,128]{3,2,1,0:T(1,128)S(1)} %collective-permute-done.16, f32[4,18,1,128]{3,2,1,0:T(1,128)S(1)} %collective-permute-done.15, ...), kind=kLoop, calls=%fused_computation.13 | loop fusion | flops 6684672 | bytes 5392512 | tf_op jit(solution)/shard_map/add | solution.py:205
  (16 shorter events, 0.0 us)
Async XLA Ops:
  3.4 8.3 %collective-permute-start = (f32[16,4,512]{2,1,0:T(4,128)}, f32[16,4,512]{2,1,0:T(4,128)S(1)}, u32[]{:S(2)}, u32[]{:S(2)}) collective-permute-start(f32[16,4,512]{2,1,0:T(4,128)} %get-tuple-element.14), channel_id=1, source_target_pairs={{0,1},{1,0},{2,3},{3,2},{16,17},{17,16},{18,19},{19,18},{4,5},{5,4... | collective-permute-start | bytes 393224 | tf_op jit(solution)/shard_map/ppermute | solution.py:196
  6.4 13.2 %collective-permute-start.1 = (f32[16,4,512]{2,1,0:T(4,128)}, f32[16,4,512]{2,1,0:T(4,128)S(1)}, u32[]{:S(2)}, u32[]{:S(2)}) collective-permute-start(f32[16,4,512]{2,1,0:T(4,128)} %get-tuple-element.15), channel_id=1, source_target_pairs={{0,2},{1,3},{2,0},{3,1},{16,18},{17,19},{18,16},{19,17},{4,6},{5,7... | collective-permute-start | bytes 393224 | tf_op jit(solution)/shard_map/ppermute | solution.py:196
  9.0 14.6 %collective-permute-start.2 = (f32[16,4,512]{2,1,0:T(4,128)}, f32[16,4,512]{2,1,0:T(4,128)S(1)}, u32[]{:S(2)}, u32[]{:S(2)}) collective-permute-start(f32[16,4,512]{2,1,0:T(4,128)} %get-tuple-element.16), channel_id=1, source_target_pairs={{0,3},{1,2},{2,1},{3,0},{16,19},{17,18},{18,17},{19,16},{4,7},{5,6... | collective-permute-start | bytes 393224 | tf_op jit(solution)/shard_map/ppermute | solution.py:196
  9.0 14.6 %collective-permute-start.3 = (f32[16,4,512]{2,1,0:T(4,128)}, f32[16,4,512]{2,1,0:T(4,128)S(1)}, u32[]{:S(2)}, u32[]{:S(2)}) collective-permute-start(f32[16,4,512]{2,1,0:T(4,128)} %get-tuple-element.17), channel_id=1, source_target_pairs={{0,16},{1,17},{2,18},{3,19},{16,0},{17,1},{18,2},{19,3},{4,20},{5,... | collective-permute-start | bytes 393224 | tf_op jit(solution)/shard_map/ppermute | solution.py:196
  10.8 12.8 %collective-permute-start.4 = (f32[16,4,512]{2,1,0:T(4,128)}, f32[16,4,512]{2,1,0:T(4,128)S(1)}, u32[]{:S(2)}, u32[]{:S(2)}) collective-permute-start(f32[16,4,512]{2,1,0:T(4,128)} %get-tuple-element.18), channel_id=1, source_target_pairs={{0,17},{1,16},{2,19},{3,18},{16,1},{17,0},{18,3},{19,2},{4,21},{5,... | collective-permute-start | bytes 393224 | tf_op jit(solution)/shard_map/ppermute | solution.py:196
  11.7 20.1 %copy-start.1 = (f32[16,4,512]{2,1,0:T(4,128)}, f32[16,4,512]{2,1,0:T(4,128)S(1)}, u32[]{:S(2)}) copy-start(f32[16,4,512]{2,1,0:T(4,128)S(1)} %collective-permute-done.refs_1_) | copy-start | bytes 393220
  11.7 20.1 %collective-permute-start.5 = (f32[16,4,512]{2,1,0:T(4,128)}, f32[16,4,512]{2,1,0:T(4,128)S(1)}, u32[]{:S(2)}, u32[]{:S(2)}) collective-permute-start(f32[16,4,512]{2,1,0:T(4,128)} %get-tuple-element.19), channel_id=1, source_target_pairs={{0,18},{1,19},{2,16},{3,17},{16,2},{17,3},{18,0},{19,1},{4,22},{5,... | collective-permute-start | bytes 393224 | tf_op jit(solution)/shard_map/ppermute | solution.py:196
  19.6 12.2 %copy-start.2 = (f32[16,4,512]{2,1,0:T(4,128)}, f32[16,4,512]{2,1,0:T(4,128)S(1)}, u32[]{:S(2)}) copy-start(f32[16,4,512]{2,1,0:T(4,128)S(1)} %collective-permute-done.1.refs_2_) | copy-start | bytes 393220
  19.6 12.2 %collective-permute-start.6 = (f32[16,4,512]{2,1,0:T(4,128)}, f32[16,4,512]{2,1,0:T(4,128)S(1)}, u32[]{:S(2)}, u32[]{:S(2)}) collective-permute-start(f32[16,4,512]{2,1,0:T(4,128)} %get-tuple-element.20), channel_id=1, source_target_pairs={{0,19},{1,18},{2,17},{3,16},{16,3},{17,2},{18,1},{19,0},{4,23},{5,... | collective-permute-start | bytes 393224 | tf_op jit(solution)/shard_map/ppermute | solution.py:196
  23.6 8.2 %copy-start.3 = (f32[16,4,512]{2,1,0:T(4,128)}, f32[16,4,512]{2,1,0:T(4,128)S(1)}, u32[]{:S(2)}) copy-start(f32[16,4,512]{2,1,0:T(4,128)S(1)} %collective-permute-done.2.refs_3_) | copy-start | bytes 393220
  23.6 8.2 %copy-start.4 = (f32[16,4,512]{2,1,0:T(4,128)}, f32[16,4,512]{2,1,0:T(4,128)S(1)}, u32[]{:S(2)}) copy-start(f32[16,4,512]{2,1,0:T(4,128)S(1)} %collective-permute-done.3.refs_4_) | copy-start | bytes 393220
  23.6 8.2 %copy-start.5 = (f32[16,4,512]{2,1,0:T(4,128)}, f32[16,4,512]{2,1,0:T(4,128)S(1)}, u32[]{:S(2)}) copy-start(f32[16,4,512]{2,1,0:T(4,128)S(1)} %collective-permute-done.4.refs_5_) | copy-start | bytes 393220
  31.7 0.7 copy-start.6
  31.8 0.7 copy-start.7
  38.2 3.9 %collective-permute-start.7 = (f32[4,1,16,128]{3,2,1,0:T(8,128)S(1)}, f32[4,1,16,128]{3,2,1,0:T(8,128)S(1)}, u32[]{:S(2)}, u32[]{:S(2)}) collective-permute-start(f32[4,1,16,128]{3,2,1,0:T(8,128)S(1)} %get-tuple-element.31), channel_id=1, source_target_pairs={{0,16},{16,0},{1,17},{17,1},{2,18},{18,2},{3,19},{19,3},{4,20},{20... | collective-permute-start | bytes 98312 | tf_op jit(solution)/shard_map/ppermute | solution.py:32
  38.7 3.9 %collective-permute-start.8 = (f32[4,1,16,128]{3,2,1,0:T(8,128)S(1)}, f32[4,1,16,128]{3,2,1,0:T(8,128)S(1)}, u32[]{:S(2)}, u32[]{:S(2)}) collective-permute-start(f32[4,1,16,128]{3,2,1,0:T(8,128)S(1)} %get-tuple-element.32), channel_id=1, source_target_pairs={{16,0},{0,16},{17,1},{1,17},{18,2},{2,18},{19,3},{3,19},{20,4},{4,... | collective-permute-start | bytes 98312 | tf_op jit(solution)/shard_map/ppermute | solution.py:34
  43.7 3.4 %collective-permute-start.9 = (f32[4,18,1,128]{3,2,1,0:T(1,128)S(1)}, f32[4,18,1,128]{3,2,1,0:T(1,128)S(1)}, u32[]{:S(2)}, u32[]{:S(2)}) collective-permute-start(f32[4,18,1,128]{3,2,1,0:T(1,128)S(1)} %get-tuple-element.27), channel_id=1, source_target_pairs={{0,4},{4,8},{8,12},{12,0},{1,5},{5,9},{9,13},{13,1},{2,6},{6,10},{... | collective-permute-start | bytes 110600 | tf_op jit(solution)/shard_map/ppermute | solution.py:32
  43.8 3.4 %collective-permute-start.10 = (f32[4,18,1,128]{3,2,1,0:T(1,128)S(1)}, f32[4,18,1,128]{3,2,1,0:T(1,128)S(1)}, u32[]{:S(2)}, u32[]{:S(2)}) collective-permute-start(f32[4,18,1,128]{3,2,1,0:T(1,128)S(1)} %get-tuple-element.28), channel_id=1, source_target_pairs={{4,0},{8,4},{12,8},{0,12},{5,1},{9,5},{13,9},{1,13},{6,2},{10,6},{... | collective-permute-start | bytes 110600 | tf_op jit(solution)/shard_map/ppermute | solution.py:34
  48.6 9.9 %copy-start = (f32[4,16,16,128]{3,2,1,0:T(8,128)S(1)}, f32[4,16,16,128]{3,2,1,0:T(8,128)}, u32[]{:S(2)}) copy-start(f32[4,16,16,128]{3,2,1,0:T(8,128)} %grid_from_boxes.1) | copy-start | bytes 1572868
  49.2 4.0 %collective-permute-start.12 = (f32[4,18,18,1]{2,0,3,1:T(4,128)S(1)}, f32[4,18,18,1]{2,0,3,1:T(4,128)S(1)}, u32[]{:S(2)}, u32[]{:S(2)}) collective-permute-start(f32[4,18,18,1]{2,0,3,1:T(4,128)S(1)} %copy.7), channel_id=1, source_target_pairs={{1,0},{2,1},{3,2},{0,3},{5,4},{6,5},{7,6},{4,7},{9,8},{10,9},{11,1... | collective-permute-start | bytes 15560 | tf_op jit(solution)/shard_map/ppermute | solution.py:34
  52.1 5.9 %collective-permute-start.11 = (f32[4,18,18,1]{2,0,3,1:T(4,128)S(1)}, f32[4,18,18,1]{2,0,3,1:T(4,128)S(1)}, u32[]{:S(2)}, u32[]{:S(2)}) collective-permute-start(f32[4,18,18,1]{2,0,3,1:T(4,128)S(1)} %copy.6), channel_id=1, source_target_pairs={{0,1},{1,2},{2,3},{3,0},{4,5},{5,6},{6,7},{7,4},{8,9},{9,10},{10,1... | collective-permute-start | bytes 15560 | tf_op jit(solution)/shard_map/ppermute | solution.py:32
  53.7 5.2 %copy-start.8 = (f32[4]{0:T(128)S(1)}, f32[4]{0:T(128)}, u32[]{:S(2)}) copy-start(f32[4]{0:T(128)} %constant.18.clone) | copy-start | bytes 52
  61.1 4.0 %collective-permute-start.13 = (f32[4,1,16,128]{3,2,1,0:T(8,128)S(1)}, f32[4,1,16,128]{3,2,1,0:T(8,128)S(1)}, u32[]{:S(2)}, u32[]{:S(2)}) collective-permute-start(f32[4,1,16,128]{3,2,1,0:T(8,128)S(1)} %get-tuple-element.29), channel_id=1, source_target_pairs={{0,16},{16,0},{1,17},{17,1},{2,18},{18,2},{3,19},{19,3},{4,20},{20... | collective-permute-start | bytes 98312 | tf_op jit(solution)/shard_map/ppermute | solution.py:32
  62.7 3.9 %collective-permute-start.14 = (f32[4,1,16,128]{3,2,1,0:T(8,128)S(1)}, f32[4,1,16,128]{3,2,1,0:T(8,128)S(1)}, u32[]{:S(2)}, u32[]{:S(2)}) collective-permute-start(f32[4,1,16,128]{3,2,1,0:T(8,128)S(1)} %get-tuple-element.30), channel_id=1, source_target_pairs={{16,0},{0,16},{17,1},{1,17},{18,2},{2,18},{19,3},{3,19},{20,4},{4,... | collective-permute-start | bytes 98312 | tf_op jit(solution)/shard_map/ppermute | solution.py:34
  66.6 3.4 %collective-permute-start.15 = (f32[4,18,1,128]{3,2,1,0:T(1,128)S(1)}, f32[4,18,1,128]{3,2,1,0:T(1,128)S(1)}, u32[]{:S(2)}, u32[]{:S(2)}) collective-permute-start(f32[4,18,1,128]{3,2,1,0:T(1,128)S(1)} %get-tuple-element.25), channel_id=1, source_target_pairs={{0,4},{4,8},{8,12},{12,0},{1,5},{5,9},{9,13},{13,1},{2,6},{6,10},{... | collective-permute-start | bytes 110600 | tf_op jit(solution)/shard_map/ppermute | solution.py:32
  66.7 3.4 %collective-permute-start.16 = (f32[4,18,1,128]{3,2,1,0:T(1,128)S(1)}, f32[4,18,1,128]{3,2,1,0:T(1,128)S(1)}, u32[]{:S(2)}, u32[]{:S(2)}) collective-permute-start(f32[4,18,1,128]{3,2,1,0:T(1,128)S(1)} %get-tuple-element.26), channel_id=1, source_target_pairs={{4,0},{8,4},{12,8},{0,12},{5,1},{9,5},{13,9},{1,13},{6,2},{10,6},{... | collective-permute-start | bytes 110600 | tf_op jit(solution)/shard_map/ppermute | solution.py:34
  71.0 4.0 %collective-permute-start.18 = (f32[4,18,18,1]{2,0,3,1:T(4,128)S(1)}, f32[4,18,18,1]{2,0,3,1:T(4,128)S(1)}, u32[]{:S(2)}, u32[]{:S(2)}) collective-permute-start(f32[4,18,18,1]{2,0,3,1:T(4,128)S(1)} %copy.13), channel_id=1, source_target_pairs={{1,0},{2,1},{3,2},{0,3},{5,4},{6,5},{7,6},{4,7},{9,8},{10,9},{11,1... | collective-permute-start | bytes 15560 | tf_op jit(solution)/shard_map/ppermute | solution.py:34
  72.3 6.1 %collective-permute-start.17 = (f32[4,18,18,1]{2,0,3,1:T(4,128)S(1)}, f32[4,18,18,1]{2,0,3,1:T(4,128)S(1)}, u32[]{:S(2)}, u32[]{:S(2)}) collective-permute-start(f32[4,18,18,1]{2,0,3,1:T(4,128)S(1)} %copy.12), channel_id=1, source_target_pairs={{0,1},{1,2},{2,3},{3,0},{4,5},{5,6},{6,7},{7,4},{8,9},{9,10},{10,1... | collective-permute-start | bytes 15560 | tf_op jit(solution)/shard_map/ppermute | solution.py:32

commit v2 on v1

v2 whole, which is shorter than its diff:
```python
import jax
import jax.numpy as jnp
from jax import lax
from jax.experimental import pallas as pl
from jax.experimental.pallas import tpu as pltpu
from jax.sharding import PartitionSpec as P

EDGE = 8
FIELDS = 4
BRICK_X = 2
BRICK_Y = 2
BRICK_Z = 16
CELLS = EDGE**3
LANES = 128
TILES = CELLS // LANES


DIFFUSION = (1.0, 3.3, 0.9, 1.2)
TIME_STEP = 0.012

VMEM = pl.BlockSpec(memory_space=pltpu.VMEM)
SMEM = pl.BlockSpec(memory_space=pltpu.SMEM)


def rank_table(owner, table, counts, group, capacity, boxes, empty):
    def clear(i, carry):
        table[i] = empty
        return carry

    lax.fori_loop(0, group * capacity, clear, 0)
    for g in range(group):
        counts[g] = g * capacity

    def place(b, carry):
        o = owner[b]
        slot = counts[o]
        table[slot] = b
        counts[o] = slot + 1
        return carry

    lax.fori_loop(0, boxes, place, 0, unroll=8)


def pack_boxes(old_fields, new_owner, me, group, capacity, split):
    boxes = new_owner.shape[0]
    pieces = group if split else 1
    rows = group * capacity // pieces

    def kernel(me_ref, owner, fields, *refs):
        outs, (table, counts) = refs[:pieces], refs[pieces:]
        rank_table(owner, table, counts, group, capacity, boxes, 0)
        for k, out in enumerate(outs):
            base = (me_ref[0] ^ k) * capacity if split else 0

            def copy(r, carry, out=out, base=base):
                out[r] = fields[table[base + r]]
                return carry

            lax.fori_loop(0, rows, copy, 0, unroll=8)

    return pl.pallas_call(
        kernel,
        out_shape=[jax.ShapeDtypeStruct((rows,) + old_fields.shape[1:], jnp.float32)] * pieces,
        in_specs=[SMEM, SMEM, VMEM],
        out_specs=[VMEM] * pieces,
        scratch_shapes=[
            pltpu.SMEM((group * capacity,), jnp.int32),
            pltpu.SMEM((group,), jnp.int32),
        ],
        name="pack_boxes",
    )(me, new_owner, old_fields)


def swap_boxes(columns):
    lane = lax.broadcasted_iota(jnp.int32, columns[0].shape, 1)
    for bit in range(4):
        width = EDGE << bit
        upper = (lane & width) != 0
        fresh = list(columns)
        for low in range(16):
            if low >> bit & 1:
                continue
            high = low | 1 << bit
            a, b = columns[low], columns[high]
            fresh[low] = jnp.where(upper, pltpu.roll(b, width, 1), a)
            fresh[high] = jnp.where(upper, b, pltpu.roll(a, LANES - width, 1))
        columns = fresh
    return columns


def ring(count, step):
    return [(i, (i + step) % count) for i in range(count)]


def boxes_in_place(arrived, old_owner, me, group, capacity, split, joined):
    boxes = old_owner.shape[0]
    pieces = len(arrived)
    rows = group * capacity // pieces
    half = boxes // BRICK_X
    face = (BRICK_Z, BRICK_Y * FIELDS, LANES)
    faces = [jax.ShapeDtypeStruct((2,) + face if joined else face, jnp.float32)] * (2 - joined)

    def kernel(me_ref, owner, *refs):
        ins, refs = refs[:pieces], refs[pieces:]
        held, outs, (table, counts) = refs[0], refs[1 : 1 + len(faces)], refs[1 + len(faces) :]
        rank_table(owner, table, counts, group, capacity, boxes, boxes)
        for k, rows_in in enumerate(ins):
            base = (me_ref[0] ^ k) * capacity if split else 0

            def scatter(r, carry, rows_in=rows_in, base=base):
                p = table[base + r]
                for t in range(TILES):
                    held[p, t // 2, pl.ds(t % 2 * FIELDS, FIELDS), :] = rows_in[
                        r, :, pl.ds(t * LANES, LANES)
                    ]
                return carry

            lax.fori_loop(0, rows, scatter, 0, unroll=4)
        for side in range(2):
            out = outs[0].at[side] if joined else outs[side]
            for by in range(BRICK_Y):
                for bz in range(BRICK_Z):
                    p = side * half + by * BRICK_Z + bz
                    out[bz, pl.ds(by * FIELDS, FIELDS), :] = held[
                        p, side, pl.ds(side * FIELDS, FIELDS), :
                    ]

    return pl.pallas_call(
        kernel,
        out_shape=[
            jax.ShapeDtypeStruct((boxes + 1, TILES // 2, 2 * FIELDS, LANES), jnp.float32)
        ]
        + faces,
        in_specs=[SMEM, SMEM] + [VMEM] * pieces,
        out_specs=[VMEM] * (1 + len(faces)),
        scratch_shapes=[
            pltpu.SMEM((group * capacity,), jnp.int32),
            pltpu.SMEM((group,), jnp.int32),
        ],
        name="boxes_in_place",
    )(me, old_owner, *arrived)


HALO = 2
NX = BRICK_X * EDGE
NY = BRICK_Y * EDGE
WIDE_X = NX + 2 * HALO
WIDE_Y = NY + EDGE
NEAR_X = NX + 2


def lay_out(columns, turned, store):
    columns = swap_boxes(columns)
    for r in range(16):
        turned[pl.ds(r * 8, 8), :] = columns[r]
    for a in range(2):
        for i in range(2):
            for f in range(FIELDS):
                store(a, i, f, turned[pl.ds(i * 64 + a * FIELDS + f, 8, stride=8), :])


def grid_from_boxes(held):
    def kernel(held, grid, turned):
        for bx in range(BRICK_X):
            for by in range(BRICK_Y):
                first = (bx * BRICK_Y + by) * BRICK_Z
                for half in range(TILES // 2):

                    def store(t, i, f, rows, x=bx * EDGE + half * 4, by=by):
                        grid[f, x + t * 2 + i, pl.ds(by * EDGE, EDGE), :] = rows

                    lay_out([held[first + bz, half] for bz in range(BRICK_Z)], turned, store)

    return pl.pallas_call(
        kernel,
        out_shape=jax.ShapeDtypeStruct((FIELDS, NX, NY, LANES), jnp.float32),
        in_specs=[VMEM],
        out_specs=VMEM,
        scratch_shapes=[pltpu.VMEM((LANES, LANES), jnp.float32)],
        cost_estimate=pl.CostEstimate(flops=2**22, bytes_accessed=2**21, transcendentals=0),
        name="grid_from_boxes",
    )(held)


def x_faces_and_y_rows(grid, faces, joined):
    def kernel(grid, *refs):
        ins, (layers, low, high, turned) = refs[: len(faces)], refs[len(faces) :]
        for side in range(2):
            face = ins[0].at[side] if joined else ins[side]

            def store(by, i, f, rows, first=0 if side else HALO):
                layers[f, first + i, pl.ds(by * EDGE, EDGE), :] = rows

            lay_out([face[bz] for bz in range(BRICK_Z)], turned, store)
        for f in range(FIELDS):
            for x in range(NEAR_X):
                cells = layers.at[f, 1 if x == 0 else 2] if x % (NX + 1) == 0 else grid.at[f, x - 1]
                low[f, x] = cells[pl.ds(0, HALO), :]
                high[f, x] = cells[pl.ds(NY - HALO, HALO), :]

    rows = jax.ShapeDtypeStruct((FIELDS, NEAR_X, HALO, LANES), jnp.float32)
    return pl.pallas_call(
        kernel,
        out_shape=[jax.ShapeDtypeStruct((FIELDS, 2 * HALO, NY, LANES), jnp.float32), rows, rows],
        in_specs=[VMEM] * (1 + len(faces)),
        out_specs=[VMEM] * 3,
        scratch_shapes=[pltpu.VMEM((LANES, LANES), jnp.float32)],
        name="x_faces_and_y_rows",
    )(grid, *faces)


def column_places():
    places = {}
    for f in range(FIELDS):
        for x in range(NX):
            places[f, x + 1] = (0, f * NX + x)
        places[f, 0] = (1, f)
        places[f, NEAR_X - 1] = (1, FIELDS + f)
    return places


def z_columns(grid, layers, below, above):
    def kernel(grid, layers, below, above, low, high, halo):
        for f in range(FIELDS):
            for x in range(NEAR_X):
                halo[f, x, pl.ds(0, HALO), :] = above[f, x]
                halo[f, x, pl.ds(EDGE - HALO, HALO), :] = below[f, x]
        for first, count in ((0, NY), (NY, EDGE)):
            pair = lax.broadcasted_iota(jnp.int32, (count, LANES), 1) // HALO
            firsts = [jnp.zeros((count, LANES), jnp.float32)] * 2
            lasts = list(firsts)
            for (f, x), (array, place) in column_places().items():
                if first:
                    cells = halo[f, x]
                elif array:
                    cells = layers[f, 2 if x else 1]
                else:
                    cells = grid[f, x - 1]
                here = pair == place
                moved = pltpu.roll(cells, place * HALO, 1) if place else cells
                firsts[array] = jnp.where(here, moved, firsts[array])
                moved = pltpu.roll(cells, (place * HALO + HALO) % LANES, 1)
                lasts[array] = jnp.where(here, moved, lasts[array])
            for array in range(2):
                low[array, pl.ds(first, count), :] = firsts[array]
                high[array, pl.ds(first, count), :] = lasts[array]

    packed = jax.ShapeDtypeStruct((2, WIDE_Y, LANES), jnp.float32)
    return pl.pallas_call(
        kernel,
        out_shape=[packed, packed],
        in_specs=[VMEM] * 4,
        out_specs=[VMEM] * 2,
        scratch_shapes=[pltpu.VMEM((FIELDS, NEAR_X, EDGE, LANES), jnp.float32)],
        name="z_columns",
    )(grid, layers, below, above)


def half_conductance(v):
    return 0.5 * (v * jnp.sqrt(v))


def whole_grid(grid, layers, below, above):
    def kernel(grid, layers, below, above, whole, halves):
        for f in range(FIELDS):
            for x in range(HALO):
                whole[f, x, pl.ds(0, NY), :] = layers[f, x]
                whole[f, HALO + NX + x, pl.ds(0, NY), :] = layers[f, HALO + x]

        def inside(x, carry):
            for f in range(FIELDS):
                whole[f, x + HALO, pl.ds(0, NY), :] = grid[f, x]
            return carry

        lax.fori_loop(0, NX, inside, 0)

        def beside(x, carry):
            for f in range(FIELDS):
                whole[f, x + 1, pl.ds(NY, HALO), :] = above[f, x]
                whole[f, x + 1, pl.ds(WIDE_Y - HALO, HALO), :] = below[f, x]
            return carry

        lax.fori_loop(0, NEAR_X, beside, 0)

        def conductances(x, carry):
            halves[x] = half_conductance(whole[0, x])
            return carry

        lax.fori_loop(0, WIDE_X, conductances, 0)

    return pl.pallas_call(
        kernel,
        out_shape=[
            jax.ShapeDtypeStruct((FIELDS, WIDE_X, WIDE_Y, LANES), jnp.float32),
            jax.ShapeDtypeStruct((WIDE_X, WIDE_Y, LANES), jnp.float32),
        ],
        in_specs=[VMEM] * 4,
        out_specs=[VMEM] * 2,
        cost_estimate=pl.CostEstimate(flops=2**22, bytes_accessed=2**21, transcendentals=0),
        name="whole_grid",
    )(grid, layers, below, above)


def section(here, beside, across, lane):
    def along_z(cells, other):
        return [
            pltpu.roll(jnp.where(lane == 0, other, cells), LANES - 1, 1),
            pltpu.roll(jnp.where(lane == LANES - 1, other, cells), 1, 1),
        ]

    def along_y(cells):
        return [pltpu.roll(cells, cells.shape[0] - 1, 0), pltpu.roll(cells, 1, 0)]

    cells, s = here
    mean = [s + n for n in along_y(s) + along_z(s, across[1]) + [b[1] for b in beside]]
    rates = []
    for f in range(FIELDS):
        v = cells[f]
        nearby = along_y(v) + along_z(v, across[0][f]) + [b[0][f] for b in beside]
        total = mean[0] * (nearby[0] - v)
        for m, n in zip(mean[1:], nearby[1:]):
            total = total + m * (n - v)
        rates.append(total)
    return rates


def two_sections(grid, halves, below, above):
    def kernel(grid, gs, below, above, out, beyond, first, first_beyond, bs, fs, fbs):
        lane = lax.broadcasted_iota(jnp.int32, (WIDE_Y, LANES), 1)
        packed = [above[0], above[1]], [below[0], below[1]]
        for (f, x), (array, place) in column_places().items():
            after, before = packed[0][array], packed[1][array]
            if place:
                after = pltpu.roll(after, LANES - place * HALO, 1)
            before = pltpu.roll(before, (LANES - HALO - place * HALO) % LANES, 1)
            beyond[f, x] = jnp.where(lane < LANES // 2, after, before)

        def conductances_beyond(x, carry):
            bs[x] = half_conductance(beyond[0, x])
            return carry

        lax.fori_loop(0, NEAR_X, conductances_beyond, 0)

        def at(ref, s, x):
            return [ref[f, x] for f in range(FIELDS)], s[x]

        def step(cells, rates):
            return [
                v + (TIME_STEP * c) * r for v, c, r in zip(cells, DIFFUSION, rates)
            ]

        def first_inside(x, carry):
            here = at(grid, gs, x + 1)
            rates = section(
                here, (at(grid, gs, x), at(grid, gs, x + 2)), at(beyond, bs, x), lane
            )
            fresh = step(here[0], rates)
            for f in range(FIELDS):
                first[f, x] = fresh[f]
            fs[x] = half_conductance(fresh[0])
            return carry

        lax.fori_loop(0, NEAR_X, first_inside, 0)

        def first_outside(x, carry):
            here = at(beyond, bs, x + 1)
            rates = section(
                here, (at(beyond, bs, x), at(beyond, bs, x + 2)), at(grid, gs, x + HALO), lane
            )
            fresh = step(here[0], rates)
            for f in range(FIELDS):
                first_beyond[f, x] = fresh[f]
            fbs[x] = half_conductance(fresh[0])
            return carry

        lax.fori_loop(0, NX, first_outside, 0)

        def second(x, carry):
            here = at(first, fs, x + 1)
            rates = section(
                here, (at(first, fs, x), at(first, fs, x + 2)), at(first_beyond, fbs, x), lane
            )
            fresh = step(here[0], rates)
            for f in range(FIELDS):
                out[f, x] = (0.5 * grid[f, x + HALO] + 0.5 * fresh[f])[:NY]
            return carry

        lax.fori_loop(0, NX, second, 0)

    def scratch(*shape):
        return pltpu.VMEM(shape + (WIDE_Y, LANES), jnp.float32)

    return pl.pallas_call(
        kernel,
        out_shape=jax.ShapeDtypeStruct((FIELDS, NX, NY, LANES), jnp.float32),
        in_specs=[VMEM] * 4,
        out_specs=VMEM,
        scratch_shapes=[
            scratch(FIELDS, NEAR_X),
            scratch(FIELDS, NEAR_X),
            scratch(FIELDS, NX),
            scratch(NEAR_X),
            scratch(NEAR_X),
            scratch(NX),
        ],
        name="two_sections",
    )(grid, halves, below, above)


def body(old_fields, new_owner, old_owner):
    across, along = lax.axis_size("gx"), lax.axis_size("gz")
    group_size = across * along
    box_count = new_owner.shape[0]
    capacity = 2 * (box_count // group_size)
    split = group_size <= 8
    joined = across == 2
    me = (lax.axis_index("gx") * along + lax.axis_index("gz")).reshape(1)
    departing = pack_boxes(old_fields, new_owner, me, group_size, capacity, split)
    if split:
        arrived = [departing[0]] + [
            lax.ppermute(departing[k], ("gx", "gz"), [(i, i ^ k) for i in range(group_size)])
            for k in range(1, group_size)
        ]
    else:
        arrived = [
            lax.all_to_all(departing[0], ("gx", "gz"), split_axis=0, concat_axis=0, tiled=True)
        ]
    held, *faces = boxes_in_place(arrived, old_owner, me, group_size, capacity, split, joined)
    if joined:
        faces = [lax.ppermute(faces[0], "gx", ring(across, 1))]
    else:
        faces = [lax.ppermute(x, "gx", ring(across, step)) for x, step in zip(faces, (-1, 1))]
    grid = grid_from_boxes(held)
    layers, low, high = x_faces_and_y_rows(grid, faces, joined)
    rows = lax.axis_size("gy")
    above = lax.ppermute(low, "gy", ring(rows, -1))
    below = lax.ppermute(high, "gy", ring(rows, 1))
    low, high = z_columns(grid, layers, below, above)
    whole, halves = whole_grid(grid, layers, below, above)
    above = lax.ppermute(low, "gz", ring(along, -1))
    below = lax.ppermute(high, "gz", ring(along, 1))
    return two_sections(whole, halves, below, above)


def solution(mesh):
    return jax.shard_map(
        body,
        mesh=mesh,
        in_specs=(P(("gx", "gy", "gz"), None, None), P(("gx", "gy", "gz")), P(("gx", "gy", "gz"))),
        out_specs=P(None, "gx", "gy", "gz"),
        check_vma=False,
    )
```

time: 82.4 us -> 67 us (0.81)
  Pallas kernels: 8.33 us -> 25.4 us
  waiting for transfers between devices: 30.7 us -> 15.9 us
  other arithmetic: 8.17 us -> 0 us
  starting transfers between devices: 28.3 us -> 22.2 us
  local copies, waits for them, and re-layouts: 6.46 us -> 2.55 us
    pallas_call x1 -> x6, Pallas kernels: 4.93 us -> 22 us  [the longest x1 8.13 us: two_sections(): pl.pallas_call(kernel, out_shape=jax.ShapeDtypeStruct((FIELDS, NX, NY, LA...]
    ppermute x12 -> x5, waiting for transfers between devices: 18.5 us -> 3.76 us  [the longest x1 2.24 us: body(): below = lax.ppermute(high, 'gy', ring(rows, 1))]
    ppermute x12 -> x5, starting transfers between devices: 12.2 us -> 6.07 us  [the longest x1 1.92 us: body(): below = lax.ppermute(high, 'gz', ring(along, 1))]
    add x2 -> x0, other arithmetic: 4.63 us -> none  [the longest x1 2.67 us: body(): 0.5 * present_state]
    slice x8 -> x0, local copies, waits for them, and re-layouts: 3.51 us -> none  [the longest x4 1.85 us: padded(): lax.slice_in_dim(cells, cells.shape[dim] - width, cells.shape[dim], axis=...]
    ppermute x4 -> x0, local copies, waits for them, and re-layouts: 2.25 us -> none  [the longest x2 1.12 us: padded(): lax.ppermute(tail, axis, [(i, (i + 1) % count) for i in range(count)])]
    unnamed x18 -> x24, local copies, waits for them, and re-layouts: 0.7 us -> 2.55 us
    concatenate x2 -> x0, other arithmetic: 1.31 us -> none  [padded(): jnp.concatenate([lax.ppermute(tail, axis, [(i, (i + 1) % count) for i in...]
  transfers between devices with their start and end apart: 19 -> 12, of which waited for: 13 -> 6; matrix products, arithmetic and copies ran while one was open for 3% -> 0% of each run, Pallas kernels for 0% -> 9%
where the time goes in v2:
time: 67 us; the launch traced here: 66.2 us
  Pallas kernels  25.4 us (38%)
  starting transfers between devices  22.2 us (33%)
  waiting for transfers between devices  15.9 us (24%)
  local copies, waits for them, and re-layouts  2.55 us (4%)
    ppermute x7, starting transfers between devices, body(): lax.ppermute(departing[k], ('gx', 'gz'), [(i, i ^ k) for i in range(group...  16.1 us
    ppermute x7, waiting for transfers between devices, body(): lax.ppermute(departing[k], ('gx', 'gz'), [(i, i ^ k) for i in range(group...  12.2 us
    pallas_call x1, Pallas kernels, two_sections(): pl.pallas_call(kernel, out_shape=jax.ShapeDtypeStruct((FIELDS, NX, NY, LA...  8.13 us
    pallas_call x1, Pallas kernels, boxes_in_place(): pl.pallas_call(kernel, out_shape=[jax.ShapeDtypeStruct((boxes + 1, TILES...  3.6 us
    pallas_call x1, Pallas kernels, pack_boxes(): pl.pallas_call(kernel, out_shape=[jax.ShapeDtypeStruct((rows,) + old_fiel...  3.4 us
    pallas_call x1, Pallas kernels, grid_from_boxes(): pl.pallas_call(kernel, out_shape=jax.ShapeDtypeStruct((FIELDS, NX, NY, LA...  3.22 us
    pallas_call x1, Pallas kernels, whole_grid(): pl.pallas_call(kernel, out_shape=[jax.ShapeDtypeStruct((FIELDS, WIDE_X, W...  2.67 us
    unnamed x24, local copies, waits for them, and re-layouts  2.55 us
  transfers between devices with their start and end apart: 12, of which 6 were waited for; matrix products, arithmetic and copies ran while one was open for 0% of the time, Pallas kernels for 9%

profile of v2, /device:TPU:0, one launch (start us, length us, event | category | flops | bytes accessed | tf_op | source)
XLA Modules:
  0.0 66.2 jit_solution(1811521915474557203)
XLA Ops:
  0.0 3.4 %pack_boxes.1 = (f32[16,4,512]{2,1,0:T(4,128)}, f32[16,4,512]{2,1,0:T(4,128)}, f32[16,4,512]{2,1,0:T(4,128)}, f32[16,4,512]{2,1,0:T(4,128)}, f32[16,4,512]{2,1,0...) custom-call(s32[1]{0:T(128)} %bitcast.me_ref, s32[64]{0:T(128)} %owner.2, ...), custom_call_target="tpu_custom_call" | custom-call | tf_op jit(solution)/shard_map/pack_boxes/pallas_call | solution.py:61
  3.4 3.0 %collective-permute-start = (f32[16,4,512]{2,1,0:T(4,128)}, f32[16,4,512]{2,1,0:T(4,128)S(1)}, u32[]{:S(2)}, u32[]{:S(2)}) collective-permute-start(f32[16,4,512]{2,1,0:T(4,128)} %get-tuple-element.23), channel_id=1, source_target_pairs={{0,1},{1,0},{2,3},{3,2},{16,17},{17,16},{18,19},{19,18},{4,5},{5,4... | collective-permute-start | bytes 393224 | tf_op jit(solution)/shard_map/ppermute | solution.py:421
  6.4 2.6 %collective-permute-start.1 = (f32[16,4,512]{2,1,0:T(4,128)}, f32[16,4,512]{2,1,0:T(4,128)S(1)}, u32[]{:S(2)}, u32[]{:S(2)}) collective-permute-start(f32[16,4,512]{2,1,0:T(4,128)} %get-tuple-element.24), channel_id=1, source_target_pairs={{0,2},{1,3},{2,0},{3,1},{16,18},{17,19},{18,16},{19,17},{4,6},{5,7... | collective-permute-start | bytes 393224 | tf_op jit(solution)/shard_map/ppermute | solution.py:421
  9.0 0.0 collective-permute-start.2
  9.0 1.7 %collective-permute-start.3 = (f32[16,4,512]{2,1,0:T(4,128)}, f32[16,4,512]{2,1,0:T(4,128)S(1)}, u32[]{:S(2)}, u32[]{:S(2)}) collective-permute-start(f32[16,4,512]{2,1,0:T(4,128)} %get-tuple-element.26), channel_id=1, source_target_pairs={{0,16},{1,17},{2,18},{3,19},{16,0},{17,1},{18,2},{19,3},{4,20},{5,... | collective-permute-start | bytes 393224 | tf_op jit(solution)/shard_map/ppermute | solution.py:421
  10.8 0.6 collective-permute-start.4
  11.4 0.3 collective-permute-done.refs_1_
  11.7 0.0 copy-start.2
  11.7 4.2 %collective-permute-start.5 = (f32[16,4,512]{2,1,0:T(4,128)}, f32[16,4,512]{2,1,0:T(4,128)S(1)}, u32[]{:S(2)}, u32[]{:S(2)}) collective-permute-start(f32[16,4,512]{2,1,0:T(4,128)} %get-tuple-element.28), channel_id=1, source_target_pairs={{0,18},{1,19},{2,16},{3,17},{16,2},{17,3},{18,0},{19,1},{4,22},{5,... | collective-permute-start | bytes 393224 | tf_op jit(solution)/shard_map/ppermute | solution.py:421
  15.8 3.7 %collective-permute-done.1.refs_2_ = f32[16,4,512]{2,1,0:T(4,128)S(1)} collective-permute-done((f32[16,4,512]{2,1,0:T(4,128)}, f32[16,4,512]{2,1,0:T(4,128)S(1)}, u32[]{:S(2)}, u32[]{:S(2)}) %collective-permute-start.1) | collective-permute-done | bytes 131104 | tf_op jit(solution)/shard_map/ppermute | solution.py:421
  19.6 0.0 copy-start.3
  19.6 4.0 %collective-permute-start.6 = (f32[16,4,512]{2,1,0:T(4,128)}, f32[16,4,512]{2,1,0:T(4,128)S(1)}, u32[]{:S(2)}, u32[]{:S(2)}) collective-permute-start(f32[16,4,512]{2,1,0:T(4,128)} %get-tuple-element.29), channel_id=1, source_target_pairs={{0,19},{1,18},{2,17},{3,16},{16,3},{17,2},{18,1},{19,0},{4,23},{5,... | collective-permute-start | bytes 393224 | tf_op jit(solution)/shard_map/ppermute | solution.py:421
  23.6 0.0 collective-permute-done.2.refs_3_
  23.6 0.0 copy-start.4
  23.6 0.0 collective-permute-done.3.refs_4_
  23.6 0.0 copy-start.5
  23.6 0.0 collective-permute-done.4.refs_5_
  23.6 0.0 copy-start.6
  23.6 8.1 %collective-permute-done.5.refs_6_ = f32[16,4,512]{2,1,0:T(4,128)S(1)} collective-permute-done((f32[16,4,512]{2,1,0:T(4,128)}, f32[16,4,512]{2,1,0:T(4,128)S(1)}, u32[]{:S(2)}, u32[]{:S(2)}) %collective-permute-start.5) | collective-permute-done | bytes 131104 | tf_op jit(solution)/shard_map/ppermute | solution.py:421
  31.8 0.0 copy-start.7
  31.8 0.0 collective-permute-done.6.refs_7_
  31.8 0.0 copy-start.8
  31.8 0.0 copy-done.2
  31.8 0.0 copy-done.3
  31.8 0.0 copy-done.4
  31.8 0.0 copy-done.5
  31.8 0.0 copy-done.6
  31.8 0.6 copy-done.7
  32.4 0.0 copy-done.8
  32.4 3.6 %boxes_in_place.1 = (f32[65,2,8,128]{3,2,1,0:T(8,128)}, f32[2,16,8,128]{3,2,1,0:T(8,128)}) custom-call(s32[1]{0:T(128)} %bitcast.me_ref, s32[64]{0:T(128)} %owner.3, f32[16,4,512]{2,1,0:T(4,128)} %get-tuple-element.22.refs_0_, f32[16,4,512]{2,1,0:T(4,128)} %copy-done.2, f32[16,4,512]{2,1,0:T(4,128)} %copy-done.3, f32[16,4,512]{2,1,0:T(4,128)} %copy-done.4, ...), custom_call_target="tpu_custom_call" | custom-call | tf_op jit(solution)/shard_map/boxes_in_place/pallas_call | solution.py:128
  36.0 0.5 collective-permute-start.7
  36.6 3.2 %grid_from_boxes.1.grid = f32[4,16,16,128]{3,2,1,0:T(8,128)} custom-call(f32[65,2,8,128]{3,2,1,0:T(8,128)} %get-tuple-element.30.held), custom_call_target="tpu_custom_call" | custom-call | flops 4194304 | bytes 2097152 | tf_op jit(solution)/shard_map/grid_from_boxes/pallas_call | solution.py:174
  39.8 1.5 %collective-permute-done.7.refs_0_ = f32[2,16,8,128]{3,2,1,0:T(8,128)S(1)} collective-permute-done((f32[2,16,8,128]{3,2,1,0:T(8,128)}, f32[2,16,8,128]{3,2,1,0:T(8,128)S(1)}, u32[]{:S(2)}, u32[]{:S(2)}) %collective-permute-start.7) | collective-permute-done | bytes 131104 | tf_op jit(solution)/shard_map/ppermute | solution.py:430
  41.2 0.0 copy-start.9
  41.2 0.7 %copy-done.9 = f32[2,16,8,128]{3,2,1,0:T(8,128)} copy-done((f32[2,16,8,128]{3,2,1,0:T(8,128)}, f32[2,16,8,128]{3,2,1,0:T(8,128)S(1)}, u32[]{:S(2)}) %copy-start.9) | copy-done | bytes 131096
  41.9 2.1 %x_faces_and_y_rows.1 = (f32[4,4,16,128]{3,2,1,0:T(8,128)}, f32[4,18,2,128]{3,2,1,0:T(2,128)}, f32[4,18,2,128]{3,2,1,0:T(2,128)}) custom-call(f32[4,16,16,128]{3,2,1,0:T(8,128)} %grid_from_boxes.1.grid, f32[2,16,8,128]{3,2,1,0:T(8,128)} %copy-done.9), custom_call_target="tpu_custom_call" | custom-call | tf_op jit(solution)/shard_map/x_faces_and_y_rows/pallas_call | solution.py:202
  44.0 0.0 collective-permute-start.8
  44.0 1.7 %collective-permute-start.9 = (f32[4,18,2,128]{3,2,1,0:T(2,128)}, f32[4,18,2,128]{3,2,1,0:T(2,128)S(1)}, u32[]{:S(2)}, u32[]{:S(2)}) collective-permute-start(f32[4,18,2,128]{3,2,1,0:T(2,128)} %get-tuple-element.34), channel_id=1, source_target_pairs={{0,12},{4,0},{8,4},{12,8},{1,13},{5,1},{9,5},{13,9},{2,14},{6,2},{... | collective-permute-start | bytes 221192 | tf_op jit(solution)/shard_map/ppermute | solution.py:436
  45.8 2.2 %collective-permute-done.8.below = f32[4,18,2,128]{3,2,1,0:T(2,128)S(1)} collective-permute-done((f32[4,18,2,128]{3,2,1,0:T(2,128)}, f32[4,18,2,128]{3,2,1,0:T(2,128)S(1)}, u32[]{:S(2)}, u32[]{:S(2)}) %collective-permute-start.8) | collective-permute-done | bytes 73760 | tf_op jit(solution)/shard_map/ppermute | solution.py:437
  48.0 0.0 copy-start
  48.0 0.1 collective-permute-done.9.above
  48.1 0.0 copy-start.1
  48.1 0.6 copy-done
  48.6 0.1 copy-done.1
  48.7 2.3 %z_columns.1 = (f32[2,24,128]{2,1,0:T(8,128)}, f32[2,24,128]{2,1,0:T(8,128)}) custom-call(f32[4,16,16,128]{3,2,1,0:T(8,128)} %grid_from_boxes.1.grid, f32[4,4,16,128]{3,2,1,0:T(8,128)} %get-tuple-element.32.layers, f32[4,18,2,128]{3,2,1,0:T(2,128)} %copy-done, f32[4,18,2,128]{3,2,1,0:T(2,128)} %copy-done.1), custom_call_target="tpu_custom_call" | custom-call | tf_op jit(solution)/shard_map/z_columns/pallas_call | solution.py:249
  51.0 1.9 %collective-permute-start.10 = (f32[2,24,128]{2,1,0:T(8,128)}, f32[2,24,128]{2,1,0:T(8,128)S(1)}, u32[]{:S(2)}, u32[]{:S(2)}) collective-permute-start(f32[2,24,128]{2,1,0:T(8,128)} %get-tuple-element.37), channel_id=1, source_target_pairs={{0,1},{1,2},{2,3},{3,0},{4,5},{5,6},{6,7},{7,4},{8,9},{9,10},{10,1... | collective-permute-start | bytes 73736 | tf_op jit(solution)/shard_map/ppermute | solution.py:441
  52.9 1.9 %collective-permute-start.11 = (f32[2,24,128]{2,1,0:T(8,128)}, f32[2,24,128]{2,1,0:T(8,128)S(1)}, u32[]{:S(2)}, u32[]{:S(2)}) collective-permute-start(f32[2,24,128]{2,1,0:T(8,128)} %get-tuple-element.38), channel_id=1, source_target_pairs={{0,3},{1,0},{2,1},{3,2},{4,7},{5,4},{6,5},{7,6},{8,11},{9,8},{10,9... | collective-permute-start | bytes 73736 | tf_op jit(solution)/shard_map/ppermute | solution.py:440
  54.8 2.7 %whole_grid.1 = (f32[4,20,24,128]{3,2,1,0:T(8,128)}, f32[20,24,128]{2,1,0:T(8,128)}) custom-call(f32[4,16,16,128]{3,2,1,0:T(8,128)} %grid_from_boxes.1.grid, f32[4,4,16,128]{3,2,1,0:T(8,128)} %get-tuple-element.32.layers, f32[4,18,2,128]{3,2,1,0:T(2,128)} %copy-done, f32[4,18,2,128]{3,2,1,0:T(2,128)} %copy-done.1), custom_call_target="tpu_custom_call" | custom-call | flops 4194304 | bytes 2097152 | tf_op jit(solution)/shard_map/whole_grid/pallas_call | solution.py:291
  57.4 0.0 collective-permute-done.10.below
  57.4 0.0 copy-start.10
  57.5 0.0 collective-permute-done.11.above
  57.5 0.0 copy-start.11
  57.5 0.6 copy-done.10
  58.0 0.0 copy-done.11
  58.1 8.1 %two_sections.1 = f32[4,16,16,128]{3,2,1,0:T(8,128)} custom-call(f32[4,20,24,128]{3,2,1,0:T(8,128)} %get-tuple-element.35.grid, f32[20,24,128]{2,1,0:T(8,128)} %get-tuple-element.36.gs, f32[2,24,128]{2,1,0:T(8,128)} %copy-done.10, f32[2,24,128]{2,1,0:T(8,128)} %copy-done.11), custom_call_target="tpu_custom_call" | custom-call | tf_op jit(solution)/shard_map/two_sections/pallas_call | solution.py:393
Async XLA Ops:
  3.4 8.3 %collective-permute-start = (f32[16,4,512]{2,1,0:T(4,128)}, f32[16,4,512]{2,1,0:T(4,128)S(1)}, u32[]{:S(2)}, u32[]{:S(2)}) collective-permute-start(f32[16,4,512]{2,1,0:T(4,128)} %get-tuple-element.23), channel_id=1, source_target_pairs={{0,1},{1,0},{2,3},{3,2},{16,17},{17,16},{18,19},{19,18},{4,5},{5,4... | collective-permute-start | bytes 393224 | tf_op jit(solution)/shard_map/ppermute | solution.py:421
  6.4 13.2 %collective-permute-start.1 = (f32[16,4,512]{2,1,0:T(4,128)}, f32[16,4,512]{2,1,0:T(4,128)S(1)}, u32[]{:S(2)}, u32[]{:S(2)}) collective-permute-start(f32[16,4,512]{2,1,0:T(4,128)} %get-tuple-element.24), channel_id=1, source_target_pairs={{0,2},{1,3},{2,0},{3,1},{16,18},{17,19},{18,16},{19,17},{4,6},{5,7... | collective-permute-start | bytes 393224 | tf_op jit(solution)/shard_map/ppermute | solution.py:421
  9.0 14.6 %collective-permute-start.2 = (f32[16,4,512]{2,1,0:T(4,128)}, f32[16,4,512]{2,1,0:T(4,128)S(1)}, u32[]{:S(2)}, u32[]{:S(2)}) collective-permute-start(f32[16,4,512]{2,1,0:T(4,128)} %get-tuple-element.25), channel_id=1, source_target_pairs={{0,3},{1,2},{2,1},{3,0},{16,19},{17,18},{18,17},{19,16},{4,7},{5,6... | collective-permute-start | bytes 393224 | tf_op jit(solution)/shard_map/ppermute | solution.py:421
  9.0 14.6 %collective-permute-start.3 = (f32[16,4,512]{2,1,0:T(4,128)}, f32[16,4,512]{2,1,0:T(4,128)S(1)}, u32[]{:S(2)}, u32[]{:S(2)}) collective-permute-start(f32[16,4,512]{2,1,0:T(4,128)} %get-tuple-element.26), channel_id=1, source_target_pairs={{0,16},{1,17},{2,18},{3,19},{16,0},{17,1},{18,2},{19,3},{4,20},{5,... | collective-permute-start | bytes 393224 | tf_op jit(solution)/shard_map/ppermute | solution.py:421
  10.8 12.8 %collective-permute-start.4 = (f32[16,4,512]{2,1,0:T(4,128)}, f32[16,4,512]{2,1,0:T(4,128)S(1)}, u32[]{:S(2)}, u32[]{:S(2)}) collective-permute-start(f32[16,4,512]{2,1,0:T(4,128)} %get-tuple-element.27), channel_id=1, source_target_pairs={{0,17},{1,16},{2,19},{3,18},{16,1},{17,0},{18,3},{19,2},{4,21},{5,... | collective-permute-start | bytes 393224 | tf_op jit(solution)/shard_map/ppermute | solution.py:421
  11.7 20.1 %copy-start.2 = (f32[16,4,512]{2,1,0:T(4,128)}, f32[16,4,512]{2,1,0:T(4,128)S(1)}, u32[]{:S(2)}) copy-start(f32[16,4,512]{2,1,0:T(4,128)S(1)} %collective-permute-done.refs_1_) | copy-start | bytes 393220
  11.7 20.1 %collective-permute-start.5 = (f32[16,4,512]{2,1,0:T(4,128)}, f32[16,4,512]{2,1,0:T(4,128)S(1)}, u32[]{:S(2)}, u32[]{:S(2)}) collective-permute-start(f32[16,4,512]{2,1,0:T(4,128)} %get-tuple-element.28), channel_id=1, source_target_pairs={{0,18},{1,19},{2,16},{3,17},{16,2},{17,3},{18,0},{19,1},{4,22},{5,... | collective-permute-start | bytes 393224 | tf_op jit(solution)/shard_map/ppermute | solution.py:421
  19.6 12.2 %copy-start.3 = (f32[16,4,512]{2,1,0:T(4,128)}, f32[16,4,512]{2,1,0:T(4,128)S(1)}, u32[]{:S(2)}) copy-start(f32[16,4,512]{2,1,0:T(4,128)S(1)} %collective-permute-done.1.refs_2_) | copy-start | bytes 393220
  19.6 12.2 %collective-permute-start.6 = (f32[16,4,512]{2,1,0:T(4,128)}, f32[16,4,512]{2,1,0:T(4,128)S(1)}, u32[]{:S(2)}, u32[]{:S(2)}) collective-permute-start(f32[16,4,512]{2,1,0:T(4,128)} %get-tuple-element.29), channel_id=1, source_target_pairs={{0,19},{1,18},{2,17},{3,16},{16,3},{17,2},{18,1},{19,0},{4,23},{5,... | collective-permute-start | bytes 393224 | tf_op jit(solution)/shard_map/ppermute | solution.py:421
  23.6 8.2 %copy-start.4 = (f32[16,4,512]{2,1,0:T(4,128)}, f32[16,4,512]{2,1,0:T(4,128)S(1)}, u32[]{:S(2)}) copy-start(f32[16,4,512]{2,1,0:T(4,128)S(1)} %collective-permute-done.2.refs_3_) | copy-start | bytes 393220
  23.6 8.2 %copy-start.5 = (f32[16,4,512]{2,1,0:T(4,128)}, f32[16,4,512]{2,1,0:T(4,128)S(1)}, u32[]{:S(2)}) copy-start(f32[16,4,512]{2,1,0:T(4,128)S(1)} %collective-permute-done.3.refs_4_) | copy-start | bytes 393220
  23.6 8.2 %copy-start.6 = (f32[16,4,512]{2,1,0:T(4,128)}, f32[16,4,512]{2,1,0:T(4,128)S(1)}, u32[]{:S(2)}) copy-start(f32[16,4,512]{2,1,0:T(4,128)S(1)} %collective-permute-done.4.refs_5_) | copy-start | bytes 393220
  31.8 0.6 copy-start.7
  31.8 0.7 %copy-start.8 = (f32[16,4,512]{2,1,0:T(4,128)}, f32[16,4,512]{2,1,0:T(4,128)S(1)}, u32[]{:S(2)}) copy-start(f32[16,4,512]{2,1,0:T(4,128)S(1)} %collective-permute-done.6.refs_7_) | copy-start | bytes 393220
  36.0 5.2 %collective-permute-start.7 = (f32[2,16,8,128]{3,2,1,0:T(8,128)}, f32[2,16,8,128]{3,2,1,0:T(8,128)S(1)}, u32[]{:S(2)}, u32[]{:S(2)}) collective-permute-start(f32[2,16,8,128]{3,2,1,0:T(8,128)} %get-tuple-element.31), channel_id=1, source_target_pairs={{0,16},{16,0},{1,17},{17,1},{2,18},{18,2},{3,19},{19,3},{4,20},{20... | collective-permute-start | bytes 393224 | tf_op jit(solution)/shard_map/ppermute | solution.py:430
  41.2 0.7 %copy-start.9 = (f32[2,16,8,128]{3,2,1,0:T(8,128)}, f32[2,16,8,128]{3,2,1,0:T(8,128)S(1)}, u32[]{:S(2)}) copy-start(f32[2,16,8,128]{3,2,1,0:T(8,128)S(1)} %collective-permute-done.7.refs_0_) | copy-start | bytes 393220
  44.0 4.0 %collective-permute-start.8 = (f32[4,18,2,128]{3,2,1,0:T(2,128)}, f32[4,18,2,128]{3,2,1,0:T(2,128)S(1)}, u32[]{:S(2)}, u32[]{:S(2)}) collective-permute-start(f32[4,18,2,128]{3,2,1,0:T(2,128)} %get-tuple-element.33), channel_id=1, source_target_pairs={{0,4},{4,8},{8,12},{12,0},{1,5},{5,9},{9,13},{13,1},{2,6},{6,10},{... | collective-permute-start | bytes 221192 | tf_op jit(solution)/shard_map/ppermute | solution.py:437
  44.0 4.0 %collective-permute-start.9 = (f32[4,18,2,128]{3,2,1,0:T(2,128)}, f32[4,18,2,128]{3,2,1,0:T(2,128)S(1)}, u32[]{:S(2)}, u32[]{:S(2)}) collective-permute-start(f32[4,18,2,128]{3,2,1,0:T(2,128)} %get-tuple-element.34), channel_id=1, source_target_pairs={{0,12},{4,0},{8,4},{12,8},{1,13},{5,1},{9,5},{13,9},{2,14},{6,2},{... | collective-permute-start | bytes 221192 | tf_op jit(solution)/shard_map/ppermute | solution.py:436
  48.0 0.6 copy-start
  48.1 0.6 copy-start.1
  51.0 6.5 %collective-permute-start.10 = (f32[2,24,128]{2,1,0:T(8,128)}, f32[2,24,128]{2,1,0:T(8,128)S(1)}, u32[]{:S(2)}, u32[]{:S(2)}) collective-permute-start(f32[2,24,128]{2,1,0:T(8,128)} %get-tuple-element.37), channel_id=1, source_target_pairs={{0,1},{1,2},{2,3},{3,0},{4,5},{5,6},{6,7},{7,4},{8,9},{9,10},{10,1... | collective-permute-start | bytes 73736 | tf_op jit(solution)/shard_map/ppermute | solution.py:441
  52.9 4.6 %collective-permute-start.11 = (f32[2,24,128]{2,1,0:T(8,128)}, f32[2,24,128]{2,1,0:T(8,128)S(1)}, u32[]{:S(2)}, u32[]{:S(2)}) collective-permute-start(f32[2,24,128]{2,1,0:T(8,128)} %get-tuple-element.38), channel_id=1, source_target_pairs={{0,3},{1,0},{2,1},{3,2},{4,7},{5,4},{6,5},{7,6},{8,11},{9,8},{10,9... | collective-permute-start | bytes 73736 | tf_op jit(solution)/shard_map/ppermute | solution.py:440
  57.4 0.6 copy-start.10
  57.5 0.6 copy-start.11

commit v3 on v2

--- a/solution.py
+++ b/solution.py
@@ -20,6 +20,7 @@
 
 VMEM = pl.BlockSpec(memory_space=pltpu.VMEM)
 SMEM = pl.BlockSpec(memory_space=pltpu.SMEM)
+ROOM = pltpu.CompilerParams(vmem_limit_bytes=16 * 2**20)
 
 
 def rank_table(owner, table, counts, group, capacity, boxes, empty):
@@ -27,7 +28,7 @@
         table[i] = empty
         return carry
 
-    lax.fori_loop(0, group * capacity, clear, 0)
+    lax.fori_loop(0, group * capacity, clear, 0, unroll=16)
     for g in range(group):
         counts[g] = g * capacity
 
@@ -67,6 +68,7 @@
             pltpu.SMEM((group * capacity,), jnp.int32),
             pltpu.SMEM((group,), jnp.int32),
         ],
+        compiler_params=ROOM,
         name="pack_boxes",
     )(me, new_owner, old_fields)
 
@@ -137,6 +139,7 @@
             pltpu.SMEM((group * capacity,), jnp.int32),
             pltpu.SMEM((group,), jnp.int32),
         ],
+        compiler_params=ROOM,
         name="boxes_in_place",
     )(me, old_owner, *arrived)
 
@@ -178,6 +181,7 @@
         out_specs=VMEM,
         scratch_shapes=[pltpu.VMEM((LANES, LANES), jnp.float32)],
         cost_estimate=pl.CostEstimate(flops=2**22, bytes_accessed=2**21, transcendentals=0),
+        compiler_params=ROOM,
         name="grid_from_boxes",
     )(held)
 
@@ -205,6 +209,7 @@
         in_specs=[VMEM] * (1 + len(faces)),
         out_specs=[VMEM] * 3,
         scratch_shapes=[pltpu.VMEM((LANES, LANES), jnp.float32)],
+        compiler_params=ROOM,
         name="x_faces_and_y_rows",
     )(grid, *faces)
 
@@ -252,6 +257,7 @@
         in_specs=[VMEM] * 4,
         out_specs=[VMEM] * 2,
         scratch_shapes=[pltpu.VMEM((FIELDS, NEAR_X, EDGE, LANES), jnp.float32)],
+        compiler_params=ROOM,
         name="z_columns",
     )(grid, layers, below, above)
 
@@ -272,7 +278,7 @@
                 whole[f, x + HALO, pl.ds(0, NY), :] = grid[f, x]
             return carry
 
-        lax.fori_loop(0, NX, inside, 0)
+        lax.fori_loop(0, NX, inside, 0, unroll=4)
 
         def beside(x, carry):
             for f in range(FIELDS):
@@ -280,13 +286,13 @@
                 whole[f, x + 1, pl.ds(WIDE_Y - HALO, HALO), :] = below[f, x]
             return carry
 
-        lax.fori_loop(0, NEAR_X, beside, 0)
+        lax.fori_loop(0, NEAR_X, beside, 0, unroll=6)
 
         def conductances(x, carry):
             halves[x] = half_conductance(whole[0, x])
             return carry
 
-        lax.fori_loop(0, WIDE_X, conductances, 0)
+        lax.fori_loop(0, WIDE_X, conductances, 0, unroll=5)
 
     return pl.pallas_call(
         kernel,
@@ -297,6 +303,7 @@
         in_specs=[VMEM] * 4,
         out_specs=[VMEM] * 2,
         cost_estimate=pl.CostEstimate(flops=2**22, bytes_accessed=2**21, transcendentals=0),
+        compiler_params=ROOM,
         name="whole_grid",
     )(grid, layers, below, above)
 
@@ -339,7 +346,7 @@
             bs[x] = half_conductance(beyond[0, x])
             return carry
 
-        lax.fori_loop(0, NEAR_X, conductances_beyond, 0)
+        lax.fori_loop(0, NEAR_X, conductances_beyond, 0, unroll=6)
 
         def at(ref, s, x):
             return [ref[f, x] for f in range(FIELDS)], s[x]
@@ -360,7 +367,7 @@
             fs[x] = half_conductance(fresh[0])
             return carry
 
-        lax.fori_loop(0, NEAR_X, first_inside, 0)
+        lax.fori_loop(0, NEAR_X, first_inside, 0, unroll=3)
 
         def first_outside(x, carry):
             here = at(beyond, bs, x + 1)
@@ -373,7 +380,7 @@
             fbs[x] = half_conductance(fresh[0])
             return carry
 
-        lax.fori_loop(0, NX, first_outside, 0)
+        lax.fori_loop(0, NX, first_outside, 0, unroll=4)
 
         def second(x, carry):
             here = at(first, fs, x + 1)
@@ -385,7 +392,7 @@
                 out[f, x] = (0.5 * grid[f, x + HALO] + 0.5 * fresh[f])[:NY]
             return carry
 
-        lax.fori_loop(0, NX, second, 0)
+        lax.fori_loop(0, NX, second, 0, unroll=4)
 
     def scratch(*shape):
         return pltpu.VMEM(shape + (WIDE_Y, LANES), jnp.float32)
@@ -403,6 +410,7 @@
             scratch(NEAR_X),
             scratch(NX),
         ],
+        compiler_params=ROOM,
         name="two_sections",
     )(grid, halves, below, above)
 

time: 67 us -> 52.4 us (0.78)
  Pallas kernels: 25.4 us -> 9.06 us
  waiting for transfers between devices: 15.9 us -> 18.8 us
  local copies, waits for them, and re-layouts: 2.55 us -> 1.7 us
    pallas_call x1, Pallas kernels: 8.13 us -> 4.06 us  [two_sections(): pl.pallas_call(kernel, out_shape=jax.ShapeDtypeStruct((FIELDS, NX, NY, LA...]
    pallas_call x1, Pallas kernels: 2.67 us -> 0.22 us  [whole_grid(): pl.pallas_call(kernel, out_shape=[jax.ShapeDtypeStruct((FIELDS, WIDE_X, W...]
    pallas_call x1, Pallas kernels: 3.6 us -> 1.32 us  [boxes_in_place(): pl.pallas_call(kernel, out_shape=[jax.ShapeDtypeStruct((boxes + 1, TILES...]
    pallas_call x1, Pallas kernels: 3.4 us -> 1.22 us  [pack_boxes(): pl.pallas_call(kernel, out_shape=[jax.ShapeDtypeStruct((rows,) + old_fiel...]
    pallas_call x1, Pallas kernels: 3.22 us -> 1.38 us  [grid_from_boxes(): pl.pallas_call(kernel, out_shape=jax.ShapeDtypeStruct((FIELDS, NX, NY, LA...]
    pallas_call x1, Pallas kernels: 2.12 us -> 0.33 us  [x_faces_and_y_rows(): pl.pallas_call(kernel, out_shape=[jax.ShapeDtypeStruct((FIELDS, 2 * HALO,...]
    pallas_call x1, Pallas kernels: 2.27 us -> 0.53 us  [z_columns(): pl.pallas_call(kernel, out_shape=[packed, packed], in_specs=[VMEM] * 4, o...]
    ppermute x1, waiting for transfers between devices: 1.46 us -> 3.08 us  [body(): faces = [lax.ppermute(faces[0], 'gx', ring(across, 1))]]
  transfers between devices with their start and end apart: 12 -> 12, of which waited for: 6 -> 7; matrix products, arithmetic and copies ran while one was open for 0% -> 0% of each run, Pallas kernels for 9% -> 3%
where the time goes in v3:
time: 52.4 us; the launch traced here: 52.2 us
  starting transfers between devices  22.6 us (43%)
  waiting for transfers between devices  18.8 us (36%)
  Pallas kernels  9.06 us (17%)
  local copies, waits for them, and re-layouts  1.7 us (3%)
    ppermute x7, starting transfers between devices, body(): lax.ppermute(departing[k], ('gx', 'gz'), [(i, i ^ k) for i in range(group...  16.4 us
    ppermute x7, waiting for transfers between devices, body(): lax.ppermute(departing[k], ('gx', 'gz'), [(i, i ^ k) for i in range(group...  11.8 us
    pallas_call x1, Pallas kernels, two_sections(): pl.pallas_call(kernel, out_shape=jax.ShapeDtypeStruct((FIELDS, NX, NY, LA...  4.06 us
    ppermute x1, waiting for transfers between devices, body(): faces = [lax.ppermute(faces[0], 'gx', ring(across, 1))]  3.08 us
    ppermute x1, waiting for transfers between devices, body(): below = lax.ppermute(high, 'gy', ring(rows, 1))  2.03 us
    ppermute x1, starting transfers between devices, body(): below = lax.ppermute(high, 'gz', ring(along, 1))  2.02 us
    ppermute x1, starting transfers between devices, body(): above = lax.ppermute(low, 'gz', ring(along, -1))  1.86 us
    ppermute x1, starting transfers between devices, body(): above = lax.ppermute(low, 'gy', ring(rows, -1))  1.73 us
  transfers between devices with their start and end apart: 12, of which 7 were waited for; matrix products, arithmetic and copies ran while one was open for 0% of the time, Pallas kernels for 3%

profile of v3, /device:TPU:0, one launch (start us, length us, event | category | flops | bytes accessed | tf_op | source)
XLA Modules:
  0.0 52.2 jit_solution(7935003230447957632)
XLA Ops:
  0.0 0.0 copy-start.2
  0.0 0.7 %copy-done.2 = s32[64]{0:T(128)S(1)} copy-done((s32[64]{0:T(128)S(1)}, s32[64]{0:T(128)}, u32[]{:S(2)}) %copy-start.2) | copy-done | bytes 280
  0.7 0.0 copy-start
  0.7 1.0 %copy-done = f32[64,4,512]{2,1,0:T(4,128)S(1)} copy-done((f32[64,4,512]{2,1,0:T(4,128)S(1)}, f32[64,4,512]{2,1,0:T(4,128)}, u32[]{:S(2)}) %copy-start) | copy-done | bytes 524312
  1.7 1.2 %pack_boxes.1 = (f32[16,4,512]{2,1,0:T(4,128)S(1)}, f32[16,4,512]{2,1,0:T(4,128)S(1)}, f32[16,4,512]{2,1,0:T(4,128)S(1)}, f32[16,4,512]{2,1,0:T(4,128)S(1)}, f32...) custom-call(s32[1]{0:T(128)} %bitcast.me_ref, ...), custom_call_target="tpu_custom_call" | custom-call | tf_op jit(solution)/shard_map/pack_boxes/pallas_call | solution.py:62
  2.9 3.1 %collective-permute-start = (f32[16,4,512]{2,1,0:T(4,128)S(1)}, f32[16,4,512]{2,1,0:T(4,128)S(1)}, u32[]{:S(2)}, u32[]{:S(2)}) collective-permute-start(f32[16,4,512]{2,1,0:T(4,128)S(1)} %get-tuple-element.23), channel_id=1, source_target_pairs={{0,1},{1,0},{2,3},{3,2},{16,17},{17,16},{18,19},{19,18},{4,5},{5,4... | collective-permute-start | bytes 393224 | tf_op jit(solution)/shard_map/ppermute | solution.py:429
  6.0 2.6 %collective-permute-start.1 = (f32[16,4,512]{2,1,0:T(4,128)S(1)}, f32[16,4,512]{2,1,0:T(4,128)S(1)}, u32[]{:S(2)}, u32[]{:S(2)}) collective-permute-start(f32[16,4,512]{2,1,0:T(4,128)S(1)} %get-tuple-element.24), channel_id=1, source_target_pairs={{0,2},{1,3},{2,0},{3,1},{16,18},{17,19},{18,16},{19,17},{4,6},{5,7... | collective-permute-start | bytes 393224 | tf_op jit(solution)/shard_map/ppermute | solution.py:429
  8.6 0.0 collective-permute-start.2
  8.6 1.7 %collective-permute-start.3 = (f32[16,4,512]{2,1,0:T(4,128)S(1)}, f32[16,4,512]{2,1,0:T(4,128)S(1)}, u32[]{:S(2)}, u32[]{:S(2)}) collective-permute-start(f32[16,4,512]{2,1,0:T(4,128)S(1)} %get-tuple-element.26), channel_id=1, source_target_pairs={{0,16},{1,17},{2,18},{3,19},{16,0},{17,1},{18,2},{19,3},{4,20},{5,... | collective-permute-start | bytes 393224 | tf_op jit(solution)/shard_map/ppermute | solution.py:429
  10.4 0.6 %collective-permute-start.4 = (f32[16,4,512]{2,1,0:T(4,128)S(1)}, f32[16,4,512]{2,1,0:T(4,128)S(1)}, u32[]{:S(2)}, u32[]{:S(2)}) collective-permute-start(f32[16,4,512]{2,1,0:T(4,128)S(1)} %get-tuple-element.27), channel_id=1, source_target_pairs={{0,17},{1,16},{2,19},{3,18},{16,1},{17,0},{18,3},{19,2},{4,21},{5,... | collective-permute-start | bytes 393224 | tf_op jit(solution)/shard_map/ppermute | solution.py:429
  11.0 0.1 collective-permute-done.refs_1_
  11.1 4.4 %collective-permute-start.5 = (f32[16,4,512]{2,1,0:T(4,128)S(1)}, f32[16,4,512]{2,1,0:T(4,128)S(1)}, u32[]{:S(2)}, u32[]{:S(2)}) collective-permute-start(f32[16,4,512]{2,1,0:T(4,128)S(1)} %get-tuple-element.28), channel_id=1, source_target_pairs={{0,18},{1,19},{2,16},{3,17},{16,2},{17,3},{18,0},{19,1},{4,22},{5,... | collective-permute-start | bytes 393224 | tf_op jit(solution)/shard_map/ppermute | solution.py:429
  15.4 3.5 %collective-permute-done.1.refs_2_ = f32[16,4,512]{2,1,0:T(4,128)S(1)} collective-permute-done((f32[16,4,512]{2,1,0:T(4,128)S(1)}, f32[16,4,512]{2,1,0:T(4,128)S(1)}, u32[]{:S(2)}, u32[]{:S(2)}) %collective-permute-start.1) | collective-permute-done | bytes 131104 | tf_op jit(solution)/shard_map/ppermute | solution.py:429
  19.0 0.0 copy-start.1
  19.0 4.0 %collective-permute-start.6 = (f32[16,4,512]{2,1,0:T(4,128)S(1)}, f32[16,4,512]{2,1,0:T(4,128)S(1)}, u32[]{:S(2)}, u32[]{:S(2)}) collective-permute-start(f32[16,4,512]{2,1,0:T(4,128)S(1)} %get-tuple-element.29), channel_id=1, source_target_pairs={{0,19},{1,18},{2,17},{3,16},{16,3},{17,2},{18,1},{19,0},{4,23},{5,... | collective-permute-start | bytes 393224 | tf_op jit(solution)/shard_map/ppermute | solution.py:429
  22.9 0.0 collective-permute-done.2.refs_3_
  23.0 0.0 collective-permute-done.3.refs_4_
  23.0 0.0 collective-permute-done.4.refs_5_
  23.0 8.2 %collective-permute-done.5.refs_6_ = f32[16,4,512]{2,1,0:T(4,128)S(1)} collective-permute-done((f32[16,4,512]{2,1,0:T(4,128)S(1)}, f32[16,4,512]{2,1,0:T(4,128)S(1)}, u32[]{:S(2)}, u32[]{:S(2)}) %collective-permute-start.5) | collective-permute-done | bytes 131104 | tf_op jit(solution)/shard_map/ppermute | solution.py:429
  31.1 0.0 collective-permute-done.6.refs_7_
  31.1 0.0 copy-done.1
  31.1 1.3 %boxes_in_place.1 = (f32[65,2,8,128]{3,2,1,0:T(8,128)S(1)}, f32[2,16,8,128]{3,2,1,0:T(8,128)S(1)}) custom-call(s32[1]{0:T(128)} %bitcast.me_ref, s32[64]{0:T(128)S(1)} %copy-done.1, f32[16,4,512]{2,1,0:T(4,128)S(1)} %get-tuple-element.22.refs_0_, f32[16,4,512]{2,1,0:T(4,128)S(1)} %collective-permute-done.refs_1_, ...), custom_call_target="tpu_custom_call" | custom-call | tf_op jit(solution)/shard_map/boxes_in_place/pallas_call | solution.py:130
  32.5 0.6 %collective-permute-start.7 = (f32[2,16,8,128]{3,2,1,0:T(8,128)S(1)}, f32[2,16,8,128]{3,2,1,0:T(8,128)S(1)}, u32[]{:S(2)}, u32[]{:S(2)}) collective-permute-start(f32[2,16,8,128]{3,2,1,0:T(8,128)S(1)} %get-tuple-element.31), channel_id=1, source_target_pairs={{0,16},{16,0},{1,17},{17,1},{2,18},{18,2},{3,19},{19,3},{4,20},{20... | collective-permute-start | bytes 393224 | tf_op jit(solution)/shard_map/ppermute | solution.py:438
  33.0 1.4 %grid_from_boxes.1.grid = f32[4,16,16,128]{3,2,1,0:T(8,128)S(1)} custom-call(f32[65,2,8,128]{3,2,1,0:T(8,128)S(1)} %get-tuple-element.30.held), custom_call_target="tpu_custom_call" | custom-call | flops 4194304 | bytes 2097152 | tf_op jit(solution)/shard_map/grid_from_boxes/pallas_call | solution.py:177
  34.4 3.1 %collective-permute-done.7.refs_0_ = f32[2,16,8,128]{3,2,1,0:T(8,128)S(1)} collective-permute-done((f32[2,16,8,128]{3,2,1,0:T(8,128)S(1)}, f32[2,16,8,128]{3,2,1,0:T(8,128)S(1)}, u32[]{:S(2)}, u32[]{:S(2)}) %collective-permute-start.7) | collective-permute-done | bytes 131104 | tf_op jit(solution)/shard_map/ppermute | solution.py:438
  37.5 0.3 x_faces_and_y_rows.1
  37.8 0.1 collective-permute-start.8
  37.9 1.7 %collective-permute-start.9 = (f32[4,18,2,128]{3,2,1,0:T(2,128)S(1)}, f32[4,18,2,128]{3,2,1,0:T(2,128)S(1)}, u32[]{:S(2)}, u32[]{:S(2)}) collective-permute-start(f32[4,18,2,128]{3,2,1,0:T(2,128)S(1)} %get-tuple-element.34), channel_id=1, source_target_pairs={{0,12},{4,0},{8,4},{12,8},{1,13},{5,1},{9,5},{13,9},{2,14},{6,2},{... | collective-permute-start | bytes 221192 | tf_op jit(solution)/shard_map/ppermute | solution.py:444
  39.6 2.0 %collective-permute-done.8.below = f32[4,18,2,128]{3,2,1,0:T(2,128)S(1)} collective-permute-done((f32[4,18,2,128]{3,2,1,0:T(2,128)S(1)}, f32[4,18,2,128]{3,2,1,0:T(2,128)S(1)}, u32[]{:S(2)}, u32[]{:S(2)}) %collective-permute-start.8) | collective-permute-done | bytes 73760 | tf_op jit(solution)/shard_map/ppermute | solution.py:445
  41.7 0.0 collective-permute-done.9.above
  41.7 0.5 %z_columns.1 = (f32[2,24,128]{2,1,0:T(8,128)S(1)}, f32[2,24,128]{2,1,0:T(8,128)S(1)}) custom-call(f32[4,16,16,128]{3,2,1,0:T(8,128)S(1)} %grid_from_boxes.1.grid, f32[4,4,16,128]{3,2,1,0:T(8,128)S(1)} %get-tuple-element.32.layers, f32[4,18,2,128]{3,2,1,0:T(2,128)S(1)} %collective-permute-done.8.below, f32[4,18,2,128]{3,2,1,0:T(2,128)S(1)} %collective-permute-done.9.above), custom_call_target="tpu_custom_call" | custom-call | tf_op jit(solution)/shard_map/z_columns/pallas_call | solution.py:254
  42.2 2.0 %collective-permute-start.10 = (f32[2,24,128]{2,1,0:T(8,128)S(1)}, f32[2,24,128]{2,1,0:T(8,128)S(1)}, u32[]{:S(2)}, u32[]{:S(2)}) collective-permute-start(f32[2,24,128]{2,1,0:T(8,128)S(1)} %get-tuple-element.37), channel_id=1, source_target_pairs={{0,1},{1,2},{2,3},{3,0},{4,5},{5,6},{6,7},{7,4},{8,9},{9,10},{10,1... | collective-permute-start | bytes 73736 | tf_op jit(solution)/shard_map/ppermute | solution.py:449
  44.2 1.9 %collective-permute-start.11 = (f32[2,24,128]{2,1,0:T(8,128)S(1)}, f32[2,24,128]{2,1,0:T(8,128)S(1)}, u32[]{:S(2)}, u32[]{:S(2)}) collective-permute-start(f32[2,24,128]{2,1,0:T(8,128)S(1)} %get-tuple-element.38), channel_id=1, source_target_pairs={{0,3},{1,0},{2,1},{3,2},{4,7},{5,4},{6,5},{7,6},{8,11},{9,8},{10,9... | collective-permute-start | bytes 73736 | tf_op jit(solution)/shard_map/ppermute | solution.py:448
  46.1 0.2 whole_grid.1
  46.3 1.6 %collective-permute-done.10.below = f32[2,24,128]{2,1,0:T(8,128)S(1)} collective-permute-done((f32[2,24,128]{2,1,0:T(8,128)S(1)}, f32[2,24,128]{2,1,0:T(8,128)S(1)}, u32[]{:S(2)}, u32[]{:S(2)}) %collective-permute-start.10) | collective-permute-done | bytes 24608 | tf_op jit(solution)/shard_map/ppermute | solution.py:449
  47.9 0.3 collective-permute-done.11.above
  48.2 4.1 %two_sections.1 = f32[4,16,16,128]{3,2,1,0:T(8,128)} custom-call(f32[4,20,24,128]{3,2,1,0:T(8,128)S(1)} %get-tuple-element.35.grid, f32[20,24,128]{2,1,0:T(8,128)S(1)} %get-tuple-element.36.gs, f32[2,24,128]{2,1,0:T(8,128)S(1)} %collective-permute-done.10.below, f32[2,24,128]{2,1,0:T(8,128)S(1)} %collective-permute-done.11.above), custom_call_target="tpu_custom_call" | custom-call | tf_op jit(solution)/shard_map/two_sections/pallas_call | solution.py:400
Async XLA Ops:
  0.0 0.7 %copy-start.2 = (s32[64]{0:T(128)S(1)}, s32[64]{0:T(128)}, u32[]{:S(2)}) copy-start(s32[64]{0:T(128)} %owner.2) | copy-start | bytes 772
  0.7 1.0 %copy-start = (f32[64,4,512]{2,1,0:T(4,128)S(1)}, f32[64,4,512]{2,1,0:T(4,128)}, u32[]{:S(2)}) copy-start(f32[64,4,512]{2,1,0:T(4,128)} %fields.1) | copy-start | bytes 1572868
  2.9 8.1 %collective-permute-start = (f32[16,4,512]{2,1,0:T(4,128)S(1)}, f32[16,4,512]{2,1,0:T(4,128)S(1)}, u32[]{:S(2)}, u32[]{:S(2)}) collective-permute-start(f32[16,4,512]{2,1,0:T(4,128)S(1)} %get-tuple-element.23), channel_id=1, source_target_pairs={{0,1},{1,0},{2,3},{3,2},{16,17},{17,16},{18,19},{19,18},{4,5},{5,4... | collective-permute-start | bytes 393224 | tf_op jit(solution)/shard_map/ppermute | solution.py:429
  6.0 12.9 %collective-permute-start.1 = (f32[16,4,512]{2,1,0:T(4,128)S(1)}, f32[16,4,512]{2,1,0:T(4,128)S(1)}, u32[]{:S(2)}, u32[]{:S(2)}) collective-permute-start(f32[16,4,512]{2,1,0:T(4,128)S(1)} %get-tuple-element.24), channel_id=1, source_target_pairs={{0,2},{1,3},{2,0},{3,1},{16,18},{17,19},{18,16},{19,17},{4,6},{5,7... | collective-permute-start | bytes 393224 | tf_op jit(solution)/shard_map/ppermute | solution.py:429
  8.6 14.3 %collective-permute-start.2 = (f32[16,4,512]{2,1,0:T(4,128)S(1)}, f32[16,4,512]{2,1,0:T(4,128)S(1)}, u32[]{:S(2)}, u32[]{:S(2)}) collective-permute-start(f32[16,4,512]{2,1,0:T(4,128)S(1)} %get-tuple-element.25), channel_id=1, source_target_pairs={{0,3},{1,2},{2,1},{3,0},{16,19},{17,18},{18,17},{19,16},{4,7},{5,6... | collective-permute-start | bytes 393224 | tf_op jit(solution)/shard_map/ppermute | solution.py:429
  8.6 14.3 %collective-permute-start.3 = (f32[16,4,512]{2,1,0:T(4,128)S(1)}, f32[16,4,512]{2,1,0:T(4,128)S(1)}, u32[]{:S(2)}, u32[]{:S(2)}) collective-permute-start(f32[16,4,512]{2,1,0:T(4,128)S(1)} %get-tuple-element.26), channel_id=1, source_target_pairs={{0,16},{1,17},{2,18},{3,19},{16,0},{17,1},{18,2},{19,3},{4,20},{5,... | collective-permute-start | bytes 393224 | tf_op jit(solution)/shard_map/ppermute | solution.py:429
  10.4 12.6 %collective-permute-start.4 = (f32[16,4,512]{2,1,0:T(4,128)S(1)}, f32[16,4,512]{2,1,0:T(4,128)S(1)}, u32[]{:S(2)}, u32[]{:S(2)}) collective-permute-start(f32[16,4,512]{2,1,0:T(4,128)S(1)} %get-tuple-element.27), channel_id=1, source_target_pairs={{0,17},{1,16},{2,19},{3,18},{16,1},{17,0},{18,3},{19,2},{4,21},{5,... | collective-permute-start | bytes 393224 | tf_op jit(solution)/shard_map/ppermute | solution.py:429
  11.1 20.1 %collective-permute-start.5 = (f32[16,4,512]{2,1,0:T(4,128)S(1)}, f32[16,4,512]{2,1,0:T(4,128)S(1)}, u32[]{:S(2)}, u32[]{:S(2)}) collective-permute-start(f32[16,4,512]{2,1,0:T(4,128)S(1)} %get-tuple-element.28), channel_id=1, source_target_pairs={{0,18},{1,19},{2,16},{3,17},{16,2},{17,3},{18,0},{19,1},{4,22},{5,... | collective-permute-start | bytes 393224 | tf_op jit(solution)/shard_map/ppermute | solution.py:429
  19.0 12.2 %copy-start.1 = (s32[64]{0:T(128)S(1)}, s32[64]{0:T(128)}, u32[]{:S(2)}) copy-start(s32[64]{0:T(128)} %owner.3) | copy-start | bytes 772
  19.0 12.2 %collective-permute-start.6 = (f32[16,4,512]{2,1,0:T(4,128)S(1)}, f32[16,4,512]{2,1,0:T(4,128)S(1)}, u32[]{:S(2)}, u32[]{:S(2)}) collective-permute-start(f32[16,4,512]{2,1,0:T(4,128)S(1)} %get-tuple-element.29), channel_id=1, source_target_pairs={{0,19},{1,18},{2,17},{3,16},{16,3},{17,2},{18,1},{19,0},{4,23},{5,... | collective-permute-start | bytes 393224 | tf_op jit(solution)/shard_map/ppermute | solution.py:429
  32.5 5.0 %collective-permute-start.7 = (f32[2,16,8,128]{3,2,1,0:T(8,128)S(1)}, f32[2,16,8,128]{3,2,1,0:T(8,128)S(1)}, u32[]{:S(2)}, u32[]{:S(2)}) collective-permute-start(f32[2,16,8,128]{3,2,1,0:T(8,128)S(1)} %get-tuple-element.31), channel_id=1, source_target_pairs={{0,16},{16,0},{1,17},{17,1},{2,18},{18,2},{3,19},{19,3},{4,20},{20... | collective-permute-start | bytes 393224 | tf_op jit(solution)/shard_map/ppermute | solution.py:438
  37.8 3.8 %collective-permute-start.8 = (f32[4,18,2,128]{3,2,1,0:T(2,128)S(1)}, f32[4,18,2,128]{3,2,1,0:T(2,128)S(1)}, u32[]{:S(2)}, u32[]{:S(2)}) collective-permute-start(f32[4,18,2,128]{3,2,1,0:T(2,128)S(1)} %get-tuple-element.33), channel_id=1, source_target_pairs={{0,4},{4,8},{8,12},{12,0},{1,5},{5,9},{9,13},{13,1},{2,6},{6,10},{... | collective-permute-start | bytes 221192 | tf_op jit(solution)/shard_map/ppermute | solution.py:445
  37.9 3.8 %collective-permute-start.9 = (f32[4,18,2,128]{3,2,1,0:T(2,128)S(1)}, f32[4,18,2,128]{3,2,1,0:T(2,128)S(1)}, u32[]{:S(2)}, u32[]{:S(2)}) collective-permute-start(f32[4,18,2,128]{3,2,1,0:T(2,128)S(1)} %get-tuple-element.34), channel_id=1, source_target_pairs={{0,12},{4,0},{8,4},{12,8},{1,13},{5,1},{9,5},{13,9},{2,14},{6,2},{... | collective-permute-start | bytes 221192 | tf_op jit(solution)/shard_map/ppermute | solution.py:444
  42.2 5.7 %collective-permute-start.10 = (f32[2,24,128]{2,1,0:T(8,128)S(1)}, f32[2,24,128]{2,1,0:T(8,128)S(1)}, u32[]{:S(2)}, u32[]{:S(2)}) collective-permute-start(f32[2,24,128]{2,1,0:T(8,128)S(1)} %get-tuple-element.37), channel_id=1, source_target_pairs={{0,1},{1,2},{2,3},{3,0},{4,5},{5,6},{6,7},{7,4},{8,9},{9,10},{10,1... | collective-permute-start | bytes 73736 | tf_op jit(solution)/shard_map/ppermute | solution.py:449
  44.2 3.9 %collective-permute-start.11 = (f32[2,24,128]{2,1,0:T(8,128)S(1)}, f32[2,24,128]{2,1,0:T(8,128)S(1)}, u32[]{:S(2)}, u32[]{:S(2)}) collective-permute-start(f32[2,24,128]{2,1,0:T(8,128)S(1)} %get-tuple-element.38), channel_id=1, source_target_pairs={{0,3},{1,0},{2,1},{3,2},{4,7},{5,4},{6,5},{7,6},{8,11},{9,8},{10,9... | collective-permute-start | bytes 73736 | tf_op jit(solution)/shard_map/ppermute | solution.py:448

commit v4 on v3

--- a/solution.py
+++ b/solution.py
@@ -12,8 +12,6 @@
 BRICK_Z = 16
 CELLS = EDGE**3
 LANES = 128
-TILES = CELLS // LANES
-
 
 DIFFUSION = (1.0, 3.3, 0.9, 1.2)
 TIME_STEP = 0.012
@@ -42,35 +40,65 @@
     lax.fori_loop(0, boxes, place, 0, unroll=8)
 
 
-def pack_boxes(old_fields, new_owner, me, group, capacity, split):
+HALVES = ((0, 3), (1, 2))
+
+
+def ranked(new_owner, group, capacity):
     boxes = new_owner.shape[0]
-    pieces = group if split else 1
-    rows = group * capacity // pieces
-
-    def kernel(me_ref, owner, fields, *refs):
-        outs, (table, counts) = refs[:pieces], refs[pieces:]
+
+    def kernel(owner, table, counts):
         rank_table(owner, table, counts, group, capacity, boxes, 0)
+
+    return pl.pallas_call(
+        kernel,
+        out_shape=jax.ShapeDtypeStruct((group * capacity,), jnp.int32),
+        in_specs=[SMEM],
+        out_specs=SMEM,
+        scratch_shapes=[pltpu.SMEM((group,), jnp.int32)],
+        compiler_params=ROOM,
+        cost_estimate=pl.CostEstimate(flops=0, bytes_accessed=2**22, transcendentals=0),
+        name="ranked",
+    )(new_owner)
+
+
+def half_of(ref, half):
+    return ref[half] if isinstance(ref, tuple) else ref.at[:, half]
+
+
+def pieces_of(refs, whole):
+    refs = list(refs)
+    return [refs.pop(0) if one else (refs.pop(0), refs.pop(0)) for one in whole], refs
+
+
+def pack_boxes(old_fields, table, me, rows, capacity, whole):
+    def kernel(me_ref, table, fields, *refs):
+        outs, _ = pieces_of(refs, whole)
         for k, out in enumerate(outs):
-            base = (me_ref[0] ^ k) * capacity if split else 0
+            base = (me_ref[0] ^ k) * capacity if len(whole) > 1 else 0
 
             def copy(r, carry, out=out, base=base):
-                out[r] = fields[table[base + r]]
+                box = table[base + r]
+                for half, pairs in enumerate(HALVES):
+                    for n, t in enumerate(pairs):
+                        half_of(out, half)[r, pl.ds(n * FIELDS, FIELDS), :] = fields[
+                            box, :, pl.ds(t * LANES, LANES)
+                        ]
                 return carry
 
             lax.fori_loop(0, rows, copy, 0, unroll=8)
 
-    return pl.pallas_call(
-        kernel,
-        out_shape=[jax.ShapeDtypeStruct((rows,) + old_fields.shape[1:], jnp.float32)] * pieces,
+    def shape(*halves):
+        return jax.ShapeDtypeStruct((rows,) + halves + (2 * FIELDS, LANES), jnp.float32)
+
+    outs = [x for one in whole for x in ([shape(2)] if one else [shape()] * 2)]
+    return pl.pallas_call(
+        kernel,
+        out_shape=outs,
         in_specs=[SMEM, SMEM, VMEM],
-        out_specs=[VMEM] * pieces,
-        scratch_shapes=[
-            pltpu.SMEM((group * capacity,), jnp.int32),
-            pltpu.SMEM((group,), jnp.int32),
-        ],
+        out_specs=[VMEM] * len(outs),
         compiler_params=ROOM,
         name="pack_boxes",
-    )(me, new_owner, old_fields)
+    )(me, table, old_fields)
 
 
 def swap_boxes(columns):
@@ -94,56 +122,6 @@
     return [(i, (i + step) % count) for i in range(count)]
 
 
-def boxes_in_place(arrived, old_owner, me, group, capacity, split, joined):
-    boxes = old_owner.shape[0]
-    pieces = len(arrived)
-    rows = group * capacity // pieces
-    half = boxes // BRICK_X
-    face = (BRICK_Z, BRICK_Y * FIELDS, LANES)
-    faces = [jax.ShapeDtypeStruct((2,) + face if joined else face, jnp.float32)] * (2 - joined)
-
-    def kernel(me_ref, owner, *refs):
-        ins, refs = refs[:pieces], refs[pieces:]
-        held, outs, (table, counts) = refs[0], refs[1 : 1 + len(faces)], refs[1 + len(faces) :]
-        rank_table(owner, table, counts, group, capacity, boxes, boxes)
-        for k, rows_in in enumerate(ins):
-            base = (me_ref[0] ^ k) * capacity if split else 0
-
-            def scatter(r, carry, rows_in=rows_in, base=base):
-                p = table[base + r]
-                for t in range(TILES):
-                    held[p, t // 2, pl.ds(t % 2 * FIELDS, FIELDS), :] = rows_in[
-                        r, :, pl.ds(t * LANES, LANES)
-                    ]
-                return carry
-
-            lax.fori_loop(0, rows, scatter, 0, unroll=4)
-        for side in range(2):
-            out = outs[0].at[side] if joined else outs[side]
-            for by in range(BRICK_Y):
-                for bz in range(BRICK_Z):
-                    p = side * half + by * BRICK_Z + bz
-                    out[bz, pl.ds(by * FIELDS, FIELDS), :] = held[
-                        p, side, pl.ds(side * FIELDS, FIELDS), :
-                    ]
-
-    return pl.pallas_call(
-        kernel,
-        out_shape=[
-            jax.ShapeDtypeStruct((boxes + 1, TILES // 2, 2 * FIELDS, LANES), jnp.float32)
-        ]
-        + faces,
-        in_specs=[SMEM, SMEM] + [VMEM] * pieces,
-        out_specs=[VMEM] * (1 + len(faces)),
-        scratch_shapes=[
-            pltpu.SMEM((group * capacity,), jnp.int32),
-            pltpu.SMEM((group,), jnp.int32),
-        ],
-        compiler_params=ROOM,
-        name="boxes_in_place",
-    )(me, old_owner, *arrived)
-
-
 HALO = 2
 NX = BRICK_X * EDGE
 NY = BRICK_Y * EDGE
@@ -162,32 +140,103 @@
                 store(a, i, f, turned[pl.ds(i * 64 + a * FIELDS + f, 8, stride=8), :])
 
 
-def grid_from_boxes(held):
-    def kernel(held, grid, turned):
-        for bx in range(BRICK_X):
+def place_rows(ins, held, table, me_ref, capacity):
+    rows = ins[0].shape[0]
+    for k, rows_in in enumerate(ins):
+        base = (me_ref[0] ^ k) * capacity if len(ins) > 1 else 0
+
+        def scatter(r, carry, rows_in=rows_in, base=base):
+            held[table[base + r]] = rows_in[r]
+            return carry
+
+        lax.fori_loop(0, rows, scatter, 0, unroll=8)
+
+
+def lay_out_half(held, turned, part, half):
+    for bx in range(BRICK_X):
+        for by in range(BRICK_Y):
+            first = (bx * BRICK_Y + by) * BRICK_Z
+
+            def store(a, i, f, rows, bx=bx, by=by):
+                part[f, bx * 4 + a * 2 + i, pl.ds(by * EDGE, EDGE), :] = rows
+
+            lay_out([held[first + bz] for bz in range(BRICK_Z)], turned, store)
+
+
+def part_of(x):
+    bx, pair, i = x // EDGE, x % EDGE // 2, x % 2
+    half = 0 if pair in HALVES[0] else 1
+    return half, bx * 4 + HALVES[half].index(pair) * 2 + i
+
+
+PART = jax.ShapeDtypeStruct((FIELDS, NX // 2, NY, LANES), jnp.float32)
+TURNED = pltpu.VMEM((LANES, LANES), jnp.float32)
+
+
+LONG = pl.CostEstimate(flops=0, bytes_accessed=2**26, transcendentals=0)
+
+
+def outer_boxes(arrived, old_owner, me, group, capacity, whole, joined):
+    boxes = old_owner.shape[0]
+    pieces = len(arrived)
+    half = boxes // BRICK_X
+    face = (BRICK_Z, BRICK_Y * FIELDS, LANES)
+    faces = [jax.ShapeDtypeStruct((2,) + face if joined else face, jnp.float32)] * (2 - joined)
+
+    def kernel(me_ref, owner, *refs):
+        ins = [ref.at[:, 0] if one else ref for ref, one in zip(refs, whole)]
+        refs = refs[pieces:]
+        (table, part), outs = refs[:2], refs[2 : 2 + len(faces)]
+        counts, held, turned = refs[2 + len(faces) :]
+        rank_table(owner, table, counts, group, capacity, boxes, boxes)
+        place_rows(ins, held, table, me_ref, capacity)
+        for side in range(2):
+            out = outs[0].at[side] if joined else outs[side]
             for by in range(BRICK_Y):
-                first = (bx * BRICK_Y + by) * BRICK_Z
-                for half in range(TILES // 2):
-
-                    def store(t, i, f, rows, x=bx * EDGE + half * 4, by=by):
-                        grid[f, x + t * 2 + i, pl.ds(by * EDGE, EDGE), :] = rows
-
-                    lay_out([held[first + bz, half] for bz in range(BRICK_Z)], turned, store)
-
-    return pl.pallas_call(
-        kernel,
-        out_shape=jax.ShapeDtypeStruct((FIELDS, NX, NY, LANES), jnp.float32),
-        in_specs=[VMEM],
+                for bz in range(BRICK_Z):
+                    p = side * half + by * BRICK_Z + bz
+                    out[bz, pl.ds(by * FIELDS, FIELDS), :] = held[p, pl.ds(side * FIELDS, FIELDS), :]
+        lay_out_half(held, turned, part, 0)
+
+    return pl.pallas_call(
+        kernel,
+        out_shape=[jax.ShapeDtypeStruct((group * capacity,), jnp.int32), PART] + faces,
+        in_specs=[SMEM, SMEM] + [VMEM] * pieces,
+        out_specs=[SMEM] + [VMEM] * (1 + len(faces)),
+        scratch_shapes=[
+            pltpu.SMEM((group,), jnp.int32),
+            pltpu.VMEM((boxes + 1, 2 * FIELDS, LANES), jnp.float32),
+            TURNED,
+        ],
+        compiler_params=ROOM,
+        cost_estimate=LONG,
+        name="outer_boxes",
+    )(me, old_owner, *arrived)
+
+
+def inner_boxes(arrived, table, me, boxes, capacity, whole):
+    pieces = len(arrived)
+
+    def kernel(me_ref, table, *refs):
+        ins = [ref.at[:, 1] if one else ref for ref, one in zip(refs, whole)]
+        inner, held, turned = refs[pieces:]
+        place_rows(ins, held, table, me_ref, capacity)
+        lay_out_half(held, turned, inner, 1)
+
+    return pl.pallas_call(
+        kernel,
+        out_shape=PART,
+        in_specs=[SMEM, SMEM] + [VMEM] * pieces,
         out_specs=VMEM,
-        scratch_shapes=[pltpu.VMEM((LANES, LANES), jnp.float32)],
-        cost_estimate=pl.CostEstimate(flops=2**22, bytes_accessed=2**21, transcendentals=0),
-        compiler_params=ROOM,
-        name="grid_from_boxes",
-    )(held)
-
-
-def x_faces_and_y_rows(grid, faces, joined):
-    def kernel(grid, *refs):
+        scratch_shapes=[pltpu.VMEM((boxes + 1, 2 * FIELDS, LANES), jnp.float32), TURNED],
+        compiler_params=ROOM,
+        cost_estimate=LONG,
+        name="inner_boxes",
+    )(me, table, *arrived)
+
+
+def x_layers_and_y_rows(parts, faces, joined):
+    def kernel(outer, inner, *refs):
         ins, (layers, low, high, turned) = refs[: len(faces)], refs[len(faces) :]
         for side in range(2):
             face = ins[0].at[side] if joined else ins[side]
@@ -198,7 +247,11 @@
             lay_out([face[bz] for bz in range(BRICK_Z)], turned, store)
         for f in range(FIELDS):
             for x in range(NEAR_X):
-                cells = layers.at[f, 1 if x == 0 else 2] if x % (NX + 1) == 0 else grid.at[f, x - 1]
+                if x % (NX + 1) == 0:
+                    cells = layers.at[f, 2 if x else 1]
+                else:
+                    half, layer = part_of(x - 1)
+                    cells = (outer, inner)[half].at[f, layer]
                 low[f, x] = cells[pl.ds(0, HALO), :]
                 high[f, x] = cells[pl.ds(NY - HALO, HALO), :]
 
@@ -206,12 +259,12 @@
     return pl.pallas_call(
         kernel,
         out_shape=[jax.ShapeDtypeStruct((FIELDS, 2 * HALO, NY, LANES), jnp.float32), rows, rows],
-        in_specs=[VMEM] * (1 + len(faces)),
+        in_specs=[VMEM] * (2 + len(faces)),
         out_specs=[VMEM] * 3,
-        scratch_shapes=[pltpu.VMEM((LANES, LANES), jnp.float32)],
-        compiler_params=ROOM,
-        name="x_faces_and_y_rows",
-    )(grid, *faces)
+        scratch_shapes=[TURNED],
+        compiler_params=ROOM,
+        name="x_layers_and_y_rows",
+    )(*parts, *faces)
 
 
 def column_places():
@@ -224,8 +277,8 @@
     return places
 
 
-def z_columns(grid, layers, below, above):
-    def kernel(grid, layers, below, above, low, high, halo):
+def z_columns(parts, layers, below, above):
+    def kernel(outer, inner, layers, below, above, low, high, halo):
         for f in range(FIELDS):
             for x in range(NEAR_X):
                 halo[f, x, pl.ds(0, HALO), :] = above[f, x]
@@ -240,7 +293,8 @@
                 elif array:
                     cells = layers[f, 2 if x else 1]
                 else:
-                    cells = grid[f, x - 1]
+                    half, layer = part_of(x - 1)
+                    cells = (outer, inner)[half][f, layer]
                 here = pair == place
                 moved = pltpu.roll(cells, place * HALO, 1) if place else cells
                 firsts[array] = jnp.where(here, moved, firsts[array])
@@ -254,31 +308,29 @@
     return pl.pallas_call(
         kernel,
         out_shape=[packed, packed],
-        in_specs=[VMEM] * 4,
+        in_specs=[VMEM] * 5,
         out_specs=[VMEM] * 2,
         scratch_shapes=[pltpu.VMEM((FIELDS, NEAR_X, EDGE, LANES), jnp.float32)],
         compiler_params=ROOM,
         name="z_columns",
-    )(grid, layers, below, above)
+    )(*parts, layers, below, above)
 
 
 def half_conductance(v):
     return 0.5 * (v * jnp.sqrt(v))
 
 
-def whole_grid(grid, layers, below, above):
-    def kernel(grid, layers, below, above, whole, halves):
+def whole_grid(parts, layers, below, above):
+    def kernel(outer, inner, layers, below, above, whole, halves):
         for f in range(FIELDS):
             for x in range(HALO):
                 whole[f, x, pl.ds(0, NY), :] = layers[f, x]
                 whole[f, HALO + NX + x, pl.ds(0, NY), :] = layers[f, HALO + x]
 
-        def inside(x, carry):
+        for x in range(NX):
+            half, layer = part_of(x)
             for f in range(FIELDS):
-                whole[f, x + HALO, pl.ds(0, NY), :] = grid[f, x]
-            return carry
-
-        lax.fori_loop(0, NX, inside, 0, unroll=4)
+                whole[f, x + HALO, pl.ds(0, NY), :] = (outer, inner)[half][f, layer]
 
         def beside(x, carry):
             for f in range(FIELDS):
@@ -300,12 +352,12 @@
             jax.ShapeDtypeStruct((FIELDS, WIDE_X, WIDE_Y, LANES), jnp.float32),
             jax.ShapeDtypeStruct((WIDE_X, WIDE_Y, LANES), jnp.float32),
         ],
-        in_specs=[VMEM] * 4,
+        in_specs=[VMEM] * 5,
         out_specs=[VMEM] * 2,
         cost_estimate=pl.CostEstimate(flops=2**22, bytes_accessed=2**21, transcendentals=0),
         compiler_params=ROOM,
         name="whole_grid",
-    )(grid, layers, below, above)
+    )(*parts, layers, below, above)
 
 
 def section(here, beside, across, lane):
@@ -421,30 +473,46 @@
     box_count = new_owner.shape[0]
     capacity = 2 * (box_count // group_size)
     split = group_size <= 8
-    joined = across == 2
+    joined = False
     me = (lax.axis_index("gx") * along + lax.axis_index("gz")).reshape(1)
-    departing = pack_boxes(old_fields, new_owner, me, group_size, capacity, split)
+    table = ranked(new_owner, group_size, capacity)
     if split:
-        arrived = [departing[0]] + [
-            lax.ppermute(departing[k], ("gx", "gz"), [(i, i ^ k) for i in range(group_size)])
-            for k in range(1, group_size)
-        ]
+        far = [k for k in range(group_size) if k % along >= along // 2]
+        whole = [k not in far for k in range(group_size)]
+        rows = capacity
     else:
-        arrived = [
-            lax.all_to_all(departing[0], ("gx", "gz"), split_axis=0, concat_axis=0, tiled=True)
-        ]
-    held, *faces = boxes_in_place(arrived, old_owner, me, group_size, capacity, split, joined)
+        far, whole, rows = [], [False], group_size * capacity
+    sent, _ = pieces_of(pack_boxes(old_fields, table, me, rows, capacity, whole), whole)
+
+    def move(piece, k):
+        if not split:
+            return lax.all_to_all(piece, ("gx", "gz"), split_axis=0, concat_axis=0, tiled=True)
+        return lax.ppermute(piece, ("gx", "gz"), [(i, i ^ k) for i in range(group_size)])
+
+    arrived = {0: sent[0]} if split else {0: tuple(move(x, 0) for x in sent[0])}
+    for k in far:
+        arrived[k] = (move(sent[k][0], k), None)
+    for k in range(1, len(sent)):
+        if k not in far:
+            arrived[k] = move(sent[k], k)
+    for k in far:
+        arrived[k] = (arrived[k][0], move(sent[k][1], k))
+    first, second = (
+        [arrived[k] if one else arrived[k][half] for k, one in enumerate(whole)] for half in range(2)
+    )
+    table, outer, *faces = outer_boxes(first, old_owner, me, group_size, capacity, whole, joined)
     if joined:
         faces = [lax.ppermute(faces[0], "gx", ring(across, 1))]
     else:
         faces = [lax.ppermute(x, "gx", ring(across, step)) for x, step in zip(faces, (-1, 1))]
-    grid = grid_from_boxes(held)
-    layers, low, high = x_faces_and_y_rows(grid, faces, joined)
+    inner = inner_boxes(second, table, me, box_count, capacity, whole)
+    parts = outer, inner
+    layers, low, high = x_layers_and_y_rows(parts, faces, joined)
     rows = lax.axis_size("gy")
     above = lax.ppermute(low, "gy", ring(rows, -1))
     below = lax.ppermute(high, "gy", ring(rows, 1))
-    low, high = z_columns(grid, layers, below, above)
-    whole, halves = whole_grid(grid, layers, below, above)
+    low, high = z_columns(parts, layers, below, above)
+    whole, halves = whole_grid(parts, layers, below, above)
     above = lax.ppermute(low, "gz", ring(along, -1))
     below = lax.ppermute(high, "gz", ring(along, 1))
     return two_sections(whole, halves, below, above)

time: 52.4 us -> 53 us (1.011)
  waiting for transfers between devices: 18.8 us -> 7.93 us
  starting transfers between devices: 22.6 us -> 32.3 us
  Pallas kernels: 9.06 us -> 10.7 us
    ppermute x8 -> x13, waiting for transfers between devices: 14.9 us -> 4.31 us  [the longest x11 2.88 us: move(): lax.ppermute(piece, ('gx', 'gz'), [(i, i ^ k) for i in range(group_size)])]
    ppermute x8 -> x13, starting transfers between devices: 17 us -> 26.7 us  [the longest x11 24.6 us: move(): lax.ppermute(piece, ('gx', 'gz'), [(i, i ^ k) for i in range(group_size)])]
    ppermute x1, starting transfers between devices: 2.02 us -> 0.06 us  [body(): below = lax.ppermute(high, 'gz', ring(along, 1))]
    ppermute x1, starting transfers between devices: 1.86 us -> 3.81 us  [body(): above = lax.ppermute(low, 'gz', ring(along, -1))]
    pallas_call x5 -> x6, Pallas kernels: 4.77 us -> 6.48 us  [the longest x1 1.95 us: outer_boxes(): pl.pallas_call(kernel, out_shape=[jax.ShapeDtypeStruct((group * capacity,...]
  transfers between devices with their start and end apart: 12 -> 17, of which waited for: 7 -> 6; matrix products, arithmetic and copies ran while one was open for 0% -> 0% of each run, Pallas kernels for 3% -> 6%
where the time goes in v4:
time: 53 us; the launch traced here: 52.8 us
  starting transfers between devices  32.3 us (61%)
  Pallas kernels  10.7 us (20%)
  waiting for transfers between devices  7.93 us (15%)
  local copies, waits for them, and re-layouts  1.7 us (3%)
    ppermute x11, starting transfers between devices, move(): lax.ppermute(piece, ('gx', 'gz'), [(i, i ^ k) for i in range(group_size)])  24.6 us
    pallas_call x1, Pallas kernels, two_sections(): pl.pallas_call(kernel, out_shape=jax.ShapeDtypeStruct((FIELDS, NX, NY, LA...  4.06 us
    ppermute x1, starting transfers between devices, body(): above = lax.ppermute(low, 'gz', ring(along, -1))  3.81 us
    ppermute x11, waiting for transfers between devices, move(): lax.ppermute(piece, ('gx', 'gz'), [(i, i ^ k) for i in range(group_size)])  2.88 us
    ppermute x2, starting transfers between devices, body(): lax.ppermute(x, 'gx', ring(across, step))  2.09 us
    ppermute x1, waiting for transfers between devices, body(): below = lax.ppermute(high, 'gy', ring(rows, 1))  2.03 us
    pallas_call x1, Pallas kernels, outer_boxes(): pl.pallas_call(kernel, out_shape=[jax.ShapeDtypeStruct((group * capacity,...  1.95 us
    ppermute x1, starting transfers between devices, body(): above = lax.ppermute(low, 'gy', ring(rows, -1))  1.73 us
  transfers between devices with their start and end apart: 17, of which 6 were waited for; matrix products, arithmetic and copies ran while one was open for 0% of the time, Pallas kernels for 6%

profile of v4, /device:TPU:0, one launch (start us, length us, event | category | flops | bytes accessed | tf_op | source)
XLA Modules:
  0.0 52.8 jit_solution(9980478267861647858)
XLA Ops:
  0.0 0.0 copy-start.2
  0.0 0.7 %copy-done.2 = s32[64]{0:T(128)S(1)} copy-done((s32[64]{0:T(128)S(1)}, s32[64]{0:T(128)}, u32[]{:S(2)}) %copy-start.2) | copy-done | bytes 280
  0.7 1.6 %ranked.1.table = s32[128]{0:T(128)S(1)} custom-call(s32[64]{0:T(128)S(1)} %copy-done.2), custom_call_target="tpu_custom_call" | custom-call | bytes 4194304 | tf_op jit(solution)/shard_map/ranked/pallas_call | solution.py:52
  2.2 0.0 copy-start
  2.3 1.0 %copy-done = f32[64,4,512]{2,1,0:T(4,128)S(1)} copy-done((f32[64,4,512]{2,1,0:T(4,128)S(1)}, f32[64,4,512]{2,1,0:T(4,128)}, u32[]{:S(2)}) %copy-start) | copy-done | bytes 524312
  3.3 0.8 %pack_boxes.1 = (f32[16,2,8,128]{3,2,1,0:T(8,128)S(1)}, f32[16,2,8,128]{3,2,1,0:T(8,128)S(1)}, f32[16,8,128]{2,1,0:T(8,128)S(1)}, f32[16,8,128]{2,1,0:T(8,128)S(...) custom-call(s32[1]{0:T(128)} %bitcast.me_ref, ...), custom_call_target="tpu_custom_call" | custom-call | tf_op jit(solution)/shard_map/pack_boxes/pallas_call | solution.py:94
  4.1 4.1 %collective-permute-start.1 = (f32[16,8,128]{2,1,0:T(8,128)S(1)}, f32[16,8,128]{2,1,0:T(8,128)S(1)}, u32[]{:S(2)}, u32[]{:S(2)}) collective-permute-start(f32[16,8,128]{2,1,0:T(8,128)S(1)} %get-tuple-element.30), channel_id=1, source_target_pairs={{0,2},{1,3},{2,0},{3,1},{16,18},{17,19},{18,16},{19,17},{4,6},{5,7... | collective-permute-start | bytes 196616 | tf_op jit(solution)/shard_map/ppermute | solution.py:490
  8.2 1.3 %collective-permute-start.2 = (f32[16,8,128]{2,1,0:T(8,128)S(1)}, f32[16,8,128]{2,1,0:T(8,128)S(1)}, u32[]{:S(2)}, u32[]{:S(2)}) collective-permute-start(f32[16,8,128]{2,1,0:T(8,128)S(1)} %get-tuple-element.31), channel_id=1, source_target_pairs={{0,3},{1,2},{2,1},{3,0},{16,19},{17,18},{18,17},{19,16},{4,7},{5,6... | collective-permute-start | bytes 196616 | tf_op jit(solution)/shard_map/ppermute | solution.py:490
  9.6 0.2 collective-permute-start
  9.8 1.5 %collective-permute-start.3 = (f32[16,2,8,128]{3,2,1,0:T(8,128)S(1)}, f32[16,2,8,128]{3,2,1,0:T(8,128)S(1)}, u32[]{:S(2)}, u32[]{:S(2)}) collective-permute-start(f32[16,2,8,128]{3,2,1,0:T(8,128)S(1)} %get-tuple-element.32), channel_id=1, source_target_pairs={{0,16},{1,17},{2,18},{3,19},{16,0},{17,1},{18,2},{19,3},{4,20},{5,... | collective-permute-start | bytes 393224 | tf_op jit(solution)/shard_map/ppermute | solution.py:490
  11.3 1.7 %collective-permute-start.4 = (f32[16,2,8,128]{3,2,1,0:T(8,128)S(1)}, f32[16,2,8,128]{3,2,1,0:T(8,128)S(1)}, u32[]{:S(2)}, u32[]{:S(2)}) collective-permute-start(f32[16,2,8,128]{3,2,1,0:T(8,128)S(1)} %get-tuple-element.33), channel_id=1, source_target_pairs={{0,17},{1,16},{2,19},{3,18},{16,1},{17,0},{18,3},{19,2},{4,21},{5,... | collective-permute-start | bytes 393224 | tf_op jit(solution)/shard_map/ppermute | solution.py:490
  13.1 0.0 collective-permute-done.1.refs_2_
  13.1 2.6 %collective-permute-start.5 = (f32[16,8,128]{2,1,0:T(8,128)S(1)}, f32[16,8,128]{2,1,0:T(8,128)S(1)}, u32[]{:S(2)}, u32[]{:S(2)}) collective-permute-start(f32[16,8,128]{2,1,0:T(8,128)S(1)} %get-tuple-element.34), channel_id=1, source_target_pairs={{0,18},{1,19},{2,16},{3,17},{16,2},{17,3},{18,0},{19,1},{4,22},{5,... | collective-permute-start | bytes 196616 | tf_op jit(solution)/shard_map/ppermute | solution.py:490
  15.7 0.0 collective-permute-done.2.refs_3_
  15.7 2.4 %collective-permute-start.6 = (f32[16,8,128]{2,1,0:T(8,128)S(1)}, f32[16,8,128]{2,1,0:T(8,128)S(1)}, u32[]{:S(2)}, u32[]{:S(2)}) collective-permute-start(f32[16,8,128]{2,1,0:T(8,128)S(1)} %get-tuple-element.35), channel_id=1, source_target_pairs={{0,19},{1,18},{2,17},{3,16},{16,3},{17,2},{18,1},{19,0},{4,23},{5,... | collective-permute-start | bytes 196616 | tf_op jit(solution)/shard_map/ppermute | solution.py:490
  18.1 1.5 %collective-permute-done.5.refs_6_ = f32[16,8,128]{2,1,0:T(8,128)S(1)} collective-permute-done((f32[16,8,128]{2,1,0:T(8,128)S(1)}, f32[16,8,128]{2,1,0:T(8,128)S(1)}, u32[]{:S(2)}, u32[]{:S(2)}) %collective-permute-start.5) | collective-permute-done | bytes 65568 | tf_op jit(solution)/shard_map/ppermute | solution.py:490
  19.6 3.9 %collective-permute-start.7 = (f32[16,8,128]{2,1,0:T(8,128)S(1)}, f32[16,8,128]{2,1,0:T(8,128)S(1)}, u32[]{:S(2)}, u32[]{:S(2)}) collective-permute-start(f32[16,8,128]{2,1,0:T(8,128)S(1)} %get-tuple-element.38), channel_id=1, source_target_pairs={{0,2},{1,3},{2,0},{3,1},{16,18},{17,19},{18,16},{19,17},{4,6},{5,7... | collective-permute-start | bytes 196616 | tf_op jit(solution)/shard_map/ppermute | solution.py:490
  23.4 0.0 collective-permute-done.6.refs_7_
  23.4 2.3 %collective-permute-start.8 = (f32[16,8,128]{2,1,0:T(8,128)S(1)}, f32[16,8,128]{2,1,0:T(8,128)S(1)}, u32[]{:S(2)}, u32[]{:S(2)}) collective-permute-start(f32[16,8,128]{2,1,0:T(8,128)S(1)} %get-tuple-element.39), channel_id=1, source_target_pairs={{0,3},{1,2},{2,1},{3,0},{16,19},{17,18},{18,17},{19,16},{4,7},{5,6... | collective-permute-start | bytes 196616 | tf_op jit(solution)/shard_map/ppermute | solution.py:490
  25.8 0.0 collective-permute-done.refs_1_
  25.8 2.8 %collective-permute-start.9 = (f32[16,8,128]{2,1,0:T(8,128)S(1)}, f32[16,8,128]{2,1,0:T(8,128)S(1)}, u32[]{:S(2)}, u32[]{:S(2)}) collective-permute-start(f32[16,8,128]{2,1,0:T(8,128)S(1)} %get-tuple-element.40), channel_id=1, source_target_pairs={{0,18},{1,19},{2,16},{3,17},{16,2},{17,3},{18,0},{19,1},{4,22},{5,... | collective-permute-start | bytes 196616 | tf_op jit(solution)/shard_map/ppermute | solution.py:490
  28.6 0.0 collective-permute-done.3.refs_4_
  28.6 0.0 copy-start.1
  28.6 1.7 %collective-permute-start.10 = (f32[16,8,128]{2,1,0:T(8,128)S(1)}, f32[16,8,128]{2,1,0:T(8,128)S(1)}, u32[]{:S(2)}, u32[]{:S(2)}) collective-permute-start(f32[16,8,128]{2,1,0:T(8,128)S(1)} %get-tuple-element.41), channel_id=1, source_target_pairs={{0,19},{1,18},{2,17},{3,16},{16,3},{17,2},{18,1},{19,0},{4,23},{5,... | collective-permute-start | bytes 196616 | tf_op jit(solution)/shard_map/ppermute | solution.py:490
  30.2 0.0 collective-permute-done.4.refs_5_
  30.2 0.0 copy-done.1
  30.2 1.9 %outer_boxes.1 = (s32[128]{0:T(128)S(1)}, f32[4,8,16,128]{3,2,1,0:T(8,128)S(1)}, f32[16,8,128]{2,1,0:T(8,128)S(1)}, f32[16,8,128]{2,1,0:T(8,128)S(1)}) custom-call(s32[1]{0:T(128)} %bitcast.me_ref, s32[64]{0:T(128)S(1)} %copy-done.1, f32[16,2,8,128]{3,2,1,0:T(8,128)S(1)} %get-tuple-element.28.refs_0_, f32[16,2,8,128]{3,2,1,0:T(8,128)S(1)} %collective-permute-done.refs_1_, ...), custom_call_target="tpu_custom_call" | custom-call | bytes 67108864 | tf_op jit(solution)/shard_map/outer_boxes/pallas_call | solution.py:201
  32.2 1.9 %collective-permute-start.11 = (f32[16,8,128]{2,1,0:T(8,128)S(1)}, f32[16,8,128]{2,1,0:T(8,128)S(1)}, u32[]{:S(2)}, u32[]{:S(2)}) collective-permute-start(f32[16,8,128]{2,1,0:T(8,128)S(1)} %get-tuple-element.42), channel_id=1, source_target_pairs={{0,16},{16,0},{1,17},{17,1},{2,18},{18,2},{3,19},{19,3},{4,20},{20... | collective-permute-start | bytes 196616 | tf_op jit(solution)/shard_map/ppermute | solution.py:507
  34.1 0.0 collective-permute-done.7.refs_2_
  34.1 0.2 collective-permute-start.12
  34.3 0.0 collective-permute-done.8.refs_3_
  34.3 0.2 collective-permute-done.9.refs_6_
  34.5 1.1 %collective-permute-done.10.refs_7_ = f32[16,8,128]{2,1,0:T(8,128)S(1)} collective-permute-done((f32[16,8,128]{2,1,0:T(8,128)S(1)}, f32[16,8,128]{2,1,0:T(8,128)S(1)}, u32[]{:S(2)}, u32[]{:S(2)}) %collective-permute-start.10) | collective-permute-done | bytes 65568 | tf_op jit(solution)/shard_map/ppermute | solution.py:490
  35.6 1.3 %inner_boxes.1.inner = f32[4,8,16,128]{3,2,1,0:T(8,128)S(1)} custom-call(s32[1]{0:T(128)} %bitcast.me_ref, s32[128]{0:T(128)S(1)} %get-tuple-element.37.table, f32[16,2,8,128]{3,2,1,0:T(8,128)S(1)} %get-tuple-element.28.refs_0_, f32[16,2,8,128]{3,2,1,0:T(8,128)S(1)} %collective-permute-done.refs_1_, f32[16,8,128]{2,1,0:T(8,128)S(1)} %collective-permute-done.7.refs_2_, ...), custom_call_target="tpu_custom_call" | custom-call | bytes 67108864 | tf_op jit(solution)/shard_map/inner_boxes/pallas_call | solution.py:226
  36.9 0.0 collective-permute-done.11.refs_0_
  36.9 1.4 %collective-permute-done.12.refs_1_ = f32[16,8,128]{2,1,0:T(8,128)S(1)} collective-permute-done((f32[16,8,128]{2,1,0:T(8,128)S(1)}, f32[16,8,128]{2,1,0:T(8,128)S(1)}, u32[]{:S(2)}, u32[]{:S(2)}) %collective-permute-start.12) | collective-permute-done | bytes 65568 | tf_op jit(solution)/shard_map/ppermute | solution.py:507
  38.4 0.3 x_layers_and_y_rows.1
  38.7 0.1 collective-permute-start.13
  38.8 1.7 %collective-permute-start.14 = (f32[4,18,2,128]{3,2,1,0:T(2,128)S(1)}, f32[4,18,2,128]{3,2,1,0:T(2,128)S(1)}, u32[]{:S(2)}, u32[]{:S(2)}) collective-permute-start(f32[4,18,2,128]{3,2,1,0:T(2,128)S(1)} %get-tuple-element.46), channel_id=1, source_target_pairs={{0,12},{4,0},{8,4},{12,8},{1,13},{5,1},{9,5},{13,9},{2,14},{6,2},{... | collective-permute-start | bytes 221192 | tf_op jit(solution)/shard_map/ppermute | solution.py:512
  40.5 2.0 %collective-permute-done.13.below = f32[4,18,2,128]{3,2,1,0:T(2,128)S(1)} collective-permute-done((f32[4,18,2,128]{3,2,1,0:T(2,128)S(1)}, f32[4,18,2,128]{3,2,1,0:T(2,128)S(1)}, u32[]{:S(2)}, u32[]{:S(2)}) %collective-permute-start.13) | collective-permute-done | bytes 73760 | tf_op jit(solution)/shard_map/ppermute | solution.py:513
  42.5 0.0 collective-permute-done.14.above
  42.5 0.5 z_columns.1
  43.1 0.1 collective-permute-start.15
  43.1 3.8 %collective-permute-start.16 = (f32[2,24,128]{2,1,0:T(8,128)S(1)}, f32[2,24,128]{2,1,0:T(8,128)S(1)}, u32[]{:S(2)}, u32[]{:S(2)}) collective-permute-start(f32[2,24,128]{2,1,0:T(8,128)S(1)} %get-tuple-element.50), channel_id=1, source_target_pairs={{0,3},{1,0},{2,1},{3,2},{4,7},{5,4},{6,5},{7,6},{8,11},{9,8},{10,9... | collective-permute-start | bytes 73736 | tf_op jit(solution)/shard_map/ppermute | solution.py:516
  47.0 0.2 whole_grid.1
  47.2 1.6 %collective-permute-done.15.below = f32[2,24,128]{2,1,0:T(8,128)S(1)} collective-permute-done((f32[2,24,128]{2,1,0:T(8,128)S(1)}, f32[2,24,128]{2,1,0:T(8,128)S(1)}, u32[]{:S(2)}, u32[]{:S(2)}) %collective-permute-start.15) | collective-permute-done | bytes 24608 | tf_op jit(solution)/shard_map/ppermute | solution.py:517
  48.8 0.0 collective-permute-done.16.above
  48.8 4.1 %two_sections.1 = f32[4,16,16,128]{3,2,1,0:T(8,128)} custom-call(f32[4,20,24,128]{3,2,1,0:T(8,128)S(1)} %get-tuple-element.47.grid, f32[20,24,128]{2,1,0:T(8,128)S(1)} %get-tuple-element.48.gs, f32[2,24,128]{2,1,0:T(8,128)S(1)} %collective-permute-done.15.below, f32[2,24,128]{2,1,0:T(8,128)S(1)} %collective-permute-done.16.above), custom_call_target="tpu_custom_call" | custom-call | tf_op jit(solution)/shard_map/two_sections/pallas_call | solution.py:452
Async XLA Ops:
  0.0 0.7 %copy-start.2 = (s32[64]{0:T(128)S(1)}, s32[64]{0:T(128)}, u32[]{:S(2)}) copy-start(s32[64]{0:T(128)} %owner.2) | copy-start | bytes 772
  2.2 1.0 %copy-start = (f32[64,4,512]{2,1,0:T(4,128)S(1)}, f32[64,4,512]{2,1,0:T(4,128)}, u32[]{:S(2)}) copy-start(f32[64,4,512]{2,1,0:T(4,128)} %fields.1) | copy-start | bytes 1572868
  4.1 8.9 %collective-permute-start.1 = (f32[16,8,128]{2,1,0:T(8,128)S(1)}, f32[16,8,128]{2,1,0:T(8,128)S(1)}, u32[]{:S(2)}, u32[]{:S(2)}) collective-permute-start(f32[16,8,128]{2,1,0:T(8,128)S(1)} %get-tuple-element.30), channel_id=1, source_target_pairs={{0,2},{1,3},{2,0},{3,1},{16,18},{17,19},{18,16},{19,17},{4,6},{5,7... | collective-permute-start | bytes 196616 | tf_op jit(solution)/shard_map/ppermute | solution.py:490
  8.2 7.5 %collective-permute-start.2 = (f32[16,8,128]{2,1,0:T(8,128)S(1)}, f32[16,8,128]{2,1,0:T(8,128)S(1)}, u32[]{:S(2)}, u32[]{:S(2)}) collective-permute-start(f32[16,8,128]{2,1,0:T(8,128)S(1)} %get-tuple-element.31), channel_id=1, source_target_pairs={{0,3},{1,2},{2,1},{3,0},{16,19},{17,18},{18,17},{19,16},{4,7},{5,6... | collective-permute-start | bytes 196616 | tf_op jit(solution)/shard_map/ppermute | solution.py:490
  9.6 16.2 %collective-permute-start = (f32[16,2,8,128]{3,2,1,0:T(8,128)S(1)}, f32[16,2,8,128]{3,2,1,0:T(8,128)S(1)}, u32[]{:S(2)}, u32[]{:S(2)}) collective-permute-start(f32[16,2,8,128]{3,2,1,0:T(8,128)S(1)} %get-tuple-element.29), channel_id=1, source_target_pairs={{0,1},{1,0},{2,3},{3,2},{16,17},{17,16},{18,19},{19,18},{4,5},{5,4... | collective-permute-start | bytes 393224 | tf_op jit(solution)/shard_map/ppermute | solution.py:490
  9.8 18.8 %collective-permute-start.3 = (f32[16,2,8,128]{3,2,1,0:T(8,128)S(1)}, f32[16,2,8,128]{3,2,1,0:T(8,128)S(1)}, u32[]{:S(2)}, u32[]{:S(2)}) collective-permute-start(f32[16,2,8,128]{3,2,1,0:T(8,128)S(1)} %get-tuple-element.32), channel_id=1, source_target_pairs={{0,16},{1,17},{2,18},{3,19},{16,0},{17,1},{18,2},{19,3},{4,20},{5,... | collective-permute-start | bytes 393224 | tf_op jit(solution)/shard_map/ppermute | solution.py:490
  11.3 18.9 %collective-permute-start.4 = (f32[16,2,8,128]{3,2,1,0:T(8,128)S(1)}, f32[16,2,8,128]{3,2,1,0:T(8,128)S(1)}, u32[]{:S(2)}, u32[]{:S(2)}) collective-permute-start(f32[16,2,8,128]{3,2,1,0:T(8,128)S(1)} %get-tuple-element.33), channel_id=1, source_target_pairs={{0,17},{1,16},{2,19},{3,18},{16,1},{17,0},{18,3},{19,2},{4,21},{5,... | collective-permute-start | bytes 393224 | tf_op jit(solution)/shard_map/ppermute | solution.py:490
  13.1 6.5 %collective-permute-start.5 = (f32[16,8,128]{2,1,0:T(8,128)S(1)}, f32[16,8,128]{2,1,0:T(8,128)S(1)}, u32[]{:S(2)}, u32[]{:S(2)}) collective-permute-start(f32[16,8,128]{2,1,0:T(8,128)S(1)} %get-tuple-element.34), channel_id=1, source_target_pairs={{0,18},{1,19},{2,16},{3,17},{16,2},{17,3},{18,0},{19,1},{4,22},{5,... | collective-permute-start | bytes 196616 | tf_op jit(solution)/shard_map/ppermute | solution.py:490
  15.7 7.7 %collective-permute-start.6 = (f32[16,8,128]{2,1,0:T(8,128)S(1)}, f32[16,8,128]{2,1,0:T(8,128)S(1)}, u32[]{:S(2)}, u32[]{:S(2)}) collective-permute-start(f32[16,8,128]{2,1,0:T(8,128)S(1)} %get-tuple-element.35), channel_id=1, source_target_pairs={{0,19},{1,18},{2,17},{3,16},{16,3},{17,2},{18,1},{19,0},{4,23},{5,... | collective-permute-start | bytes 196616 | tf_op jit(solution)/shard_map/ppermute | solution.py:490
  19.6 14.5 %collective-permute-start.7 = (f32[16,8,128]{2,1,0:T(8,128)S(1)}, f32[16,8,128]{2,1,0:T(8,128)S(1)}, u32[]{:S(2)}, u32[]{:S(2)}) collective-permute-start(f32[16,8,128]{2,1,0:T(8,128)S(1)} %get-tuple-element.38), channel_id=1, source_target_pairs={{0,2},{1,3},{2,0},{3,1},{16,18},{17,19},{18,16},{19,17},{4,6},{5,7... | collective-permute-start | bytes 196616 | tf_op jit(solution)/shard_map/ppermute | solution.py:490
  23.4 10.9 %collective-permute-start.8 = (f32[16,8,128]{2,1,0:T(8,128)S(1)}, f32[16,8,128]{2,1,0:T(8,128)S(1)}, u32[]{:S(2)}, u32[]{:S(2)}) collective-permute-start(f32[16,8,128]{2,1,0:T(8,128)S(1)} %get-tuple-element.39), channel_id=1, source_target_pairs={{0,3},{1,2},{2,1},{3,0},{16,19},{17,18},{18,17},{19,16},{4,7},{5,6... | collective-permute-start | bytes 196616 | tf_op jit(solution)/shard_map/ppermute | solution.py:490
  25.8 8.7 %collective-permute-start.9 = (f32[16,8,128]{2,1,0:T(8,128)S(1)}, f32[16,8,128]{2,1,0:T(8,128)S(1)}, u32[]{:S(2)}, u32[]{:S(2)}) collective-permute-start(f32[16,8,128]{2,1,0:T(8,128)S(1)} %get-tuple-element.40), channel_id=1, source_target_pairs={{0,18},{1,19},{2,16},{3,17},{16,2},{17,3},{18,0},{19,1},{4,22},{5,... | collective-permute-start | bytes 196616 | tf_op jit(solution)/shard_map/ppermute | solution.py:490
  28.6 1.7 %copy-start.1 = (s32[64]{0:T(128)S(1)}, s32[64]{0:T(128)}, u32[]{:S(2)}) copy-start(s32[64]{0:T(128)} %owner.3) | copy-start | bytes 772
  28.6 7.1 %collective-permute-start.10 = (f32[16,8,128]{2,1,0:T(8,128)S(1)}, f32[16,8,128]{2,1,0:T(8,128)S(1)}, u32[]{:S(2)}, u32[]{:S(2)}) collective-permute-start(f32[16,8,128]{2,1,0:T(8,128)S(1)} %get-tuple-element.41), channel_id=1, source_target_pairs={{0,19},{1,18},{2,17},{3,16},{16,3},{17,2},{18,1},{19,0},{4,23},{5,... | collective-permute-start | bytes 196616 | tf_op jit(solution)/shard_map/ppermute | solution.py:490
  32.2 4.7 %collective-permute-start.11 = (f32[16,8,128]{2,1,0:T(8,128)S(1)}, f32[16,8,128]{2,1,0:T(8,128)S(1)}, u32[]{:S(2)}, u32[]{:S(2)}) collective-permute-start(f32[16,8,128]{2,1,0:T(8,128)S(1)} %get-tuple-element.42), channel_id=1, source_target_pairs={{0,16},{16,0},{1,17},{17,1},{2,18},{18,2},{3,19},{19,3},{4,20},{20... | collective-permute-start | bytes 196616 | tf_op jit(solution)/shard_map/ppermute | solution.py:507
  34.1 4.3 %collective-permute-start.12 = (f32[16,8,128]{2,1,0:T(8,128)S(1)}, f32[16,8,128]{2,1,0:T(8,128)S(1)}, u32[]{:S(2)}, u32[]{:S(2)}) collective-permute-start(f32[16,8,128]{2,1,0:T(8,128)S(1)} %get-tuple-element.43), channel_id=1, source_target_pairs={{0,16},{16,0},{1,17},{17,1},{2,18},{18,2},{3,19},{19,3},{4,20},{20... | collective-permute-start | bytes 196616 | tf_op jit(solution)/shard_map/ppermute | solution.py:507
  38.7 3.8 %collective-permute-start.13 = (f32[4,18,2,128]{3,2,1,0:T(2,128)S(1)}, f32[4,18,2,128]{3,2,1,0:T(2,128)S(1)}, u32[]{:S(2)}, u32[]{:S(2)}) collective-permute-start(f32[4,18,2,128]{3,2,1,0:T(2,128)S(1)} %get-tuple-element.45), channel_id=1, source_target_pairs={{0,4},{4,8},{8,12},{12,0},{1,5},{5,9},{9,13},{13,1},{2,6},{6,10},{... | collective-permute-start | bytes 221192 | tf_op jit(solution)/shard_map/ppermute | solution.py:513
  38.8 3.8 %collective-permute-start.14 = (f32[4,18,2,128]{3,2,1,0:T(2,128)S(1)}, f32[4,18,2,128]{3,2,1,0:T(2,128)S(1)}, u32[]{:S(2)}, u32[]{:S(2)}) collective-permute-start(f32[4,18,2,128]{3,2,1,0:T(2,128)S(1)} %get-tuple-element.46), channel_id=1, source_target_pairs={{0,12},{4,0},{8,4},{12,8},{1,13},{5,1},{9,5},{13,9},{2,14},{6,2},{... | collective-permute-start | bytes 221192 | tf_op jit(solution)/shard_map/ppermute | solution.py:512
  43.1 5.7 %collective-permute-start.15 = (f32[2,24,128]{2,1,0:T(8,128)S(1)}, f32[2,24,128]{2,1,0:T(8,128)S(1)}, u32[]{:S(2)}, u32[]{:S(2)}) collective-permute-start(f32[2,24,128]{2,1,0:T(8,128)S(1)} %get-tuple-element.49), channel_id=1, source_target_pairs={{0,1},{1,2},{2,3},{3,0},{4,5},{5,6},{6,7},{7,4},{8,9},{9,10},{10,1... | collective-permute-start | bytes 73736 | tf_op jit(solution)/shard_map/ppermute | solution.py:517
  43.1 5.6 %collective-permute-start.16 = (f32[2,24,128]{2,1,0:T(8,128)S(1)}, f32[2,24,128]{2,1,0:T(8,128)S(1)}, u32[]{:S(2)}, u32[]{:S(2)}) collective-permute-start(f32[2,24,128]{2,1,0:T(8,128)S(1)} %get-tuple-element.50), channel_id=1, source_target_pairs={{0,3},{1,0},{2,1},{3,2},{4,7},{5,4},{6,5},{7,6},{8,11},{9,8},{10,9... | collective-permute-start | bytes 73736 | tf_op jit(solution)/shard_map/ppermute | solution.py:516

commit v5 on v3

v5 whole, which is shorter than its diff:
```python
import jax
import jax.numpy as jnp
from jax import lax
from jax.experimental import pallas as pl
from jax.experimental.pallas import tpu as pltpu
from jax.sharding import PartitionSpec as P

EDGE = 8
FIELDS = 4
BRICK_X = 2
BRICK_Y = 2
BRICK_Z = 16
CELLS = EDGE**3
LANES = 128
TILES = CELLS // LANES
BOX = (TILES // 2, 2 * FIELDS, LANES)


DIFFUSION = (1.0, 3.3, 0.9, 1.2)
TIME_STEP = 0.012

VMEM = pl.BlockSpec(memory_space=pltpu.VMEM)
SMEM = pl.BlockSpec(memory_space=pltpu.SMEM)
ROOM = pltpu.CompilerParams(vmem_limit_bytes=16 * 2**20)


def rank_table(owner, table, counts, group, capacity, boxes, empty):
    def clear(i, carry):
        table[i] = empty
        return carry

    lax.fori_loop(0, group * capacity, clear, 0, unroll=16)
    for g in range(group):
        counts[g] = g * capacity

    def place(b, carry):
        o = owner[b]
        slot = counts[o]
        table[slot] = b
        counts[o] = slot + 1
        return carry

    lax.fori_loop(0, boxes, place, 0, unroll=8)


def pack_boxes(old_fields, new_owner, me, group, capacity, split):
    boxes = new_owner.shape[0]
    pieces = group if split else 1
    rows = group * capacity // pieces

    def kernel(me_ref, owner, fields, *refs):
        outs, (table, counts) = refs[:pieces], refs[pieces:]
        rank_table(owner, table, counts, group, capacity, boxes, 0)
        for k, out in enumerate(outs):
            base = (me_ref[0] ^ k) * capacity if split else 0

            def copy(r, carry, out=out, base=base):
                box = table[base + r]
                for t in range(TILES):
                    out[r, t // 2, pl.ds(t % 2 * FIELDS, FIELDS), :] = fields[
                        box, :, pl.ds(t * LANES, LANES)
                    ]
                return carry

            lax.fori_loop(0, rows, copy, 0, unroll=8)

    return pl.pallas_call(
        kernel,
        out_shape=[jax.ShapeDtypeStruct((rows,) + BOX, jnp.float32)] * pieces,
        in_specs=[SMEM, SMEM, VMEM],
        out_specs=[VMEM] * pieces,
        scratch_shapes=[
            pltpu.SMEM((group * capacity,), jnp.int32),
            pltpu.SMEM((group,), jnp.int32),
        ],
        compiler_params=ROOM,
        name="pack_boxes",
    )(me, new_owner, old_fields)


def swap_boxes(columns):
    lane = lax.broadcasted_iota(jnp.int32, columns[0].shape, 1)
    for bit in range(4):
        width = EDGE << bit
        upper = (lane & width) != 0
        fresh = list(columns)
        for low in range(16):
            if low >> bit & 1:
                continue
            high = low | 1 << bit
            a, b = columns[low], columns[high]
            fresh[low] = jnp.where(upper, pltpu.roll(b, width, 1), a)
            fresh[high] = jnp.where(upper, b, pltpu.roll(a, LANES - width, 1))
        columns = fresh
    return columns


def ring(count, step):
    return [(i, (i + step) % count) for i in range(count)]


def boxes_in_place(arrived, old_owner, me, group, capacity, split, joined):
    boxes = old_owner.shape[0]
    pieces = len(arrived)
    rows = group * capacity // pieces
    half = boxes // BRICK_X
    face = (BRICK_Z, BRICK_Y * FIELDS, LANES)
    faces = [jax.ShapeDtypeStruct((2,) + face if joined else face, jnp.float32)] * (2 - joined)
    end = jax.ShapeDtypeStruct((BRICK_X * BRICK_Y,) + BOX, jnp.float32)

    def kernel(me_ref, owner, *refs):
        ins, refs = refs[:pieces], refs[pieces:]
        (held, low, high), refs = refs[:3], refs[3:]
        outs, (table, counts) = refs[: len(faces)], refs[len(faces) :]
        rank_table(owner, table, counts, group, capacity, boxes, boxes)
        for k, rows_in in enumerate(ins):
            base = (me_ref[0] ^ k) * capacity if split else 0

            def scatter(r, carry, rows_in=rows_in, base=base):
                held[table[base + r]] = rows_in[r]
                return carry

            lax.fori_loop(0, rows, scatter, 0, unroll=8)
        for side in range(2):
            out = outs[0].at[side] if joined else outs[side]
            for by in range(BRICK_Y):
                for bz in range(BRICK_Z):
                    p = side * half + by * BRICK_Z + bz
                    out[bz, pl.ds(by * FIELDS, FIELDS), :] = held[
                        p, side, pl.ds(side * FIELDS, FIELDS), :
                    ]
        for b in range(BRICK_X * BRICK_Y):
            low[b] = held[b * BRICK_Z]
            high[b] = held[b * BRICK_Z + BRICK_Z - 1]

    return pl.pallas_call(
        kernel,
        out_shape=[jax.ShapeDtypeStruct((boxes + 1,) + BOX, jnp.float32), end, end] + faces,
        in_specs=[SMEM, SMEM] + [VMEM] * pieces,
        out_specs=[VMEM] * (3 + len(faces)),
        scratch_shapes=[
            pltpu.SMEM((group * capacity,), jnp.int32),
            pltpu.SMEM((group,), jnp.int32),
        ],
        compiler_params=ROOM,
        name="boxes_in_place",
    )(me, old_owner, *arrived)


HALO = 2
NX = BRICK_X * EDGE
NY = BRICK_Y * EDGE
WIDE_X = NX + 2 * HALO
WIDE_Y = NY + EDGE
NEAR_X = NX + 2


def lay_out(columns, turned, store):
    for r in range(16):
        turned[pl.ds(r * 8, 8), :] = columns[r]
    for a in range(2):
        for i in range(2):
            for f in range(FIELDS):
                store(a, i, f, turned[pl.ds(i * 64 + a * FIELDS + f, 8, stride=8), :])


def grid_from_boxes(held):
    def kernel(held, grid, turned):
        for bx in range(BRICK_X):
            for by in range(BRICK_Y):
                first = (bx * BRICK_Y + by) * BRICK_Z
                for half in range(TILES // 2):

                    def store(t, i, f, rows, x=bx * EDGE + half * 4, by=by):
                        grid[f, x + t * 2 + i, pl.ds(by * EDGE, EDGE), :] = rows

                    columns = swap_boxes([held[first + bz, half] for bz in range(BRICK_Z)])
                    lay_out(columns, turned, store)

    return pl.pallas_call(
        kernel,
        out_shape=jax.ShapeDtypeStruct((FIELDS, NX, NY, LANES), jnp.float32),
        in_specs=[VMEM],
        out_specs=VMEM,
        scratch_shapes=[pltpu.VMEM((LANES, LANES), jnp.float32)],
        cost_estimate=pl.CostEstimate(flops=2**22, bytes_accessed=2**21, transcendentals=0),
        compiler_params=ROOM,
        name="grid_from_boxes",
    )(held)


ROWS = FIELDS * NEAR_X * HALO
EDGES = ROWS + EDGE


def row_of(f, x):
    return (f * NEAR_X + x) * HALO


def faces_and_rows(grid, faces, above, below, joined):
    side_shape = (FIELDS, NY, LANES)
    sides = [jax.ShapeDtypeStruct((2,) + side_shape if joined else side_shape, jnp.float32)] * (
        2 - joined
    )

    def kernel(grid, above, below, *refs):
        ins, refs = refs[: len(faces)], refs[len(faces) :]
        (layers, beyond, low, high), refs = refs[:4], refs[4:]
        outs, (turned,) = refs[: len(sides)], refs[len(sides) :]
        for side in range(2):
            face = ins[0].at[side] if joined else ins[side]

            def store(by, i, f, rows, first=0 if side else HALO):
                layers[f, first + i, pl.ds(by * EDGE, EDGE), :] = rows

            lay_out(swap_boxes([face[bz] for bz in range(BRICK_Z)]), turned, store)
        lane = lax.broadcasted_iota(jnp.int32, (EDGE, LANES), 1)
        for bx in range(BRICK_X):
            for by in range(BRICK_Y):
                for half in range(TILES // 2):
                    after, before = above[bx * BRICK_Y + by, half], below[bx * BRICK_Y + by, half]
                    columns = [
                        jnp.where(
                            lane < LANES // 2,
                            pltpu.roll(after, (LANES - EDGE * r) % LANES, 1),
                            pltpu.roll(before, LANES - EDGE - EDGE * r, 1),
                        )
                        for r in range(16)
                    ]

                    def store(t, i, f, rows, x=bx * EDGE + half * 4, by=by):
                        beyond[f, x + t * 2 + i, pl.ds(by * EDGE, EDGE), :] = rows

                    lay_out(columns, turned, store)
        for f in range(FIELDS):
            for x in range(NEAR_X):
                cells = layers.at[f, 2 if x else 1] if x % (NX + 1) == 0 else grid.at[f, x - 1]
                low[pl.ds(row_of(f, x), HALO), :] = cells[pl.ds(0, HALO), :]
                high[pl.ds(row_of(f, x), HALO), :] = cells[pl.ds(NY - HALO, HALO), :]
        pair = lane // 2
        for first, out in ((0, low), (NY - EDGE, high)):
            edge = jnp.zeros((EDGE, LANES), jnp.float32)
            for f in range(FIELDS):
                for x in range(NX):
                    place = f * NX + x
                    moved = pltpu.roll(beyond[f, x, pl.ds(first, EDGE), :], 2 * place + 1, 1)
                    edge = jnp.where(pair == place, moved, edge)
            out[pl.ds(ROWS, EDGE), :] = edge
        for side in range(2):
            out = outs[0].at[side] if joined else outs[side]
            for f in range(FIELDS):
                out[f] = beyond[f, side * (NX - 1)]

    rows = jax.ShapeDtypeStruct((EDGES, LANES), jnp.float32)
    return pl.pallas_call(
        kernel,
        out_shape=[
            jax.ShapeDtypeStruct((FIELDS, 2 * HALO, NY, LANES), jnp.float32),
            jax.ShapeDtypeStruct((FIELDS, NX, NY, LANES), jnp.float32),
            rows,
            rows,
        ]
        + sides,
        in_specs=[VMEM] * (3 + len(faces)),
        out_specs=[VMEM] * (4 + len(sides)),
        scratch_shapes=[pltpu.VMEM((LANES, LANES), jnp.float32)],
        compiler_params=ROOM,
        name="faces_and_rows",
    )(grid, above, below, *faces)


def half_conductance(v):
    return 0.5 * (v * jnp.sqrt(v))


def wide_grid(grid, layers):
    def kernel(grid, layers, wide, halves):
        for f in range(FIELDS):
            for x in range(WIDE_X):
                inside = HALO <= x < HALO + NX
                wide[f, x] = grid[f, x - HALO] if inside else layers[f, x % (NX + HALO) + (x > HALO) * HALO]

        def conductances(x, carry):
            halves[x] = half_conductance(wide[0, x])
            return carry

        lax.fori_loop(0, WIDE_X, conductances, 0, unroll=5)

    return pl.pallas_call(
        kernel,
        out_shape=[
            jax.ShapeDtypeStruct((FIELDS, WIDE_X, NY, LANES), jnp.float32),
            jax.ShapeDtypeStruct((WIDE_X, NY, LANES), jnp.float32),
        ],
        in_specs=[VMEM] * 2,
        out_specs=[VMEM] * 2,
        compiler_params=ROOM,
        cost_estimate=pl.CostEstimate(flops=2**22, bytes_accessed=2**21, transcendentals=0),
        name="wide_grid",
    )(grid, layers)


def section(here, beside, across, rows):
    lane = lax.broadcasted_iota(jnp.int32, (rows, LANES), 1)

    def nearby(cells, other, left, right):
        inside, other = cells[:rows], other[:rows]
        return [
            pltpu.roll(cells, WIDE_Y - 1, 0)[:rows],
            pltpu.roll(cells, 1, 0)[:rows],
            pltpu.roll(jnp.where(lane == 0, other, inside), LANES - 1, 1),
            pltpu.roll(jnp.where(lane == LANES - 1, other, inside), 1, 1),
            left[:rows],
            right[:rows],
        ]

    (cells, s), ((left, s_left), (right, s_right)), (other, s_other) = here, beside, across
    mean = [s[:rows] + n for n in nearby(s, s_other, s_left, s_right)]
    rates = []
    for f in range(FIELDS):
        v = cells[f][:rows]
        terms = [m * (n - v) for m, n in zip(mean, nearby(cells[f], other[f], left[f], right[f]))]
        rates.append(sum(terms[1:], terms[0]))
    return rates


def two_sections(wide, halves, beyond, above, below, sides, joined):
    def kernel(wide, halves, inner_beyond, above, below, *refs):
        ins, refs = refs[: len(sides)], refs[len(sides) :]
        out, ring_rows, ring_halves, beyond, first, first_beyond, bs, fs, fbs = refs
        for f in range(FIELDS):
            for x in range(NEAR_X):
                ring_rows[f, x, pl.ds(0, HALO), :] = above[pl.ds(row_of(f, x), HALO), :]
                ring_rows[f, x, pl.ds(EDGE - HALO, HALO), :] = below[pl.ds(row_of(f, x), HALO), :]
        row = lax.broadcasted_iota(jnp.int32, (EDGE, LANES), 0)
        edge = jnp.where(row < EDGE // 2, above[pl.ds(ROWS, EDGE), :], below[pl.ds(ROWS, EDGE), :])
        for f in range(FIELDS):
            for x in range(NX):
                beyond[f, x + 1, pl.ds(0, NY), :] = inner_beyond[f, x]
                beyond[f, x + 1, pl.ds(NY, EDGE), :] = pltpu.roll(
                    edge, LANES - 1 - 2 * (f * NX + x), 1
                )
            for side in range(2):
                got = ins[0].at[side] if joined else ins[side]
                beyond[f, 0 if side else NX + 1, pl.ds(0, NY), :] = got[f]

        def conductances(x, carry):
            ring_halves[x] = half_conductance(ring_rows[0, x])
            bs[x] = half_conductance(beyond[0, x])
            return carry

        lax.fori_loop(0, NEAR_X, conductances, 0, unroll=6)

        def at(ref, s, x):
            return [ref[f, x] for f in range(FIELDS)], s[x]

        def whole(x):
            cells = [
                jnp.concatenate([wide[f, x + 1], ring_rows[f, x]], 0) for f in range(FIELDS)
            ]
            return cells, jnp.concatenate([halves[x + 1], ring_halves[x]], 0)

        def step(cells, rates):
            rows = rates[0].shape[0]
            return [
                v[:rows] + (TIME_STEP * c) * r for v, c, r in zip(cells, DIFFUSION, rates)
            ]

        def first_inside(x, carry):
            here = whole(x)
            rates = section(here, (narrow(x), narrow(x + 2)), at(beyond, bs, x), WIDE_Y)
            fresh = step(here[0], rates)
            for f in range(FIELDS):
                first[f, x] = fresh[f]
            fs[x] = half_conductance(fresh[0])
            return carry

        def narrow(x):
            inner = jnp.clip(x - 1, 0, NEAR_X - 1)
            cells = [
                jnp.concatenate([wide[f, x], ring_rows[f, inner]], 0) for f in range(FIELDS)
            ]
            return cells, jnp.concatenate([halves[x], ring_halves[inner]], 0)

        lax.fori_loop(0, NEAR_X, first_inside, 0, unroll=3)

        def first_outside(x, carry):
            here = at(beyond, bs, x + 1)
            across = [wide[f, x + HALO] for f in range(FIELDS)], halves[x + HALO]
            rates = section(here, (at(beyond, bs, x), at(beyond, bs, x + 2)), across, NY)
            fresh = step(here[0], rates)
            for f in range(FIELDS):
                first_beyond[f, x] = fresh[f]
            fbs[x] = half_conductance(fresh[0])
            return carry

        lax.fori_loop(0, NX, first_outside, 0, unroll=4)

        def second(x, carry):
            here = at(first, fs, x + 1)
            beside = at(first, fs, x), at(first, fs, x + 2)
            fresh = step(here[0], section(here, beside, at(first_beyond, fbs, x), NY))
            for f in range(FIELDS):
                out[f, x] = 0.5 * wide[f, x + HALO] + 0.5 * fresh[f]
            return carry

        lax.fori_loop(0, NX, second, 0, unroll=4)

    def scratch(*shape):
        return pltpu.VMEM(shape + (LANES,), jnp.float32)

    return pl.pallas_call(
        kernel,
        out_shape=jax.ShapeDtypeStruct((FIELDS, NX, NY, LANES), jnp.float32),
        in_specs=[VMEM] * (5 + len(sides)),
        out_specs=VMEM,
        scratch_shapes=[
            scratch(FIELDS, NEAR_X, EDGE),
            scratch(NEAR_X, EDGE),
            scratch(FIELDS, NEAR_X, WIDE_Y),
            scratch(FIELDS, NEAR_X, WIDE_Y),
            scratch(FIELDS, NX, NY),
            scratch(NEAR_X, WIDE_Y),
            scratch(NEAR_X, WIDE_Y),
            scratch(NX, NY),
        ],
        compiler_params=ROOM,
        name="two_sections",
    )(wide, halves, beyond, above, below, *sides)


def body(old_fields, new_owner, old_owner):
    across, along = lax.axis_size("gx"), lax.axis_size("gz")
    group_size = across * along
    box_count = new_owner.shape[0]
    capacity = 2 * (box_count // group_size)
    split = group_size <= 8
    joined = across == 2
    me = (lax.axis_index("gx") * along + lax.axis_index("gz")).reshape(1)
    departing = pack_boxes(old_fields, new_owner, me, group_size, capacity, split)
    if split:
        arrived = [departing[0]] + [
            lax.ppermute(departing[k], ("gx", "gz"), [(i, i ^ k) for i in range(group_size)])
            for k in range(1, group_size)
        ]
    else:
        arrived = [
            lax.all_to_all(departing[0], ("gx", "gz"), split_axis=0, concat_axis=0, tiled=True)
        ]
    held, low, high, *faces = boxes_in_place(
        arrived, old_owner, me, group_size, capacity, split, joined
    )

    def along_x(sides):
        if joined:
            return [lax.ppermute(sides[0], "gx", ring(across, 1))]
        return [lax.ppermute(side, "gx", ring(across, step)) for side, step in zip(sides, (-1, 1))]

    faces = along_x(faces)
    above = lax.ppermute(low, "gz", ring(along, -1))
    below = lax.ppermute(high, "gz", ring(along, 1))
    grid = grid_from_boxes(held)
    layers, beyond, low, high, *sides = faces_and_rows(grid, faces, above, below, joined)
    rows = lax.axis_size("gy")
    above = lax.ppermute(low, "gy", ring(rows, -1))
    below = lax.ppermute(high, "gy", ring(rows, 1))
    sides = along_x(sides)
    wide, halves = wide_grid(grid, layers)
    return two_sections(wide, halves, beyond, above, below, sides, joined)


def solution(mesh):
    return jax.shard_map(
        body,
        mesh=mesh,
        in_specs=(P(("gx", "gy", "gz"), None, None), P(("gx", "gy", "gz")), P(("gx", "gy", "gz"))),
        out_specs=P(None, "gx", "gy", "gz"),
        check_vma=False,
    )
```

time: 52.4 us -> 50.9 us (0.971)
  starting transfers between devices: 22.6 us -> 21.4 us
  Pallas kernels: 9.06 us -> 8.3 us
    ppermute x1, waiting for transfers between devices: 1.58 us -> 4.11 us  [body(): below = lax.ppermute(high, 'gz', ring(along, 1))]
    ppermute x1, waiting for transfers between devices: 2.03 us -> 0.01 us  [body(): below = lax.ppermute(high, 'gy', ring(rows, 1))]
    ppermute x1, starting transfers between devices: 2.02 us -> 0.01 us  [body(): below = lax.ppermute(high, 'gz', ring(along, 1))]
    ppermute x1, starting transfers between devices: 1.73 us -> 0.06 us  [body(): above = lax.ppermute(low, 'gy', ring(rows, -1))]
    ppermute x1 -> x2, starting transfers between devices: 0.57 us -> 2.09 us  [along_x(): return [lax.ppermute(sides[0], 'gx', ring(across, 1))]]
    pallas_call x5 -> x4, Pallas kernels: 3.62 us -> 3.32 us  [the longest x1 1.27 us: boxes_in_place(): pl.pallas_call(kernel, out_shape=[jax.ShapeDtypeStruct((boxes + 1,) + BOX...]
    ppermute x1 -> x2, waiting for transfers between devices: 3.08 us -> 3.14 us  [along_x(): return [lax.ppermute(sides[0], 'gx', ring(across, 1))]]
  transfers between devices with their start and end apart: 12 -> 13, of which waited for: 7 -> 6; matrix products, arithmetic and copies ran while one was open for 0% -> 0% of each run, Pallas kernels for 3% -> 3%
where the time goes in v5:
time: 50.9 us; the launch traced here: 50.7 us
  starting transfers between devices  21.4 us (42%)
  waiting for transfers between devices  19.3 us (38%)
  Pallas kernels  8.3 us (16%)
  local copies, waits for them, and re-layouts  1.7 us (3%)
    ppermute x7, starting transfers between devices, body(): lax.ppermute(departing[k], ('gx', 'gz'), [(i, i ^ k) for i in range(group...  16.4 us
    ppermute x7, waiting for transfers between devices, body(): lax.ppermute(departing[k], ('gx', 'gz'), [(i, i ^ k) for i in range(group...  11.8 us
    ppermute x1, waiting for transfers between devices, body(): below = lax.ppermute(high, 'gz', ring(along, 1))  4.11 us
    pallas_call x1, Pallas kernels, two_sections(): pl.pallas_call(kernel, out_shape=jax.ShapeDtypeStruct((FIELDS, NX, NY, LA...  3.6 us
    ppermute x2, waiting for transfers between devices, along_x(): return [lax.ppermute(sides[0], 'gx', ring(across, 1))]  3.14 us
    ppermute x1, starting transfers between devices, body(): above = lax.ppermute(low, 'gz', ring(along, -1))  2.33 us
    ppermute x2, starting transfers between devices, along_x(): return [lax.ppermute(sides[0], 'gx', ring(across, 1))]  2.09 us
    unnamed x6, local copies, waits for them, and re-layouts  1.7 us
  transfers between devices with their start and end apart: 13, of which 6 were waited for; matrix products, arithmetic and copies ran while one was open for 0% of the time, Pallas kernels for 3%

profile of v5, /device:TPU:0, one launch (start us, length us, event | category | flops | bytes accessed | tf_op | source)
XLA Modules:
  0.0 50.7 jit_solution(13069360500238352066)
XLA Ops:
  0.0 0.0 copy-start.2
  0.0 0.7 %copy-done.2 = s32[64]{0:T(128)S(1)} copy-done((s32[64]{0:T(128)S(1)}, s32[64]{0:T(128)}, u32[]{:S(2)}) %copy-start.2) | copy-done | bytes 280
  0.7 0.0 copy-start
  0.7 1.0 %copy-done = f32[64,4,512]{2,1,0:T(4,128)S(1)} copy-done((f32[64,4,512]{2,1,0:T(4,128)S(1)}, f32[64,4,512]{2,1,0:T(4,128)}, u32[]{:S(2)}) %copy-start) | copy-done | bytes 524312
  1.7 1.2 %pack_boxes.1 = (f32[16,2,8,128]{3,2,1,0:T(8,128)S(1)}, f32[16,2,8,128]{3,2,1,0:T(8,128)S(1)}, f32[16,2,8,128]{3,2,1,0:T(8,128)S(1)}, f32[16,2,8,128]{3,2,1,0:T(...) custom-call(s32[1]{0:T(128)} %bitcast.me_ref, ...), custom_call_target="tpu_custom_call" | custom-call | tf_op jit(solution)/shard_map/pack_boxes/pallas_call | solution.py:67
  2.9 3.1 %collective-permute-start = (f32[16,2,8,128]{3,2,1,0:T(8,128)S(1)}, f32[16,2,8,128]{3,2,1,0:T(8,128)S(1)}, u32[]{:S(2)}, u32[]{:S(2)}) collective-permute-start(f32[16,2,8,128]{3,2,1,0:T(8,128)S(1)} %get-tuple-element.25), channel_id=1, source_target_pairs={{0,1},{1,0},{2,3},{3,2},{16,17},{17,16},{18,19},{19,18},{4,5},{5,4... | collective-permute-start | bytes 393224 | tf_op jit(solution)/shard_map/ppermute | solution.py:443
  6.0 2.6 %collective-permute-start.1 = (f32[16,2,8,128]{3,2,1,0:T(8,128)S(1)}, f32[16,2,8,128]{3,2,1,0:T(8,128)S(1)}, u32[]{:S(2)}, u32[]{:S(2)}) collective-permute-start(f32[16,2,8,128]{3,2,1,0:T(8,128)S(1)} %get-tuple-element.26), channel_id=1, source_target_pairs={{0,2},{1,3},{2,0},{3,1},{16,18},{17,19},{18,16},{19,17},{4,6},{5,7... | collective-permute-start | bytes 393224 | tf_op jit(solution)/shard_map/ppermute | solution.py:443
  8.6 0.0 collective-permute-start.2
  8.6 1.7 %collective-permute-start.3 = (f32[16,2,8,128]{3,2,1,0:T(8,128)S(1)}, f32[16,2,8,128]{3,2,1,0:T(8,128)S(1)}, u32[]{:S(2)}, u32[]{:S(2)}) collective-permute-start(f32[16,2,8,128]{3,2,1,0:T(8,128)S(1)} %get-tuple-element.28), channel_id=1, source_target_pairs={{0,16},{1,17},{2,18},{3,19},{16,0},{17,1},{18,2},{19,3},{4,20},{5,... | collective-permute-start | bytes 393224 | tf_op jit(solution)/shard_map/ppermute | solution.py:443
  10.4 0.6 %collective-permute-start.4 = (f32[16,2,8,128]{3,2,1,0:T(8,128)S(1)}, f32[16,2,8,128]{3,2,1,0:T(8,128)S(1)}, u32[]{:S(2)}, u32[]{:S(2)}) collective-permute-start(f32[16,2,8,128]{3,2,1,0:T(8,128)S(1)} %get-tuple-element.29), channel_id=1, source_target_pairs={{0,17},{1,16},{2,19},{3,18},{16,1},{17,0},{18,3},{19,2},{4,21},{5,... | collective-permute-start | bytes 393224 | tf_op jit(solution)/shard_map/ppermute | solution.py:443
  11.0 0.1 collective-permute-done.refs_1_
  11.1 4.4 %collective-permute-start.5 = (f32[16,2,8,128]{3,2,1,0:T(8,128)S(1)}, f32[16,2,8,128]{3,2,1,0:T(8,128)S(1)}, u32[]{:S(2)}, u32[]{:S(2)}) collective-permute-start(f32[16,2,8,128]{3,2,1,0:T(8,128)S(1)} %get-tuple-element.30), channel_id=1, source_target_pairs={{0,18},{1,19},{2,16},{3,17},{16,2},{17,3},{18,0},{19,1},{4,22},{5,... | collective-permute-start | bytes 393224 | tf_op jit(solution)/shard_map/ppermute | solution.py:443
  15.4 3.5 %collective-permute-done.1.refs_2_ = f32[16,2,8,128]{3,2,1,0:T(8,128)S(1)} collective-permute-done((f32[16,2,8,128]{3,2,1,0:T(8,128)S(1)}, f32[16,2,8,128]{3,2,1,0:T(8,128)S(1)}, u32[]{:S(2)}, u32[]{:S(2)}) %collective-permute-start.1) | collective-permute-done | bytes 131104 | tf_op jit(solution)/shard_map/ppermute | solution.py:443
  19.0 0.0 copy-start.1
  19.0 4.0 %collective-permute-start.6 = (f32[16,2,8,128]{3,2,1,0:T(8,128)S(1)}, f32[16,2,8,128]{3,2,1,0:T(8,128)S(1)}, u32[]{:S(2)}, u32[]{:S(2)}) collective-permute-start(f32[16,2,8,128]{3,2,1,0:T(8,128)S(1)} %get-tuple-element.31), channel_id=1, source_target_pairs={{0,19},{1,18},{2,17},{3,16},{16,3},{17,2},{18,1},{19,0},{4,23},{5,... | collective-permute-start | bytes 393224 | tf_op jit(solution)/shard_map/ppermute | solution.py:443
  22.9 0.0 collective-permute-done.2.refs_3_
  23.0 0.0 collective-permute-done.3.refs_4_
  23.0 0.0 collective-permute-done.4.refs_5_
  23.0 8.2 %collective-permute-done.5.refs_6_ = f32[16,2,8,128]{3,2,1,0:T(8,128)S(1)} collective-permute-done((f32[16,2,8,128]{3,2,1,0:T(8,128)S(1)}, f32[16,2,8,128]{3,2,1,0:T(8,128)S(1)}, u32[]{:S(2)}, u32[]{:S(2)}) %collective-permute-start.5) | collective-permute-done | bytes 131104 | tf_op jit(solution)/shard_map/ppermute | solution.py:443
  31.1 0.0 collective-permute-done.6.refs_7_
  31.1 0.0 copy-done.1
  31.1 1.3 %boxes_in_place.1 = (f32[65,2,8,128]{3,2,1,0:T(8,128)S(1)}, f32[4,2,8,128]{3,2,1,0:T(8,128)S(1)}, f32[4,2,8,128]{3,2,1,0:T(8,128)S(1)}, f32[2,16,8,128]{3,2,1,0:T(8,128)S(1)}) custom-call(s32[1]{0:T(128)} %bitcast.me_ref, s32[64]{0:T(128)S(1)} %copy-done.1, f32[16,2,8,128]{3,2,1,0:T(8,128)S(1)} %get-tuple-element.24.refs_0_, ...), custom_call_target="tpu_custom_call" | custom-call | tf_op jit(solution)/shard_map/boxes_in_place/pallas_call | solution.py:136
  32.4 0.6 %collective-permute-start.9 = (f32[2,16,8,128]{3,2,1,0:T(8,128)S(1)}, f32[2,16,8,128]{3,2,1,0:T(8,128)S(1)}, u32[]{:S(2)}, u32[]{:S(2)}) collective-permute-start(f32[2,16,8,128]{3,2,1,0:T(8,128)S(1)} %get-tuple-element.35), channel_id=1, source_target_pairs={{0,16},{16,0},{1,17},{17,1},{2,18},{18,2},{3,19},{19,3},{4,20},{20... | collective-permute-start | bytes 393224 | tf_op jit(solution)/shard_map/ppermute | solution.py:456
  33.0 2.3 %collective-permute-start.7 = (f32[4,2,8,128]{3,2,1,0:T(8,128)S(1)}, f32[4,2,8,128]{3,2,1,0:T(8,128)S(1)}, u32[]{:S(2)}, u32[]{:S(2)}) collective-permute-start(f32[4,2,8,128]{3,2,1,0:T(8,128)S(1)} %get-tuple-element.33), channel_id=1, source_target_pairs={{0,3},{1,0},{2,1},{3,2},{4,7},{5,4},{6,5},{7,6},{8,11},{9,8},{10,9... | collective-permute-start | bytes 98312 | tf_op jit(solution)/shard_map/ppermute | solution.py:460
  35.3 0.0 collective-permute-start.8
  35.3 1.4 %grid_from_boxes.1.grid = f32[4,16,16,128]{3,2,1,0:T(8,128)S(1)} custom-call(f32[65,2,8,128]{3,2,1,0:T(8,128)S(1)} %get-tuple-element.32.held), custom_call_target="tpu_custom_call" | custom-call | flops 4194304 | bytes 2097152 | tf_op jit(solution)/shard_map/grid_from_boxes/pallas_call | solution.py:180
  36.7 0.2 collective-permute-done.7.above
  36.9 4.1 %collective-permute-done.8.below = f32[4,2,8,128]{3,2,1,0:T(8,128)S(1)} collective-permute-done((f32[4,2,8,128]{3,2,1,0:T(8,128)S(1)}, f32[4,2,8,128]{3,2,1,0:T(8,128)S(1)}, u32[]{:S(2)}, u32[]{:S(2)}) %collective-permute-start.8) | collective-permute-done | bytes 32800 | tf_op jit(solution)/shard_map/ppermute | solution.py:461
  41.0 0.0 collective-permute-done.9.refs_0_
  41.0 0.7 %faces_and_rows.1 = (f32[4,4,16,128]{3,2,1,0:T(8,128)S(1)}, f32[4,16,16,128]{3,2,1,0:T(8,128)S(1)}, f32[152,128]{1,0:T(8,128)S(1)}, f32[152,128]{1,0:T(8,128)S(1)}, f32[2,4,16,128]{3,2,1,0:T(8,128)S(1)}) custom-call(f32[4,16,16,128]{3,2,1,0:T(8,128)S(1)} %grid_from_boxes.1.grid, f32[4,2,8,128]{3,2,1,0:T(8,128)S(1)} %collective-permute-done.7.above, ...), custom_call_target="tpu_custom_call" | custom-call | tf_op jit(solution)/shard_map/faces_and_rows/pallas_call | solution.py:255
  41.8 0.1 collective-permute-start.10
  41.8 0.5 collective-permute-start.11
  42.3 1.5 %collective-permute-start.12 = (f32[2,4,16,128]{3,2,1,0:T(8,128)S(1)}, f32[2,4,16,128]{3,2,1,0:T(8,128)S(1)}, u32[]{:S(2)}, u32[]{:S(2)}) collective-permute-start(f32[2,4,16,128]{3,2,1,0:T(8,128)S(1)} %get-tuple-element.42), channel_id=1, source_target_pairs={{0,16},{16,0},{1,17},{17,1},{2,18},{18,2},{3,19},{19,3},{4,20},{20... | collective-permute-start | bytes 196616 | tf_op jit(solution)/shard_map/ppermute | solution.py:456
  43.8 0.1 wide_grid.1
  44.0 3.1 %collective-permute-done.12.refs_0_ = f32[2,4,16,128]{3,2,1,0:T(8,128)S(1)} collective-permute-done((f32[2,4,16,128]{3,2,1,0:T(8,128)S(1)}, f32[2,4,16,128]{3,2,1,0:T(8,128)S(1)}, u32[]{:S(2)}, u32[]{:S(2)}) %collective-permute-start.12) | collective-permute-done | bytes 65568 | tf_op jit(solution)/shard_map/ppermute | solution.py:456
  47.1 0.0 collective-permute-done.10.above
  47.1 0.0 collective-permute-done.11.below
  47.1 3.6 %two_sections.1 = f32[4,16,16,128]{3,2,1,0:T(8,128)} custom-call(f32[4,20,16,128]{3,2,1,0:T(8,128)S(1)} %get-tuple-element.37.wide, f32[20,16,128]{2,1,0:T(8,128)S(1)} %get-tuple-element.38.halves, f32[4,16,16,128]{3,2,1,0:T(8,128)S(1)} %get-tuple-element.39.inner_beyond, f32[152,128]{1,0:T(8,128)S(1)} %collective-permute-done.10.above, ...), custom_call_target="tpu_custom_call" | custom-call | tf_op jit(solution)/shard_map/two_sections/pallas_call | solution.py:412
Async XLA Ops:
  0.0 0.7 %copy-start.2 = (s32[64]{0:T(128)S(1)}, s32[64]{0:T(128)}, u32[]{:S(2)}) copy-start(s32[64]{0:T(128)} %owner.2) | copy-start | bytes 772
  0.7 1.0 %copy-start = (f32[64,4,512]{2,1,0:T(4,128)S(1)}, f32[64,4,512]{2,1,0:T(4,128)}, u32[]{:S(2)}) copy-start(f32[64,4,512]{2,1,0:T(4,128)} %fields.1) | copy-start | bytes 1572868
  2.9 8.1 %collective-permute-start = (f32[16,2,8,128]{3,2,1,0:T(8,128)S(1)}, f32[16,2,8,128]{3,2,1,0:T(8,128)S(1)}, u32[]{:S(2)}, u32[]{:S(2)}) collective-permute-start(f32[16,2,8,128]{3,2,1,0:T(8,128)S(1)} %get-tuple-element.25), channel_id=1, source_target_pairs={{0,1},{1,0},{2,3},{3,2},{16,17},{17,16},{18,19},{19,18},{4,5},{5,4... | collective-permute-start | bytes 393224 | tf_op jit(solution)/shard_map/ppermute | solution.py:443
  6.0 12.9 %collective-permute-start.1 = (f32[16,2,8,128]{3,2,1,0:T(8,128)S(1)}, f32[16,2,8,128]{3,2,1,0:T(8,128)S(1)}, u32[]{:S(2)}, u32[]{:S(2)}) collective-permute-start(f32[16,2,8,128]{3,2,1,0:T(8,128)S(1)} %get-tuple-element.26), channel_id=1, source_target_pairs={{0,2},{1,3},{2,0},{3,1},{16,18},{17,19},{18,16},{19,17},{4,6},{5,7... | collective-permute-start | bytes 393224 | tf_op jit(solution)/shard_map/ppermute | solution.py:443
  8.6 14.3 %collective-permute-start.2 = (f32[16,2,8,128]{3,2,1,0:T(8,128)S(1)}, f32[16,2,8,128]{3,2,1,0:T(8,128)S(1)}, u32[]{:S(2)}, u32[]{:S(2)}) collective-permute-start(f32[16,2,8,128]{3,2,1,0:T(8,128)S(1)} %get-tuple-element.27), channel_id=1, source_target_pairs={{0,3},{1,2},{2,1},{3,0},{16,19},{17,18},{18,17},{19,16},{4,7},{5,6... | collective-permute-start | bytes 393224 | tf_op jit(solution)/shard_map/ppermute | solution.py:443
  8.6 14.3 %collective-permute-start.3 = (f32[16,2,8,128]{3,2,1,0:T(8,128)S(1)}, f32[16,2,8,128]{3,2,1,0:T(8,128)S(1)}, u32[]{:S(2)}, u32[]{:S(2)}) collective-permute-start(f32[16,2,8,128]{3,2,1,0:T(8,128)S(1)} %get-tuple-element.28), channel_id=1, source_target_pairs={{0,16},{1,17},{2,18},{3,19},{16,0},{17,1},{18,2},{19,3},{4,20},{5,... | collective-permute-start | bytes 393224 | tf_op jit(solution)/shard_map/ppermute | solution.py:443
  10.4 12.6 %collective-permute-start.4 = (f32[16,2,8,128]{3,2,1,0:T(8,128)S(1)}, f32[16,2,8,128]{3,2,1,0:T(8,128)S(1)}, u32[]{:S(2)}, u32[]{:S(2)}) collective-permute-start(f32[16,2,8,128]{3,2,1,0:T(8,128)S(1)} %get-tuple-element.29), channel_id=1, source_target_pairs={{0,17},{1,16},{2,19},{3,18},{16,1},{17,0},{18,3},{19,2},{4,21},{5,... | collective-permute-start | bytes 393224 | tf_op jit(solution)/shard_map/ppermute | solution.py:443
  11.1 20.1 %collective-permute-start.5 = (f32[16,2,8,128]{3,2,1,0:T(8,128)S(1)}, f32[16,2,8,128]{3,2,1,0:T(8,128)S(1)}, u32[]{:S(2)}, u32[]{:S(2)}) collective-permute-start(f32[16,2,8,128]{3,2,1,0:T(8,128)S(1)} %get-tuple-element.30), channel_id=1, source_target_pairs={{0,18},{1,19},{2,16},{3,17},{16,2},{17,3},{18,0},{19,1},{4,22},{5,... | collective-permute-start | bytes 393224 | tf_op jit(solution)/shard_map/ppermute | solution.py:443
  19.0 12.2 %copy-start.1 = (s32[64]{0:T(128)S(1)}, s32[64]{0:T(128)}, u32[]{:S(2)}) copy-start(s32[64]{0:T(128)} %owner.3) | copy-start | bytes 772
  19.0 12.2 %collective-permute-start.6 = (f32[16,2,8,128]{3,2,1,0:T(8,128)S(1)}, f32[16,2,8,128]{3,2,1,0:T(8,128)S(1)}, u32[]{:S(2)}, u32[]{:S(2)}) collective-permute-start(f32[16,2,8,128]{3,2,1,0:T(8,128)S(1)} %get-tuple-element.31), channel_id=1, source_target_pairs={{0,19},{1,18},{2,17},{3,16},{16,3},{17,2},{18,1},{19,0},{4,23},{5,... | collective-permute-start | bytes 393224 | tf_op jit(solution)/shard_map/ppermute | solution.py:443
  32.4 8.6 %collective-permute-start.9 = (f32[2,16,8,128]{3,2,1,0:T(8,128)S(1)}, f32[2,16,8,128]{3,2,1,0:T(8,128)S(1)}, u32[]{:S(2)}, u32[]{:S(2)}) collective-permute-start(f32[2,16,8,128]{3,2,1,0:T(8,128)S(1)} %get-tuple-element.35), channel_id=1, source_target_pairs={{0,16},{16,0},{1,17},{17,1},{2,18},{18,2},{3,19},{19,3},{4,20},{20... | collective-permute-start | bytes 393224 | tf_op jit(solution)/shard_map/ppermute | solution.py:456
  33.0 3.9 %collective-permute-start.7 = (f32[4,2,8,128]{3,2,1,0:T(8,128)S(1)}, f32[4,2,8,128]{3,2,1,0:T(8,128)S(1)}, u32[]{:S(2)}, u32[]{:S(2)}) collective-permute-start(f32[4,2,8,128]{3,2,1,0:T(8,128)S(1)} %get-tuple-element.33), channel_id=1, source_target_pairs={{0,3},{1,0},{2,1},{3,2},{4,7},{5,4},{6,5},{7,6},{8,11},{9,8},{10,9... | collective-permute-start | bytes 98312 | tf_op jit(solution)/shard_map/ppermute | solution.py:460
  35.3 5.7 %collective-permute-start.8 = (f32[4,2,8,128]{3,2,1,0:T(8,128)S(1)}, f32[4,2,8,128]{3,2,1,0:T(8,128)S(1)}, u32[]{:S(2)}, u32[]{:S(2)}) collective-permute-start(f32[4,2,8,128]{3,2,1,0:T(8,128)S(1)} %get-tuple-element.34), channel_id=1, source_target_pairs={{0,1},{1,2},{2,3},{3,0},{4,5},{5,6},{6,7},{7,4},{8,9},{9,10},{10,1... | collective-permute-start | bytes 98312 | tf_op jit(solution)/shard_map/ppermute | solution.py:461
  41.8 5.3 %collective-permute-start.10 = (f32[152,128]{1,0:T(8,128)S(1)}, f32[152,128]{1,0:T(8,128)S(1)}, u32[]{:S(2)}, u32[]{:S(2)}) collective-permute-start(f32[152,128]{1,0:T(8,128)S(1)} %get-tuple-element.40), channel_id=1, source_target_pairs={{0,12},{4,0},{8,4},{12,8},{1,13},{5,1},{9,5},{13,9},{2,14},{6,2},{... | collective-permute-start | bytes 233480 | tf_op jit(solution)/shard_map/ppermute | solution.py:465
  41.8 5.3 %collective-permute-start.11 = (f32[152,128]{1,0:T(8,128)S(1)}, f32[152,128]{1,0:T(8,128)S(1)}, u32[]{:S(2)}, u32[]{:S(2)}) collective-permute-start(f32[152,128]{1,0:T(8,128)S(1)} %get-tuple-element.41), channel_id=1, source_target_pairs={{0,4},{4,8},{8,12},{12,0},{1,5},{5,9},{9,13},{13,1},{2,6},{6,10},{... | collective-permute-start | bytes 233480 | tf_op jit(solution)/shard_map/ppermute | solution.py:466
  42.3 4.8 %collective-permute-start.12 = (f32[2,4,16,128]{3,2,1,0:T(8,128)S(1)}, f32[2,4,16,128]{3,2,1,0:T(8,128)S(1)}, u32[]{:S(2)}, u32[]{:S(2)}) collective-permute-start(f32[2,4,16,128]{3,2,1,0:T(8,128)S(1)} %get-tuple-element.42), channel_id=1, source_target_pairs={{0,16},{16,0},{1,17},{17,1},{2,18},{18,2},{3,19},{19,3},{4,20},{20... | collective-permute-start | bytes 196616 | tf_op jit(solution)/shard_map/ppermute | solution.py:456

commit v6 on v5

--- a/solution.py
+++ b/solution.py
@@ -76,6 +76,24 @@
         compiler_params=ROOM,
         name="pack_boxes",
     )(me, new_owner, old_fields)
+
+
+def position_table(old_owner, group, capacity):
+    boxes = old_owner.shape[0]
+
+    def kernel(owner, table, counts):
+        rank_table(owner, table, counts, group, capacity, boxes, boxes)
+
+    return pl.pallas_call(
+        kernel,
+        out_shape=jax.ShapeDtypeStruct((group * capacity,), jnp.int32),
+        in_specs=[SMEM],
+        out_specs=SMEM,
+        scratch_shapes=[pltpu.SMEM((group,), jnp.int32)],
+        compiler_params=ROOM,
+        cost_estimate=pl.CostEstimate(flops=0, bytes_accessed=2**22, transcendentals=0),
+        name="position_table",
+    )(old_owner)
 
 
 def swap_boxes(columns):
@@ -99,20 +117,17 @@
     return [(i, (i + step) % count) for i in range(count)]
 
 
-def boxes_in_place(arrived, old_owner, me, group, capacity, split, joined):
-    boxes = old_owner.shape[0]
+def boxes_in_place(arrived, table, me, boxes, capacity, split, joined):
     pieces = len(arrived)
-    rows = group * capacity // pieces
+    rows = table.shape[0] // pieces
     half = boxes // BRICK_X
     face = (BRICK_Z, BRICK_Y * FIELDS, LANES)
     faces = [jax.ShapeDtypeStruct((2,) + face if joined else face, jnp.float32)] * (2 - joined)
-    end = jax.ShapeDtypeStruct((BRICK_X * BRICK_Y,) + BOX, jnp.float32)
-
-    def kernel(me_ref, owner, *refs):
+    end = jax.ShapeDtypeStruct((2, 2 * FIELDS, LANES), jnp.float32)
+
+    def kernel(me_ref, table, *refs):
         ins, refs = refs[:pieces], refs[pieces:]
-        (held, low, high), refs = refs[:3], refs[3:]
-        outs, (table, counts) = refs[: len(faces)], refs[len(faces) :]
-        rank_table(owner, table, counts, group, capacity, boxes, boxes)
+        held, low, high, *outs = refs
         for k, rows_in in enumerate(ins):
             base = (me_ref[0] ^ k) * capacity if split else 0
 
@@ -129,22 +144,25 @@
                     out[bz, pl.ds(by * FIELDS, FIELDS), :] = held[
                         p, side, pl.ds(side * FIELDS, FIELDS), :
                     ]
-        for b in range(BRICK_X * BRICK_Y):
-            low[b] = held[b * BRICK_Z]
-            high[b] = held[b * BRICK_Z + BRICK_Z - 1]
+        pair = lax.broadcasted_iota(jnp.int32, (2 * FIELDS, LANES), 1) % EDGE // HALO
+        for out, bz, first in ((low, 0, 0), (high, BRICK_Z - 1, EDGE - HALO)):
+            for group in range(2):
+                packed = jnp.zeros((2 * FIELDS, LANES), jnp.float32)
+                for n in range(4):
+                    b, part = divmod(group * 4 + n, 2)
+                    cells = held[b * BRICK_Z + bz, part]
+                    shift = (n * HALO - first) % LANES
+                    packed = jnp.where(pair == n, pltpu.roll(cells, shift, 1) if shift else cells, packed)
+                out[group] = packed
 
     return pl.pallas_call(
         kernel,
         out_shape=[jax.ShapeDtypeStruct((boxes + 1,) + BOX, jnp.float32), end, end] + faces,
         in_specs=[SMEM, SMEM] + [VMEM] * pieces,
         out_specs=[VMEM] * (3 + len(faces)),
-        scratch_shapes=[
-            pltpu.SMEM((group * capacity,), jnp.int32),
-            pltpu.SMEM((group,), jnp.int32),
-        ],
         compiler_params=ROOM,
         name="boxes_in_place",
-    )(me, old_owner, *arrived)
+    )(me, table, *arrived)
 
 
 HALO = 2
@@ -197,11 +215,12 @@
     return (f * NEAR_X + x) * HALO
 
 
+def side_place(side, f):
+    return side * FIELDS + f
+
+
 def faces_and_rows(grid, faces, above, below, joined):
-    side_shape = (FIELDS, NY, LANES)
-    sides = [jax.ShapeDtypeStruct((2,) + side_shape if joined else side_shape, jnp.float32)] * (
-        2 - joined
-    )
+    sides = [jax.ShapeDtypeStruct((NY, LANES), jnp.float32)] * (2 - joined)
 
     def kernel(grid, above, below, *refs):
         ins, refs = refs[: len(faces)], refs[len(faces) :]
@@ -218,12 +237,13 @@
         for bx in range(BRICK_X):
             for by in range(BRICK_Y):
                 for half in range(TILES // 2):
-                    after, before = above[bx * BRICK_Y + by, half], below[bx * BRICK_Y + by, half]
+                    group, n = divmod((bx * BRICK_Y + by) * 2 + half, 4)
+                    after, before = above[group], below[group]
                     columns = [
                         jnp.where(
                             lane < LANES // 2,
-                            pltpu.roll(after, (LANES - EDGE * r) % LANES, 1),
-                            pltpu.roll(before, LANES - EDGE - EDGE * r, 1),
+                            pltpu.roll(after, (LANES - EDGE * r - HALO * n) % LANES, 1),
+                            pltpu.roll(before, (2 * LANES - HALO - EDGE * r - HALO * n) % LANES, 1),
                         )
                         for r in range(16)
                     ]
@@ -246,10 +266,17 @@
                     moved = pltpu.roll(beyond[f, x, pl.ds(first, EDGE), :], 2 * place + 1, 1)
                     edge = jnp.where(pair == place, moved, edge)
             out[pl.ds(ROWS, EDGE), :] = edge
+        pair = lax.broadcasted_iota(jnp.int32, (NY, LANES), 1) // 2
+        edges = [jnp.zeros((NY, LANES), jnp.float32)] * 2
         for side in range(2):
-            out = outs[0].at[side] if joined else outs[side]
             for f in range(FIELDS):
-                out[f] = beyond[f, side * (NX - 1)]
+                moved = pltpu.roll(beyond[f, side * (NX - 1)], 2 * side_place(side, f) + 1, 1)
+                edges[side] = jnp.where(pair == side_place(side, f), moved, edges[side])
+        if joined:
+            outs[0][...] = jnp.where(pair < FIELDS, edges[0], edges[1])
+        else:
+            for out, edge in zip(outs, edges):
+                out[...] = edge
 
     rows = jax.ShapeDtypeStruct((EDGES, LANES), jnp.float32)
     return pl.pallas_call(
@@ -273,135 +300,232 @@
     return 0.5 * (v * jnp.sqrt(v))
 
 
-def wide_grid(grid, layers):
-    def kernel(grid, layers, wide, halves):
+def step(cells, rates):
+    return [v + (TIME_STEP * c) * r for v, c, r in zip(cells, DIFFUSION, rates)]
+
+
+def rates(cells, s, beside):
+    means = [s + n for _, n in beside]
+    sums = []
+    for f, v in enumerate(cells):
+        terms = [m * (fields[f] - v) for m, (fields, _) in zip(means, beside)]
+        sums.append(sum(terms[1:], terms[0]))
+    return sums
+
+
+def each(function, cells, *others):
+    fields, s = cells
+    columns = zip(fields, *[other[0] for other in others])
+    return [function(*c) for c in columns], function(s, *[other[1] for other in others])
+
+
+def z_beside(cells, across):
+    lane = lax.broadcasted_iota(jnp.int32, cells[1].shape, 1)
+
+    def after(v, other):
+        return pltpu.roll(jnp.where(lane == 0, other, v), LANES - 1, 1)
+
+    def before(v, other):
+        return pltpu.roll(jnp.where(lane == LANES - 1, other, v), 1, 1)
+
+    return [each(after, cells, across), each(before, cells, across)]
+
+
+def y_beside(cells):
+    row = lax.broadcasted_iota(jnp.int32, (NY, LANES), 0)
+
+    def after(v):
+        return jnp.where(row == NY - 1, v, pltpu.roll(v, NY - 1, 0))
+
+    def before(v):
+        return jnp.where(row == 0, v, pltpu.roll(v, 1, 0))
+
+    return [each(after, cells), each(before, cells)]
+
+
+def first_inside(grid, layers, beyond):
+    def kernel(grid, layers, beyond, wide, halves, first, first_beyond, halves_beyond):
         for f in range(FIELDS):
-            for x in range(WIDE_X):
-                inside = HALO <= x < HALO + NX
-                wide[f, x] = grid[f, x - HALO] if inside else layers[f, x % (NX + HALO) + (x > HALO) * HALO]
-
-        def conductances(x, carry):
-            halves[x] = half_conductance(wide[0, x])
+            for x in range(HALO):
+                wide[f, x] = layers[f, x]
+                wide[f, HALO + NX + x] = layers[f, HALO + x]
+        for x in range(HALO):
+            halves[x] = half_conductance(layers[0, x])
+            halves[HALO + NX + x] = half_conductance(layers[0, HALO + x])
+
+        def prepare(x, carry):
+            for f in range(FIELDS):
+                wide[f, x + HALO] = grid[f, x]
+            halves[x + HALO] = half_conductance(grid[0, x])
+            halves_beyond[x] = half_conductance(beyond[0, x])
             return carry
 
-        lax.fori_loop(0, WIDE_X, conductances, 0, unroll=5)
+        lax.fori_loop(0, NX, prepare, 0, unroll=4)
+
+        def at(ref, s, x):
+            return [ref[f, x] for f in range(FIELDS)], s[x]
+
+        def inside(x, carry):
+            here, over = at(wide, halves, x + HALO), at(beyond, halves_beyond, x)
+            beside = [at(wide, halves, x + HALO - 1), at(wide, halves, x + HALO + 1)]
+            beside += y_beside(here) + z_beside(here, over)
+            for f, v in enumerate(step(here[0], rates(*here, beside))):
+                first[f, x] = v
+            left, right = jnp.maximum(x - 1, 0), jnp.minimum(x + 1, NX - 1)
+            beside = [at(beyond, halves_beyond, left), at(beyond, halves_beyond, right)]
+            beside += y_beside(over) + z_beside(over, here)
+            for f, v in enumerate(step(over[0], rates(*over, beside))):
+                first_beyond[f, x] = v
+            return carry
+
+        lax.fori_loop(0, NX, inside, 0, unroll=2)
+
+    def shape(*sizes):
+        return jax.ShapeDtypeStruct(sizes + (NY, LANES), jnp.float32)
 
     return pl.pallas_call(
         kernel,
         out_shape=[
-            jax.ShapeDtypeStruct((FIELDS, WIDE_X, NY, LANES), jnp.float32),
-            jax.ShapeDtypeStruct((WIDE_X, NY, LANES), jnp.float32),
+            shape(FIELDS, WIDE_X),
+            shape(WIDE_X),
+            shape(FIELDS, NX),
+            shape(FIELDS, NX),
+            shape(NX),
         ],
-        in_specs=[VMEM] * 2,
-        out_specs=[VMEM] * 2,
+        in_specs=[VMEM] * 3,
+        out_specs=[VMEM] * 5,
         compiler_params=ROOM,
         cost_estimate=pl.CostEstimate(flops=2**22, bytes_accessed=2**21, transcendentals=0),
-        name="wide_grid",
-    )(grid, layers)
-
-
-def section(here, beside, across, rows):
-    lane = lax.broadcasted_iota(jnp.int32, (rows, LANES), 1)
-
-    def nearby(cells, other, left, right):
-        inside, other = cells[:rows], other[:rows]
-        return [
-            pltpu.roll(cells, WIDE_Y - 1, 0)[:rows],
-            pltpu.roll(cells, 1, 0)[:rows],
-            pltpu.roll(jnp.where(lane == 0, other, inside), LANES - 1, 1),
-            pltpu.roll(jnp.where(lane == LANES - 1, other, inside), 1, 1),
-            left[:rows],
-            right[:rows],
-        ]
-
-    (cells, s), ((left, s_left), (right, s_right)), (other, s_other) = here, beside, across
-    mean = [s[:rows] + n for n in nearby(s, s_other, s_left, s_right)]
-    rates = []
-    for f in range(FIELDS):
-        v = cells[f][:rows]
-        terms = [m * (n - v) for m, n in zip(mean, nearby(cells[f], other[f], left[f], right[f]))]
-        rates.append(sum(terms[1:], terms[0]))
-    return rates
-
-
-def two_sections(wide, halves, beyond, above, below, sides, joined):
-    def kernel(wide, halves, inner_beyond, above, below, *refs):
-        ins, refs = refs[: len(sides)], refs[len(sides) :]
-        out, ring_rows, ring_halves, beyond, first, first_beyond, bs, fs, fbs = refs
-        for f in range(FIELDS):
-            for x in range(NEAR_X):
-                ring_rows[f, x, pl.ds(0, HALO), :] = above[pl.ds(row_of(f, x), HALO), :]
-                ring_rows[f, x, pl.ds(EDGE - HALO, HALO), :] = below[pl.ds(row_of(f, x), HALO), :]
+        name="first_inside",
+    )(grid, layers, beyond)
+
+
+def last_sections(wide, halves, first, first_beyond, beyond, halves_beyond, above, below, sides):
+    def kernel(wide, halves, first_in, beyond_in, beyond, halves_beyond, above, below, *refs):
+        ins, (out, edges, first, first_beyond, around, fs, fbs) = refs[: len(sides)], refs[len(sides) :]
+        factors = [TIME_STEP * c for c in DIFFUSION]
         row = lax.broadcasted_iota(jnp.int32, (EDGE, LANES), 0)
-        edge = jnp.where(row < EDGE // 2, above[pl.ds(ROWS, EDGE), :], below[pl.ds(ROWS, EDGE), :])
+
+        def side_edge(side):
+            packed = ins[0 if len(ins) == 1 else side][...]
+            fields = [
+                pltpu.roll(packed, LANES - 1 - 2 * side_place(side, f), 1) for f in range(FIELDS)
+            ]
+            return fields, half_conductance(fields[0])
+
+        edge = jnp.where(
+            row < EDGE // 2,
+            pltpu.roll(below[pl.ds(ROWS, EDGE), :], 1, 0),
+            pltpu.roll(above[pl.ds(ROWS, EDGE), :], EDGE - 1, 0),
+        )
         for f in range(FIELDS):
             for x in range(NX):
-                beyond[f, x + 1, pl.ds(0, NY), :] = inner_beyond[f, x]
-                beyond[f, x + 1, pl.ds(NY, EDGE), :] = pltpu.roll(
+                edges[pl.ds((f * NX + x) * EDGE, EDGE), :] = pltpu.roll(
                     edge, LANES - 1 - 2 * (f * NX + x), 1
                 )
-            for side in range(2):
-                got = ins[0].at[side] if joined else ins[side]
-                beyond[f, 0 if side else NX + 1, pl.ds(0, NY), :] = got[f]
-
-        def conductances(x, carry):
-            ring_halves[x] = half_conductance(ring_rows[0, x])
-            bs[x] = half_conductance(beyond[0, x])
-            return carry
-
-        lax.fori_loop(0, NEAR_X, conductances, 0, unroll=6)
 
         def at(ref, s, x):
             return [ref[f, x] for f in range(FIELDS)], s[x]
 
-        def whole(x):
-            cells = [
-                jnp.concatenate([wide[f, x + 1], ring_rows[f, x]], 0) for f in range(FIELDS)
+        for side, x in ((1, 0), (0, NX + 1)):
+            here = at(wide, halves, x + 1)
+            beside = [at(wide, halves, x), at(wide, halves, x + 2)]
+            beside += y_beside(here) + z_beside(here, side_edge(side))
+            for f, v in enumerate(step(here[0], rates(*here, beside))):
+                first[pl.ds((f * NEAR_X + x) * NY, NY), :] = v
+        for f in range(FIELDS):
+            for x in range(NX):
+                first[pl.ds((f * NEAR_X + x + 1) * NY, NY), :] = first_in[f, x]
+
+        wide_rows = wide.reshape(FIELDS * WIDE_X * NY, LANES)
+        half_rows = halves.reshape(WIDE_X * NY, LANES)
+
+        def sent(ref, depth, f, x, count):
+            return ref[pl.ds(row_of(f, x) + depth, count, stride=HALO), :]
+
+        for ref, depth, y, tile_row in ((below, 1, 0, 7), (above, 0, NY - 1, 0)):
+            for x, count in ((0, 8), (8, 8), (16, 2)):
+                s = half_rows[pl.ds((x + 1) * NY + y, count, stride=NY), :]
+                mean = s + half_conductance(sent(ref, depth, 0, x, count))
+                for f in range(FIELDS):
+                    v = wide_rows[pl.ds((f * WIDE_X + x + 1) * NY + y, count, stride=NY), :]
+                    rows = pl.ds((f * NEAR_X + x) * NY + y, count, stride=NY)
+                    more = mean * (sent(ref, depth, f, x, count) - v)
+                    first[rows, :] = first[rows, :] + factors[f] * more
+            for x in (0, 8):
+
+                def line(depth, shift):
+                    fields = [sent(ref, depth, f, x + 1 + shift, 8) for f in range(FIELDS)]
+                    return fields, half_conductance(fields[0])
+
+                here = line(depth, 0)
+                inner = (
+                    [
+                        wide_rows[pl.ds((f * WIDE_X + x + HALO) * NY + y, 8, stride=NY), :]
+                        for f in range(FIELDS)
+                    ],
+                    half_rows[pl.ds((x + HALO) * NY + y, 8, stride=NY), :],
+                )
+                over = [
+                    edges[pl.ds((f * NX + x) * EDGE + 7 - tile_row, 8, stride=EDGE), :]
+                    for f in range(FIELDS)
+                ]
+                beside = [line(1 - depth, 0), inner, line(depth, -1), line(depth, 1)]
+                beside += z_beside(here, (over, half_conductance(over[0])))
+                for f, v in enumerate(step(here[0], rates(*here, beside))):
+                    around[pl.ds((f * NX + x) * EDGE + tile_row, 8, stride=EDGE), :] = v
+
+        for x in range(NX):
+            s = halves_beyond[x]
+            near = half_conductance(edges[pl.ds(x * EDGE, EDGE), :])
+            for f in range(FIELDS):
+                tile = edges[pl.ds((f * NX + x) * EDGE, EDGE), :]
+                v, fresh = beyond[f, x], beyond_in[f, x]
+                more = [
+                    jnp.where(row == at_row, (near + s[n * EDGE :][:EDGE]) * (tile - v[n * EDGE :][:EDGE]), 0.0)
+                    for n, at_row in enumerate((0, EDGE - 1))
+                ]
+                first_beyond[f, x] = fresh + factors[f] * jnp.concatenate(more, 0)
+        for side, x in ((1, 0), (0, NX - 1)):
+            fields, s = side_edge(side)
+            for f in range(FIELDS):
+                more = (s + halves_beyond[x]) * (fields[f] - beyond[f, x])
+                first_beyond[f, x] = first_beyond[f, x] + factors[f] * more
+
+        def near(x):
+            return [
+                first[pl.ds(pl.multiple_of((f * NEAR_X + x) * NY, NY), NY), :] for f in range(FIELDS)
             ]
-            return cells, jnp.concatenate([halves[x + 1], ring_halves[x]], 0)
-
-        def step(cells, rates):
-            rows = rates[0].shape[0]
-            return [
-                v[:rows] + (TIME_STEP * c) * r for v, c, r in zip(cells, DIFFUSION, rates)
+
+        def conductances(x, carry):
+            fs[x] = half_conductance(near(x)[0])
+            return carry
+
+        lax.fori_loop(0, NEAR_X, conductances, 0, unroll=6)
+
+        def conductances_beyond(x, carry):
+            fbs[x] = half_conductance(first_beyond[0, x])
+            return carry
+
+        lax.fori_loop(0, NX, conductances_beyond, 0, unroll=4)
+
+        def second(x, carry):
+            here = near(x + 1), fs[x + 1]
+            tiles = [
+                around[pl.ds(pl.multiple_of((f * NX + x) * EDGE, EDGE), EDGE), :]
+                for f in range(FIELDS)
             ]
-
-        def first_inside(x, carry):
-            here = whole(x)
-            rates = section(here, (narrow(x), narrow(x + 2)), at(beyond, bs, x), WIDE_Y)
-            fresh = step(here[0], rates)
-            for f in range(FIELDS):
-                first[f, x] = fresh[f]
-            fs[x] = half_conductance(fresh[0])
-            return carry
-
-        def narrow(x):
-            inner = jnp.clip(x - 1, 0, NEAR_X - 1)
-            cells = [
-                jnp.concatenate([wide[f, x], ring_rows[f, inner]], 0) for f in range(FIELDS)
+            ring_of = each(
+                lambda v, tile: jnp.concatenate([v, tile], 0), here, (tiles, half_conductance(tiles[0]))
+            )
+            beside = [(near(x), fs[x]), (near(x + 2), fs[x + 2])]
+            beside += [
+                each(lambda v: pltpu.roll(v, WIDE_Y - 1, 0)[:NY], ring_of),
+                each(lambda v: pltpu.roll(v, 1, 0)[:NY], ring_of),
             ]
-            return cells, jnp.concatenate([halves[x], ring_halves[inner]], 0)
-
-        lax.fori_loop(0, NEAR_X, first_inside, 0, unroll=3)
-
-        def first_outside(x, carry):
-            here = at(beyond, bs, x + 1)
-            across = [wide[f, x + HALO] for f in range(FIELDS)], halves[x + HALO]
-            rates = section(here, (at(beyond, bs, x), at(beyond, bs, x + 2)), across, NY)
-            fresh = step(here[0], rates)
-            for f in range(FIELDS):
-                first_beyond[f, x] = fresh[f]
-            fbs[x] = half_conductance(fresh[0])
-            return carry
-
-        lax.fori_loop(0, NX, first_outside, 0, unroll=4)
-
-        def second(x, carry):
-            here = at(first, fs, x + 1)
-            beside = at(first, fs, x), at(first, fs, x + 2)
-            fresh = step(here[0], section(here, beside, at(first_beyond, fbs, x), NY))
-            for f in range(FIELDS):
-                out[f, x] = 0.5 * wide[f, x + HALO] + 0.5 * fresh[f]
+            beside += z_beside(here, at(first_beyond, fbs, x))
+            for f, v in enumerate(step(here[0], rates(*here, beside))):
+                out[f, x] = 0.5 * wide[f, x + HALO] + 0.5 * v
             return carry
 
         lax.fori_loop(0, NX, second, 0, unroll=4)
@@ -412,21 +536,19 @@
     return pl.pallas_call(
         kernel,
         out_shape=jax.ShapeDtypeStruct((FIELDS, NX, NY, LANES), jnp.float32),
-        in_specs=[VMEM] * (5 + len(sides)),
+        in_specs=[VMEM] * (8 + len(sides)),
         out_specs=VMEM,
         scratch_shapes=[
-            scratch(FIELDS, NEAR_X, EDGE),
-            scratch(NEAR_X, EDGE),
-            scratch(FIELDS, NEAR_X, WIDE_Y),
-            scratch(FIELDS, NEAR_X, WIDE_Y),
+            scratch(FIELDS * NX * EDGE),
+            scratch(FIELDS * NEAR_X * NY),
             scratch(FIELDS, NX, NY),
-            scratch(NEAR_X, WIDE_Y),
-            scratch(NEAR_X, WIDE_Y),
+            scratch(FIELDS * NX * EDGE),
+            scratch(NEAR_X, NY),
             scratch(NX, NY),
         ],
         compiler_params=ROOM,
-        name="two_sections",
-    )(wide, halves, beyond, above, below, *sides)
+        name="last_sections",
+    )(wide, halves, first, first_beyond, beyond, halves_beyond, above, below, *sides)
 
 
 def body(old_fields, new_owner, old_owner):
@@ -438,6 +560,7 @@
     joined = across == 2
     me = (lax.axis_index("gx") * along + lax.axis_index("gz")).reshape(1)
     departing = pack_boxes(old_fields, new_owner, me, group_size, capacity, split)
+    table = position_table(old_owner, group_size, capacity)
     if split:
         arrived = [departing[0]] + [
             lax.ppermute(departing[k], ("gx", "gz"), [(i, i ^ k) for i in range(group_size)])
@@ -448,7 +571,7 @@
             lax.all_to_all(departing[0], ("gx", "gz"), split_axis=0, concat_axis=0, tiled=True)
         ]
     held, low, high, *faces = boxes_in_place(
-        arrived, old_owner, me, group_size, capacity, split, joined
+        arrived, table, me, box_count, capacity, split, joined
     )
 
     def along_x(sides):
@@ -465,8 +588,10 @@
     above = lax.ppermute(low, "gy", ring(rows, -1))
     below = lax.ppermute(high, "gy", ring(rows, 1))
     sides = along_x(sides)
-    wide, halves = wide_grid(grid, layers)
-    return two_sections(wide, halves, beyond, above, below, sides, joined)
+    wide, halves, first, first_beyond, halves_beyond = first_inside(grid, layers, beyond)
+    return last_sections(
+        wide, halves, first, first_beyond, beyond, halves_beyond, above, below, sides
+    )
 
 
 def solution(mesh):

time: 50.9 us -> 48.1 us (0.945)
  waiting for transfers between devices: 19.3 us -> 15.4 us
  Pallas kernels: 8.3 us -> 9.43 us
    ppermute x2, waiting for transfers between devices: 3.14 us -> 0.62 us  [along_x(): return [lax.ppermute(sides[0], 'gx', ring(across, 1))]]
    ppermute x7, waiting for transfers between devices: 11.8 us -> 10.2 us  [body(): lax.ppermute(departing[k], ('gx', 'gz'), [(i, i ^ k) for i in range(group...]
    pallas_call x2 -> x3, Pallas kernels: 3.71 us -> 5.2 us  [the longest x1 2.12 us: last_sections(): pl.pallas_call(kernel, out_shape=jax.ShapeDtypeStruct((FIELDS, NX, NY, LA...]
    ppermute x1, waiting for transfers between devices: 0.01 us -> 0.54 us  [body(): below = lax.ppermute(high, 'gy', ring(rows, 1))]
  transfers between devices with their start and end apart: 13 -> 13, of which waited for: 6 -> 6; matrix products, arithmetic and copies ran while one was open for 0% -> 0% of each run, Pallas kernels for 3% -> 9%
where the time goes in v6:
time: 48.1 us; the launch traced here: 48 us
  starting transfers between devices  21.3 us (44%)
  waiting for transfers between devices  15.4 us (32%)
  Pallas kernels  9.43 us (20%)
  local copies, waits for them, and re-layouts  1.7 us (4%)
    ppermute x7, starting transfers between devices, body(): lax.ppermute(departing[k], ('gx', 'gz'), [(i, i ^ k) for i in range(group...  16.4 us
    ppermute x7, waiting for transfers between devices, body(): lax.ppermute(departing[k], ('gx', 'gz'), [(i, i ^ k) for i in range(group...  10.2 us
    ppermute x1, waiting for transfers between devices, body(): below = lax.ppermute(high, 'gz', ring(along, 1))  4.05 us
    ppermute x1, starting transfers between devices, body(): above = lax.ppermute(low, 'gz', ring(along, -1))  2.33 us
    pallas_call x1, Pallas kernels, last_sections(): pl.pallas_call(kernel, out_shape=jax.ShapeDtypeStruct((FIELDS, NX, NY, LA...  2.12 us
    ppermute x2, starting transfers between devices, along_x(): return [lax.ppermute(sides[0], 'gx', ring(across, 1))]  2.07 us
    unnamed x6, local copies, waits for them, and re-layouts  1.7 us
    pallas_call x1, Pallas kernels, position_table(): pl.pallas_call(kernel, out_shape=jax.ShapeDtypeStruct((group * capacity,)...  1.58 us
  transfers between devices with their start and end apart: 13, of which 6 were waited for; matrix products, arithmetic and copies ran while one was open for 0% of the time, Pallas kernels for 9%

profile of v6, /device:TPU:0, one launch (start us, length us, event | category | flops | bytes accessed | tf_op | source)
XLA Modules:
  0.0 48.0 jit_solution(15152299012552245776)
XLA Ops:
  0.0 0.0 copy-start.1
  0.0 0.7 %copy-done.1 = s32[64]{0:T(128)S(1)} copy-done((s32[64]{0:T(128)S(1)}, s32[64]{0:T(128)}, u32[]{:S(2)}) %copy-start.1) | copy-done | bytes 280
  0.7 0.0 copy-start
  0.7 1.0 %copy-done = f32[64,4,512]{2,1,0:T(4,128)S(1)} copy-done((f32[64,4,512]{2,1,0:T(4,128)S(1)}, f32[64,4,512]{2,1,0:T(4,128)}, u32[]{:S(2)}) %copy-start) | copy-done | bytes 524312
  1.7 1.2 %pack_boxes.1 = (f32[16,2,8,128]{3,2,1,0:T(8,128)S(1)}, f32[16,2,8,128]{3,2,1,0:T(8,128)S(1)}, f32[16,2,8,128]{3,2,1,0:T(8,128)S(1)}, f32[16,2,8,128]{3,2,1,0:T(...) custom-call(s32[1]{0:T(128)} %bitcast.me_ref, ...), custom_call_target="tpu_custom_call" | custom-call | tf_op jit(solution)/shard_map/pack_boxes/pallas_call | solution.py:67
  2.9 3.1 %collective-permute-start = (f32[16,2,8,128]{3,2,1,0:T(8,128)S(1)}, f32[16,2,8,128]{3,2,1,0:T(8,128)S(1)}, u32[]{:S(2)}, u32[]{:S(2)}) collective-permute-start(f32[16,2,8,128]{3,2,1,0:T(8,128)S(1)} %get-tuple-element.28), channel_id=1, source_target_pairs={{0,1},{1,0},{2,3},{3,2},{16,17},{17,16},{18,19},{19,18},{4,5},{5,4... | collective-permute-start | bytes 393224 | tf_op jit(solution)/shard_map/ppermute | solution.py:566
  6.0 2.6 %collective-permute-start.1 = (f32[16,2,8,128]{3,2,1,0:T(8,128)S(1)}, f32[16,2,8,128]{3,2,1,0:T(8,128)S(1)}, u32[]{:S(2)}, u32[]{:S(2)}) collective-permute-start(f32[16,2,8,128]{3,2,1,0:T(8,128)S(1)} %get-tuple-element.29), channel_id=1, source_target_pairs={{0,2},{1,3},{2,0},{3,1},{16,18},{17,19},{18,16},{19,17},{4,6},{5,7... | collective-permute-start | bytes 393224 | tf_op jit(solution)/shard_map/ppermute | solution.py:566
  8.6 0.0 collective-permute-start.2
  8.6 1.7 %collective-permute-start.3 = (f32[16,2,8,128]{3,2,1,0:T(8,128)S(1)}, f32[16,2,8,128]{3,2,1,0:T(8,128)S(1)}, u32[]{:S(2)}, u32[]{:S(2)}) collective-permute-start(f32[16,2,8,128]{3,2,1,0:T(8,128)S(1)} %get-tuple-element.31), channel_id=1, source_target_pairs={{0,16},{1,17},{2,18},{3,19},{16,0},{17,1},{18,2},{19,3},{4,20},{5,... | collective-permute-start | bytes 393224 | tf_op jit(solution)/shard_map/ppermute | solution.py:566
  10.4 0.6 %collective-permute-start.4 = (f32[16,2,8,128]{3,2,1,0:T(8,128)S(1)}, f32[16,2,8,128]{3,2,1,0:T(8,128)S(1)}, u32[]{:S(2)}, u32[]{:S(2)}) collective-permute-start(f32[16,2,8,128]{3,2,1,0:T(8,128)S(1)} %get-tuple-element.32), channel_id=1, source_target_pairs={{0,17},{1,16},{2,19},{3,18},{16,1},{17,0},{18,3},{19,2},{4,21},{5,... | collective-permute-start | bytes 393224 | tf_op jit(solution)/shard_map/ppermute | solution.py:566
  11.0 0.1 collective-permute-done.refs_1_
  11.1 0.0 copy-start.2
  11.1 4.4 %collective-permute-start.5 = (f32[16,2,8,128]{3,2,1,0:T(8,128)S(1)}, f32[16,2,8,128]{3,2,1,0:T(8,128)S(1)}, u32[]{:S(2)}, u32[]{:S(2)}) collective-permute-start(f32[16,2,8,128]{3,2,1,0:T(8,128)S(1)} %get-tuple-element.33), channel_id=1, source_target_pairs={{0,18},{1,19},{2,16},{3,17},{16,2},{17,3},{18,0},{19,1},{4,22},{5,... | collective-permute-start | bytes 393224 | tf_op jit(solution)/shard_map/ppermute | solution.py:566
  15.4 3.5 %collective-permute-done.1.refs_2_ = f32[16,2,8,128]{3,2,1,0:T(8,128)S(1)} collective-permute-done((f32[16,2,8,128]{3,2,1,0:T(8,128)S(1)}, f32[16,2,8,128]{3,2,1,0:T(8,128)S(1)}, u32[]{:S(2)}, u32[]{:S(2)}) %collective-permute-start.1) | collective-permute-done | bytes 131104 | tf_op jit(solution)/shard_map/ppermute | solution.py:566
  19.0 4.0 %collective-permute-start.6 = (f32[16,2,8,128]{3,2,1,0:T(8,128)S(1)}, f32[16,2,8,128]{3,2,1,0:T(8,128)S(1)}, u32[]{:S(2)}, u32[]{:S(2)}) collective-permute-start(f32[16,2,8,128]{3,2,1,0:T(8,128)S(1)} %get-tuple-element.34), channel_id=1, source_target_pairs={{0,19},{1,18},{2,17},{3,16},{16,3},{17,2},{18,1},{19,0},{4,23},{5,... | collective-permute-start | bytes 393224 | tf_op jit(solution)/shard_map/ppermute | solution.py:566
  22.9 0.0 copy-done.2
  23.0 1.6 %position_table.1.table = s32[128]{0:T(128)S(1)} custom-call(s32[64]{0:T(128)S(1)} %copy-done.2), custom_call_target="tpu_custom_call" | custom-call | bytes 4194304 | tf_op jit(solution)/shard_map/position_table/pallas_call | solution.py:87
  24.5 0.0 collective-permute-done.2.refs_3_
  24.5 0.0 collective-permute-done.3.refs_4_
  24.6 0.0 collective-permute-done.4.refs_5_
  24.6 6.6 %collective-permute-done.5.refs_6_ = f32[16,2,8,128]{3,2,1,0:T(8,128)S(1)} collective-permute-done((f32[16,2,8,128]{3,2,1,0:T(8,128)S(1)}, f32[16,2,8,128]{3,2,1,0:T(8,128)S(1)}, u32[]{:S(2)}, u32[]{:S(2)}) %collective-permute-start.5) | collective-permute-done | bytes 131104 | tf_op jit(solution)/shard_map/ppermute | solution.py:566
  31.1 0.0 collective-permute-done.6.refs_7_
  31.1 0.9 %boxes_in_place.1 = (f32[65,2,8,128]{3,2,1,0:T(8,128)S(1)}, f32[2,8,128]{2,1,0:T(8,128)S(1)}, f32[2,8,128]{2,1,0:T(8,128)S(1)}, f32[2,16,8,128]{3,2,1,0:T(8,128)S(1)}) custom-call(s32[1]{0:T(128)} %bitcast.me_ref, s32[128]{0:T(128)S(1)} %position_table.1.table, f32[16,2,8,128]{3,2,1,0:T(8,128)S(1)} %get-tuple-element.27.refs_0_, ...), custom_call_target="tpu_custom_call" | custom-call | tf_op jit(solution)/shard_map/boxes_in_place/pallas_call | solution.py:158
  32.0 0.5 %collective-permute-start.9 = (f32[2,16,8,128]{3,2,1,0:T(8,128)S(1)}, f32[2,16,8,128]{3,2,1,0:T(8,128)S(1)}, u32[]{:S(2)}, u32[]{:S(2)}) collective-permute-start(f32[2,16,8,128]{3,2,1,0:T(8,128)S(1)} %get-tuple-element.38), channel_id=1, source_target_pairs={{0,16},{16,0},{1,17},{17,1},{2,18},{18,2},{3,19},{19,3},{4,20},{20... | collective-permute-start | bytes 393224 | tf_op jit(solution)/shard_map/ppermute | solution.py:579
  32.6 2.3 %collective-permute-start.7 = (f32[2,8,128]{2,1,0:T(8,128)S(1)}, f32[2,8,128]{2,1,0:T(8,128)S(1)}, u32[]{:S(2)}, u32[]{:S(2)}) collective-permute-start(f32[2,8,128]{2,1,0:T(8,128)S(1)} %get-tuple-element.36), channel_id=1, source_target_pairs={{0,3},{1,0},{2,1},{3,2},{4,7},{5,4},{6,5},{7,6},{8,11},{9,8},{10,9... | collective-permute-start | bytes 24584 | tf_op jit(solution)/shard_map/ppermute | solution.py:583
  34.9 0.0 collective-permute-start.8
  34.9 1.4 %grid_from_boxes.1.grid = f32[4,16,16,128]{3,2,1,0:T(8,128)S(1)} custom-call(f32[65,2,8,128]{3,2,1,0:T(8,128)S(1)} %get-tuple-element.35.held), custom_call_target="tpu_custom_call" | custom-call | flops 4194304 | bytes 2097152 | tf_op jit(solution)/shard_map/grid_from_boxes/pallas_call | solution.py:198
  36.3 0.0 collective-permute-done.7.above
  36.3 4.1 %collective-permute-done.8.below = f32[2,8,128]{2,1,0:T(8,128)S(1)} collective-permute-done((f32[2,8,128]{2,1,0:T(8,128)S(1)}, f32[2,8,128]{2,1,0:T(8,128)S(1)}, u32[]{:S(2)}, u32[]{:S(2)}) %collective-permute-start.8) | collective-permute-done | bytes 8224 | tf_op jit(solution)/shard_map/ppermute | solution.py:584
  40.4 0.0 collective-permute-done.9.refs_0_
  40.4 0.7 %faces_and_rows.1 = (f32[4,4,16,128]{3,2,1,0:T(8,128)S(1)}, f32[4,16,16,128]{3,2,1,0:T(8,128)S(1)}, f32[152,128]{1,0:T(8,128)S(1)}, f32[152,128]{1,0:T(8,128)S(1)}, f32[16,128]{1,0:T(8,128)S(1)}) custom-call(f32[4,16,16,128]{3,2,1,0:T(8,128)S(1)} %grid_from_boxes.1.grid, f32[2,8,128]{2,1,0:T(8,128)S(1)} %collective-permute-done.7.above, ...), custom_call_target="tpu_custom_call" | custom-call | tf_op jit(solution)/shard_map/faces_and_rows/pallas_call | solution.py:282
  41.1 0.1 collective-permute-start.10
  41.2 0.5 %collective-permute-start.11 = (f32[152,128]{1,0:T(8,128)S(1)}, f32[152,128]{1,0:T(8,128)S(1)}, u32[]{:S(2)}, u32[]{:S(2)}) collective-permute-start(f32[152,128]{1,0:T(8,128)S(1)} %get-tuple-element.47), channel_id=1, source_target_pairs={{0,4},{4,8},{8,12},{12,0},{1,5},{5,9},{9,13},{13,1},{2,6},{6,10},{... | collective-permute-start | bytes 233480 | tf_op jit(solution)/shard_map/ppermute | solution.py:589
  41.7 1.5 %collective-permute-start.12 = (f32[16,128]{1,0:T(8,128)S(1)}, f32[16,128]{1,0:T(8,128)S(1)}, u32[]{:S(2)}, u32[]{:S(2)}) collective-permute-start(f32[16,128]{1,0:T(8,128)S(1)} %get-tuple-element.48), channel_id=1, source_target_pairs={{0,16},{16,0},{1,17},{17,1},{2,18},{18,2},{3,19},{19,3},{4,20},{20... | collective-permute-start | bytes 24584 | tf_op jit(solution)/shard_map/ppermute | solution.py:579
  43.2 1.5 %first_inside.1 = (f32[4,20,16,128]{3,2,1,0:T(8,128)S(1)}, f32[20,16,128]{2,1,0:T(8,128)S(1)}, f32[4,16,16,128]{3,2,1,0:T(8,128)S(1)}, f32[4,16,16,128]{3,2,1,0:T(8,128)S(1)}, f32[16,16,128]{2,1,0:T(8,128)S(1)}) custom-call(f32[4,16,16,128]{3,2,1,0:T(8,128)S(1)} %grid_from_boxes.1.grid, f32[4,4,16,128]{3,2,1,0:T(8,128)S(1)} %get-tuple-element.39.layers, ...), custom_call_target="tpu_custom_call" | custom-call | flops 4194304 | bytes 2097152 | tf_op jit(solution)/shard_map/first_inside/pallas_call | solution.py:386
  44.7 0.6 %collective-permute-done.12.refs_0_ = f32[16,128]{1,0:T(8,128)S(1)} collective-permute-done((f32[16,128]{1,0:T(8,128)S(1)}, f32[16,128]{1,0:T(8,128)S(1)}, u32[]{:S(2)}, u32[]{:S(2)}) %collective-permute-start.12) | collective-permute-done | bytes 8224 | tf_op jit(solution)/shard_map/ppermute | solution.py:579
  45.3 0.0 collective-permute-done.10.above
  45.3 0.5 %collective-permute-done.11.below = f32[152,128]{1,0:T(8,128)S(1)} collective-permute-done((f32[152,128]{1,0:T(8,128)S(1)}, f32[152,128]{1,0:T(8,128)S(1)}, u32[]{:S(2)}, u32[]{:S(2)}) %collective-permute-start.11) | collective-permute-done | bytes 77856 | tf_op jit(solution)/shard_map/ppermute | solution.py:589
  45.9 2.1 %last_sections.1 = f32[4,16,16,128]{3,2,1,0:T(8,128)} custom-call(f32[4,20,16,128]{3,2,1,0:T(8,128)S(1)} %get-tuple-element.41.wide, f32[20,16,128]{2,1,0:T(8,128)S(1)} %get-tuple-element.42.halves, f32[4,16,16,128]{3,2,1,0:T(8,128)S(1)} %get-tuple-element.43.first_in, f32[4,16,16,128]{3,2,1,0:T(8,128)S(1)} %get-tuple-element.44.beyond_in, ...), custom_call_target="tpu_custom_call" | custom-call | tf_op jit(solution)/shard_map/last_sections/pallas_call | solution.py:536
Async XLA Ops:
  0.0 0.7 %copy-start.1 = (s32[64]{0:T(128)S(1)}, s32[64]{0:T(128)}, u32[]{:S(2)}) copy-start(s32[64]{0:T(128)} %owner.3) | copy-start | bytes 772
  0.7 1.0 %copy-start = (f32[64,4,512]{2,1,0:T(4,128)S(1)}, f32[64,4,512]{2,1,0:T(4,128)}, u32[]{:S(2)}) copy-start(f32[64,4,512]{2,1,0:T(4,128)} %fields.1) | copy-start | bytes 1572868
  2.9 8.1 %collective-permute-start = (f32[16,2,8,128]{3,2,1,0:T(8,128)S(1)}, f32[16,2,8,128]{3,2,1,0:T(8,128)S(1)}, u32[]{:S(2)}, u32[]{:S(2)}) collective-permute-start(f32[16,2,8,128]{3,2,1,0:T(8,128)S(1)} %get-tuple-element.28), channel_id=1, source_target_pairs={{0,1},{1,0},{2,3},{3,2},{16,17},{17,16},{18,19},{19,18},{4,5},{5,4... | collective-permute-start | bytes 393224 | tf_op jit(solution)/shard_map/ppermute | solution.py:566
  6.0 12.9 %collective-permute-start.1 = (f32[16,2,8,128]{3,2,1,0:T(8,128)S(1)}, f32[16,2,8,128]{3,2,1,0:T(8,128)S(1)}, u32[]{:S(2)}, u32[]{:S(2)}) collective-permute-start(f32[16,2,8,128]{3,2,1,0:T(8,128)S(1)} %get-tuple-element.29), channel_id=1, source_target_pairs={{0,2},{1,3},{2,0},{3,1},{16,18},{17,19},{18,16},{19,17},{4,6},{5,7... | collective-permute-start | bytes 393224 | tf_op jit(solution)/shard_map/ppermute | solution.py:566
  8.6 15.9 %collective-permute-start.2 = (f32[16,2,8,128]{3,2,1,0:T(8,128)S(1)}, f32[16,2,8,128]{3,2,1,0:T(8,128)S(1)}, u32[]{:S(2)}, u32[]{:S(2)}) collective-permute-start(f32[16,2,8,128]{3,2,1,0:T(8,128)S(1)} %get-tuple-element.30), channel_id=1, source_target_pairs={{0,3},{1,2},{2,1},{3,0},{16,19},{17,18},{18,17},{19,16},{4,7},{5,6... | collective-permute-start | bytes 393224 | tf_op jit(solution)/shard_map/ppermute | solution.py:566
  8.6 15.9 %collective-permute-start.3 = (f32[16,2,8,128]{3,2,1,0:T(8,128)S(1)}, f32[16,2,8,128]{3,2,1,0:T(8,128)S(1)}, u32[]{:S(2)}, u32[]{:S(2)}) collective-permute-start(f32[16,2,8,128]{3,2,1,0:T(8,128)S(1)} %get-tuple-element.31), channel_id=1, source_target_pairs={{0,16},{1,17},{2,18},{3,19},{16,0},{17,1},{18,2},{19,3},{4,20},{5,... | collective-permute-start | bytes 393224 | tf_op jit(solution)/shard_map/ppermute | solution.py:566
  10.4 14.2 %collective-permute-start.4 = (f32[16,2,8,128]{3,2,1,0:T(8,128)S(1)}, f32[16,2,8,128]{3,2,1,0:T(8,128)S(1)}, u32[]{:S(2)}, u32[]{:S(2)}) collective-permute-start(f32[16,2,8,128]{3,2,1,0:T(8,128)S(1)} %get-tuple-element.32), channel_id=1, source_target_pairs={{0,17},{1,16},{2,19},{3,18},{16,1},{17,0},{18,3},{19,2},{4,21},{5,... | collective-permute-start | bytes 393224 | tf_op jit(solution)/shard_map/ppermute | solution.py:566
  11.1 11.9 %copy-start.2 = (s32[64]{0:T(128)S(1)}, s32[64]{0:T(128)}, u32[]{:S(2)}) copy-start(s32[64]{0:T(128)} %owner.2) | copy-start | bytes 772
  11.1 20.1 %collective-permute-start.5 = (f32[16,2,8,128]{3,2,1,0:T(8,128)S(1)}, f32[16,2,8,128]{3,2,1,0:T(8,128)S(1)}, u32[]{:S(2)}, u32[]{:S(2)}) collective-permute-start(f32[16,2,8,128]{3,2,1,0:T(8,128)S(1)} %get-tuple-element.33), channel_id=1, source_target_pairs={{0,18},{1,19},{2,16},{3,17},{16,2},{17,3},{18,0},{19,1},{4,22},{5,... | collective-permute-start | bytes 393224 | tf_op jit(solution)/shard_map/ppermute | solution.py:566
  19.0 12.2 %collective-permute-start.6 = (f32[16,2,8,128]{3,2,1,0:T(8,128)S(1)}, f32[16,2,8,128]{3,2,1,0:T(8,128)S(1)}, u32[]{:S(2)}, u32[]{:S(2)}) collective-permute-start(f32[16,2,8,128]{3,2,1,0:T(8,128)S(1)} %get-tuple-element.34), channel_id=1, source_target_pairs={{0,19},{1,18},{2,17},{3,16},{16,3},{17,2},{18,1},{19,0},{4,23},{5,... | collective-permute-start | bytes 393224 | tf_op jit(solution)/shard_map/ppermute | solution.py:566
  32.0 8.3 %collective-permute-start.9 = (f32[2,16,8,128]{3,2,1,0:T(8,128)S(1)}, f32[2,16,8,128]{3,2,1,0:T(8,128)S(1)}, u32[]{:S(2)}, u32[]{:S(2)}) collective-permute-start(f32[2,16,8,128]{3,2,1,0:T(8,128)S(1)} %get-tuple-element.38), channel_id=1, source_target_pairs={{0,16},{16,0},{1,17},{17,1},{2,18},{18,2},{3,19},{19,3},{4,20},{20... | collective-permute-start | bytes 393224 | tf_op jit(solution)/shard_map/ppermute | solution.py:579
  32.6 3.7 %collective-permute-start.7 = (f32[2,8,128]{2,1,0:T(8,128)S(1)}, f32[2,8,128]{2,1,0:T(8,128)S(1)}, u32[]{:S(2)}, u32[]{:S(2)}) collective-permute-start(f32[2,8,128]{2,1,0:T(8,128)S(1)} %get-tuple-element.36), channel_id=1, source_target_pairs={{0,3},{1,0},{2,1},{3,2},{4,7},{5,4},{6,5},{7,6},{8,11},{9,8},{10,9... | collective-permute-start | bytes 24584 | tf_op jit(solution)/shard_map/ppermute | solution.py:583
  34.9 5.4 %collective-permute-start.8 = (f32[2,8,128]{2,1,0:T(8,128)S(1)}, f32[2,8,128]{2,1,0:T(8,128)S(1)}, u32[]{:S(2)}, u32[]{:S(2)}) collective-permute-start(f32[2,8,128]{2,1,0:T(8,128)S(1)} %get-tuple-element.37), channel_id=1, source_target_pairs={{0,1},{1,2},{2,3},{3,0},{4,5},{5,6},{6,7},{7,4},{8,9},{9,10},{10,1... | collective-permute-start | bytes 24584 | tf_op jit(solution)/shard_map/ppermute | solution.py:584
  41.1 4.2 %collective-permute-start.10 = (f32[152,128]{1,0:T(8,128)S(1)}, f32[152,128]{1,0:T(8,128)S(1)}, u32[]{:S(2)}, u32[]{:S(2)}) collective-permute-start(f32[152,128]{1,0:T(8,128)S(1)} %get-tuple-element.46), channel_id=1, source_target_pairs={{0,12},{4,0},{8,4},{12,8},{1,13},{5,1},{9,5},{13,9},{2,14},{6,2},{... | collective-permute-start | bytes 233480 | tf_op jit(solution)/shard_map/ppermute | solution.py:588
  41.2 4.7 %collective-permute-start.11 = (f32[152,128]{1,0:T(8,128)S(1)}, f32[152,128]{1,0:T(8,128)S(1)}, u32[]{:S(2)}, u32[]{:S(2)}) collective-permute-start(f32[152,128]{1,0:T(8,128)S(1)} %get-tuple-element.47), channel_id=1, source_target_pairs={{0,4},{4,8},{8,12},{12,0},{1,5},{5,9},{9,13},{13,1},{2,6},{6,10},{... | collective-permute-start | bytes 233480 | tf_op jit(solution)/shard_map/ppermute | solution.py:589
  41.7 3.7 %collective-permute-start.12 = (f32[16,128]{1,0:T(8,128)S(1)}, f32[16,128]{1,0:T(8,128)S(1)}, u32[]{:S(2)}, u32[]{:S(2)}) collective-permute-start(f32[16,128]{1,0:T(8,128)S(1)} %get-tuple-element.48), channel_id=1, source_target_pairs={{0,16},{16,0},{1,17},{17,1},{2,18},{18,2},{3,19},{19,3},{4,20},{20... | collective-permute-start | bytes 24584 | tf_op jit(solution)/shard_map/ppermute | solution.py:579

commit v7 on v6

--- a/solution.py
+++ b/solution.py
@@ -117,6 +117,16 @@
     return [(i, (i + step) % count) for i in range(count)]
 
 
+def with_both_sides(axis, first, second):
+    count = lax.axis_size(axis)
+    pairs = [(i, i ^ 1) for i in range(count)], [((i + 1) % count, ((i ^ 1) + 1) % count) for i in range(count)]
+    return [lax.ppermute(x, axis, p) for x, p in zip((first, second), pairs)]
+
+
+def by_parity(odd, low, high):
+    return jnp.where(odd, low, high), jnp.where(odd, high, low)
+
+
 def boxes_in_place(arrived, table, me, boxes, capacity, split, joined):
     pieces = len(arrived)
     rows = table.shape[0] // pieces
@@ -128,6 +138,7 @@
     def kernel(me_ref, table, *refs):
         ins, refs = refs[:pieces], refs[pieces:]
         held, low, high, *outs = refs
+        odd = me_ref[2] != 0
         for k, rows_in in enumerate(ins):
             base = (me_ref[0] ^ k) * capacity if split else 0
 
@@ -145,15 +156,17 @@
                         p, side, pl.ds(side * FIELDS, FIELDS), :
                     ]
         pair = lax.broadcasted_iota(jnp.int32, (2 * FIELDS, LANES), 1) % EDGE // HALO
-        for out, bz, first in ((low, 0, 0), (high, BRICK_Z - 1, EDGE - HALO)):
-            for group in range(2):
+        for group in range(2):
+            ends = []
+            for bz, first in ((0, 0), (BRICK_Z - 1, EDGE - HALO)):
                 packed = jnp.zeros((2 * FIELDS, LANES), jnp.float32)
                 for n in range(4):
                     b, part = divmod(group * 4 + n, 2)
                     cells = held[b * BRICK_Z + bz, part]
                     shift = (n * HALO - first) % LANES
                     packed = jnp.where(pair == n, pltpu.roll(cells, shift, 1) if shift else cells, packed)
-                out[group] = packed
+                ends.append(packed)
+            low[group], high[group] = by_parity(odd, *ends)
 
     return pl.pallas_call(
         kernel,
@@ -219,13 +232,13 @@
     return side * FIELDS + f
 
 
-def faces_and_rows(grid, faces, above, below, joined):
+def faces_and_rows(grid, faces, me, ends, joined):
     sides = [jax.ShapeDtypeStruct((NY, LANES), jnp.float32)] * (2 - joined)
 
-    def kernel(grid, above, below, *refs):
+    def kernel(me_ref, grid, near, other, *refs):
         ins, refs = refs[: len(faces)], refs[len(faces) :]
-        (layers, beyond, low, high), refs = refs[:4], refs[4:]
-        outs, (turned,) = refs[: len(sides)], refs[len(sides) :]
+        (layers, beyond, near_rows, other_rows), refs = refs[:4], refs[4:]
+        outs, (turned, low, high) = refs[: len(sides)], refs[len(sides) :]
         for side in range(2):
             face = ins[0].at[side] if joined else ins[side]
 
@@ -238,7 +251,7 @@
             for by in range(BRICK_Y):
                 for half in range(TILES // 2):
                     group, n = divmod((bx * BRICK_Y + by) * 2 + half, 4)
-                    after, before = above[group], below[group]
+                    before, after = by_parity(me_ref[2] != 0, near[group], other[group])
                     columns = [
                         jnp.where(
                             lane < LANES // 2,
@@ -266,6 +279,7 @@
                     moved = pltpu.roll(beyond[f, x, pl.ds(first, EDGE), :], 2 * place + 1, 1)
                     edge = jnp.where(pair == place, moved, edge)
             out[pl.ds(ROWS, EDGE), :] = edge
+        near_rows[...], other_rows[...] = by_parity(me_ref[1] != 0, low[...], high[...])
         pair = lax.broadcasted_iota(jnp.int32, (NY, LANES), 1) // 2
         edges = [jnp.zeros((NY, LANES), jnp.float32)] * 2
         for side in range(2):
@@ -288,12 +302,13 @@
             rows,
         ]
         + sides,
-        in_specs=[VMEM] * (3 + len(faces)),
+        in_specs=[SMEM] + [VMEM] * (3 + len(faces)),
         out_specs=[VMEM] * (4 + len(sides)),
-        scratch_shapes=[pltpu.VMEM((LANES, LANES), jnp.float32)],
+        scratch_shapes=[pltpu.VMEM((LANES, LANES), jnp.float32)]
+        + [pltpu.VMEM((EDGES, LANES), jnp.float32)] * 2,
         compiler_params=ROOM,
         name="faces_and_rows",
-    )(grid, above, below, *faces)
+    )(me, grid, *ends, *faces)
 
 
 def half_conductance(v):
@@ -400,9 +415,13 @@
     )(grid, layers, beyond)
 
 
-def last_sections(wide, halves, first, first_beyond, beyond, halves_beyond, above, below, sides):
-    def kernel(wide, halves, first_in, beyond_in, beyond, halves_beyond, above, below, *refs):
-        ins, (out, edges, first, first_beyond, around, fs, fbs) = refs[: len(sides)], refs[len(sides) :]
+def last_sections(me, wide, halves, first, first_beyond, beyond, halves_beyond, near, other, sides):
+    def kernel(
+        me_ref, wide, halves, first_in, beyond_in, beyond, halves_beyond, near_rows, other_rows, *refs
+    ):
+        ins, (out, *refs) = refs[: len(sides)], refs[len(sides) :]
+        edges, first, first_beyond, around, fs, fbs, above, below = refs
+        below[...], above[...] = by_parity(me_ref[1] != 0, near_rows[...], other_rows[...])
         factors = [TIME_STEP * c for c in DIFFUSION]
         row = lax.broadcasted_iota(jnp.int32, (EDGE, LANES), 0)
 
@@ -536,7 +555,7 @@
     return pl.pallas_call(
         kernel,
         out_shape=jax.ShapeDtypeStruct((FIELDS, NX, NY, LANES), jnp.float32),
-        in_specs=[VMEM] * (8 + len(sides)),
+        in_specs=[SMEM] + [VMEM] * (8 + len(sides)),
         out_specs=VMEM,
         scratch_shapes=[
             scratch(FIELDS * NX * EDGE),
@@ -545,10 +564,12 @@
             scratch(FIELDS * NX * EDGE),
             scratch(NEAR_X, NY),
             scratch(NX, NY),
+            scratch(EDGES),
+            scratch(EDGES),
         ],
         compiler_params=ROOM,
         name="last_sections",
-    )(wide, halves, first, first_beyond, beyond, halves_beyond, above, below, *sides)
+    )(me, wide, halves, first, first_beyond, beyond, halves_beyond, near, other, *sides)
 
 
 def body(old_fields, new_owner, old_owner):
@@ -558,7 +579,8 @@
     capacity = 2 * (box_count // group_size)
     split = group_size <= 8
     joined = across == 2
-    me = (lax.axis_index("gx") * along + lax.axis_index("gz")).reshape(1)
+    place = lax.axis_index("gx") * along + lax.axis_index("gz")
+    me = jnp.stack([place, lax.axis_index("gy") & 1, lax.axis_index("gz") & 1])
     departing = pack_boxes(old_fields, new_owner, me, group_size, capacity, split)
     table = position_table(old_owner, group_size, capacity)
     if split:
@@ -570,7 +592,7 @@
         arrived = [
             lax.all_to_all(departing[0], ("gx", "gz"), split_axis=0, concat_axis=0, tiled=True)
         ]
-    held, low, high, *faces = boxes_in_place(
+    held, near, other, *faces = boxes_in_place(
         arrived, table, me, box_count, capacity, split, joined
     )
 
@@ -580,17 +602,14 @@
         return [lax.ppermute(side, "gx", ring(across, step)) for side, step in zip(sides, (-1, 1))]
 
     faces = along_x(faces)
-    above = lax.ppermute(low, "gz", ring(along, -1))
-    below = lax.ppermute(high, "gz", ring(along, 1))
+    ends = with_both_sides("gz", near, other)
     grid = grid_from_boxes(held)
-    layers, beyond, low, high, *sides = faces_and_rows(grid, faces, above, below, joined)
-    rows = lax.axis_size("gy")
-    above = lax.ppermute(low, "gy", ring(rows, -1))
-    below = lax.ppermute(high, "gy", ring(rows, 1))
+    layers, beyond, near, other, *sides = faces_and_rows(grid, faces, me, ends, joined)
+    near, other = with_both_sides("gy", near, other)
     sides = along_x(sides)
     wide, halves, first, first_beyond, halves_beyond = first_inside(grid, layers, beyond)
     return last_sections(
-        wide, halves, first, first_beyond, beyond, halves_beyond, above, below, sides
+        me, wide, halves, first, first_beyond, beyond, halves_beyond, near, other, sides
     )
 
 

time: 48.1 us -> 49.5 us (1.029)
  starting transfers between devices: 21.3 us -> 24.6 us
  waiting for transfers between devices: 15.4 us -> 12.4 us
  Pallas kernels: 9.43 us -> 10.6 us
    ppermute x4, starting transfers between devices: 2.89 us -> 6.15 us  [with_both_sides(): return [lax.ppermute(x, axis, p) for x, p in zip((first, second), pairs)]]
    ppermute x4, waiting for transfers between devices: 4.59 us -> 1.56 us  [with_both_sides(): return [lax.ppermute(x, axis, p) for x, p in zip((first, second), pairs)]]
    pallas_call x1, Pallas kernels: 2.12 us -> 2.7 us  [last_sections(): pl.pallas_call(kernel, out_shape=jax.ShapeDtypeStruct((FIELDS, NX, NY, LA...]
    pallas_call x1, Pallas kernels: 0.75 us -> 1.28 us  [faces_and_rows(): pl.pallas_call(kernel, out_shape=[jax.ShapeDtypeStruct((FIELDS, 2 * HALO,...]
  transfers between devices with their start and end apart: 13 -> 13, of which waited for: 6 -> 5; matrix products, arithmetic and copies ran while one was open for 0% -> 0% of each run, Pallas kernels for 9% -> 9%
where the time goes in v7:
time: 49.5 us; the launch traced here: 49.3 us
  starting transfers between devices  24.6 us (50%)
  waiting for transfers between devices  12.4 us (25%)
  Pallas kernels  10.6 us (21%)
  local copies, waits for them, and re-layouts  1.62 us (3%)
    ppermute x7, starting transfers between devices, body(): lax.ppermute(departing[k], ('gx', 'gz'), [(i, i ^ k) for i in range(group...  16.4 us
    ppermute x7, waiting for transfers between devices, body(): lax.ppermute(departing[k], ('gx', 'gz'), [(i, i ^ k) for i in range(group...  10.2 us
    ppermute x4, starting transfers between devices, with_both_sides(): return [lax.ppermute(x, axis, p) for x, p in zip((first, second), pairs)]  6.15 us
    pallas_call x1, Pallas kernels, last_sections(): pl.pallas_call(kernel, out_shape=jax.ShapeDtypeStruct((FIELDS, NX, NY, LA...  2.7 us
    ppermute x2, starting transfers between devices, along_x(): return [lax.ppermute(sides[0], 'gx', ring(across, 1))]  2.09 us
    unnamed x6, local copies, waits for them, and re-layouts  1.62 us
    pallas_call x1, Pallas kernels, position_table(): pl.pallas_call(kernel, out_shape=jax.ShapeDtypeStruct((group * capacity,)...  1.58 us
    ppermute x4, waiting for transfers between devices, with_both_sides(): return [lax.ppermute(x, axis, p) for x, p in zip((first, second), pairs)]  1.56 us
  transfers between devices with their start and end apart: 13, of which 5 were waited for; matrix products, arithmetic and copies ran while one was open for 0% of the time, Pallas kernels for 9%

profile of v7, /device:TPU:0, one launch (start us, length us, event | category | flops | bytes accessed | tf_op | source)
XLA Modules:
  0.0 49.3 jit_solution(8035968286004452365)
XLA Ops:
  0.0 0.0 copy-start.1
  0.0 0.1 pad_add_fusion.me_ref
  0.1 0.6 %copy-done.1 = s32[64]{0:T(128)S(1)} copy-done((s32[64]{0:T(128)S(1)}, s32[64]{0:T(128)}, u32[]{:S(2)}) %copy-start.1) | copy-done | bytes 280
  0.7 0.0 copy-start
  0.7 1.0 %copy-done = f32[64,4,512]{2,1,0:T(4,128)S(1)} copy-done((f32[64,4,512]{2,1,0:T(4,128)S(1)}, f32[64,4,512]{2,1,0:T(4,128)}, u32[]{:S(2)}) %copy-start) | copy-done | bytes 524312
  1.7 1.2 %pack_boxes.1 = (f32[16,2,8,128]{3,2,1,0:T(8,128)S(1)}, f32[16,2,8,128]{3,2,1,0:T(8,128)S(1)}, f32[16,2,8,128]{3,2,1,0:T(8,128)S(1)}, f32[16,2,8,128]{3,2,1,0:T(...) custom-call(s32[3]{0:T(128)S(1)} %pad_add_fusion.me_ref, ...), custom_call_target="tpu_custom_call" | custom-call | tf_op jit(solution)/shard_map/pack_boxes/pallas_call | solution.py:67
  2.9 3.1 %collective-permute-start = (f32[16,2,8,128]{3,2,1,0:T(8,128)S(1)}, f32[16,2,8,128]{3,2,1,0:T(8,128)S(1)}, u32[]{:S(2)}, u32[]{:S(2)}) collective-permute-start(f32[16,2,8,128]{3,2,1,0:T(8,128)S(1)} %get-tuple-element.28), channel_id=1, source_target_pairs={{0,1},{1,0},{2,3},{3,2},{16,17},{17,16},{18,19},{19,18},{4,5},{5,4... | collective-permute-start | bytes 393224 | tf_op jit(solution)/shard_map/ppermute | solution.py:588
  6.0 2.6 %collective-permute-start.1 = (f32[16,2,8,128]{3,2,1,0:T(8,128)S(1)}, f32[16,2,8,128]{3,2,1,0:T(8,128)S(1)}, u32[]{:S(2)}, u32[]{:S(2)}) collective-permute-start(f32[16,2,8,128]{3,2,1,0:T(8,128)S(1)} %get-tuple-element.29), channel_id=1, source_target_pairs={{0,2},{1,3},{2,0},{3,1},{16,18},{17,19},{18,16},{19,17},{4,6},{5,7... | collective-permute-start | bytes 393224 | tf_op jit(solution)/shard_map/ppermute | solution.py:588
  8.6 0.0 collective-permute-start.2
  8.6 1.7 %collective-permute-start.3 = (f32[16,2,8,128]{3,2,1,0:T(8,128)S(1)}, f32[16,2,8,128]{3,2,1,0:T(8,128)S(1)}, u32[]{:S(2)}, u32[]{:S(2)}) collective-permute-start(f32[16,2,8,128]{3,2,1,0:T(8,128)S(1)} %get-tuple-element.31), channel_id=1, source_target_pairs={{0,16},{1,17},{2,18},{3,19},{16,0},{17,1},{18,2},{19,3},{4,20},{5,... | collective-permute-start | bytes 393224 | tf_op jit(solution)/shard_map/ppermute | solution.py:588
  10.4 0.6 %collective-permute-start.4 = (f32[16,2,8,128]{3,2,1,0:T(8,128)S(1)}, f32[16,2,8,128]{3,2,1,0:T(8,128)S(1)}, u32[]{:S(2)}, u32[]{:S(2)}) collective-permute-start(f32[16,2,8,128]{3,2,1,0:T(8,128)S(1)} %get-tuple-element.32), channel_id=1, source_target_pairs={{0,17},{1,16},{2,19},{3,18},{16,1},{17,0},{18,3},{19,2},{4,21},{5,... | collective-permute-start | bytes 393224 | tf_op jit(solution)/shard_map/ppermute | solution.py:588
  11.0 0.1 collective-permute-done.refs_1_
  11.1 0.0 copy-start.2
  11.1 4.4 %collective-permute-start.5 = (f32[16,2,8,128]{3,2,1,0:T(8,128)S(1)}, f32[16,2,8,128]{3,2,1,0:T(8,128)S(1)}, u32[]{:S(2)}, u32[]{:S(2)}) collective-permute-start(f32[16,2,8,128]{3,2,1,0:T(8,128)S(1)} %get-tuple-element.33), channel_id=1, source_target_pairs={{0,18},{1,19},{2,16},{3,17},{16,2},{17,3},{18,0},{19,1},{4,22},{5,... | collective-permute-start | bytes 393224 | tf_op jit(solution)/shard_map/ppermute | solution.py:588
  15.4 3.5 %collective-permute-done.1.refs_2_ = f32[16,2,8,128]{3,2,1,0:T(8,128)S(1)} collective-permute-done((f32[16,2,8,128]{3,2,1,0:T(8,128)S(1)}, f32[16,2,8,128]{3,2,1,0:T(8,128)S(1)}, u32[]{:S(2)}, u32[]{:S(2)}) %collective-permute-start.1) | collective-permute-done | bytes 131104 | tf_op jit(solution)/shard_map/ppermute | solution.py:588
  19.0 4.0 %collective-permute-start.6 = (f32[16,2,8,128]{3,2,1,0:T(8,128)S(1)}, f32[16,2,8,128]{3,2,1,0:T(8,128)S(1)}, u32[]{:S(2)}, u32[]{:S(2)}) collective-permute-start(f32[16,2,8,128]{3,2,1,0:T(8,128)S(1)} %get-tuple-element.34), channel_id=1, source_target_pairs={{0,19},{1,18},{2,17},{3,16},{16,3},{17,2},{18,1},{19,0},{4,23},{5,... | collective-permute-start | bytes 393224 | tf_op jit(solution)/shard_map/ppermute | solution.py:588
  23.0 0.0 copy-done.2
  23.0 1.6 %position_table.1.table = s32[128]{0:T(128)S(1)} custom-call(s32[64]{0:T(128)S(1)} %copy-done.2), custom_call_target="tpu_custom_call" | custom-call | bytes 4194304 | tf_op jit(solution)/shard_map/position_table/pallas_call | solution.py:87
  24.5 0.0 collective-permute-done.2.refs_3_
  24.5 0.0 collective-permute-done.3.refs_4_
  24.6 0.0 collective-permute-done.4.refs_5_
  24.6 6.6 %collective-permute-done.5.refs_6_ = f32[16,2,8,128]{3,2,1,0:T(8,128)S(1)} collective-permute-done((f32[16,2,8,128]{3,2,1,0:T(8,128)S(1)}, f32[16,2,8,128]{3,2,1,0:T(8,128)S(1)}, u32[]{:S(2)}, u32[]{:S(2)}) %collective-permute-start.5) | collective-permute-done | bytes 131104 | tf_op jit(solution)/shard_map/ppermute | solution.py:588
  31.1 0.0 collective-permute-done.6.refs_7_
  31.1 0.9 %boxes_in_place.1 = (f32[65,2,8,128]{3,2,1,0:T(8,128)S(1)}, f32[2,8,128]{2,1,0:T(8,128)S(1)}, f32[2,8,128]{2,1,0:T(8,128)S(1)}, f32[2,16,8,128]{3,2,1,0:T(8,128)S(1)}) custom-call(s32[3]{0:T(128)S(1)} %pad_add_fusion.me_ref, s32[128]{0:T(128)S(1)} %position_table.1.table, f32[16,2,8,128]{3,2,1,0:T(8,128)S(1)} %get-tuple-element.27.refs_0_, ...), custom_call_target="tpu_custom_call" | custom-call | tf_op jit(solution)/shard_map/boxes_in_place/pallas_call | solution.py:171
  32.0 0.6 %collective-permute-start.9 = (f32[2,16,8,128]{3,2,1,0:T(8,128)S(1)}, f32[2,16,8,128]{3,2,1,0:T(8,128)S(1)}, u32[]{:S(2)}, u32[]{:S(2)}) collective-permute-start(f32[2,16,8,128]{3,2,1,0:T(8,128)S(1)} %get-tuple-element.38), channel_id=1, source_target_pairs={{0,16},{16,0},{1,17},{17,1},{2,18},{18,2},{3,19},{19,3},{4,20},{20... | collective-permute-start | bytes 393224 | tf_op jit(solution)/shard_map/ppermute | solution.py:601
  32.6 2.0 %collective-permute-start.7 = (f32[2,8,128]{2,1,0:T(8,128)S(1)}, f32[2,8,128]{2,1,0:T(8,128)S(1)}, u32[]{:S(2)}, u32[]{:S(2)}) collective-permute-start(f32[2,8,128]{2,1,0:T(8,128)S(1)} %get-tuple-element.36), channel_id=1, source_target_pairs={{0,1},{1,0},{2,3},{3,2},{4,5},{5,4},{6,7},{7,6},{8,9},{9,8},{10,11... | collective-permute-start | bytes 24584 | tf_op jit(solution)/shard_map/ppermute | solution.py:123
  34.6 2.5 %collective-permute-start.8 = (f32[2,8,128]{2,1,0:T(8,128)S(1)}, f32[2,8,128]{2,1,0:T(8,128)S(1)}, u32[]{:S(2)}, u32[]{:S(2)}) collective-permute-start(f32[2,8,128]{2,1,0:T(8,128)S(1)} %get-tuple-element.37), channel_id=1, source_target_pairs={{1,2},{2,1},{3,0},{0,3},{5,6},{6,5},{7,4},{4,7},{9,10},{10,9},{11,... | collective-permute-start | bytes 24584 | tf_op jit(solution)/shard_map/ppermute | solution.py:123
  37.1 1.4 %grid_from_boxes.1.grid = f32[4,16,16,128]{3,2,1,0:T(8,128)S(1)} custom-call(f32[65,2,8,128]{3,2,1,0:T(8,128)S(1)} %get-tuple-element.35.held), custom_call_target="tpu_custom_call" | custom-call | flops 4194304 | bytes 2097152 | tf_op jit(solution)/shard_map/grid_from_boxes/pallas_call | solution.py:211
  38.5 0.0 collective-permute-done.7.near
  38.5 1.5 %collective-permute-done.8.other = f32[2,8,128]{2,1,0:T(8,128)S(1)} collective-permute-done((f32[2,8,128]{2,1,0:T(8,128)S(1)}, f32[2,8,128]{2,1,0:T(8,128)S(1)}, u32[]{:S(2)}, u32[]{:S(2)}) %collective-permute-start.8) | collective-permute-done | bytes 8224 | tf_op jit(solution)/shard_map/ppermute | solution.py:123
  40.0 0.0 collective-permute-done.9.refs_0_
  40.0 1.3 %faces_and_rows.1 = (f32[4,4,16,128]{3,2,1,0:T(8,128)S(1)}, f32[4,16,16,128]{3,2,1,0:T(8,128)S(1)}, f32[152,128]{1,0:T(8,128)S(1)}, f32[152,128]{1,0:T(8,128)S(1)}, f32[16,128]{1,0:T(8,128)S(1)}) custom-call(s32[3]{0:T(128)S(1)} %pad_add_fusion.me_ref, f32[4,16,16,128]{3,2,1,0:T(8,128)S(1)} %grid_from_boxes.1.grid, ...), custom_call_target="tpu_custom_call" | custom-call | tf_op jit(solution)/shard_map/faces_and_rows/pallas_call | solution.py:296
  41.3 0.1 collective-permute-start.10
  41.4 1.6 %collective-permute-start.11 = (f32[152,128]{1,0:T(8,128)S(1)}, f32[152,128]{1,0:T(8,128)S(1)}, u32[]{:S(2)}, u32[]{:S(2)}) collective-permute-start(f32[152,128]{1,0:T(8,128)S(1)} %get-tuple-element.47), channel_id=1, source_target_pairs={{4,8},{8,4},{12,0},{0,12},{5,9},{9,5},{13,1},{1,13},{6,10},{10,6},... | collective-permute-start | bytes 233480 | tf_op jit(solution)/shard_map/ppermute | solution.py:123
  43.0 1.5 %collective-permute-start.12 = (f32[16,128]{1,0:T(8,128)S(1)}, f32[16,128]{1,0:T(8,128)S(1)}, u32[]{:S(2)}, u32[]{:S(2)}) collective-permute-start(f32[16,128]{1,0:T(8,128)S(1)} %get-tuple-element.48), channel_id=1, source_target_pairs={{0,16},{16,0},{1,17},{17,1},{2,18},{18,2},{3,19},{19,3},{4,20},{20... | collective-permute-start | bytes 24584 | tf_op jit(solution)/shard_map/ppermute | solution.py:601
  44.5 1.5 %first_inside.1 = (f32[4,20,16,128]{3,2,1,0:T(8,128)S(1)}, f32[20,16,128]{2,1,0:T(8,128)S(1)}, f32[4,16,16,128]{3,2,1,0:T(8,128)S(1)}, f32[4,16,16,128]{3,2,1,0:T(8,128)S(1)}, f32[16,16,128]{2,1,0:T(8,128)S(1)}) custom-call(f32[4,16,16,128]{3,2,1,0:T(8,128)S(1)} %grid_from_boxes.1.grid, f32[4,4,16,128]{3,2,1,0:T(8,128)S(1)} %get-tuple-element.39.layers, ...), custom_call_target="tpu_custom_call" | custom-call | flops 4194304 | bytes 2097152 | tf_op jit(solution)/shard_map/first_inside/pallas_call | solution.py:401
  46.0 0.6 %collective-permute-done.12.refs_0_ = f32[16,128]{1,0:T(8,128)S(1)} collective-permute-done((f32[16,128]{1,0:T(8,128)S(1)}, f32[16,128]{1,0:T(8,128)S(1)}, u32[]{:S(2)}, u32[]{:S(2)}) %collective-permute-start.12) | collective-permute-done | bytes 8224 | tf_op jit(solution)/shard_map/ppermute | solution.py:601
  46.6 0.0 collective-permute-done.10.near_rows
  46.6 0.0 collective-permute-done.11.other_rows
  46.7 2.7 %last_sections.1 = f32[4,16,16,128]{3,2,1,0:T(8,128)} custom-call(s32[3]{0:T(128)S(1)} %pad_add_fusion.me_ref, f32[4,20,16,128]{3,2,1,0:T(8,128)S(1)} %get-tuple-element.41.wide, f32[20,16,128]{2,1,0:T(8,128)S(1)} %get-tuple-element.42.halves, f32[4,16,16,128]{3,2,1,0:T(8,128)S(1)} %get-tuple-element.43.first_in, ...), custom_call_target="tpu_custom_call" | custom-call | tf_op jit(solution)/shard_map/last_sections/pallas_call | solution.py:555
Async XLA Ops:
  0.0 0.7 %copy-start.1 = (s32[64]{0:T(128)S(1)}, s32[64]{0:T(128)}, u32[]{:S(2)}) copy-start(s32[64]{0:T(128)} %owner.3) | copy-start | bytes 772
  0.7 1.0 %copy-start = (f32[64,4,512]{2,1,0:T(4,128)S(1)}, f32[64,4,512]{2,1,0:T(4,128)}, u32[]{:S(2)}) copy-start(f32[64,4,512]{2,1,0:T(4,128)} %fields.1) | copy-start | bytes 1572868
  2.9 8.1 %collective-permute-start = (f32[16,2,8,128]{3,2,1,0:T(8,128)S(1)}, f32[16,2,8,128]{3,2,1,0:T(8,128)S(1)}, u32[]{:S(2)}, u32[]{:S(2)}) collective-permute-start(f32[16,2,8,128]{3,2,1,0:T(8,128)S(1)} %get-tuple-element.28), channel_id=1, source_target_pairs={{0,1},{1,0},{2,3},{3,2},{16,17},{17,16},{18,19},{19,18},{4,5},{5,4... | collective-permute-start | bytes 393224 | tf_op jit(solution)/shard_map/ppermute | solution.py:588
  6.0 12.9 %collective-permute-start.1 = (f32[16,2,8,128]{3,2,1,0:T(8,128)S(1)}, f32[16,2,8,128]{3,2,1,0:T(8,128)S(1)}, u32[]{:S(2)}, u32[]{:S(2)}) collective-permute-start(f32[16,2,8,128]{3,2,1,0:T(8,128)S(1)} %get-tuple-element.29), channel_id=1, source_target_pairs={{0,2},{1,3},{2,0},{3,1},{16,18},{17,19},{18,16},{19,17},{4,6},{5,7... | collective-permute-start | bytes 393224 | tf_op jit(solution)/shard_map/ppermute | solution.py:588
  8.6 15.9 %collective-permute-start.2 = (f32[16,2,8,128]{3,2,1,0:T(8,128)S(1)}, f32[16,2,8,128]{3,2,1,0:T(8,128)S(1)}, u32[]{:S(2)}, u32[]{:S(2)}) collective-permute-start(f32[16,2,8,128]{3,2,1,0:T(8,128)S(1)} %get-tuple-element.30), channel_id=1, source_target_pairs={{0,3},{1,2},{2,1},{3,0},{16,19},{17,18},{18,17},{19,16},{4,7},{5,6... | collective-permute-start | bytes 393224 | tf_op jit(solution)/shard_map/ppermute | solution.py:588
  8.6 15.9 %collective-permute-start.3 = (f32[16,2,8,128]{3,2,1,0:T(8,128)S(1)}, f32[16,2,8,128]{3,2,1,0:T(8,128)S(1)}, u32[]{:S(2)}, u32[]{:S(2)}) collective-permute-start(f32[16,2,8,128]{3,2,1,0:T(8,128)S(1)} %get-tuple-element.31), channel_id=1, source_target_pairs={{0,16},{1,17},{2,18},{3,19},{16,0},{17,1},{18,2},{19,3},{4,20},{5,... | collective-permute-start | bytes 393224 | tf_op jit(solution)/shard_map/ppermute | solution.py:588
  10.4 14.2 %collective-permute-start.4 = (f32[16,2,8,128]{3,2,1,0:T(8,128)S(1)}, f32[16,2,8,128]{3,2,1,0:T(8,128)S(1)}, u32[]{:S(2)}, u32[]{:S(2)}) collective-permute-start(f32[16,2,8,128]{3,2,1,0:T(8,128)S(1)} %get-tuple-element.32), channel_id=1, source_target_pairs={{0,17},{1,16},{2,19},{3,18},{16,1},{17,0},{18,3},{19,2},{4,21},{5,... | collective-permute-start | bytes 393224 | tf_op jit(solution)/shard_map/ppermute | solution.py:588
  11.1 11.9 %copy-start.2 = (s32[64]{0:T(128)S(1)}, s32[64]{0:T(128)}, u32[]{:S(2)}) copy-start(s32[64]{0:T(128)} %owner.2) | copy-start | bytes 772
  11.1 20.1 %collective-permute-start.5 = (f32[16,2,8,128]{3,2,1,0:T(8,128)S(1)}, f32[16,2,8,128]{3,2,1,0:T(8,128)S(1)}, u32[]{:S(2)}, u32[]{:S(2)}) collective-permute-start(f32[16,2,8,128]{3,2,1,0:T(8,128)S(1)} %get-tuple-element.33), channel_id=1, source_target_pairs={{0,18},{1,19},{2,16},{3,17},{16,2},{17,3},{18,0},{19,1},{4,22},{5,... | collective-permute-start | bytes 393224 | tf_op jit(solution)/shard_map/ppermute | solution.py:588
  19.0 12.2 %collective-permute-start.6 = (f32[16,2,8,128]{3,2,1,0:T(8,128)S(1)}, f32[16,2,8,128]{3,2,1,0:T(8,128)S(1)}, u32[]{:S(2)}, u32[]{:S(2)}) collective-permute-start(f32[16,2,8,128]{3,2,1,0:T(8,128)S(1)} %get-tuple-element.34), channel_id=1, source_target_pairs={{0,19},{1,18},{2,17},{3,16},{16,3},{17,2},{18,1},{19,0},{4,23},{5,... | collective-permute-start | bytes 393224 | tf_op jit(solution)/shard_map/ppermute | solution.py:588
  32.0 8.0 %collective-permute-start.9 = (f32[2,16,8,128]{3,2,1,0:T(8,128)S(1)}, f32[2,16,8,128]{3,2,1,0:T(8,128)S(1)}, u32[]{:S(2)}, u32[]{:S(2)}) collective-permute-start(f32[2,16,8,128]{3,2,1,0:T(8,128)S(1)} %get-tuple-element.38), channel_id=1, source_target_pairs={{0,16},{16,0},{1,17},{17,1},{2,18},{18,2},{3,19},{19,3},{4,20},{20... | collective-permute-start | bytes 393224 | tf_op jit(solution)/shard_map/ppermute | solution.py:601
  32.6 5.9 %collective-permute-start.7 = (f32[2,8,128]{2,1,0:T(8,128)S(1)}, f32[2,8,128]{2,1,0:T(8,128)S(1)}, u32[]{:S(2)}, u32[]{:S(2)}) collective-permute-start(f32[2,8,128]{2,1,0:T(8,128)S(1)} %get-tuple-element.36), channel_id=1, source_target_pairs={{0,1},{1,0},{2,3},{3,2},{4,5},{5,4},{6,7},{7,6},{8,9},{9,8},{10,11... | collective-permute-start | bytes 24584 | tf_op jit(solution)/shard_map/ppermute | solution.py:123
  34.6 5.4 %collective-permute-start.8 = (f32[2,8,128]{2,1,0:T(8,128)S(1)}, f32[2,8,128]{2,1,0:T(8,128)S(1)}, u32[]{:S(2)}, u32[]{:S(2)}) collective-permute-start(f32[2,8,128]{2,1,0:T(8,128)S(1)} %get-tuple-element.37), channel_id=1, source_target_pairs={{1,2},{2,1},{3,0},{0,3},{5,6},{6,5},{7,4},{4,7},{9,10},{10,9},{11,... | collective-permute-start | bytes 24584 | tf_op jit(solution)/shard_map/ppermute | solution.py:123
  41.3 5.3 %collective-permute-start.10 = (f32[152,128]{1,0:T(8,128)S(1)}, f32[152,128]{1,0:T(8,128)S(1)}, u32[]{:S(2)}, u32[]{:S(2)}) collective-permute-start(f32[152,128]{1,0:T(8,128)S(1)} %get-tuple-element.46), channel_id=1, source_target_pairs={{0,4},{4,0},{8,12},{12,8},{1,5},{5,1},{9,13},{13,9},{2,6},{6,2},{1... | collective-permute-start | bytes 233480 | tf_op jit(solution)/shard_map/ppermute | solution.py:123
  41.4 5.3 %collective-permute-start.11 = (f32[152,128]{1,0:T(8,128)S(1)}, f32[152,128]{1,0:T(8,128)S(1)}, u32[]{:S(2)}, u32[]{:S(2)}) collective-permute-start(f32[152,128]{1,0:T(8,128)S(1)} %get-tuple-element.47), channel_id=1, source_target_pairs={{4,8},{8,4},{12,0},{0,12},{5,9},{9,5},{13,1},{1,13},{6,10},{10,6},... | collective-permute-start | bytes 233480 | tf_op jit(solution)/shard_map/ppermute | solution.py:123
  43.0 3.7 %collective-permute-start.12 = (f32[16,128]{1,0:T(8,128)S(1)}, f32[16,128]{1,0:T(8,128)S(1)}, u32[]{:S(2)}, u32[]{:S(2)}) collective-permute-start(f32[16,128]{1,0:T(8,128)S(1)} %get-tuple-element.48), channel_id=1, source_target_pairs={{0,16},{16,0},{1,17},{17,1},{2,18},{18,2},{3,19},{19,3},{4,20},{20... | collective-permute-start | bytes 24584 | tf_op jit(solution)/shard_map/ppermute | solution.py:601

commit v8 on v6

--- a/solution.py
+++ b/solution.py
@@ -117,6 +117,10 @@
     return [(i, (i + step) % count) for i in range(count)]
 
 
+def pairs(count, first):
+    return [((i + first) % count, ((i ^ 1) + first) % count) for i in range(count)]
+
+
 def boxes_in_place(arrived, table, me, boxes, capacity, split, joined):
     pieces = len(arrived)
     rows = table.shape[0] // pieces
@@ -127,7 +131,8 @@
 
     def kernel(me_ref, table, *refs):
         ins, refs = refs[:pieces], refs[pieces:]
-        held, low, high, *outs = refs
+        held, odd_pairs, even_pairs, *outs = refs
+        odd = me_ref[1] != 0
         for k, rows_in in enumerate(ins):
             base = (me_ref[0] ^ k) * capacity if split else 0
 
@@ -145,15 +150,18 @@
                         p, side, pl.ds(side * FIELDS, FIELDS), :
                     ]
         pair = lax.broadcasted_iota(jnp.int32, (2 * FIELDS, LANES), 1) % EDGE // HALO
-        for out, bz, first in ((low, 0, 0), (high, BRICK_Z - 1, EDGE - HALO)):
-            for group in range(2):
+        for group in range(2):
+            ends = []
+            for bz, first in ((0, 0), (BRICK_Z - 1, EDGE - HALO)):
                 packed = jnp.zeros((2 * FIELDS, LANES), jnp.float32)
                 for n in range(4):
                     b, part = divmod(group * 4 + n, 2)
                     cells = held[b * BRICK_Z + bz, part]
                     shift = (n * HALO - first) % LANES
                     packed = jnp.where(pair == n, pltpu.roll(cells, shift, 1) if shift else cells, packed)
-                out[group] = packed
+                ends.append(packed)
+            odd_pairs[group] = jnp.where(odd, ends[1], ends[0])
+            even_pairs[group] = jnp.where(odd, ends[0], ends[1])
 
     return pl.pallas_call(
         kernel,
@@ -219,13 +227,15 @@
     return side * FIELDS + f
 
 
-def faces_and_rows(grid, faces, above, below, joined):
+def faces_and_rows(grid, faces, me, odd_pairs, even_pairs, joined):
     sides = [jax.ShapeDtypeStruct((NY, LANES), jnp.float32)] * (2 - joined)
 
-    def kernel(grid, above, below, *refs):
+    def kernel(me_ref, grid, odd_pairs, even_pairs, *refs):
         ins, refs = refs[: len(faces)], refs[len(faces) :]
         (layers, beyond, low, high), refs = refs[:4], refs[4:]
-        outs, (turned,) = refs[: len(sides)], refs[len(sides) :]
+        outs, (turned, ends) = refs[: len(sides)], refs[len(sides) :]
+        ends[me_ref[1]] = even_pairs[...]
+        ends[1 - me_ref[1]] = odd_pairs[...]
         for side in range(2):
             face = ins[0].at[side] if joined else ins[side]
 
@@ -238,7 +248,7 @@
             for by in range(BRICK_Y):
                 for half in range(TILES // 2):
                     group, n = divmod((bx * BRICK_Y + by) * 2 + half, 4)
-                    after, before = above[group], below[group]
+                    after, before = ends[0, group], ends[1, group]
                     columns = [
                         jnp.where(
                             lane < LANES // 2,
@@ -288,12 +298,15 @@
             rows,
         ]
         + sides,
-        in_specs=[VMEM] * (3 + len(faces)),
+        in_specs=[SMEM] + [VMEM] * (3 + len(faces)),
         out_specs=[VMEM] * (4 + len(sides)),
-        scratch_shapes=[pltpu.VMEM((LANES, LANES), jnp.float32)],
+        scratch_shapes=[
+            pltpu.VMEM((LANES, LANES), jnp.float32),
+            pltpu.VMEM((2, 2, 2 * FIELDS, LANES), jnp.float32),
+        ],
         compiler_params=ROOM,
         name="faces_and_rows",
-    )(grid, above, below, *faces)
+    )(me, grid, odd_pairs, even_pairs, *faces)
 
 
 def half_conductance(v):
@@ -558,7 +571,8 @@
     capacity = 2 * (box_count // group_size)
     split = group_size <= 8
     joined = across == 2
-    me = (lax.axis_index("gx") * along + lax.axis_index("gz")).reshape(1)
+    place = lax.axis_index("gx") * along + lax.axis_index("gz")
+    me = jnp.stack([place, lax.axis_index("gz") & 1])
     departing = pack_boxes(old_fields, new_owner, me, group_size, capacity, split)
     table = position_table(old_owner, group_size, capacity)
     if split:
@@ -570,7 +584,7 @@
         arrived = [
             lax.all_to_all(departing[0], ("gx", "gz"), split_axis=0, concat_axis=0, tiled=True)
         ]
-    held, low, high, *faces = boxes_in_place(
+    held, odd_pairs, even_pairs, *faces = boxes_in_place(
         arrived, table, me, box_count, capacity, split, joined
     )
 
@@ -580,10 +594,12 @@
         return [lax.ppermute(side, "gx", ring(across, step)) for side, step in zip(sides, (-1, 1))]
 
     faces = along_x(faces)
-    above = lax.ppermute(low, "gz", ring(along, -1))
-    below = lax.ppermute(high, "gz", ring(along, 1))
+    odd_pairs = lax.ppermute(odd_pairs, "gz", pairs(along, 1))
+    even_pairs = lax.ppermute(even_pairs, "gz", pairs(along, 0))
     grid = grid_from_boxes(held)
-    layers, beyond, low, high, *sides = faces_and_rows(grid, faces, above, below, joined)
+    layers, beyond, low, high, *sides = faces_and_rows(
+        grid, faces, me, odd_pairs, even_pairs, joined
+    )
     rows = lax.axis_size("gy")
     above = lax.ppermute(low, "gy", ring(rows, -1))
     below = lax.ppermute(high, "gy", ring(rows, 1))

time: 48.1 us -> 46.9 us (0.975)
  waiting for transfers between devices: 15.4 us -> 12.4 us
  starting transfers between devices: 21.3 us -> 22.6 us
  Pallas kernels: 9.43 us -> 9.97 us
    ppermute x2, waiting for transfers between devices: 4.05 us -> 1.03 us  [the longest x1 0.53 us: body(): even_pairs = lax.ppermute(even_pairs, 'gz', pairs(along, 0))]
    ppermute x2, starting transfers between devices: 2.33 us -> 3.57 us  [the longest x1 2.33 us: body(): odd_pairs = lax.ppermute(odd_pairs, 'gz', pairs(along, 1))]
    pallas_call x1, Pallas kernels: 0.75 us -> 1.28 us  [faces_and_rows(): pl.pallas_call(kernel, out_shape=[jax.ShapeDtypeStruct((FIELDS, 2 * HALO,...]
  transfers between devices with their start and end apart: 13 -> 13, of which waited for: 6 -> 7; matrix products, arithmetic and copies ran while one was open for 0% -> 0% of each run, Pallas kernels for 9% -> 10%
where the time goes in v8:
time: 46.9 us; the launch traced here: 46.7 us
  starting transfers between devices  22.6 us (48%)
  waiting for transfers between devices  12.4 us (26%)
  Pallas kernels  9.97 us (21%)
  local copies, waits for them, and re-layouts  1.62 us (3%)
    ppermute x7, starting transfers between devices, body(): lax.ppermute(departing[k], ('gx', 'gz'), [(i, i ^ k) for i in range(group...  16.4 us
    ppermute x7, waiting for transfers between devices, body(): lax.ppermute(departing[k], ('gx', 'gz'), [(i, i ^ k) for i in range(group...  10.2 us
    ppermute x1, starting transfers between devices, body(): odd_pairs = lax.ppermute(odd_pairs, 'gz', pairs(along, 1))  2.33 us
    pallas_call x1, Pallas kernels, last_sections(): pl.pallas_call(kernel, out_shape=jax.ShapeDtypeStruct((FIELDS, NX, NY, LA...  2.12 us
    ppermute x2, starting transfers between devices, along_x(): return [lax.ppermute(sides[0], 'gx', ring(across, 1))]  2.09 us
    unnamed x6, local copies, waits for them, and re-layouts  1.62 us
    pallas_call x1, Pallas kernels, position_table(): pl.pallas_call(kernel, out_shape=jax.ShapeDtypeStruct((group * capacity,)...  1.58 us
    pallas_call x1, Pallas kernels, first_inside(): pl.pallas_call(kernel, out_shape=[shape(FIELDS, WIDE_X), shape(WIDE_X), s...  1.5 us
  transfers between devices with their start and end apart: 13, of which 7 were waited for; matrix products, arithmetic and copies ran while one was open for 0% of the time, Pallas kernels for 10%

profile of v8, /device:TPU:0, one launch (start us, length us, event | category | flops | bytes accessed | tf_op | source)
XLA Modules:
  0.0 46.7 jit_solution(16404108637024360046)
XLA Ops:
  0.0 0.0 copy-start.1
  0.0 0.1 pad_add_fusion.me_ref
  0.1 0.6 %copy-done.1 = s32[64]{0:T(128)S(1)} copy-done((s32[64]{0:T(128)S(1)}, s32[64]{0:T(128)}, u32[]{:S(2)}) %copy-start.1) | copy-done | bytes 280
  0.7 0.0 copy-start
  0.7 1.0 %copy-done = f32[64,4,512]{2,1,0:T(4,128)S(1)} copy-done((f32[64,4,512]{2,1,0:T(4,128)S(1)}, f32[64,4,512]{2,1,0:T(4,128)}, u32[]{:S(2)}) %copy-start) | copy-done | bytes 524312
  1.7 1.2 %pack_boxes.1 = (f32[16,2,8,128]{3,2,1,0:T(8,128)S(1)}, f32[16,2,8,128]{3,2,1,0:T(8,128)S(1)}, f32[16,2,8,128]{3,2,1,0:T(8,128)S(1)}, f32[16,2,8,128]{3,2,1,0:T(...) custom-call(s32[2]{0:T(128)S(1)} %pad_add_fusion.me_ref, ...), custom_call_target="tpu_custom_call" | custom-call | tf_op jit(solution)/shard_map/pack_boxes/pallas_call | solution.py:67
  2.9 3.1 %collective-permute-start = (f32[16,2,8,128]{3,2,1,0:T(8,128)S(1)}, f32[16,2,8,128]{3,2,1,0:T(8,128)S(1)}, u32[]{:S(2)}, u32[]{:S(2)}) collective-permute-start(f32[16,2,8,128]{3,2,1,0:T(8,128)S(1)} %get-tuple-element.28), channel_id=1, source_target_pairs={{0,1},{1,0},{2,3},{3,2},{16,17},{17,16},{18,19},{19,18},{4,5},{5,4... | collective-permute-start | bytes 393224 | tf_op jit(solution)/shard_map/ppermute | solution.py:580
  6.0 2.6 %collective-permute-start.1 = (f32[16,2,8,128]{3,2,1,0:T(8,128)S(1)}, f32[16,2,8,128]{3,2,1,0:T(8,128)S(1)}, u32[]{:S(2)}, u32[]{:S(2)}) collective-permute-start(f32[16,2,8,128]{3,2,1,0:T(8,128)S(1)} %get-tuple-element.29), channel_id=1, source_target_pairs={{0,2},{1,3},{2,0},{3,1},{16,18},{17,19},{18,16},{19,17},{4,6},{5,7... | collective-permute-start | bytes 393224 | tf_op jit(solution)/shard_map/ppermute | solution.py:580
  8.6 0.0 collective-permute-start.2
  8.6 1.7 %collective-permute-start.3 = (f32[16,2,8,128]{3,2,1,0:T(8,128)S(1)}, f32[16,2,8,128]{3,2,1,0:T(8,128)S(1)}, u32[]{:S(2)}, u32[]{:S(2)}) collective-permute-start(f32[16,2,8,128]{3,2,1,0:T(8,128)S(1)} %get-tuple-element.31), channel_id=1, source_target_pairs={{0,16},{1,17},{2,18},{3,19},{16,0},{17,1},{18,2},{19,3},{4,20},{5,... | collective-permute-start | bytes 393224 | tf_op jit(solution)/shard_map/ppermute | solution.py:580
  10.4 0.6 %collective-permute-start.4 = (f32[16,2,8,128]{3,2,1,0:T(8,128)S(1)}, f32[16,2,8,128]{3,2,1,0:T(8,128)S(1)}, u32[]{:S(2)}, u32[]{:S(2)}) collective-permute-start(f32[16,2,8,128]{3,2,1,0:T(8,128)S(1)} %get-tuple-element.32), channel_id=1, source_target_pairs={{0,17},{1,16},{2,19},{3,18},{16,1},{17,0},{18,3},{19,2},{4,21},{5,... | collective-permute-start | bytes 393224 | tf_op jit(solution)/shard_map/ppermute | solution.py:580
  11.0 0.1 collective-permute-done.refs_1_
  11.1 0.0 copy-start.2
  11.1 4.4 %collective-permute-start.5 = (f32[16,2,8,128]{3,2,1,0:T(8,128)S(1)}, f32[16,2,8,128]{3,2,1,0:T(8,128)S(1)}, u32[]{:S(2)}, u32[]{:S(2)}) collective-permute-start(f32[16,2,8,128]{3,2,1,0:T(8,128)S(1)} %get-tuple-element.33), channel_id=1, source_target_pairs={{0,18},{1,19},{2,16},{3,17},{16,2},{17,3},{18,0},{19,1},{4,22},{5,... | collective-permute-start | bytes 393224 | tf_op jit(solution)/shard_map/ppermute | solution.py:580
  15.4 3.5 %collective-permute-done.1.refs_2_ = f32[16,2,8,128]{3,2,1,0:T(8,128)S(1)} collective-permute-done((f32[16,2,8,128]{3,2,1,0:T(8,128)S(1)}, f32[16,2,8,128]{3,2,1,0:T(8,128)S(1)}, u32[]{:S(2)}, u32[]{:S(2)}) %collective-permute-start.1) | collective-permute-done | bytes 131104 | tf_op jit(solution)/shard_map/ppermute | solution.py:580
  19.0 4.0 %collective-permute-start.6 = (f32[16,2,8,128]{3,2,1,0:T(8,128)S(1)}, f32[16,2,8,128]{3,2,1,0:T(8,128)S(1)}, u32[]{:S(2)}, u32[]{:S(2)}) collective-permute-start(f32[16,2,8,128]{3,2,1,0:T(8,128)S(1)} %get-tuple-element.34), channel_id=1, source_target_pairs={{0,19},{1,18},{2,17},{3,16},{16,3},{17,2},{18,1},{19,0},{4,23},{5,... | collective-permute-start | bytes 393224 | tf_op jit(solution)/shard_map/ppermute | solution.py:580
  23.0 0.0 copy-done.2
  23.0 1.6 %position_table.1.table = s32[128]{0:T(128)S(1)} custom-call(s32[64]{0:T(128)S(1)} %copy-done.2), custom_call_target="tpu_custom_call" | custom-call | bytes 4194304 | tf_op jit(solution)/shard_map/position_table/pallas_call | solution.py:87
  24.5 0.0 collective-permute-done.2.refs_3_
  24.5 0.0 collective-permute-done.3.refs_4_
  24.6 0.0 collective-permute-done.4.refs_5_
  24.6 6.6 %collective-permute-done.5.refs_6_ = f32[16,2,8,128]{3,2,1,0:T(8,128)S(1)} collective-permute-done((f32[16,2,8,128]{3,2,1,0:T(8,128)S(1)}, f32[16,2,8,128]{3,2,1,0:T(8,128)S(1)}, u32[]{:S(2)}, u32[]{:S(2)}) %collective-permute-start.5) | collective-permute-done | bytes 131104 | tf_op jit(solution)/shard_map/ppermute | solution.py:580
  31.1 0.0 collective-permute-done.6.refs_7_
  31.1 0.9 %boxes_in_place.1 = (f32[65,2,8,128]{3,2,1,0:T(8,128)S(1)}, f32[2,8,128]{2,1,0:T(8,128)S(1)}, f32[2,8,128]{2,1,0:T(8,128)S(1)}, f32[2,16,8,128]{3,2,1,0:T(8,128)S(1)}) custom-call(s32[2]{0:T(128)S(1)} %pad_add_fusion.me_ref, s32[128]{0:T(128)S(1)} %position_table.1.table, f32[16,2,8,128]{3,2,1,0:T(8,128)S(1)} %get-tuple-element.27.refs_0_, ...), custom_call_target="tpu_custom_call" | custom-call | tf_op jit(solution)/shard_map/boxes_in_place/pallas_call | solution.py:166
  32.0 0.6 %collective-permute-start.9 = (f32[2,16,8,128]{3,2,1,0:T(8,128)S(1)}, f32[2,16,8,128]{3,2,1,0:T(8,128)S(1)}, u32[]{:S(2)}, u32[]{:S(2)}) collective-permute-start(f32[2,16,8,128]{3,2,1,0:T(8,128)S(1)} %get-tuple-element.38), channel_id=1, source_target_pairs={{0,16},{16,0},{1,17},{17,1},{2,18},{18,2},{3,19},{19,3},{4,20},{20... | collective-permute-start | bytes 393224 | tf_op jit(solution)/shard_map/ppermute | solution.py:593
  32.6 2.3 %collective-permute-start.7 = (f32[2,8,128]{2,1,0:T(8,128)S(1)}, f32[2,8,128]{2,1,0:T(8,128)S(1)}, u32[]{:S(2)}, u32[]{:S(2)}) collective-permute-start(f32[2,8,128]{2,1,0:T(8,128)S(1)} %get-tuple-element.36), channel_id=1, source_target_pairs={{1,2},{2,1},{3,0},{0,3},{5,6},{6,5},{7,4},{4,7},{9,10},{10,9},{11,... | collective-permute-start | bytes 24584 | tf_op jit(solution)/shard_map/ppermute | solution.py:597
  34.9 1.2 %collective-permute-start.8 = (f32[2,8,128]{2,1,0:T(8,128)S(1)}, f32[2,8,128]{2,1,0:T(8,128)S(1)}, u32[]{:S(2)}, u32[]{:S(2)}) collective-permute-start(f32[2,8,128]{2,1,0:T(8,128)S(1)} %get-tuple-element.37), channel_id=1, source_target_pairs={{0,1},{1,0},{2,3},{3,2},{4,5},{5,4},{6,7},{7,6},{8,9},{9,8},{10,11... | collective-permute-start | bytes 24584 | tf_op jit(solution)/shard_map/ppermute | solution.py:598
  36.2 1.4 %grid_from_boxes.1.grid = f32[4,16,16,128]{3,2,1,0:T(8,128)S(1)} custom-call(f32[65,2,8,128]{3,2,1,0:T(8,128)S(1)} %get-tuple-element.35.held), custom_call_target="tpu_custom_call" | custom-call | flops 4194304 | bytes 2097152 | tf_op jit(solution)/shard_map/grid_from_boxes/pallas_call | solution.py:206
  37.6 0.5 %collective-permute-done.7.odd_pairs = f32[2,8,128]{2,1,0:T(8,128)S(1)} collective-permute-done((f32[2,8,128]{2,1,0:T(8,128)S(1)}, f32[2,8,128]{2,1,0:T(8,128)S(1)}, u32[]{:S(2)}, u32[]{:S(2)}) %collective-permute-start.7) | collective-permute-done | bytes 8224 | tf_op jit(solution)/shard_map/ppermute | solution.py:597
  38.1 0.5 %collective-permute-done.8.even_pairs = f32[2,8,128]{2,1,0:T(8,128)S(1)} collective-permute-done((f32[2,8,128]{2,1,0:T(8,128)S(1)}, f32[2,8,128]{2,1,0:T(8,128)S(1)}, u32[]{:S(2)}, u32[]{:S(2)}) %collective-permute-start.8) | collective-permute-done | bytes 8224 | tf_op jit(solution)/shard_map/ppermute | solution.py:598
  38.6 0.0 collective-permute-done.9.refs_0_
  38.6 1.3 %faces_and_rows.1 = (f32[4,4,16,128]{3,2,1,0:T(8,128)S(1)}, f32[4,16,16,128]{3,2,1,0:T(8,128)S(1)}, f32[152,128]{1,0:T(8,128)S(1)}, f32[152,128]{1,0:T(8,128)S(1)}, f32[16,128]{1,0:T(8,128)S(1)}) custom-call(s32[2]{0:T(128)S(1)} %pad_add_fusion.me_ref, f32[4,16,16,128]{3,2,1,0:T(8,128)S(1)} %grid_from_boxes.1.grid, ...), custom_call_target="tpu_custom_call" | custom-call | tf_op jit(solution)/shard_map/faces_and_rows/pallas_call | solution.py:292
  39.9 0.1 collective-permute-start.10
  39.9 0.5 %collective-permute-start.11 = (f32[152,128]{1,0:T(8,128)S(1)}, f32[152,128]{1,0:T(8,128)S(1)}, u32[]{:S(2)}, u32[]{:S(2)}) collective-permute-start(f32[152,128]{1,0:T(8,128)S(1)} %get-tuple-element.47), channel_id=1, source_target_pairs={{0,4},{4,8},{8,12},{12,0},{1,5},{5,9},{9,13},{13,1},{2,6},{6,10},{... | collective-permute-start | bytes 233480 | tf_op jit(solution)/shard_map/ppermute | solution.py:605
  40.4 1.5 %collective-permute-start.12 = (f32[16,128]{1,0:T(8,128)S(1)}, f32[16,128]{1,0:T(8,128)S(1)}, u32[]{:S(2)}, u32[]{:S(2)}) collective-permute-start(f32[16,128]{1,0:T(8,128)S(1)} %get-tuple-element.48), channel_id=1, source_target_pairs={{0,16},{16,0},{1,17},{17,1},{2,18},{18,2},{3,19},{19,3},{4,20},{20... | collective-permute-start | bytes 24584 | tf_op jit(solution)/shard_map/ppermute | solution.py:593
  42.0 1.5 %first_inside.1 = (f32[4,20,16,128]{3,2,1,0:T(8,128)S(1)}, f32[20,16,128]{2,1,0:T(8,128)S(1)}, f32[4,16,16,128]{3,2,1,0:T(8,128)S(1)}, f32[4,16,16,128]{3,2,1,0:T(8,128)S(1)}, f32[16,16,128]{2,1,0:T(8,128)S(1)}) custom-call(f32[4,16,16,128]{3,2,1,0:T(8,128)S(1)} %grid_from_boxes.1.grid, f32[4,4,16,128]{3,2,1,0:T(8,128)S(1)} %get-tuple-element.39.layers, ...), custom_call_target="tpu_custom_call" | custom-call | flops 4194304 | bytes 2097152 | tf_op jit(solution)/shard_map/first_inside/pallas_call | solution.py:399
  43.5 0.6 %collective-permute-done.12.refs_0_ = f32[16,128]{1,0:T(8,128)S(1)} collective-permute-done((f32[16,128]{1,0:T(8,128)S(1)}, f32[16,128]{1,0:T(8,128)S(1)}, u32[]{:S(2)}, u32[]{:S(2)}) %collective-permute-start.12) | collective-permute-done | bytes 8224 | tf_op jit(solution)/shard_map/ppermute | solution.py:593
  44.1 0.0 collective-permute-done.10.above
  44.1 0.5 %collective-permute-done.11.below = f32[152,128]{1,0:T(8,128)S(1)} collective-permute-done((f32[152,128]{1,0:T(8,128)S(1)}, f32[152,128]{1,0:T(8,128)S(1)}, u32[]{:S(2)}, u32[]{:S(2)}) %collective-permute-start.11) | collective-permute-done | bytes 77856 | tf_op jit(solution)/shard_map/ppermute | solution.py:605
  44.6 2.1 %last_sections.1 = f32[4,16,16,128]{3,2,1,0:T(8,128)} custom-call(f32[4,20,16,128]{3,2,1,0:T(8,128)S(1)} %get-tuple-element.41.wide, f32[20,16,128]{2,1,0:T(8,128)S(1)} %get-tuple-element.42.halves, f32[4,16,16,128]{3,2,1,0:T(8,128)S(1)} %get-tuple-element.43.first_in, f32[4,16,16,128]{3,2,1,0:T(8,128)S(1)} %get-tuple-element.44.beyond_in, ...), custom_call_target="tpu_custom_call" | custom-call | tf_op jit(solution)/shard_map/last_sections/pallas_call | solution.py:549
Async XLA Ops:
  0.0 0.7 %copy-start.1 = (s32[64]{0:T(128)S(1)}, s32[64]{0:T(128)}, u32[]{:S(2)}) copy-start(s32[64]{0:T(128)} %owner.3) | copy-start | bytes 772
  0.7 1.0 %copy-start = (f32[64,4,512]{2,1,0:T(4,128)S(1)}, f32[64,4,512]{2,1,0:T(4,128)}, u32[]{:S(2)}) copy-start(f32[64,4,512]{2,1,0:T(4,128)} %fields.1) | copy-start | bytes 1572868
  2.9 8.1 %collective-permute-start = (f32[16,2,8,128]{3,2,1,0:T(8,128)S(1)}, f32[16,2,8,128]{3,2,1,0:T(8,128)S(1)}, u32[]{:S(2)}, u32[]{:S(2)}) collective-permute-start(f32[16,2,8,128]{3,2,1,0:T(8,128)S(1)} %get-tuple-element.28), channel_id=1, source_target_pairs={{0,1},{1,0},{2,3},{3,2},{16,17},{17,16},{18,19},{19,18},{4,5},{5,4... | collective-permute-start | bytes 393224 | tf_op jit(solution)/shard_map/ppermute | solution.py:580
  6.0 12.9 %collective-permute-start.1 = (f32[16,2,8,128]{3,2,1,0:T(8,128)S(1)}, f32[16,2,8,128]{3,2,1,0:T(8,128)S(1)}, u32[]{:S(2)}, u32[]{:S(2)}) collective-permute-start(f32[16,2,8,128]{3,2,1,0:T(8,128)S(1)} %get-tuple-element.29), channel_id=1, source_target_pairs={{0,2},{1,3},{2,0},{3,1},{16,18},{17,19},{18,16},{19,17},{4,6},{5,7... | collective-permute-start | bytes 393224 | tf_op jit(solution)/shard_map/ppermute | solution.py:580
  8.6 15.9 %collective-permute-start.2 = (f32[16,2,8,128]{3,2,1,0:T(8,128)S(1)}, f32[16,2,8,128]{3,2,1,0:T(8,128)S(1)}, u32[]{:S(2)}, u32[]{:S(2)}) collective-permute-start(f32[16,2,8,128]{3,2,1,0:T(8,128)S(1)} %get-tuple-element.30), channel_id=1, source_target_pairs={{0,3},{1,2},{2,1},{3,0},{16,19},{17,18},{18,17},{19,16},{4,7},{5,6... | collective-permute-start | bytes 393224 | tf_op jit(solution)/shard_map/ppermute | solution.py:580
  8.6 15.9 %collective-permute-start.3 = (f32[16,2,8,128]{3,2,1,0:T(8,128)S(1)}, f32[16,2,8,128]{3,2,1,0:T(8,128)S(1)}, u32[]{:S(2)}, u32[]{:S(2)}) collective-permute-start(f32[16,2,8,128]{3,2,1,0:T(8,128)S(1)} %get-tuple-element.31), channel_id=1, source_target_pairs={{0,16},{1,17},{2,18},{3,19},{16,0},{17,1},{18,2},{19,3},{4,20},{5,... | collective-permute-start | bytes 393224 | tf_op jit(solution)/shard_map/ppermute | solution.py:580
  10.4 14.2 %collective-permute-start.4 = (f32[16,2,8,128]{3,2,1,0:T(8,128)S(1)}, f32[16,2,8,128]{3,2,1,0:T(8,128)S(1)}, u32[]{:S(2)}, u32[]{:S(2)}) collective-permute-start(f32[16,2,8,128]{3,2,1,0:T(8,128)S(1)} %get-tuple-element.32), channel_id=1, source_target_pairs={{0,17},{1,16},{2,19},{3,18},{16,1},{17,0},{18,3},{19,2},{4,21},{5,... | collective-permute-start | bytes 393224 | tf_op jit(solution)/shard_map/ppermute | solution.py:580
  11.1 11.9 %copy-start.2 = (s32[64]{0:T(128)S(1)}, s32[64]{0:T(128)}, u32[]{:S(2)}) copy-start(s32[64]{0:T(128)} %owner.2) | copy-start | bytes 772
  11.1 20.1 %collective-permute-start.5 = (f32[16,2,8,128]{3,2,1,0:T(8,128)S(1)}, f32[16,2,8,128]{3,2,1,0:T(8,128)S(1)}, u32[]{:S(2)}, u32[]{:S(2)}) collective-permute-start(f32[16,2,8,128]{3,2,1,0:T(8,128)S(1)} %get-tuple-element.33), channel_id=1, source_target_pairs={{0,18},{1,19},{2,16},{3,17},{16,2},{17,3},{18,0},{19,1},{4,22},{5,... | collective-permute-start | bytes 393224 | tf_op jit(solution)/shard_map/ppermute | solution.py:580
  19.0 12.2 %collective-permute-start.6 = (f32[16,2,8,128]{3,2,1,0:T(8,128)S(1)}, f32[16,2,8,128]{3,2,1,0:T(8,128)S(1)}, u32[]{:S(2)}, u32[]{:S(2)}) collective-permute-start(f32[16,2,8,128]{3,2,1,0:T(8,128)S(1)} %get-tuple-element.34), channel_id=1, source_target_pairs={{0,19},{1,18},{2,17},{3,16},{16,3},{17,2},{18,1},{19,0},{4,23},{5,... | collective-permute-start | bytes 393224 | tf_op jit(solution)/shard_map/ppermute | solution.py:580
  32.0 6.6 %collective-permute-start.9 = (f32[2,16,8,128]{3,2,1,0:T(8,128)S(1)}, f32[2,16,8,128]{3,2,1,0:T(8,128)S(1)}, u32[]{:S(2)}, u32[]{:S(2)}) collective-permute-start(f32[2,16,8,128]{3,2,1,0:T(8,128)S(1)} %get-tuple-element.38), channel_id=1, source_target_pairs={{0,16},{16,0},{1,17},{17,1},{2,18},{18,2},{3,19},{19,3},{4,20},{20... | collective-permute-start | bytes 393224 | tf_op jit(solution)/shard_map/ppermute | solution.py:593
  32.6 5.4 %collective-permute-start.7 = (f32[2,8,128]{2,1,0:T(8,128)S(1)}, f32[2,8,128]{2,1,0:T(8,128)S(1)}, u32[]{:S(2)}, u32[]{:S(2)}) collective-permute-start(f32[2,8,128]{2,1,0:T(8,128)S(1)} %get-tuple-element.36), channel_id=1, source_target_pairs={{1,2},{2,1},{3,0},{0,3},{5,6},{6,5},{7,4},{4,7},{9,10},{10,9},{11,... | collective-permute-start | bytes 24584 | tf_op jit(solution)/shard_map/ppermute | solution.py:597
  34.9 3.7 %collective-permute-start.8 = (f32[2,8,128]{2,1,0:T(8,128)S(1)}, f32[2,8,128]{2,1,0:T(8,128)S(1)}, u32[]{:S(2)}, u32[]{:S(2)}) collective-permute-start(f32[2,8,128]{2,1,0:T(8,128)S(1)} %get-tuple-element.37), channel_id=1, source_target_pairs={{0,1},{1,0},{2,3},{3,2},{4,5},{5,4},{6,7},{7,6},{8,9},{9,8},{10,11... | collective-permute-start | bytes 24584 | tf_op jit(solution)/shard_map/ppermute | solution.py:598
  39.9 4.2 %collective-permute-start.10 = (f32[152,128]{1,0:T(8,128)S(1)}, f32[152,128]{1,0:T(8,128)S(1)}, u32[]{:S(2)}, u32[]{:S(2)}) collective-permute-start(f32[152,128]{1,0:T(8,128)S(1)} %get-tuple-element.46), channel_id=1, source_target_pairs={{0,12},{4,0},{8,4},{12,8},{1,13},{5,1},{9,5},{13,9},{2,14},{6,2},{... | collective-permute-start | bytes 233480 | tf_op jit(solution)/shard_map/ppermute | solution.py:604
  39.9 4.7 %collective-permute-start.11 = (f32[152,128]{1,0:T(8,128)S(1)}, f32[152,128]{1,0:T(8,128)S(1)}, u32[]{:S(2)}, u32[]{:S(2)}) collective-permute-start(f32[152,128]{1,0:T(8,128)S(1)} %get-tuple-element.47), channel_id=1, source_target_pairs={{0,4},{4,8},{8,12},{12,0},{1,5},{5,9},{9,13},{13,1},{2,6},{6,10},{... | collective-permute-start | bytes 233480 | tf_op jit(solution)/shard_map/ppermute | solution.py:605
  40.4 3.7 %collective-permute-start.12 = (f32[16,128]{1,0:T(8,128)S(1)}, f32[16,128]{1,0:T(8,128)S(1)}, u32[]{:S(2)}, u32[]{:S(2)}) collective-permute-start(f32[16,128]{1,0:T(8,128)S(1)} %get-tuple-element.48), channel_id=1, source_target_pairs={{0,16},{16,0},{1,17},{17,1},{2,18},{18,2},{3,19},{19,3},{4,20},{20... | collective-permute-start | bytes 24584 | tf_op jit(solution)/shard_map/ppermute | solution.py:593

commit v9 on v8

--- a/solution.py
+++ b/solution.py
@@ -21,7 +21,16 @@
 
 VMEM = pl.BlockSpec(memory_space=pltpu.VMEM)
 SMEM = pl.BlockSpec(memory_space=pltpu.SMEM)
+HBM = pl.BlockSpec(memory_space=pltpu.HBM)
 ROOM = pltpu.CompilerParams(vmem_limit_bytes=16 * 2**20)
+
+
+def in_hbm(array):
+    return pltpu.with_memory_space_constraint(array, pltpu.HBM)
+
+
+def group_place():
+    return lax.axis_index("gx") * lax.axis_size("gz") + lax.axis_index("gz")
 
 
 def rank_table(owner, table, counts, group, capacity, boxes, empty):
@@ -43,16 +52,22 @@
     lax.fori_loop(0, boxes, place, 0, unroll=8)
 
 
-def pack_boxes(old_fields, new_owner, me, group, capacity, split):
+def pack_boxes(old_fields, new_owner, group, capacity, split):
     boxes = new_owner.shape[0]
     pieces = group if split else 1
     rows = group * capacity // pieces
 
-    def kernel(me_ref, owner, fields, *refs):
-        outs, (table, counts) = refs[:pieces], refs[pieces:]
+    def kernel(owner_hbm, fields_hbm, *refs):
+        outs, (owner, fields, table, counts, sems) = refs[:pieces], refs[pieces:]
+        fetch_owner = pltpu.make_async_copy(owner_hbm, owner, sems.at[0])
+        fetch_fields = pltpu.make_async_copy(fields_hbm, fields, sems.at[1])
+        fetch_owner.start()
+        fetch_fields.start()
+        fetch_owner.wait()
         rank_table(owner, table, counts, group, capacity, boxes, 0)
+        fetch_fields.wait()
         for k, out in enumerate(outs):
-            base = (me_ref[0] ^ k) * capacity if split else 0
+            base = (group_place() ^ k) * capacity if split else 0
 
             def copy(r, carry, out=out, base=base):
                 box = table[base + r]
@@ -67,15 +82,18 @@
     return pl.pallas_call(
         kernel,
         out_shape=[jax.ShapeDtypeStruct((rows,) + BOX, jnp.float32)] * pieces,
-        in_specs=[SMEM, SMEM, VMEM],
+        in_specs=[HBM, HBM],
         out_specs=[VMEM] * pieces,
         scratch_shapes=[
+            pltpu.SMEM((boxes,), jnp.int32),
+            pltpu.VMEM(old_fields.shape, jnp.float32),
             pltpu.SMEM((group * capacity,), jnp.int32),
             pltpu.SMEM((group,), jnp.int32),
+            pltpu.SemaphoreType.DMA((2,)),
         ],
         compiler_params=ROOM,
         name="pack_boxes",
-    )(me, new_owner, old_fields)
+    )(in_hbm(new_owner), in_hbm(old_fields))
 
 
 def position_table(old_owner, group, capacity):
@@ -86,7 +104,7 @@
 
     return pl.pallas_call(
         kernel,
-        out_shape=jax.ShapeDtypeStruct((group * capacity,), jnp.int32),
+        out_shape=pltpu.SMEM((group * capacity,), jnp.int32),
         in_specs=[SMEM],
         out_specs=SMEM,
         scratch_shapes=[pltpu.SMEM((group,), jnp.int32)],
@@ -121,7 +139,7 @@
     return [((i + first) % count, ((i ^ 1) + first) % count) for i in range(count)]
 
 
-def boxes_in_place(arrived, table, me, boxes, capacity, split, joined):
+def boxes_in_place(arrived, table, boxes, capacity, split, joined):
     pieces = len(arrived)
     rows = table.shape[0] // pieces
     half = boxes // BRICK_X
@@ -129,12 +147,12 @@
     faces = [jax.ShapeDtypeStruct((2,) + face if joined else face, jnp.float32)] * (2 - joined)
     end = jax.ShapeDtypeStruct((2, 2 * FIELDS, LANES), jnp.float32)
 
-    def kernel(me_ref, table, *refs):
+    def kernel(table, *refs):
         ins, refs = refs[:pieces], refs[pieces:]
         held, odd_pairs, even_pairs, *outs = refs
-        odd = me_ref[1] != 0
+        odd = lax.axis_index("gz") & 1 != 0
         for k, rows_in in enumerate(ins):
-            base = (me_ref[0] ^ k) * capacity if split else 0
+            base = (group_place() ^ k) * capacity if split else 0
 
             def scatter(r, carry, rows_in=rows_in, base=base):
                 held[table[base + r]] = rows_in[r]
@@ -166,11 +184,11 @@
     return pl.pallas_call(
         kernel,
         out_shape=[jax.ShapeDtypeStruct((boxes + 1,) + BOX, jnp.float32), end, end] + faces,
-        in_specs=[SMEM, SMEM] + [VMEM] * pieces,
+        in_specs=[SMEM] + [VMEM] * pieces,
         out_specs=[VMEM] * (3 + len(faces)),
         compiler_params=ROOM,
         name="boxes_in_place",
-    )(me, table, *arrived)
+    )(pltpu.with_memory_space_constraint(table, pltpu.SMEM), *arrived)
 
 
 HALO = 2
@@ -227,15 +245,16 @@
     return side * FIELDS + f
 
 
-def faces_and_rows(grid, faces, me, odd_pairs, even_pairs, joined):
+def faces_and_rows(grid, faces, odd_pairs, even_pairs, joined):
     sides = [jax.ShapeDtypeStruct((NY, LANES), jnp.float32)] * (2 - joined)
 
-    def kernel(me_ref, grid, odd_pairs, even_pairs, *refs):
+    def kernel(grid, odd_pairs, even_pairs, *refs):
         ins, refs = refs[: len(faces)], refs[len(faces) :]
         (layers, beyond, low, high), refs = refs[:4], refs[4:]
         outs, (turned, ends) = refs[: len(sides)], refs[len(sides) :]
-        ends[me_ref[1]] = even_pairs[...]
-        ends[1 - me_ref[1]] = odd_pairs[...]
+        odd = lax.axis_index("gz") & 1
+        ends[odd] = even_pairs[...]
+        ends[1 - odd] = odd_pairs[...]
         for side in range(2):
             face = ins[0].at[side] if joined else ins[side]
 
@@ -298,7 +317,7 @@
             rows,
         ]
         + sides,
-        in_specs=[SMEM] + [VMEM] * (3 + len(faces)),
+        in_specs=[VMEM] * (3 + len(faces)),
         out_specs=[VMEM] * (4 + len(sides)),
         scratch_shapes=[
             pltpu.VMEM((LANES, LANES), jnp.float32),
@@ -306,7 +325,7 @@
         ],
         compiler_params=ROOM,
         name="faces_and_rows",
-    )(me, grid, odd_pairs, even_pairs, *faces)
+    )(grid, odd_pairs, even_pairs, *faces)
 
 
 def half_conductance(v):
@@ -571,9 +590,7 @@
     capacity = 2 * (box_count // group_size)
     split = group_size <= 8
     joined = across == 2
-    place = lax.axis_index("gx") * along + lax.axis_index("gz")
-    me = jnp.stack([place, lax.axis_index("gz") & 1])
-    departing = pack_boxes(old_fields, new_owner, me, group_size, capacity, split)
+    departing = pack_boxes(old_fields, new_owner, group_size, capacity, split)
     table = position_table(old_owner, group_size, capacity)
     if split:
         arrived = [departing[0]] + [
@@ -585,7 +602,7 @@
             lax.all_to_all(departing[0], ("gx", "gz"), split_axis=0, concat_axis=0, tiled=True)
         ]
     held, odd_pairs, even_pairs, *faces = boxes_in_place(
-        arrived, table, me, box_count, capacity, split, joined
+        arrived, table, box_count, capacity, split, joined
     )
 
     def along_x(sides):
@@ -598,7 +615,7 @@
     even_pairs = lax.ppermute(even_pairs, "gz", pairs(along, 0))
     grid = grid_from_boxes(held)
     layers, beyond, low, high, *sides = faces_and_rows(
-        grid, faces, me, odd_pairs, even_pairs, joined
+        grid, faces, odd_pairs, even_pairs, joined
     )
     rows = lax.axis_size("gy")
     above = lax.ppermute(low, "gy", ring(rows, -1))

time: 46.9 us -> 44.2 us (0.942)
  local copies, waits for them, and re-layouts: 1.62 us -> 0.01 us
  Pallas kernels: 9.97 us -> 8.43 us
  waiting for transfers between devices: 12.4 us -> 13.1 us
    unnamed x6 -> x2, local copies, waits for them, and re-layouts: 1.62 us -> 0.01 us
    ppermute x7, waiting for transfers between devices: 10.2 us -> 10.9 us  [body(): lax.ppermute(departing[k], ('gx', 'gz'), [(i, i ^ k) for i in range(group...]
    pallas_call x1, Pallas kernels: 1.58 us -> 0.98 us  [position_table(): pl.pallas_call(kernel, out_shape=pltpu.SMEM((group * capacity,), jnp.int3...]
    pallas_call x1, Pallas kernels: 0.89 us -> 0.32 us  [boxes_in_place(): pl.pallas_call(kernel, out_shape=[jax.ShapeDtypeStruct((boxes + 1,) + BOX...]
    pallas_call x1, Pallas kernels: 1.28 us -> 0.75 us  [faces_and_rows(): pl.pallas_call(kernel, out_shape=[jax.ShapeDtypeStruct((FIELDS, 2 * HALO,...]
  transfers between devices with their start and end apart: 13 -> 13, of which waited for: 7 -> 7; matrix products, arithmetic and copies ran while one was open for 0% -> 0% of each run, Pallas kernels for 10% -> 9%
where the time goes in v9:
time: 44.2 us; the launch traced here: 44.1 us
  starting transfers between devices  22.5 us (51%)
  waiting for transfers between devices  13.1 us (30%)
  Pallas kernels  8.43 us (19%)
    ppermute x7, starting transfers between devices, body(): lax.ppermute(departing[k], ('gx', 'gz'), [(i, i ^ k) for i in range(group...  16.4 us
    ppermute x7, waiting for transfers between devices, body(): lax.ppermute(departing[k], ('gx', 'gz'), [(i, i ^ k) for i in range(group...  10.9 us
    ppermute x1, starting transfers between devices, body(): odd_pairs = lax.ppermute(odd_pairs, 'gz', pairs(along, 1))  2.23 us
    pallas_call x1, Pallas kernels, last_sections(): pl.pallas_call(kernel, out_shape=jax.ShapeDtypeStruct((FIELDS, NX, NY, LA...  2.12 us
    ppermute x2, starting transfers between devices, along_x(): return [lax.ppermute(sides[0], 'gx', ring(across, 1))]  2.08 us
    pallas_call x1, Pallas kernels, first_inside(): pl.pallas_call(kernel, out_shape=[shape(FIELDS, WIDE_X), shape(WIDE_X), s...  1.5 us
    pallas_call x1, Pallas kernels, grid_from_boxes(): pl.pallas_call(kernel, out_shape=jax.ShapeDtypeStruct((FIELDS, NX, NY, LA...  1.38 us
    pallas_call x1, Pallas kernels, pack_boxes(): pl.pallas_call(kernel, out_shape=[jax.ShapeDtypeStruct((rows,) + BOX, jnp...  1.38 us
  transfers between devices with their start and end apart: 13, of which 7 were waited for; matrix products, arithmetic and copies ran while one was open for 0% of the time, Pallas kernels for 9%

profile of v9, /device:TPU:0, one launch (start us, length us, event | category | flops | bytes accessed | tf_op | source)
XLA Modules:
  0.0 44.1 jit_solution(681961211998029989)
XLA Ops:
  0.0 1.4 %pack_boxes.1 = (f32[16,2,8,128]{3,2,1,0:T(8,128)S(1)}, f32[16,2,8,128]{3,2,1,0:T(8,128)S(1)}, f32[16,2,8,128]{3,2,1,0:T(8,128)S(1)}, f32[16,2,8,128]{3,2,1,0:T(...) custom-call(s32[64]{0:T(128)} %owner_hbm.1, ...), custom_call_target="tpu_custom_call" | custom-call | tf_op jit(solution)/shard_map/pack_boxes/pallas_call | solution.py:82
  1.4 3.1 %collective-permute-start = (f32[16,2,8,128]{3,2,1,0:T(8,128)S(1)}, f32[16,2,8,128]{3,2,1,0:T(8,128)S(1)}, u32[]{:S(2)}, u32[]{:S(2)}) collective-permute-start(f32[16,2,8,128]{3,2,1,0:T(8,128)S(1)} %get-tuple-element.28), channel_id=1, source_target_pairs={{0,1},{1,0},{2,3},{3,2},{16,17},{17,16},{18,19},{19,18},{4,5},{5,4... | collective-permute-start | bytes 393224 | tf_op jit(solution)/shard_map/ppermute | solution.py:597
  4.5 2.6 %collective-permute-start.1 = (f32[16,2,8,128]{3,2,1,0:T(8,128)S(1)}, f32[16,2,8,128]{3,2,1,0:T(8,128)S(1)}, u32[]{:S(2)}, u32[]{:S(2)}) collective-permute-start(f32[16,2,8,128]{3,2,1,0:T(8,128)S(1)} %get-tuple-element.29), channel_id=1, source_target_pairs={{0,2},{1,3},{2,0},{3,1},{16,18},{17,19},{18,16},{19,17},{4,6},{5,7... | collective-permute-start | bytes 393224 | tf_op jit(solution)/shard_map/ppermute | solution.py:597
  7.1 0.0 collective-permute-start.2
  7.1 1.7 %collective-permute-start.3 = (f32[16,2,8,128]{3,2,1,0:T(8,128)S(1)}, f32[16,2,8,128]{3,2,1,0:T(8,128)S(1)}, u32[]{:S(2)}, u32[]{:S(2)}) collective-permute-start(f32[16,2,8,128]{3,2,1,0:T(8,128)S(1)} %get-tuple-element.31), channel_id=1, source_target_pairs={{0,16},{1,17},{2,18},{3,19},{16,0},{17,1},{18,2},{19,3},{4,20},{5,... | collective-permute-start | bytes 393224 | tf_op jit(solution)/shard_map/ppermute | solution.py:597
  8.8 0.6 %collective-permute-start.4 = (f32[16,2,8,128]{3,2,1,0:T(8,128)S(1)}, f32[16,2,8,128]{3,2,1,0:T(8,128)S(1)}, u32[]{:S(2)}, u32[]{:S(2)}) collective-permute-start(f32[16,2,8,128]{3,2,1,0:T(8,128)S(1)} %get-tuple-element.32), channel_id=1, source_target_pairs={{0,17},{1,16},{2,19},{3,18},{16,1},{17,0},{18,3},{19,2},{4,21},{5,... | collective-permute-start | bytes 393224 | tf_op jit(solution)/shard_map/ppermute | solution.py:597
  9.4 0.1 collective-permute-done.refs_1_
  9.5 0.0 copy-start
  9.5 4.4 %collective-permute-start.5 = (f32[16,2,8,128]{3,2,1,0:T(8,128)S(1)}, f32[16,2,8,128]{3,2,1,0:T(8,128)S(1)}, u32[]{:S(2)}, u32[]{:S(2)}) collective-permute-start(f32[16,2,8,128]{3,2,1,0:T(8,128)S(1)} %get-tuple-element.33), channel_id=1, source_target_pairs={{0,18},{1,19},{2,16},{3,17},{16,2},{17,3},{18,0},{19,1},{4,22},{5,... | collective-permute-start | bytes 393224 | tf_op jit(solution)/shard_map/ppermute | solution.py:597
  13.9 3.5 %collective-permute-done.1.refs_2_ = f32[16,2,8,128]{3,2,1,0:T(8,128)S(1)} collective-permute-done((f32[16,2,8,128]{3,2,1,0:T(8,128)S(1)}, f32[16,2,8,128]{3,2,1,0:T(8,128)S(1)}, u32[]{:S(2)}, u32[]{:S(2)}) %collective-permute-start.1) | collective-permute-done | bytes 131104 | tf_op jit(solution)/shard_map/ppermute | solution.py:597
  17.4 4.0 %collective-permute-start.6 = (f32[16,2,8,128]{3,2,1,0:T(8,128)S(1)}, f32[16,2,8,128]{3,2,1,0:T(8,128)S(1)}, u32[]{:S(2)}, u32[]{:S(2)}) collective-permute-start(f32[16,2,8,128]{3,2,1,0:T(8,128)S(1)} %get-tuple-element.34), channel_id=1, source_target_pairs={{0,19},{1,18},{2,17},{3,16},{16,3},{17,2},{18,1},{19,0},{4,23},{5,... | collective-permute-start | bytes 393224 | tf_op jit(solution)/shard_map/ppermute | solution.py:597
  21.4 0.0 copy-done
  21.4 1.0 %position_table.1.table = s32[128]{0:T(128)S(4)} custom-call(s32[64]{0:T(128)S(1)} %copy-done), custom_call_target="tpu_custom_call" | custom-call | bytes 4194304 | tf_op jit(solution)/shard_map/position_table/pallas_call | solution.py:105
  22.4 0.0 collective-permute-done.2.refs_3_
  22.4 0.0 collective-permute-done.3.refs_4_
  22.4 0.0 collective-permute-done.4.refs_5_
  22.4 7.3 %collective-permute-done.5.refs_6_ = f32[16,2,8,128]{3,2,1,0:T(8,128)S(1)} collective-permute-done((f32[16,2,8,128]{3,2,1,0:T(8,128)S(1)}, f32[16,2,8,128]{3,2,1,0:T(8,128)S(1)}, u32[]{:S(2)}, u32[]{:S(2)}) %collective-permute-start.5) | collective-permute-done | bytes 131104 | tf_op jit(solution)/shard_map/ppermute | solution.py:597
  29.7 0.0 collective-permute-done.6.refs_7_
  29.7 0.3 boxes_in_place.1
  30.0 0.6 %collective-permute-start.9 = (f32[2,16,8,128]{3,2,1,0:T(8,128)S(1)}, f32[2,16,8,128]{3,2,1,0:T(8,128)S(1)}, u32[]{:S(2)}, u32[]{:S(2)}) collective-permute-start(f32[2,16,8,128]{3,2,1,0:T(8,128)S(1)} %get-tuple-element.38), channel_id=1, source_target_pairs={{0,16},{16,0},{1,17},{17,1},{2,18},{18,2},{3,19},{19,3},{4,20},{20... | collective-permute-start | bytes 393224 | tf_op jit(solution)/shard_map/ppermute | solution.py:610
  30.6 2.2 %collective-permute-start.7 = (f32[2,8,128]{2,1,0:T(8,128)S(1)}, f32[2,8,128]{2,1,0:T(8,128)S(1)}, u32[]{:S(2)}, u32[]{:S(2)}) collective-permute-start(f32[2,8,128]{2,1,0:T(8,128)S(1)} %get-tuple-element.36), channel_id=1, source_target_pairs={{1,2},{2,1},{3,0},{0,3},{5,6},{6,5},{7,4},{4,7},{9,10},{10,9},{11,... | collective-permute-start | bytes 24584 | tf_op jit(solution)/shard_map/ppermute | solution.py:614
  32.8 1.2 %collective-permute-start.8 = (f32[2,8,128]{2,1,0:T(8,128)S(1)}, f32[2,8,128]{2,1,0:T(8,128)S(1)}, u32[]{:S(2)}, u32[]{:S(2)}) collective-permute-start(f32[2,8,128]{2,1,0:T(8,128)S(1)} %get-tuple-element.37), channel_id=1, source_target_pairs={{0,1},{1,0},{2,3},{3,2},{4,5},{5,4},{6,7},{7,6},{8,9},{9,8},{10,11... | collective-permute-start | bytes 24584 | tf_op jit(solution)/shard_map/ppermute | solution.py:615
  34.0 1.4 %grid_from_boxes.1.grid = f32[4,16,16,128]{3,2,1,0:T(8,128)S(1)} custom-call(f32[65,2,8,128]{3,2,1,0:T(8,128)S(1)} %get-tuple-element.35.held), custom_call_target="tpu_custom_call" | custom-call | flops 4194304 | bytes 2097152 | tf_op jit(solution)/shard_map/grid_from_boxes/pallas_call | solution.py:224
  35.4 0.6 %collective-permute-done.7.odd_pairs = f32[2,8,128]{2,1,0:T(8,128)S(1)} collective-permute-done((f32[2,8,128]{2,1,0:T(8,128)S(1)}, f32[2,8,128]{2,1,0:T(8,128)S(1)}, u32[]{:S(2)}, u32[]{:S(2)}) %collective-permute-start.7) | collective-permute-done | bytes 8224 | tf_op jit(solution)/shard_map/ppermute | solution.py:614
  36.0 0.4 collective-permute-done.8.even_pairs
  36.5 0.0 collective-permute-done.9.refs_0_
  36.5 0.8 %faces_and_rows.1 = (f32[4,4,16,128]{3,2,1,0:T(8,128)S(1)}, f32[4,16,16,128]{3,2,1,0:T(8,128)S(1)}, f32[152,128]{1,0:T(8,128)S(1)}, f32[152,128]{1,0:T(8,128)S(1)}, f32[16,128]{1,0:T(8,128)S(1)}) custom-call(f32[4,16,16,128]{3,2,1,0:T(8,128)S(1)} %grid_from_boxes.1.grid, f32[2,8,128]{2,1,0:T(8,128)S(1)} %collective-permute-done.7.odd_pairs, ...), custom_call_target="tpu_custom_call" | custom-call | tf_op jit(solution)/shard_map/faces_and_rows/pallas_call | solution.py:311
  37.2 0.1 collective-permute-start.10
  37.3 0.5 %collective-permute-start.11 = (f32[152,128]{1,0:T(8,128)S(1)}, f32[152,128]{1,0:T(8,128)S(1)}, u32[]{:S(2)}, u32[]{:S(2)}) collective-permute-start(f32[152,128]{1,0:T(8,128)S(1)} %get-tuple-element.47), channel_id=1, source_target_pairs={{0,4},{4,8},{8,12},{12,0},{1,5},{5,9},{9,13},{13,1},{2,6},{6,10},{... | collective-permute-start | bytes 233480 | tf_op jit(solution)/shard_map/ppermute | solution.py:622
  37.8 1.5 %collective-permute-start.12 = (f32[16,128]{1,0:T(8,128)S(1)}, f32[16,128]{1,0:T(8,128)S(1)}, u32[]{:S(2)}, u32[]{:S(2)}) collective-permute-start(f32[16,128]{1,0:T(8,128)S(1)} %get-tuple-element.48), channel_id=1, source_target_pairs={{0,16},{16,0},{1,17},{17,1},{2,18},{18,2},{3,19},{19,3},{4,20},{20... | collective-permute-start | bytes 24584 | tf_op jit(solution)/shard_map/ppermute | solution.py:610
  39.3 1.5 %first_inside.1 = (f32[4,20,16,128]{3,2,1,0:T(8,128)S(1)}, f32[20,16,128]{2,1,0:T(8,128)S(1)}, f32[4,16,16,128]{3,2,1,0:T(8,128)S(1)}, f32[4,16,16,128]{3,2,1,0:T(8,128)S(1)}, f32[16,16,128]{2,1,0:T(8,128)S(1)}) custom-call(f32[4,16,16,128]{3,2,1,0:T(8,128)S(1)} %grid_from_boxes.1.grid, f32[4,4,16,128]{3,2,1,0:T(8,128)S(1)} %get-tuple-element.39.layers, ...), custom_call_target="tpu_custom_call" | custom-call | flops 4194304 | bytes 2097152 | tf_op jit(solution)/shard_map/first_inside/pallas_call | solution.py:418
  40.8 0.6 %collective-permute-done.12.refs_0_ = f32[16,128]{1,0:T(8,128)S(1)} collective-permute-done((f32[16,128]{1,0:T(8,128)S(1)}, f32[16,128]{1,0:T(8,128)S(1)}, u32[]{:S(2)}, u32[]{:S(2)}) %collective-permute-start.12) | collective-permute-done | bytes 8224 | tf_op jit(solution)/shard_map/ppermute | solution.py:610
  41.4 0.0 collective-permute-done.10.above
  41.4 0.5 %collective-permute-done.11.below = f32[152,128]{1,0:T(8,128)S(1)} collective-permute-done((f32[152,128]{1,0:T(8,128)S(1)}, f32[152,128]{1,0:T(8,128)S(1)}, u32[]{:S(2)}, u32[]{:S(2)}) %collective-permute-start.11) | collective-permute-done | bytes 77856 | tf_op jit(solution)/shard_map/ppermute | solution.py:622
  42.0 2.1 %last_sections.1 = f32[4,16,16,128]{3,2,1,0:T(8,128)} custom-call(f32[4,20,16,128]{3,2,1,0:T(8,128)S(1)} %get-tuple-element.41.wide, f32[20,16,128]{2,1,0:T(8,128)S(1)} %get-tuple-element.42.halves, f32[4,16,16,128]{3,2,1,0:T(8,128)S(1)} %get-tuple-element.43.first_in, f32[4,16,16,128]{3,2,1,0:T(8,128)S(1)} %get-tuple-element.44.beyond_in, ...), custom_call_target="tpu_custom_call" | custom-call | tf_op jit(solution)/shard_map/last_sections/pallas_call | solution.py:568
Async XLA Ops:
  1.4 8.1 %collective-permute-start = (f32[16,2,8,128]{3,2,1,0:T(8,128)S(1)}, f32[16,2,8,128]{3,2,1,0:T(8,128)S(1)}, u32[]{:S(2)}, u32[]{:S(2)}) collective-permute-start(f32[16,2,8,128]{3,2,1,0:T(8,128)S(1)} %get-tuple-element.28), channel_id=1, source_target_pairs={{0,1},{1,0},{2,3},{3,2},{16,17},{17,16},{18,19},{19,18},{4,5},{5,4... | collective-permute-start | bytes 393224 | tf_op jit(solution)/shard_map/ppermute | solution.py:597
  4.5 12.9 %collective-permute-start.1 = (f32[16,2,8,128]{3,2,1,0:T(8,128)S(1)}, f32[16,2,8,128]{3,2,1,0:T(8,128)S(1)}, u32[]{:S(2)}, u32[]{:S(2)}) collective-permute-start(f32[16,2,8,128]{3,2,1,0:T(8,128)S(1)} %get-tuple-element.29), channel_id=1, source_target_pairs={{0,2},{1,3},{2,0},{3,1},{16,18},{17,19},{18,16},{19,17},{4,6},{5,7... | collective-permute-start | bytes 393224 | tf_op jit(solution)/shard_map/ppermute | solution.py:597
  7.1 15.3 %collective-permute-start.2 = (f32[16,2,8,128]{3,2,1,0:T(8,128)S(1)}, f32[16,2,8,128]{3,2,1,0:T(8,128)S(1)}, u32[]{:S(2)}, u32[]{:S(2)}) collective-permute-start(f32[16,2,8,128]{3,2,1,0:T(8,128)S(1)} %get-tuple-element.30), channel_id=1, source_target_pairs={{0,3},{1,2},{2,1},{3,0},{16,19},{17,18},{18,17},{19,16},{4,7},{5,6... | collective-permute-start | bytes 393224 | tf_op jit(solution)/shard_map/ppermute | solution.py:597
  7.1 15.3 %collective-permute-start.3 = (f32[16,2,8,128]{3,2,1,0:T(8,128)S(1)}, f32[16,2,8,128]{3,2,1,0:T(8,128)S(1)}, u32[]{:S(2)}, u32[]{:S(2)}) collective-permute-start(f32[16,2,8,128]{3,2,1,0:T(8,128)S(1)} %get-tuple-element.31), channel_id=1, source_target_pairs={{0,16},{1,17},{2,18},{3,19},{16,0},{17,1},{18,2},{19,3},{4,20},{5,... | collective-permute-start | bytes 393224 | tf_op jit(solution)/shard_map/ppermute | solution.py:597
  8.8 13.6 %collective-permute-start.4 = (f32[16,2,8,128]{3,2,1,0:T(8,128)S(1)}, f32[16,2,8,128]{3,2,1,0:T(8,128)S(1)}, u32[]{:S(2)}, u32[]{:S(2)}) collective-permute-start(f32[16,2,8,128]{3,2,1,0:T(8,128)S(1)} %get-tuple-element.32), channel_id=1, source_target_pairs={{0,17},{1,16},{2,19},{3,18},{16,1},{17,0},{18,3},{19,2},{4,21},{5,... | collective-permute-start | bytes 393224 | tf_op jit(solution)/shard_map/ppermute | solution.py:597
  9.5 11.9 %copy-start = (s32[64]{0:T(128)S(1)}, s32[64]{0:T(128)}, u32[]{:S(2)}) copy-start(s32[64]{0:T(128)} %owner.1) | copy-start | bytes 772
  9.5 20.2 %collective-permute-start.5 = (f32[16,2,8,128]{3,2,1,0:T(8,128)S(1)}, f32[16,2,8,128]{3,2,1,0:T(8,128)S(1)}, u32[]{:S(2)}, u32[]{:S(2)}) collective-permute-start(f32[16,2,8,128]{3,2,1,0:T(8,128)S(1)} %get-tuple-element.33), channel_id=1, source_target_pairs={{0,18},{1,19},{2,16},{3,17},{16,2},{17,3},{18,0},{19,1},{4,22},{5,... | collective-permute-start | bytes 393224 | tf_op jit(solution)/shard_map/ppermute | solution.py:597
  17.4 12.3 %collective-permute-start.6 = (f32[16,2,8,128]{3,2,1,0:T(8,128)S(1)}, f32[16,2,8,128]{3,2,1,0:T(8,128)S(1)}, u32[]{:S(2)}, u32[]{:S(2)}) collective-permute-start(f32[16,2,8,128]{3,2,1,0:T(8,128)S(1)} %get-tuple-element.34), channel_id=1, source_target_pairs={{0,19},{1,18},{2,17},{3,16},{16,3},{17,2},{18,1},{19,0},{4,23},{5,... | collective-permute-start | bytes 393224 | tf_op jit(solution)/shard_map/ppermute | solution.py:597
  30.0 6.4 %collective-permute-start.9 = (f32[2,16,8,128]{3,2,1,0:T(8,128)S(1)}, f32[2,16,8,128]{3,2,1,0:T(8,128)S(1)}, u32[]{:S(2)}, u32[]{:S(2)}) collective-permute-start(f32[2,16,8,128]{3,2,1,0:T(8,128)S(1)} %get-tuple-element.38), channel_id=1, source_target_pairs={{0,16},{16,0},{1,17},{17,1},{2,18},{18,2},{3,19},{19,3},{4,20},{20... | collective-permute-start | bytes 393224 | tf_op jit(solution)/shard_map/ppermute | solution.py:610
  30.6 5.4 %collective-permute-start.7 = (f32[2,8,128]{2,1,0:T(8,128)S(1)}, f32[2,8,128]{2,1,0:T(8,128)S(1)}, u32[]{:S(2)}, u32[]{:S(2)}) collective-permute-start(f32[2,8,128]{2,1,0:T(8,128)S(1)} %get-tuple-element.36), channel_id=1, source_target_pairs={{1,2},{2,1},{3,0},{0,3},{5,6},{6,5},{7,4},{4,7},{9,10},{10,9},{11,... | collective-permute-start | bytes 24584 | tf_op jit(solution)/shard_map/ppermute | solution.py:614
  32.8 3.7 %collective-permute-start.8 = (f32[2,8,128]{2,1,0:T(8,128)S(1)}, f32[2,8,128]{2,1,0:T(8,128)S(1)}, u32[]{:S(2)}, u32[]{:S(2)}) collective-permute-start(f32[2,8,128]{2,1,0:T(8,128)S(1)} %get-tuple-element.37), channel_id=1, source_target_pairs={{0,1},{1,0},{2,3},{3,2},{4,5},{5,4},{6,7},{7,6},{8,9},{9,8},{10,11... | collective-permute-start | bytes 24584 | tf_op jit(solution)/shard_map/ppermute | solution.py:615
  37.2 4.2 %collective-permute-start.10 = (f32[152,128]{1,0:T(8,128)S(1)}, f32[152,128]{1,0:T(8,128)S(1)}, u32[]{:S(2)}, u32[]{:S(2)}) collective-permute-start(f32[152,128]{1,0:T(8,128)S(1)} %get-tuple-element.46), channel_id=1, source_target_pairs={{0,12},{4,0},{8,4},{12,8},{1,13},{5,1},{9,5},{13,9},{2,14},{6,2},{... | collective-permute-start | bytes 233480 | tf_op jit(solution)/shard_map/ppermute | solution.py:621
  37.3 4.7 %collective-permute-start.11 = (f32[152,128]{1,0:T(8,128)S(1)}, f32[152,128]{1,0:T(8,128)S(1)}, u32[]{:S(2)}, u32[]{:S(2)}) collective-permute-start(f32[152,128]{1,0:T(8,128)S(1)} %get-tuple-element.47), channel_id=1, source_target_pairs={{0,4},{4,8},{8,12},{12,0},{1,5},{5,9},{9,13},{13,1},{2,6},{6,10},{... | collective-permute-start | bytes 233480 | tf_op jit(solution)/shard_map/ppermute | solution.py:622
  37.8 3.7 %collective-permute-start.12 = (f32[16,128]{1,0:T(8,128)S(1)}, f32[16,128]{1,0:T(8,128)S(1)}, u32[]{:S(2)}, u32[]{:S(2)}) collective-permute-start(f32[16,128]{1,0:T(8,128)S(1)} %get-tuple-element.48), channel_id=1, source_target_pairs={{0,16},{16,0},{1,17},{17,1},{2,18},{18,2},{3,19},{19,3},{4,20},{20... | collective-permute-start | bytes 24584 | tf_op jit(solution)/shard_map/ppermute | solution.py:610

commit v10 on v9

--- a/solution.py
+++ b/solution.py
@@ -139,7 +139,7 @@
     return [((i + first) % count, ((i ^ 1) + first) % count) for i in range(count)]
 
 
-def boxes_in_place(arrived, table, boxes, capacity, split, joined):
+def boxes_in_place(arrived, order, table, boxes, capacity, split, joined):
     pieces = len(arrived)
     rows = table.shape[0] // pieces
     half = boxes // BRICK_X
@@ -151,7 +151,7 @@
         ins, refs = refs[:pieces], refs[pieces:]
         held, odd_pairs, even_pairs, *outs = refs
         odd = lax.axis_index("gz") & 1 != 0
-        for k, rows_in in enumerate(ins):
+        for k, rows_in in zip(order, ins):
             base = (group_place() ^ k) * capacity if split else 0
 
             def scatter(r, carry, rows_in=rows_in, base=base):
@@ -432,9 +432,13 @@
     )(grid, layers, beyond)
 
 
+PARTS = 4
+
+
 def last_sections(wide, halves, first, first_beyond, beyond, halves_beyond, above, below, sides):
     def kernel(wide, halves, first_in, beyond_in, beyond, halves_beyond, above, below, *refs):
-        ins, (out, edges, first, first_beyond, around, fs, fbs) = refs[: len(sides)], refs[len(sides) :]
+        ins, (out, *refs) = refs[: len(sides)], refs[len(sides) :]
+        edges, first, first_beyond, around, fs, fbs, result, sems = refs
         factors = [TIME_STEP * c for c in DIFFUSION]
         row = lax.broadcasted_iota(jnp.int32, (EDGE, LANES), 0)
 
@@ -557,10 +561,20 @@
             ]
             beside += z_beside(here, at(first_beyond, fbs, x))
             for f, v in enumerate(step(here[0], rates(*here, beside))):
-                out[f, x] = 0.5 * wide[f, x + HALO] + 0.5 * v
+                result[f, x] = 0.5 * wide[f, x + HALO] + 0.5 * v
             return carry
 
-        lax.fori_loop(0, NX, second, 0, unroll=4)
+        copies = []
+        for part in range(PARTS):
+            start = part * (NX // PARTS)
+            lax.fori_loop(start, start + NX // PARTS, second, 0, unroll=NX // PARTS)
+            layers = pl.ds(start, NX // PARTS)
+            copies.append(
+                pltpu.make_async_copy(result.at[:, layers], out.at[:, layers], sems.at[part])
+            )
+            copies[-1].start()
+        for copy in copies:
+            copy.wait()
 
     def scratch(*shape):
         return pltpu.VMEM(shape + (LANES,), jnp.float32)
@@ -569,7 +583,7 @@
         kernel,
         out_shape=jax.ShapeDtypeStruct((FIELDS, NX, NY, LANES), jnp.float32),
         in_specs=[VMEM] * (8 + len(sides)),
-        out_specs=VMEM,
+        out_specs=HBM,
         scratch_shapes=[
             scratch(FIELDS * NX * EDGE),
             scratch(FIELDS * NEAR_X * NY),
@@ -577,6 +591,8 @@
             scratch(FIELDS * NX * EDGE),
             scratch(NEAR_X, NY),
             scratch(NX, NY),
+            scratch(FIELDS, NX, NY),
+            pltpu.SemaphoreType.DMA((PARTS,)),
         ],
         compiler_params=ROOM,
         name="last_sections",
@@ -593,16 +609,20 @@
     departing = pack_boxes(old_fields, new_owner, group_size, capacity, split)
     table = position_table(old_owner, group_size, capacity)
     if split:
-        arrived = [departing[0]] + [
+        order = (3, 1, 2, 4, 6, 5, 7, 0)
+        arrived = [
             lax.ppermute(departing[k], ("gx", "gz"), [(i, i ^ k) for i in range(group_size)])
-            for k in range(1, group_size)
+            if k
+            else departing[k]
+            for k in order
         ]
     else:
+        order = [0]
         arrived = [
             lax.all_to_all(departing[0], ("gx", "gz"), split_axis=0, concat_axis=0, tiled=True)
         ]
     held, odd_pairs, even_pairs, *faces = boxes_in_place(
-        arrived, table, box_count, capacity, split, joined
+        arrived, order, table, box_count, capacity, split, joined
     )
 
     def along_x(sides):

time: 44.2 us -> 42.4 us (0.959)
  waiting for transfers between devices: 13.1 us -> 11.7 us
    ppermute x7, waiting for transfers between devices: 10.9 us -> 9.96 us  [body(): lax.ppermute(departing[k], ('gx', 'gz'), [(i, i ^ k) for i in range(group...]
    ppermute x7, starting transfers between devices: 16.4 us -> 15.6 us  [body(): lax.ppermute(departing[k], ('gx', 'gz'), [(i, i ^ k) for i in range(group...]
    ppermute x1, waiting for transfers between devices: 0.6 us -> 0.09 us  [body(): odd_pairs = lax.ppermute(odd_pairs, 'gz', pairs(along, 1))]
  transfers between devices with their start and end apart: 13 -> 13, of which waited for: 7 -> 6; matrix products, arithmetic and copies ran while one was open for 0% -> 0% of each run, Pallas kernels for 9% -> 9%
where the time goes in v10:
time: 42.4 us; the launch traced here: 42.2 us
  starting transfers between devices  22.2 us (52%)
  waiting for transfers between devices  11.7 us (28%)
  Pallas kernels  8.27 us (20%)
    ppermute x7, starting transfers between devices, body(): lax.ppermute(departing[k], ('gx', 'gz'), [(i, i ^ k) for i in range(group...  15.6 us
    ppermute x7, waiting for transfers between devices, body(): lax.ppermute(departing[k], ('gx', 'gz'), [(i, i ^ k) for i in range(group...  9.96 us
    ppermute x1, starting transfers between devices, body(): odd_pairs = lax.ppermute(odd_pairs, 'gz', pairs(along, 1))  2.31 us
    ppermute x2, starting transfers between devices, along_x(): return [lax.ppermute(sides[0], 'gx', ring(across, 1))]  2.07 us
    pallas_call x1, Pallas kernels, last_sections(): pl.pallas_call(kernel, out_shape=jax.ShapeDtypeStruct((FIELDS, NX, NY, LA...  1.95 us
    ppermute x1, starting transfers between devices, body(): even_pairs = lax.ppermute(even_pairs, 'gz', pairs(along, 0))  1.67 us
    pallas_call x1, Pallas kernels, first_inside(): pl.pallas_call(kernel, out_shape=[shape(FIELDS, WIDE_X), shape(WIDE_X), s...  1.5 us
    pallas_call x1, Pallas kernels, grid_from_boxes(): pl.pallas_call(kernel, out_shape=jax.ShapeDtypeStruct((FIELDS, NX, NY, LA...  1.38 us
  transfers between devices with their start and end apart: 13, of which 6 were waited for; matrix products, arithmetic and copies ran while one was open for 0% of the time, Pallas kernels for 9%

profile of v10, /device:TPU:0, one launch (start us, length us, event | category | flops | bytes accessed | tf_op | source)
XLA Modules:
  0.0 42.2 jit_solution(10306718146682519376)
XLA Ops:
  0.0 1.4 %pack_boxes.1 = (f32[16,2,8,128]{3,2,1,0:T(8,128)S(1)}, f32[16,2,8,128]{3,2,1,0:T(8,128)S(1)}, f32[16,2,8,128]{3,2,1,0:T(8,128)S(1)}, f32[16,2,8,128]{3,2,1,0:T(...) custom-call(s32[64]{0:T(128)} %owner_hbm.1, ...), custom_call_target="tpu_custom_call" | custom-call | tf_op jit(solution)/shard_map/pack_boxes/pallas_call | solution.py:82
  1.4 5.1 %collective-permute-start = (f32[16,2,8,128]{3,2,1,0:T(8,128)S(1)}, f32[16,2,8,128]{3,2,1,0:T(8,128)S(1)}, u32[]{:S(2)}, u32[]{:S(2)}) collective-permute-start(f32[16,2,8,128]{3,2,1,0:T(8,128)S(1)} %get-tuple-element.27), channel_id=1, source_target_pairs={{0,3},{1,2},{2,1},{3,0},{16,19},{17,18},{18,17},{19,16},{4,7},{5,6... | collective-permute-start | bytes 393224 | tf_op jit(solution)/shard_map/ppermute | solution.py:614
  6.5 0.0 collective-permute-start.1
  6.5 0.6 %collective-permute-start.2 = (f32[16,2,8,128]{3,2,1,0:T(8,128)S(1)}, f32[16,2,8,128]{3,2,1,0:T(8,128)S(1)}, u32[]{:S(2)}, u32[]{:S(2)}) collective-permute-start(f32[16,2,8,128]{3,2,1,0:T(8,128)S(1)} %get-tuple-element.29), channel_id=1, source_target_pairs={{0,2},{1,3},{2,0},{3,1},{16,18},{17,19},{18,16},{19,17},{4,6},{5,7... | collective-permute-start | bytes 393224 | tf_op jit(solution)/shard_map/ppermute | solution.py:614
  7.1 1.7 %collective-permute-start.3 = (f32[16,2,8,128]{3,2,1,0:T(8,128)S(1)}, f32[16,2,8,128]{3,2,1,0:T(8,128)S(1)}, u32[]{:S(2)}, u32[]{:S(2)}) collective-permute-start(f32[16,2,8,128]{3,2,1,0:T(8,128)S(1)} %get-tuple-element.30), channel_id=1, source_target_pairs={{0,16},{1,17},{2,18},{3,19},{16,0},{17,1},{18,2},{19,3},{4,20},{5,... | collective-permute-start | bytes 393224 | tf_op jit(solution)/shard_map/ppermute | solution.py:614
  8.8 2.1 %collective-permute-start.4 = (f32[16,2,8,128]{3,2,1,0:T(8,128)S(1)}, f32[16,2,8,128]{3,2,1,0:T(8,128)S(1)}, u32[]{:S(2)}, u32[]{:S(2)}) collective-permute-start(f32[16,2,8,128]{3,2,1,0:T(8,128)S(1)} %get-tuple-element.31), channel_id=1, source_target_pairs={{0,18},{1,19},{2,16},{3,17},{16,2},{17,3},{18,0},{19,1},{4,22},{5,... | collective-permute-start | bytes 393224 | tf_op jit(solution)/shard_map/ppermute | solution.py:614
  10.9 0.0 collective-permute-done.refs_0_
  10.9 0.0 copy-start
  10.9 4.6 %collective-permute-start.5 = (f32[16,2,8,128]{3,2,1,0:T(8,128)S(1)}, f32[16,2,8,128]{3,2,1,0:T(8,128)S(1)}, u32[]{:S(2)}, u32[]{:S(2)}) collective-permute-start(f32[16,2,8,128]{3,2,1,0:T(8,128)S(1)} %get-tuple-element.32), channel_id=1, source_target_pairs={{0,17},{1,16},{2,19},{3,18},{16,1},{17,0},{18,3},{19,2},{4,21},{5,... | collective-permute-start | bytes 393224 | tf_op jit(solution)/shard_map/ppermute | solution.py:614
  15.5 0.0 collective-permute-done.1.refs_1_
  15.5 1.5 %collective-permute-start.6 = (f32[16,2,8,128]{3,2,1,0:T(8,128)S(1)}, f32[16,2,8,128]{3,2,1,0:T(8,128)S(1)}, u32[]{:S(2)}, u32[]{:S(2)}) collective-permute-start(f32[16,2,8,128]{3,2,1,0:T(8,128)S(1)} %get-tuple-element.33), channel_id=1, source_target_pairs={{0,19},{1,18},{2,17},{3,16},{16,3},{17,2},{18,1},{19,0},{4,23},{5,... | collective-permute-start | bytes 393224 | tf_op jit(solution)/shard_map/ppermute | solution.py:614
  17.0 0.0 copy-done
  17.0 1.0 %position_table.1.table = s32[128]{0:T(128)S(4)} custom-call(s32[64]{0:T(128)S(1)} %copy-done), custom_call_target="tpu_custom_call" | custom-call | bytes 4194304 | tf_op jit(solution)/shard_map/position_table/pallas_call | solution.py:105
  18.0 3.9 %collective-permute-done.2.refs_2_ = f32[16,2,8,128]{3,2,1,0:T(8,128)S(1)} collective-permute-done((f32[16,2,8,128]{3,2,1,0:T(8,128)S(1)}, f32[16,2,8,128]{3,2,1,0:T(8,128)S(1)}, u32[]{:S(2)}, u32[]{:S(2)}) %collective-permute-start.2) | collective-permute-done | bytes 131104 | tf_op jit(solution)/shard_map/ppermute | solution.py:614
  21.8 0.0 collective-permute-done.3.refs_3_
  21.8 6.1 %collective-permute-done.4.refs_4_ = f32[16,2,8,128]{3,2,1,0:T(8,128)S(1)} collective-permute-done((f32[16,2,8,128]{3,2,1,0:T(8,128)S(1)}, f32[16,2,8,128]{3,2,1,0:T(8,128)S(1)}, u32[]{:S(2)}, u32[]{:S(2)}) %collective-permute-start.4) | collective-permute-done | bytes 131104 | tf_op jit(solution)/shard_map/ppermute | solution.py:614
  27.9 0.0 collective-permute-done.5.refs_5_
  27.9 0.0 collective-permute-done.6.refs_6_
  27.9 0.3 boxes_in_place.1
  28.2 0.6 %collective-permute-start.9 = (f32[2,16,8,128]{3,2,1,0:T(8,128)S(1)}, f32[2,16,8,128]{3,2,1,0:T(8,128)S(1)}, u32[]{:S(2)}, u32[]{:S(2)}) collective-permute-start(f32[2,16,8,128]{3,2,1,0:T(8,128)S(1)} %get-tuple-element.38), channel_id=1, source_target_pairs={{0,16},{16,0},{1,17},{17,1},{2,18},{18,2},{3,19},{19,3},{4,20},{20... | collective-permute-start | bytes 393224 | tf_op jit(solution)/shard_map/ppermute | solution.py:630
  28.8 2.3 %collective-permute-start.7 = (f32[2,8,128]{2,1,0:T(8,128)S(1)}, f32[2,8,128]{2,1,0:T(8,128)S(1)}, u32[]{:S(2)}, u32[]{:S(2)}) collective-permute-start(f32[2,8,128]{2,1,0:T(8,128)S(1)} %get-tuple-element.36), channel_id=1, source_target_pairs={{1,2},{2,1},{3,0},{0,3},{5,6},{6,5},{7,4},{4,7},{9,10},{10,9},{11,... | collective-permute-start | bytes 24584 | tf_op jit(solution)/shard_map/ppermute | solution.py:634
  31.1 1.7 %collective-permute-start.8 = (f32[2,8,128]{2,1,0:T(8,128)S(1)}, f32[2,8,128]{2,1,0:T(8,128)S(1)}, u32[]{:S(2)}, u32[]{:S(2)}) collective-permute-start(f32[2,8,128]{2,1,0:T(8,128)S(1)} %get-tuple-element.37), channel_id=1, source_target_pairs={{0,1},{1,0},{2,3},{3,2},{4,5},{5,4},{6,7},{7,6},{8,9},{9,8},{10,11... | collective-permute-start | bytes 24584 | tf_op jit(solution)/shard_map/ppermute | solution.py:635
  32.8 1.4 %grid_from_boxes.1.grid = f32[4,16,16,128]{3,2,1,0:T(8,128)S(1)} custom-call(f32[65,2,8,128]{3,2,1,0:T(8,128)S(1)} %get-tuple-element.35.held), custom_call_target="tpu_custom_call" | custom-call | flops 4194304 | bytes 2097152 | tf_op jit(solution)/shard_map/grid_from_boxes/pallas_call | solution.py:224
  34.2 0.1 collective-permute-done.7.odd_pairs
  34.2 0.5 %collective-permute-done.8.even_pairs = f32[2,8,128]{2,1,0:T(8,128)S(1)} collective-permute-done((f32[2,8,128]{2,1,0:T(8,128)S(1)}, f32[2,8,128]{2,1,0:T(8,128)S(1)}, u32[]{:S(2)}, u32[]{:S(2)}) %collective-permute-start.8) | collective-permute-done | bytes 8224 | tf_op jit(solution)/shard_map/ppermute | solution.py:635
  34.8 0.0 collective-permute-done.9.refs_0_
  34.8 0.8 %faces_and_rows.1 = (f32[4,4,16,128]{3,2,1,0:T(8,128)S(1)}, f32[4,16,16,128]{3,2,1,0:T(8,128)S(1)}, f32[152,128]{1,0:T(8,128)S(1)}, f32[152,128]{1,0:T(8,128)S(1)}, f32[16,128]{1,0:T(8,128)S(1)}) custom-call(f32[4,16,16,128]{3,2,1,0:T(8,128)S(1)} %grid_from_boxes.1.grid, f32[2,8,128]{2,1,0:T(8,128)S(1)} %collective-permute-done.7.odd_pairs, ...), custom_call_target="tpu_custom_call" | custom-call | tf_op jit(solution)/shard_map/faces_and_rows/pallas_call | solution.py:311
  35.5 0.1 collective-permute-start.10
  35.6 0.5 %collective-permute-start.11 = (f32[152,128]{1,0:T(8,128)S(1)}, f32[152,128]{1,0:T(8,128)S(1)}, u32[]{:S(2)}, u32[]{:S(2)}) collective-permute-start(f32[152,128]{1,0:T(8,128)S(1)} %get-tuple-element.47), channel_id=1, source_target_pairs={{0,4},{4,8},{8,12},{12,0},{1,5},{5,9},{9,13},{13,1},{2,6},{6,10},{... | collective-permute-start | bytes 233480 | tf_op jit(solution)/shard_map/ppermute | solution.py:642
  36.1 1.5 %collective-permute-start.12 = (f32[16,128]{1,0:T(8,128)S(1)}, f32[16,128]{1,0:T(8,128)S(1)}, u32[]{:S(2)}, u32[]{:S(2)}) collective-permute-start(f32[16,128]{1,0:T(8,128)S(1)} %get-tuple-element.48), channel_id=1, source_target_pairs={{0,16},{16,0},{1,17},{17,1},{2,18},{18,2},{3,19},{19,3},{4,20},{20... | collective-permute-start | bytes 24584 | tf_op jit(solution)/shard_map/ppermute | solution.py:630
  37.6 1.5 %first_inside.1 = (f32[4,20,16,128]{3,2,1,0:T(8,128)S(1)}, f32[20,16,128]{2,1,0:T(8,128)S(1)}, f32[4,16,16,128]{3,2,1,0:T(8,128)S(1)}, f32[4,16,16,128]{3,2,1,0:T(8,128)S(1)}, f32[16,16,128]{2,1,0:T(8,128)S(1)}) custom-call(f32[4,16,16,128]{3,2,1,0:T(8,128)S(1)} %grid_from_boxes.1.grid, f32[4,4,16,128]{3,2,1,0:T(8,128)S(1)} %get-tuple-element.39.layers, ...), custom_call_target="tpu_custom_call" | custom-call | flops 4194304 | bytes 2097152 | tf_op jit(solution)/shard_map/first_inside/pallas_call | solution.py:418
  39.1 0.6 %collective-permute-done.12.refs_0_ = f32[16,128]{1,0:T(8,128)S(1)} collective-permute-done((f32[16,128]{1,0:T(8,128)S(1)}, f32[16,128]{1,0:T(8,128)S(1)}, u32[]{:S(2)}, u32[]{:S(2)}) %collective-permute-start.12) | collective-permute-done | bytes 8224 | tf_op jit(solution)/shard_map/ppermute | solution.py:630
  39.7 0.0 collective-permute-done.10.above
  39.7 0.5 %collective-permute-done.11.below = f32[152,128]{1,0:T(8,128)S(1)} collective-permute-done((f32[152,128]{1,0:T(8,128)S(1)}, f32[152,128]{1,0:T(8,128)S(1)}, u32[]{:S(2)}, u32[]{:S(2)}) %collective-permute-start.11) | collective-permute-done | bytes 77856 | tf_op jit(solution)/shard_map/ppermute | solution.py:642
  40.3 2.0 %last_sections.1 = f32[4,16,16,128]{3,2,1,0:T(8,128)} custom-call(f32[4,20,16,128]{3,2,1,0:T(8,128)S(1)} %get-tuple-element.41.wide, f32[20,16,128]{2,1,0:T(8,128)S(1)} %get-tuple-element.42.halves, f32[4,16,16,128]{3,2,1,0:T(8,128)S(1)} %get-tuple-element.43.first_in, f32[4,16,16,128]{3,2,1,0:T(8,128)S(1)} %get-tuple-element.44.beyond_in, ...), custom_call_target="tpu_custom_call" | custom-call | tf_op jit(solution)/shard_map/last_sections/pallas_call | solution.py:582
Async XLA Ops:
  1.4 9.5 %collective-permute-start = (f32[16,2,8,128]{3,2,1,0:T(8,128)S(1)}, f32[16,2,8,128]{3,2,1,0:T(8,128)S(1)}, u32[]{:S(2)}, u32[]{:S(2)}) collective-permute-start(f32[16,2,8,128]{3,2,1,0:T(8,128)S(1)} %get-tuple-element.27), channel_id=1, source_target_pairs={{0,3},{1,2},{2,1},{3,0},{16,19},{17,18},{18,17},{19,16},{4,7},{5,6... | collective-permute-start | bytes 393224 | tf_op jit(solution)/shard_map/ppermute | solution.py:614
  6.5 9.0 %collective-permute-start.1 = (f32[16,2,8,128]{3,2,1,0:T(8,128)S(1)}, f32[16,2,8,128]{3,2,1,0:T(8,128)S(1)}, u32[]{:S(2)}, u32[]{:S(2)}) collective-permute-start(f32[16,2,8,128]{3,2,1,0:T(8,128)S(1)} %get-tuple-element.28), channel_id=1, source_target_pairs={{0,1},{1,0},{2,3},{3,2},{16,17},{17,16},{18,19},{19,18},{4,5},{5,4... | collective-permute-start | bytes 393224 | tf_op jit(solution)/shard_map/ppermute | solution.py:614
  6.5 15.3 %collective-permute-start.2 = (f32[16,2,8,128]{3,2,1,0:T(8,128)S(1)}, f32[16,2,8,128]{3,2,1,0:T(8,128)S(1)}, u32[]{:S(2)}, u32[]{:S(2)}) collective-permute-start(f32[16,2,8,128]{3,2,1,0:T(8,128)S(1)} %get-tuple-element.29), channel_id=1, source_target_pairs={{0,2},{1,3},{2,0},{3,1},{16,18},{17,19},{18,16},{19,17},{4,6},{5,7... | collective-permute-start | bytes 393224 | tf_op jit(solution)/shard_map/ppermute | solution.py:614
  7.1 14.7 %collective-permute-start.3 = (f32[16,2,8,128]{3,2,1,0:T(8,128)S(1)}, f32[16,2,8,128]{3,2,1,0:T(8,128)S(1)}, u32[]{:S(2)}, u32[]{:S(2)}) collective-permute-start(f32[16,2,8,128]{3,2,1,0:T(8,128)S(1)} %get-tuple-element.30), channel_id=1, source_target_pairs={{0,16},{1,17},{2,18},{3,19},{16,0},{17,1},{18,2},{19,3},{4,20},{5,... | collective-permute-start | bytes 393224 | tf_op jit(solution)/shard_map/ppermute | solution.py:614
  8.8 19.1 %collective-permute-start.4 = (f32[16,2,8,128]{3,2,1,0:T(8,128)S(1)}, f32[16,2,8,128]{3,2,1,0:T(8,128)S(1)}, u32[]{:S(2)}, u32[]{:S(2)}) collective-permute-start(f32[16,2,8,128]{3,2,1,0:T(8,128)S(1)} %get-tuple-element.31), channel_id=1, source_target_pairs={{0,18},{1,19},{2,16},{3,17},{16,2},{17,3},{18,0},{19,1},{4,22},{5,... | collective-permute-start | bytes 393224 | tf_op jit(solution)/shard_map/ppermute | solution.py:614
  10.9 6.1 %copy-start = (s32[64]{0:T(128)S(1)}, s32[64]{0:T(128)}, u32[]{:S(2)}) copy-start(s32[64]{0:T(128)} %owner.1) | copy-start | bytes 772
  10.9 17.0 %collective-permute-start.5 = (f32[16,2,8,128]{3,2,1,0:T(8,128)S(1)}, f32[16,2,8,128]{3,2,1,0:T(8,128)S(1)}, u32[]{:S(2)}, u32[]{:S(2)}) collective-permute-start(f32[16,2,8,128]{3,2,1,0:T(8,128)S(1)} %get-tuple-element.32), channel_id=1, source_target_pairs={{0,17},{1,16},{2,19},{3,18},{16,1},{17,0},{18,3},{19,2},{4,21},{5,... | collective-permute-start | bytes 393224 | tf_op jit(solution)/shard_map/ppermute | solution.py:614
  15.5 12.4 %collective-permute-start.6 = (f32[16,2,8,128]{3,2,1,0:T(8,128)S(1)}, f32[16,2,8,128]{3,2,1,0:T(8,128)S(1)}, u32[]{:S(2)}, u32[]{:S(2)}) collective-permute-start(f32[16,2,8,128]{3,2,1,0:T(8,128)S(1)} %get-tuple-element.33), channel_id=1, source_target_pairs={{0,19},{1,18},{2,17},{3,16},{16,3},{17,2},{18,1},{19,0},{4,23},{5,... | collective-permute-start | bytes 393224 | tf_op jit(solution)/shard_map/ppermute | solution.py:614
  28.2 6.5 %collective-permute-start.9 = (f32[2,16,8,128]{3,2,1,0:T(8,128)S(1)}, f32[2,16,8,128]{3,2,1,0:T(8,128)S(1)}, u32[]{:S(2)}, u32[]{:S(2)}) collective-permute-start(f32[2,16,8,128]{3,2,1,0:T(8,128)S(1)} %get-tuple-element.38), channel_id=1, source_target_pairs={{0,16},{16,0},{1,17},{17,1},{2,18},{18,2},{3,19},{19,3},{4,20},{20... | collective-permute-start | bytes 393224 | tf_op jit(solution)/shard_map/ppermute | solution.py:630
  28.8 5.4 %collective-permute-start.7 = (f32[2,8,128]{2,1,0:T(8,128)S(1)}, f32[2,8,128]{2,1,0:T(8,128)S(1)}, u32[]{:S(2)}, u32[]{:S(2)}) collective-permute-start(f32[2,8,128]{2,1,0:T(8,128)S(1)} %get-tuple-element.36), channel_id=1, source_target_pairs={{1,2},{2,1},{3,0},{0,3},{5,6},{6,5},{7,4},{4,7},{9,10},{10,9},{11,... | collective-permute-start | bytes 24584 | tf_op jit(solution)/shard_map/ppermute | solution.py:634
  31.1 3.7 %collective-permute-start.8 = (f32[2,8,128]{2,1,0:T(8,128)S(1)}, f32[2,8,128]{2,1,0:T(8,128)S(1)}, u32[]{:S(2)}, u32[]{:S(2)}) collective-permute-start(f32[2,8,128]{2,1,0:T(8,128)S(1)} %get-tuple-element.37), channel_id=1, source_target_pairs={{0,1},{1,0},{2,3},{3,2},{4,5},{5,4},{6,7},{7,6},{8,9},{9,8},{10,11... | collective-permute-start | bytes 24584 | tf_op jit(solution)/shard_map/ppermute | solution.py:635
  35.5 4.2 %collective-permute-start.10 = (f32[152,128]{1,0:T(8,128)S(1)}, f32[152,128]{1,0:T(8,128)S(1)}, u32[]{:S(2)}, u32[]{:S(2)}) collective-permute-start(f32[152,128]{1,0:T(8,128)S(1)} %get-tuple-element.46), channel_id=1, source_target_pairs={{0,12},{4,0},{8,4},{12,8},{1,13},{5,1},{9,5},{13,9},{2,14},{6,2},{... | collective-permute-start | bytes 233480 | tf_op jit(solution)/shard_map/ppermute | solution.py:641
  35.6 4.7 %collective-permute-start.11 = (f32[152,128]{1,0:T(8,128)S(1)}, f32[152,128]{1,0:T(8,128)S(1)}, u32[]{:S(2)}, u32[]{:S(2)}) collective-permute-start(f32[152,128]{1,0:T(8,128)S(1)} %get-tuple-element.47), channel_id=1, source_target_pairs={{0,4},{4,8},{8,12},{12,0},{1,5},{5,9},{9,13},{13,1},{2,6},{6,10},{... | collective-permute-start | bytes 233480 | tf_op jit(solution)/shard_map/ppermute | solution.py:642
  36.1 3.7 %collective-permute-start.12 = (f32[16,128]{1,0:T(8,128)S(1)}, f32[16,128]{1,0:T(8,128)S(1)}, u32[]{:S(2)}, u32[]{:S(2)}) collective-permute-start(f32[16,128]{1,0:T(8,128)S(1)} %get-tuple-element.48), channel_id=1, source_target_pairs={{0,16},{16,0},{1,17},{17,1},{2,18},{18,2},{3,19},{19,3},{4,20},{20... | collective-permute-start | bytes 24584 | tf_op jit(solution)/shard_map/ppermute | solution.py:630

commit v11 on v10

--- a/solution.py
+++ b/solution.py
@@ -241,6 +241,21 @@
     return (f * NEAR_X + x) * HALO
 
 
+def beyond_ends(ends, bx, by, half, r):
+    group, n = divmod((bx * BRICK_Y + by) * 2 + half, 4)
+    lane = lax.broadcasted_iota(jnp.int32, (EDGE, LANES), 1)
+    first = EDGE * r + HALO * n
+    return jnp.where(
+        lane < LANES // 2,
+        pltpu.roll(ends[0, group], (LANES - first) % LANES, 1),
+        pltpu.roll(ends[1, group], (2 * LANES - HALO - first) % LANES, 1),
+    )
+
+
+def edge_place(bx, half, i):
+    return (bx * 2 + half) * 2 + i
+
+
 def side_place(side, f):
     return side * FIELDS + f
 
@@ -250,8 +265,8 @@
 
     def kernel(grid, odd_pairs, even_pairs, *refs):
         ins, refs = refs[: len(faces)], refs[len(faces) :]
-        (layers, beyond, low, high), refs = refs[:4], refs[4:]
-        outs, (turned, ends) = refs[: len(sides)], refs[len(sides) :]
+        (layers, ends, low, high), refs = refs[:4], refs[4:]
+        outs, (turned,) = refs[: len(sides)], refs[len(sides) :]
         odd = lax.axis_index("gz") & 1
         ends[odd] = even_pairs[...]
         ends[1 - odd] = odd_pairs[...]
@@ -262,45 +277,37 @@
                 layers[f, first + i, pl.ds(by * EDGE, EDGE), :] = rows
 
             lay_out(swap_boxes([face[bz] for bz in range(BRICK_Z)]), turned, store)
-        lane = lax.broadcasted_iota(jnp.int32, (EDGE, LANES), 1)
-        for bx in range(BRICK_X):
-            for by in range(BRICK_Y):
-                for half in range(TILES // 2):
-                    group, n = divmod((bx * BRICK_Y + by) * 2 + half, 4)
-                    after, before = ends[0, group], ends[1, group]
-                    columns = [
-                        jnp.where(
-                            lane < LANES // 2,
-                            pltpu.roll(after, (LANES - EDGE * r - HALO * n) % LANES, 1),
-                            pltpu.roll(before, (2 * LANES - HALO - EDGE * r - HALO * n) % LANES, 1),
-                        )
-                        for r in range(16)
-                    ]
-
-                    def store(t, i, f, rows, x=bx * EDGE + half * 4, by=by):
-                        beyond[f, x + t * 2 + i, pl.ds(by * EDGE, EDGE), :] = rows
-
-                    lay_out(columns, turned, store)
         for f in range(FIELDS):
             for x in range(NEAR_X):
                 cells = layers.at[f, 2 if x else 1] if x % (NX + 1) == 0 else grid.at[f, x - 1]
                 low[pl.ds(row_of(f, x), HALO), :] = cells[pl.ds(0, HALO), :]
                 high[pl.ds(row_of(f, x), HALO), :] = cells[pl.ds(NY - HALO, HALO), :]
-        pair = lane // 2
-        for first, out in ((0, low), (NY - EDGE, high)):
+        lane = lax.broadcasted_iota(jnp.int32, (EDGE, LANES), 1)
+        for by, j, out in ((0, 0, low), (1, EDGE - 1, high)):
             edge = jnp.zeros((EDGE, LANES), jnp.float32)
-            for f in range(FIELDS):
-                for x in range(NX):
-                    place = f * NX + x
-                    moved = pltpu.roll(beyond[f, x, pl.ds(first, EDGE), :], 2 * place + 1, 1)
-                    edge = jnp.where(pair == place, moved, edge)
+            for bx in range(BRICK_X):
+                for half in range(TILES // 2):
+                    group, n = divmod((bx * BRICK_Y + by) * 2 + half, 4)
+                    for i in range(2):
+                        place = 2 * edge_place(bx, half, i)
+                        lane_in = EDGE * (i * EDGE + j) + HALO * n
+                        after = pltpu.roll(ends[0, group], (place + 1 - lane_in) % LANES, 1)
+                        before = pltpu.roll(ends[1, group], (place - 1 - lane_in) % LANES, 1)
+                        edge = jnp.where(lane == place, before, jnp.where(lane == place + 1, after, edge))
             out[pl.ds(ROWS, EDGE), :] = edge
         pair = lax.broadcasted_iota(jnp.int32, (NY, LANES), 1) // 2
         edges = [jnp.zeros((NY, LANES), jnp.float32)] * 2
         for side in range(2):
+            cells = [[], [], [], []]
+            for by in range(BRICK_Y):
+                for j in range(EDGE):
+                    turned[pl.ds(j * EDGE, EDGE), :] = beyond_ends(ends, side, by, side, side * EDGE + j)
+                for f in range(FIELDS):
+                    cells[f].append(turned[pl.ds(side * FIELDS + f, EDGE, stride=EDGE), :])
             for f in range(FIELDS):
-                moved = pltpu.roll(beyond[f, side * (NX - 1)], 2 * side_place(side, f) + 1, 1)
-                edges[side] = jnp.where(pair == side_place(side, f), moved, edges[side])
+                place = side_place(side, f)
+                moved = pltpu.roll(jnp.concatenate(cells[f], 0), 2 * place + 1, 1)
+                edges[side] = jnp.where(pair == place, moved, edges[side])
         if joined:
             outs[0][...] = jnp.where(pair < FIELDS, edges[0], edges[1])
         else:
@@ -312,17 +319,14 @@
         kernel,
         out_shape=[
             jax.ShapeDtypeStruct((FIELDS, 2 * HALO, NY, LANES), jnp.float32),
-            jax.ShapeDtypeStruct((FIELDS, NX, NY, LANES), jnp.float32),
+            jax.ShapeDtypeStruct((2, 2, 2 * FIELDS, LANES), jnp.float32),
             rows,
             rows,
         ]
         + sides,
         in_specs=[VMEM] * (3 + len(faces)),
         out_specs=[VMEM] * (4 + len(sides)),
-        scratch_shapes=[
-            pltpu.VMEM((LANES, LANES), jnp.float32),
-            pltpu.VMEM((2, 2, 2 * FIELDS, LANES), jnp.float32),
-        ],
+        scratch_shapes=[pltpu.VMEM((LANES, LANES), jnp.float32)],
         compiler_params=ROOM,
         name="faces_and_rows",
     )(grid, odd_pairs, even_pairs, *faces)
@@ -375,8 +379,18 @@
     return [each(after, cells), each(before, cells)]
 
 
-def first_inside(grid, layers, beyond):
-    def kernel(grid, layers, beyond, wide, halves, first, first_beyond, halves_beyond):
+def first_inside(grid, layers, ends):
+    def kernel(
+        grid, layers, ends, wide, halves, beyond, first, first_beyond, halves_beyond, turned
+    ):
+        for bx in range(BRICK_X):
+            for by in range(BRICK_Y):
+                for half in range(TILES // 2):
+
+                    def store(t, i, f, rows, x=bx * EDGE + half * 4, by=by):
+                        beyond[f, x + t * 2 + i, pl.ds(by * EDGE, EDGE), :] = rows
+
+                    lay_out([beyond_ends(ends, bx, by, half, r) for r in range(16)], turned, store)
         for f in range(FIELDS):
             for x in range(HALO):
                 wide[f, x] = layers[f, x]
@@ -422,14 +436,16 @@
             shape(WIDE_X),
             shape(FIELDS, NX),
             shape(FIELDS, NX),
+            shape(FIELDS, NX),
             shape(NX),
         ],
         in_specs=[VMEM] * 3,
-        out_specs=[VMEM] * 5,
+        out_specs=[VMEM] * 6,
+        scratch_shapes=[pltpu.VMEM((LANES, LANES), jnp.float32)],
         compiler_params=ROOM,
         cost_estimate=pl.CostEstimate(flops=2**22, bytes_accessed=2**21, transcendentals=0),
         name="first_inside",
-    )(grid, layers, beyond)
+    )(grid, layers, ends)
 
 
 PARTS = 4
@@ -449,16 +465,16 @@
             ]
             return fields, half_conductance(fields[0])
 
-        edge = jnp.where(
-            row < EDGE // 2,
-            pltpu.roll(below[pl.ds(ROWS, EDGE), :], 1, 0),
-            pltpu.roll(above[pl.ds(ROWS, EDGE), :], EDGE - 1, 0),
-        )
-        for f in range(FIELDS):
-            for x in range(NX):
-                edges[pl.ds((f * NX + x) * EDGE, EDGE), :] = pltpu.roll(
-                    edge, LANES - 1 - 2 * (f * NX + x), 1
-                )
+        for sent_edge, at_row in ((below, 0), (above, EDGE - 1)):
+            edge = sent_edge[pl.ds(ROWS, EDGE), :]
+            for bx in range(BRICK_X):
+                for half in range(TILES // 2):
+                    for i in range(2):
+                        tile = pltpu.roll(edge, LANES - 1 - 2 * edge_place(bx, half, i), 1)
+                        for t in range(2):
+                            x = bx * EDGE + half * 4 + t * 2 + i
+                            rows = pl.ds(x * EDGE + at_row, FIELDS, stride=NX * EDGE)
+                            edges[rows, :] = tile[t * FIELDS :][:FIELDS]
 
         def at(ref, s, x):
             return [ref[f, x] for f in range(FIELDS)], s[x]
@@ -634,14 +650,14 @@
     odd_pairs = lax.ppermute(odd_pairs, "gz", pairs(along, 1))
     even_pairs = lax.ppermute(even_pairs, "gz", pairs(along, 0))
     grid = grid_from_boxes(held)
-    layers, beyond, low, high, *sides = faces_and_rows(
+    layers, ends, low, high, *sides = faces_and_rows(
         grid, faces, odd_pairs, even_pairs, joined
     )
     rows = lax.axis_size("gy")
     above = lax.ppermute(low, "gy", ring(rows, -1))
     below = lax.ppermute(high, "gy", ring(rows, 1))
     sides = along_x(sides)
-    wide, halves, first, first_beyond, halves_beyond = first_inside(grid, layers, beyond)
+    wide, halves, beyond, first, first_beyond, halves_beyond = first_inside(grid, layers, ends)
     return last_sections(
         wide, halves, first, first_beyond, beyond, halves_beyond, above, below, sides
     )

time: 42.4 us -> 42.1 us (level)
  transfers between devices with their start and end apart: 13 -> 13, of which waited for: 6 -> 6; matrix products, arithmetic and copies ran while one was open for 0% -> 0% of each run, Pallas kernels for 9% -> 10%
where the time goes in v11:
time: 42.1 us; the launch traced here: 41.9 us
  starting transfers between devices  22.2 us (53%)
  waiting for transfers between devices  11.3 us (27%)
  Pallas kernels  8.39 us (20%)
    ppermute x7, starting transfers between devices, body(): lax.ppermute(departing[k], ('gx', 'gz'), [(i, i ^ k) for i in range(group...  15.6 us
    ppermute x7, waiting for transfers between devices, body(): lax.ppermute(departing[k], ('gx', 'gz'), [(i, i ^ k) for i in range(group...  9.96 us
    ppermute x1, starting transfers between devices, body(): odd_pairs = lax.ppermute(odd_pairs, 'gz', pairs(along, 1))  2.31 us
    ppermute x2, starting transfers between devices, along_x(): return [lax.ppermute(sides[0], 'gx', ring(across, 1))]  2.07 us
    pallas_call x1, Pallas kernels, last_sections(): pl.pallas_call(kernel, out_shape=jax.ShapeDtypeStruct((FIELDS, NX, NY, LA...  1.97 us
    pallas_call x1, Pallas kernels, first_inside(): pl.pallas_call(kernel, out_shape=[shape(FIELDS, WIDE_X), shape(WIDE_X), s...  1.91 us
    ppermute x1, starting transfers between devices, body(): even_pairs = lax.ppermute(even_pairs, 'gz', pairs(along, 0))  1.67 us
    pallas_call x1, Pallas kernels, grid_from_boxes(): pl.pallas_call(kernel, out_shape=jax.ShapeDtypeStruct((FIELDS, NX, NY, LA...  1.38 us
  transfers between devices with their start and end apart: 13, of which 6 were waited for; matrix products, arithmetic and copies ran while one was open for 0% of the time, Pallas kernels for 10%

profile of v11, /device:TPU:0, one launch (start us, length us, event | category | flops | bytes accessed | tf_op | source)
XLA Modules:
  0.0 41.9 jit_solution(6177112835829654186)
XLA Ops:
  0.0 1.4 %pack_boxes.1 = (f32[16,2,8,128]{3,2,1,0:T(8,128)S(1)}, f32[16,2,8,128]{3,2,1,0:T(8,128)S(1)}, f32[16,2,8,128]{3,2,1,0:T(8,128)S(1)}, f32[16,2,8,128]{3,2,1,0:T(...) custom-call(s32[64]{0:T(128)} %owner_hbm.1, ...), custom_call_target="tpu_custom_call" | custom-call | tf_op jit(solution)/shard_map/pack_boxes/pallas_call | solution.py:82
  1.4 5.1 %collective-permute-start = (f32[16,2,8,128]{3,2,1,0:T(8,128)S(1)}, f32[16,2,8,128]{3,2,1,0:T(8,128)S(1)}, u32[]{:S(2)}, u32[]{:S(2)}) collective-permute-start(f32[16,2,8,128]{3,2,1,0:T(8,128)S(1)} %get-tuple-element.28), channel_id=1, source_target_pairs={{0,3},{1,2},{2,1},{3,0},{16,19},{17,18},{18,17},{19,16},{4,7},{5,6... | collective-permute-start | bytes 393224 | tf_op jit(solution)/shard_map/ppermute | solution.py:630
  6.5 0.0 collective-permute-start.1
  6.5 0.6 %collective-permute-start.2 = (f32[16,2,8,128]{3,2,1,0:T(8,128)S(1)}, f32[16,2,8,128]{3,2,1,0:T(8,128)S(1)}, u32[]{:S(2)}, u32[]{:S(2)}) collective-permute-start(f32[16,2,8,128]{3,2,1,0:T(8,128)S(1)} %get-tuple-element.30), channel_id=1, source_target_pairs={{0,2},{1,3},{2,0},{3,1},{16,18},{17,19},{18,16},{19,17},{4,6},{5,7... | collective-permute-start | bytes 393224 | tf_op jit(solution)/shard_map/ppermute | solution.py:630
  7.1 1.7 %collective-permute-start.3 = (f32[16,2,8,128]{3,2,1,0:T(8,128)S(1)}, f32[16,2,8,128]{3,2,1,0:T(8,128)S(1)}, u32[]{:S(2)}, u32[]{:S(2)}) collective-permute-start(f32[16,2,8,128]{3,2,1,0:T(8,128)S(1)} %get-tuple-element.31), channel_id=1, source_target_pairs={{0,16},{1,17},{2,18},{3,19},{16,0},{17,1},{18,2},{19,3},{4,20},{5,... | collective-permute-start | bytes 393224 | tf_op jit(solution)/shard_map/ppermute | solution.py:630
  8.8 2.1 %collective-permute-start.4 = (f32[16,2,8,128]{3,2,1,0:T(8,128)S(1)}, f32[16,2,8,128]{3,2,1,0:T(8,128)S(1)}, u32[]{:S(2)}, u32[]{:S(2)}) collective-permute-start(f32[16,2,8,128]{3,2,1,0:T(8,128)S(1)} %get-tuple-element.32), channel_id=1, source_target_pairs={{0,18},{1,19},{2,16},{3,17},{16,2},{17,3},{18,0},{19,1},{4,22},{5,... | collective-permute-start | bytes 393224 | tf_op jit(solution)/shard_map/ppermute | solution.py:630
  10.9 0.0 collective-permute-done.refs_0_
  10.9 0.0 copy-start
  10.9 4.6 %collective-permute-start.5 = (f32[16,2,8,128]{3,2,1,0:T(8,128)S(1)}, f32[16,2,8,128]{3,2,1,0:T(8,128)S(1)}, u32[]{:S(2)}, u32[]{:S(2)}) collective-permute-start(f32[16,2,8,128]{3,2,1,0:T(8,128)S(1)} %get-tuple-element.33), channel_id=1, source_target_pairs={{0,17},{1,16},{2,19},{3,18},{16,1},{17,0},{18,3},{19,2},{4,21},{5,... | collective-permute-start | bytes 393224 | tf_op jit(solution)/shard_map/ppermute | solution.py:630
  15.5 0.0 collective-permute-done.1.refs_1_
  15.5 1.5 %collective-permute-start.6 = (f32[16,2,8,128]{3,2,1,0:T(8,128)S(1)}, f32[16,2,8,128]{3,2,1,0:T(8,128)S(1)}, u32[]{:S(2)}, u32[]{:S(2)}) collective-permute-start(f32[16,2,8,128]{3,2,1,0:T(8,128)S(1)} %get-tuple-element.34), channel_id=1, source_target_pairs={{0,19},{1,18},{2,17},{3,16},{16,3},{17,2},{18,1},{19,0},{4,23},{5,... | collective-permute-start | bytes 393224 | tf_op jit(solution)/shard_map/ppermute | solution.py:630
  17.0 0.0 copy-done
  17.0 1.0 %position_table.1.table = s32[128]{0:T(128)S(4)} custom-call(s32[64]{0:T(128)S(1)} %copy-done), custom_call_target="tpu_custom_call" | custom-call | bytes 4194304 | tf_op jit(solution)/shard_map/position_table/pallas_call | solution.py:105
  18.0 3.9 %collective-permute-done.2.refs_2_ = f32[16,2,8,128]{3,2,1,0:T(8,128)S(1)} collective-permute-done((f32[16,2,8,128]{3,2,1,0:T(8,128)S(1)}, f32[16,2,8,128]{3,2,1,0:T(8,128)S(1)}, u32[]{:S(2)}, u32[]{:S(2)}) %collective-permute-start.2) | collective-permute-done | bytes 131104 | tf_op jit(solution)/shard_map/ppermute | solution.py:630
  21.8 0.0 collective-permute-done.3.refs_3_
  21.8 6.1 %collective-permute-done.4.refs_4_ = f32[16,2,8,128]{3,2,1,0:T(8,128)S(1)} collective-permute-done((f32[16,2,8,128]{3,2,1,0:T(8,128)S(1)}, f32[16,2,8,128]{3,2,1,0:T(8,128)S(1)}, u32[]{:S(2)}, u32[]{:S(2)}) %collective-permute-start.4) | collective-permute-done | bytes 131104 | tf_op jit(solution)/shard_map/ppermute | solution.py:630
  27.9 0.0 collective-permute-done.5.refs_5_
  27.9 0.0 collective-permute-done.6.refs_6_
  27.9 0.3 boxes_in_place.1
  28.2 0.6 %collective-permute-start.9 = (f32[2,16,8,128]{3,2,1,0:T(8,128)S(1)}, f32[2,16,8,128]{3,2,1,0:T(8,128)S(1)}, u32[]{:S(2)}, u32[]{:S(2)}) collective-permute-start(f32[2,16,8,128]{3,2,1,0:T(8,128)S(1)} %get-tuple-element.39), channel_id=1, source_target_pairs={{0,16},{16,0},{1,17},{17,1},{2,18},{18,2},{3,19},{19,3},{4,20},{20... | collective-permute-start | bytes 393224 | tf_op jit(solution)/shard_map/ppermute | solution.py:646
  28.8 2.3 %collective-permute-start.7 = (f32[2,8,128]{2,1,0:T(8,128)S(1)}, f32[2,8,128]{2,1,0:T(8,128)S(1)}, u32[]{:S(2)}, u32[]{:S(2)}) collective-permute-start(f32[2,8,128]{2,1,0:T(8,128)S(1)} %get-tuple-element.37), channel_id=1, source_target_pairs={{1,2},{2,1},{3,0},{0,3},{5,6},{6,5},{7,4},{4,7},{9,10},{10,9},{11,... | collective-permute-start | bytes 24584 | tf_op jit(solution)/shard_map/ppermute | solution.py:650
  31.1 1.7 %collective-permute-start.8 = (f32[2,8,128]{2,1,0:T(8,128)S(1)}, f32[2,8,128]{2,1,0:T(8,128)S(1)}, u32[]{:S(2)}, u32[]{:S(2)}) collective-permute-start(f32[2,8,128]{2,1,0:T(8,128)S(1)} %get-tuple-element.38), channel_id=1, source_target_pairs={{0,1},{1,0},{2,3},{3,2},{4,5},{5,4},{6,7},{7,6},{8,9},{9,8},{10,11... | collective-permute-start | bytes 24584 | tf_op jit(solution)/shard_map/ppermute | solution.py:651
  32.8 1.4 %grid_from_boxes.1.grid = f32[4,16,16,128]{3,2,1,0:T(8,128)S(1)} custom-call(f32[65,2,8,128]{3,2,1,0:T(8,128)S(1)} %get-tuple-element.36.held), custom_call_target="tpu_custom_call" | custom-call | flops 4194304 | bytes 2097152 | tf_op jit(solution)/shard_map/grid_from_boxes/pallas_call | solution.py:224
  34.2 0.1 collective-permute-done.7.odd_pairs
  34.2 0.5 %collective-permute-done.8.even_pairs = f32[2,8,128]{2,1,0:T(8,128)S(1)} collective-permute-done((f32[2,8,128]{2,1,0:T(8,128)S(1)}, f32[2,8,128]{2,1,0:T(8,128)S(1)}, u32[]{:S(2)}, u32[]{:S(2)}) %collective-permute-start.8) | collective-permute-done | bytes 8224 | tf_op jit(solution)/shard_map/ppermute | solution.py:651
  34.8 0.0 collective-permute-done.9.refs_0_
  34.8 0.5 %faces_and_rows.1 = (f32[4,4,16,128]{3,2,1,0:T(8,128)S(1)}, f32[2,2,8,128]{3,2,1,0:T(8,128)S(1)}, f32[152,128]{1,0:T(8,128)S(1)}, f32[152,128]{1,0:T(8,128)S(1)}, f32[16,128]{1,0:T(8,128)S(1)}) custom-call(f32[4,16,16,128]{3,2,1,0:T(8,128)S(1)} %grid_from_boxes.1.grid, f32[2,8,128]{2,1,0:T(8,128)S(1)} %collective-permute-done.7.odd_pairs, ...), custom_call_target="tpu_custom_call" | custom-call | tf_op jit(solution)/shard_map/faces_and_rows/pallas_call | solution.py:318
  35.2 0.1 collective-permute-start.10
  35.3 0.5 %collective-permute-start.11 = (f32[152,128]{1,0:T(8,128)S(1)}, f32[152,128]{1,0:T(8,128)S(1)}, u32[]{:S(2)}, u32[]{:S(2)}) collective-permute-start(f32[152,128]{1,0:T(8,128)S(1)} %get-tuple-element.49), channel_id=1, source_target_pairs={{0,4},{4,8},{8,12},{12,0},{1,5},{5,9},{9,13},{13,1},{2,6},{6,10},{... | collective-permute-start | bytes 233480 | tf_op jit(solution)/shard_map/ppermute | solution.py:658
  35.8 1.5 %collective-permute-start.12 = (f32[16,128]{1,0:T(8,128)S(1)}, f32[16,128]{1,0:T(8,128)S(1)}, u32[]{:S(2)}, u32[]{:S(2)}) collective-permute-start(f32[16,128]{1,0:T(8,128)S(1)} %get-tuple-element.50), channel_id=1, source_target_pairs={{0,16},{16,0},{1,17},{17,1},{2,18},{18,2},{3,19},{19,3},{4,20},{20... | collective-permute-start | bytes 24584 | tf_op jit(solution)/shard_map/ppermute | solution.py:646
  37.3 1.9 %first_inside.1 = (f32[4,20,16,128]{3,2,1,0:T(8,128)S(1)}, f32[20,16,128]{2,1,0:T(8,128)S(1)}, f32[4,16,16,128]{3,2,1,0:T(8,128)S(1)}, f32[4,16,16,128]{3,2,1,0:...) custom-call(f32[4,16,16,128]{3,2,1,0:T(8,128)S(1)} %grid_from_boxes.1.grid, ...), custom_call_target="tpu_custom_call" | custom-call | flops 4194304 | bytes 2097152 | tf_op jit(solution)/shard_map/first_inside/pallas_call | solution.py:432
  39.2 0.2 collective-permute-done.12.refs_0_
  39.4 0.0 collective-permute-done.10.above
  39.4 0.5 %collective-permute-done.11.below = f32[152,128]{1,0:T(8,128)S(1)} collective-permute-done((f32[152,128]{1,0:T(8,128)S(1)}, f32[152,128]{1,0:T(8,128)S(1)}, u32[]{:S(2)}, u32[]{:S(2)}) %collective-permute-start.11) | collective-permute-done | bytes 77856 | tf_op jit(solution)/shard_map/ppermute | solution.py:658
  40.0 2.0 %last_sections.1 = f32[4,16,16,128]{3,2,1,0:T(8,128)} custom-call(f32[4,20,16,128]{3,2,1,0:T(8,128)S(1)} %get-tuple-element.42.wide, f32[20,16,128]{2,1,0:T(8,128)S(1)} %get-tuple-element.43.halves, f32[4,16,16,128]{3,2,1,0:T(8,128)S(1)} %get-tuple-element.44.first_in, f32[4,16,16,128]{3,2,1,0:T(8,128)S(1)} %get-tuple-element.45.beyond_in, ...), custom_call_target="tpu_custom_call" | custom-call | tf_op jit(solution)/shard_map/last_sections/pallas_call | solution.py:598
Async XLA Ops:
  1.4 9.5 %collective-permute-start = (f32[16,2,8,128]{3,2,1,0:T(8,128)S(1)}, f32[16,2,8,128]{3,2,1,0:T(8,128)S(1)}, u32[]{:S(2)}, u32[]{:S(2)}) collective-permute-start(f32[16,2,8,128]{3,2,1,0:T(8,128)S(1)} %get-tuple-element.28), channel_id=1, source_target_pairs={{0,3},{1,2},{2,1},{3,0},{16,19},{17,18},{18,17},{19,16},{4,7},{5,6... | collective-permute-start | bytes 393224 | tf_op jit(solution)/shard_map/ppermute | solution.py:630
  6.5 9.0 %collective-permute-start.1 = (f32[16,2,8,128]{3,2,1,0:T(8,128)S(1)}, f32[16,2,8,128]{3,2,1,0:T(8,128)S(1)}, u32[]{:S(2)}, u32[]{:S(2)}) collective-permute-start(f32[16,2,8,128]{3,2,1,0:T(8,128)S(1)} %get-tuple-element.29), channel_id=1, source_target_pairs={{0,1},{1,0},{2,3},{3,2},{16,17},{17,16},{18,19},{19,18},{4,5},{5,4... | collective-permute-start | bytes 393224 | tf_op jit(solution)/shard_map/ppermute | solution.py:630
  6.5 15.3 %collective-permute-start.2 = (f32[16,2,8,128]{3,2,1,0:T(8,128)S(1)}, f32[16,2,8,128]{3,2,1,0:T(8,128)S(1)}, u32[]{:S(2)}, u32[]{:S(2)}) collective-permute-start(f32[16,2,8,128]{3,2,1,0:T(8,128)S(1)} %get-tuple-element.30), channel_id=1, source_target_pairs={{0,2},{1,3},{2,0},{3,1},{16,18},{17,19},{18,16},{19,17},{4,6},{5,7... | collective-permute-start | bytes 393224 | tf_op jit(solution)/shard_map/ppermute | solution.py:630
  7.1 14.7 %collective-permute-start.3 = (f32[16,2,8,128]{3,2,1,0:T(8,128)S(1)}, f32[16,2,8,128]{3,2,1,0:T(8,128)S(1)}, u32[]{:S(2)}, u32[]{:S(2)}) collective-permute-start(f32[16,2,8,128]{3,2,1,0:T(8,128)S(1)} %get-tuple-element.31), channel_id=1, source_target_pairs={{0,16},{1,17},{2,18},{3,19},{16,0},{17,1},{18,2},{19,3},{4,20},{5,... | collective-permute-start | bytes 393224 | tf_op jit(solution)/shard_map/ppermute | solution.py:630
  8.8 19.1 %collective-permute-start.4 = (f32[16,2,8,128]{3,2,1,0:T(8,128)S(1)}, f32[16,2,8,128]{3,2,1,0:T(8,128)S(1)}, u32[]{:S(2)}, u32[]{:S(2)}) collective-permute-start(f32[16,2,8,128]{3,2,1,0:T(8,128)S(1)} %get-tuple-element.32), channel_id=1, source_target_pairs={{0,18},{1,19},{2,16},{3,17},{16,2},{17,3},{18,0},{19,1},{4,22},{5,... | collective-permute-start | bytes 393224 | tf_op jit(solution)/shard_map/ppermute | solution.py:630
  10.9 6.1 %copy-start = (s32[64]{0:T(128)S(1)}, s32[64]{0:T(128)}, u32[]{:S(2)}) copy-start(s32[64]{0:T(128)} %owner.1) | copy-start | bytes 772
  10.9 17.0 %collective-permute-start.5 = (f32[16,2,8,128]{3,2,1,0:T(8,128)S(1)}, f32[16,2,8,128]{3,2,1,0:T(8,128)S(1)}, u32[]{:S(2)}, u32[]{:S(2)}) collective-permute-start(f32[16,2,8,128]{3,2,1,0:T(8,128)S(1)} %get-tuple-element.33), channel_id=1, source_target_pairs={{0,17},{1,16},{2,19},{3,18},{16,1},{17,0},{18,3},{19,2},{4,21},{5,... | collective-permute-start | bytes 393224 | tf_op jit(solution)/shard_map/ppermute | solution.py:630
  15.5 12.4 %collective-permute-start.6 = (f32[16,2,8,128]{3,2,1,0:T(8,128)S(1)}, f32[16,2,8,128]{3,2,1,0:T(8,128)S(1)}, u32[]{:S(2)}, u32[]{:S(2)}) collective-permute-start(f32[16,2,8,128]{3,2,1,0:T(8,128)S(1)} %get-tuple-element.34), channel_id=1, source_target_pairs={{0,19},{1,18},{2,17},{3,16},{16,3},{17,2},{18,1},{19,0},{4,23},{5,... | collective-permute-start | bytes 393224 | tf_op jit(solution)/shard_map/ppermute | solution.py:630
  28.2 6.5 %collective-permute-start.9 = (f32[2,16,8,128]{3,2,1,0:T(8,128)S(1)}, f32[2,16,8,128]{3,2,1,0:T(8,128)S(1)}, u32[]{:S(2)}, u32[]{:S(2)}) collective-permute-start(f32[2,16,8,128]{3,2,1,0:T(8,128)S(1)} %get-tuple-element.39), channel_id=1, source_target_pairs={{0,16},{16,0},{1,17},{17,1},{2,18},{18,2},{3,19},{19,3},{4,20},{20... | collective-permute-start | bytes 393224 | tf_op jit(solution)/shard_map/ppermute | solution.py:646
  28.8 5.4 %collective-permute-start.7 = (f32[2,8,128]{2,1,0:T(8,128)S(1)}, f32[2,8,128]{2,1,0:T(8,128)S(1)}, u32[]{:S(2)}, u32[]{:S(2)}) collective-permute-start(f32[2,8,128]{2,1,0:T(8,128)S(1)} %get-tuple-element.37), channel_id=1, source_target_pairs={{1,2},{2,1},{3,0},{0,3},{5,6},{6,5},{7,4},{4,7},{9,10},{10,9},{11,... | collective-permute-start | bytes 24584 | tf_op jit(solution)/shard_map/ppermute | solution.py:650
  31.1 3.7 %collective-permute-start.8 = (f32[2,8,128]{2,1,0:T(8,128)S(1)}, f32[2,8,128]{2,1,0:T(8,128)S(1)}, u32[]{:S(2)}, u32[]{:S(2)}) collective-permute-start(f32[2,8,128]{2,1,0:T(8,128)S(1)} %get-tuple-element.38), channel_id=1, source_target_pairs={{0,1},{1,0},{2,3},{3,2},{4,5},{5,4},{6,7},{7,6},{8,9},{9,8},{10,11... | collective-permute-start | bytes 24584 | tf_op jit(solution)/shard_map/ppermute | solution.py:651
  35.2 4.2 %collective-permute-start.10 = (f32[152,128]{1,0:T(8,128)S(1)}, f32[152,128]{1,0:T(8,128)S(1)}, u32[]{:S(2)}, u32[]{:S(2)}) collective-permute-start(f32[152,128]{1,0:T(8,128)S(1)} %get-tuple-element.48), channel_id=1, source_target_pairs={{0,12},{4,0},{8,4},{12,8},{1,13},{5,1},{9,5},{13,9},{2,14},{6,2},{... | collective-permute-start | bytes 233480 | tf_op jit(solution)/shard_map/ppermute | solution.py:657
  35.3 4.7 %collective-permute-start.11 = (f32[152,128]{1,0:T(8,128)S(1)}, f32[152,128]{1,0:T(8,128)S(1)}, u32[]{:S(2)}, u32[]{:S(2)}) collective-permute-start(f32[152,128]{1,0:T(8,128)S(1)} %get-tuple-element.49), channel_id=1, source_target_pairs={{0,4},{4,8},{8,12},{12,0},{1,5},{5,9},{9,13},{13,1},{2,6},{6,10},{... | collective-permute-start | bytes 233480 | tf_op jit(solution)/shard_map/ppermute | solution.py:658
  35.8 3.7 %collective-permute-start.12 = (f32[16,128]{1,0:T(8,128)S(1)}, f32[16,128]{1,0:T(8,128)S(1)}, u32[]{:S(2)}, u32[]{:S(2)}) collective-permute-start(f32[16,128]{1,0:T(8,128)S(1)} %get-tuple-element.50), channel_id=1, source_target_pairs={{0,16},{16,0},{1,17},{17,1},{2,18},{18,2},{3,19},{19,3},{4,20},{20... | collective-permute-start | bytes 24584 | tf_op jit(solution)/shard_map/ppermute | solution.py:646

commit v12 on v11

--- a/solution.py
+++ b/solution.py
@@ -342,10 +342,11 @@
 
 def rates(cells, s, beside):
     means = [s + n for _, n in beside]
+    total = sum(means[1:], means[0])
     sums = []
     for f, v in enumerate(cells):
-        terms = [m * (fields[f] - v) for m, (fields, _) in zip(means, beside)]
-        sums.append(sum(terms[1:], terms[0]))
+        terms = [m * fields[f] for m, (fields, _) in zip(means, beside)]
+        sums.append(sum(terms[1:], terms[0]) - v * total)
     return sums
 
 
@@ -448,13 +449,13 @@
     )(grid, layers, ends)
 
 
-PARTS = 4
+PARTS = 8
 
 
 def last_sections(wide, halves, first, first_beyond, beyond, halves_beyond, above, below, sides):
     def kernel(wide, halves, first_in, beyond_in, beyond, halves_beyond, above, below, *refs):
         ins, (out, *refs) = refs[: len(sides)], refs[len(sides) :]
-        edges, first, first_beyond, around, fs, fbs, result, sems = refs
+        edges, first, first_beyond, around, fs, fbs, below_halves, above_halves, result, sems = refs
         factors = [TIME_STEP * c for c in DIFFUSION]
         row = lax.broadcasted_iota(jnp.int32, (EDGE, LANES), 0)
 
@@ -492,13 +493,19 @@
         wide_rows = wide.reshape(FIELDS * WIDE_X * NY, LANES)
         half_rows = halves.reshape(WIDE_X * NY, LANES)
 
+        for ref, sent_halves in ((below, below_halves), (above, above_halves)):
+            sent_halves[...] = half_conductance(ref[pl.ds(0, sent_halves.shape[0]), :])
+
         def sent(ref, depth, f, x, count):
             return ref[pl.ds(row_of(f, x) + depth, count, stride=HALO), :]
 
-        for ref, depth, y, tile_row in ((below, 1, 0, 7), (above, 0, NY - 1, 0)):
+        for ref, ref_halves, depth, y, tile_row in (
+            (below, below_halves, 1, 0, 7),
+            (above, above_halves, 0, NY - 1, 0),
+        ):
             for x, count in ((0, 8), (8, 8), (16, 2)):
                 s = half_rows[pl.ds((x + 1) * NY + y, count, stride=NY), :]
-                mean = s + half_conductance(sent(ref, depth, 0, x, count))
+                mean = s + sent(ref_halves, depth, 0, x, count)
                 for f in range(FIELDS):
                     v = wide_rows[pl.ds((f * WIDE_X + x + 1) * NY + y, count, stride=NY), :]
                     rows = pl.ds((f * NEAR_X + x) * NY + y, count, stride=NY)
@@ -508,7 +515,7 @@
 
                 def line(depth, shift):
                     fields = [sent(ref, depth, f, x + 1 + shift, 8) for f in range(FIELDS)]
-                    return fields, half_conductance(fields[0])
+                    return fields, sent(ref_halves, depth, 0, x + 1 + shift, 8)
 
                 here = line(depth, 0)
                 inner = (
@@ -607,6 +614,8 @@
             scratch(FIELDS * NX * EDGE),
             scratch(NEAR_X, NY),
             scratch(NX, NY),
+            scratch(5 * EDGE),
+            scratch(5 * EDGE),
             scratch(FIELDS, NX, NY),
             pltpu.SemaphoreType.DMA((PARTS,)),
         ],

time: 42.1 us -> 42 us (level)
  no operation moved by 1% of the time
where the time goes in v12:
time: 42 us; the launch traced here: 41.9 us
  starting transfers between devices  22.2 us (53%)
  waiting for transfers between devices  11.4 us (27%)
  Pallas kernels  8.27 us (20%)
    ppermute x7, starting transfers between devices, body(): lax.ppermute(departing[k], ('gx', 'gz'), [(i, i ^ k) for i in range(group...  15.6 us
    ppermute x7, waiting for transfers between devices, body(): lax.ppermute(departing[k], ('gx', 'gz'), [(i, i ^ k) for i in range(group...  9.96 us
    ppermute x1, starting transfers between devices, body(): odd_pairs = lax.ppermute(odd_pairs, 'gz', pairs(along, 1))  2.31 us
    ppermute x2, starting transfers between devices, along_x(): return [lax.ppermute(sides[0], 'gx', ring(across, 1))]  2.07 us
    pallas_call x1, Pallas kernels, last_sections(): pl.pallas_call(kernel, out_shape=jax.ShapeDtypeStruct((FIELDS, NX, NY, LA...  1.91 us
    pallas_call x1, Pallas kernels, first_inside(): pl.pallas_call(kernel, out_shape=[shape(FIELDS, WIDE_X), shape(WIDE_X), s...  1.85 us
    ppermute x1, starting transfers between devices, body(): even_pairs = lax.ppermute(even_pairs, 'gz', pairs(along, 0))  1.67 us
    pallas_call x1, Pallas kernels, grid_from_boxes(): pl.pallas_call(kernel, out_shape=jax.ShapeDtypeStruct((FIELDS, NX, NY, LA...  1.38 us
  transfers between devices with their start and end apart: 13, of which 6 were waited for; matrix products, arithmetic and copies ran while one was open for 0% of the time, Pallas kernels for 10%

profile of v12, /device:TPU:0, one launch (start us, length us, event | category | flops | bytes accessed | tf_op | source)
XLA Modules:
  0.0 41.9 jit_solution(9830089968813283992)
XLA Ops:
  0.0 1.4 %pack_boxes.1 = (f32[16,2,8,128]{3,2,1,0:T(8,128)S(1)}, f32[16,2,8,128]{3,2,1,0:T(8,128)S(1)}, f32[16,2,8,128]{3,2,1,0:T(8,128)S(1)}, f32[16,2,8,128]{3,2,1,0:T(...) custom-call(s32[64]{0:T(128)} %owner_hbm.1, ...), custom_call_target="tpu_custom_call" | custom-call | tf_op jit(solution)/shard_map/pack_boxes/pallas_call | solution.py:82
  1.4 5.1 %collective-permute-start = (f32[16,2,8,128]{3,2,1,0:T(8,128)S(1)}, f32[16,2,8,128]{3,2,1,0:T(8,128)S(1)}, u32[]{:S(2)}, u32[]{:S(2)}) collective-permute-start(f32[16,2,8,128]{3,2,1,0:T(8,128)S(1)} %get-tuple-element.28), channel_id=1, source_target_pairs={{0,3},{1,2},{2,1},{3,0},{16,19},{17,18},{18,17},{19,16},{4,7},{5,6... | collective-permute-start | bytes 393224 | tf_op jit(solution)/shard_map/ppermute | solution.py:639
  6.5 0.0 collective-permute-start.1
  6.5 0.6 %collective-permute-start.2 = (f32[16,2,8,128]{3,2,1,0:T(8,128)S(1)}, f32[16,2,8,128]{3,2,1,0:T(8,128)S(1)}, u32[]{:S(2)}, u32[]{:S(2)}) collective-permute-start(f32[16,2,8,128]{3,2,1,0:T(8,128)S(1)} %get-tuple-element.30), channel_id=1, source_target_pairs={{0,2},{1,3},{2,0},{3,1},{16,18},{17,19},{18,16},{19,17},{4,6},{5,7... | collective-permute-start | bytes 393224 | tf_op jit(solution)/shard_map/ppermute | solution.py:639
  7.1 1.7 %collective-permute-start.3 = (f32[16,2,8,128]{3,2,1,0:T(8,128)S(1)}, f32[16,2,8,128]{3,2,1,0:T(8,128)S(1)}, u32[]{:S(2)}, u32[]{:S(2)}) collective-permute-start(f32[16,2,8,128]{3,2,1,0:T(8,128)S(1)} %get-tuple-element.31), channel_id=1, source_target_pairs={{0,16},{1,17},{2,18},{3,19},{16,0},{17,1},{18,2},{19,3},{4,20},{5,... | collective-permute-start | bytes 393224 | tf_op jit(solution)/shard_map/ppermute | solution.py:639
  8.8 2.1 %collective-permute-start.4 = (f32[16,2,8,128]{3,2,1,0:T(8,128)S(1)}, f32[16,2,8,128]{3,2,1,0:T(8,128)S(1)}, u32[]{:S(2)}, u32[]{:S(2)}) collective-permute-start(f32[16,2,8,128]{3,2,1,0:T(8,128)S(1)} %get-tuple-element.32), channel_id=1, source_target_pairs={{0,18},{1,19},{2,16},{3,17},{16,2},{17,3},{18,0},{19,1},{4,22},{5,... | collective-permute-start | bytes 393224 | tf_op jit(solution)/shard_map/ppermute | solution.py:639
  10.9 0.0 collective-permute-done.refs_0_
  10.9 0.0 copy-start
  10.9 4.6 %collective-permute-start.5 = (f32[16,2,8,128]{3,2,1,0:T(8,128)S(1)}, f32[16,2,8,128]{3,2,1,0:T(8,128)S(1)}, u32[]{:S(2)}, u32[]{:S(2)}) collective-permute-start(f32[16,2,8,128]{3,2,1,0:T(8,128)S(1)} %get-tuple-element.33), channel_id=1, source_target_pairs={{0,17},{1,16},{2,19},{3,18},{16,1},{17,0},{18,3},{19,2},{4,21},{5,... | collective-permute-start | bytes 393224 | tf_op jit(solution)/shard_map/ppermute | solution.py:639
  15.5 0.0 collective-permute-done.1.refs_1_
  15.5 1.5 %collective-permute-start.6 = (f32[16,2,8,128]{3,2,1,0:T(8,128)S(1)}, f32[16,2,8,128]{3,2,1,0:T(8,128)S(1)}, u32[]{:S(2)}, u32[]{:S(2)}) collective-permute-start(f32[16,2,8,128]{3,2,1,0:T(8,128)S(1)} %get-tuple-element.34), channel_id=1, source_target_pairs={{0,19},{1,18},{2,17},{3,16},{16,3},{17,2},{18,1},{19,0},{4,23},{5,... | collective-permute-start | bytes 393224 | tf_op jit(solution)/shard_map/ppermute | solution.py:639
  17.0 0.0 copy-done
  17.0 1.0 %position_table.1.table = s32[128]{0:T(128)S(4)} custom-call(s32[64]{0:T(128)S(1)} %copy-done), custom_call_target="tpu_custom_call" | custom-call | bytes 4194304 | tf_op jit(solution)/shard_map/position_table/pallas_call | solution.py:105
  18.0 3.9 %collective-permute-done.2.refs_2_ = f32[16,2,8,128]{3,2,1,0:T(8,128)S(1)} collective-permute-done((f32[16,2,8,128]{3,2,1,0:T(8,128)S(1)}, f32[16,2,8,128]{3,2,1,0:T(8,128)S(1)}, u32[]{:S(2)}, u32[]{:S(2)}) %collective-permute-start.2) | collective-permute-done | bytes 131104 | tf_op jit(solution)/shard_map/ppermute | solution.py:639
  21.8 0.0 collective-permute-done.3.refs_3_
  21.8 6.1 %collective-permute-done.4.refs_4_ = f32[16,2,8,128]{3,2,1,0:T(8,128)S(1)} collective-permute-done((f32[16,2,8,128]{3,2,1,0:T(8,128)S(1)}, f32[16,2,8,128]{3,2,1,0:T(8,128)S(1)}, u32[]{:S(2)}, u32[]{:S(2)}) %collective-permute-start.4) | collective-permute-done | bytes 131104 | tf_op jit(solution)/shard_map/ppermute | solution.py:639
  27.9 0.0 collective-permute-done.5.refs_5_
  27.9 0.0 collective-permute-done.6.refs_6_
  27.9 0.3 boxes_in_place.1
  28.2 0.6 %collective-permute-start.9 = (f32[2,16,8,128]{3,2,1,0:T(8,128)S(1)}, f32[2,16,8,128]{3,2,1,0:T(8,128)S(1)}, u32[]{:S(2)}, u32[]{:S(2)}) collective-permute-start(f32[2,16,8,128]{3,2,1,0:T(8,128)S(1)} %get-tuple-element.39), channel_id=1, source_target_pairs={{0,16},{16,0},{1,17},{17,1},{2,18},{18,2},{3,19},{19,3},{4,20},{20... | collective-permute-start | bytes 393224 | tf_op jit(solution)/shard_map/ppermute | solution.py:655
  28.8 2.3 %collective-permute-start.7 = (f32[2,8,128]{2,1,0:T(8,128)S(1)}, f32[2,8,128]{2,1,0:T(8,128)S(1)}, u32[]{:S(2)}, u32[]{:S(2)}) collective-permute-start(f32[2,8,128]{2,1,0:T(8,128)S(1)} %get-tuple-element.37), channel_id=1, source_target_pairs={{1,2},{2,1},{3,0},{0,3},{5,6},{6,5},{7,4},{4,7},{9,10},{10,9},{11,... | collective-permute-start | bytes 24584 | tf_op jit(solution)/shard_map/ppermute | solution.py:659
  31.1 1.7 %collective-permute-start.8 = (f32[2,8,128]{2,1,0:T(8,128)S(1)}, f32[2,8,128]{2,1,0:T(8,128)S(1)}, u32[]{:S(2)}, u32[]{:S(2)}) collective-permute-start(f32[2,8,128]{2,1,0:T(8,128)S(1)} %get-tuple-element.38), channel_id=1, source_target_pairs={{0,1},{1,0},{2,3},{3,2},{4,5},{5,4},{6,7},{7,6},{8,9},{9,8},{10,11... | collective-permute-start | bytes 24584 | tf_op jit(solution)/shard_map/ppermute | solution.py:660
  32.8 1.4 %grid_from_boxes.1.grid = f32[4,16,16,128]{3,2,1,0:T(8,128)S(1)} custom-call(f32[65,2,8,128]{3,2,1,0:T(8,128)S(1)} %get-tuple-element.36.held), custom_call_target="tpu_custom_call" | custom-call | flops 4194304 | bytes 2097152 | tf_op jit(solution)/shard_map/grid_from_boxes/pallas_call | solution.py:224
  34.2 0.1 collective-permute-done.7.odd_pairs
  34.2 0.5 %collective-permute-done.8.even_pairs = f32[2,8,128]{2,1,0:T(8,128)S(1)} collective-permute-done((f32[2,8,128]{2,1,0:T(8,128)S(1)}, f32[2,8,128]{2,1,0:T(8,128)S(1)}, u32[]{:S(2)}, u32[]{:S(2)}) %collective-permute-start.8) | collective-permute-done | bytes 8224 | tf_op jit(solution)/shard_map/ppermute | solution.py:660
  34.8 0.0 collective-permute-done.9.refs_0_
  34.8 0.5 %faces_and_rows.1 = (f32[4,4,16,128]{3,2,1,0:T(8,128)S(1)}, f32[2,2,8,128]{3,2,1,0:T(8,128)S(1)}, f32[152,128]{1,0:T(8,128)S(1)}, f32[152,128]{1,0:T(8,128)S(1)}, f32[16,128]{1,0:T(8,128)S(1)}) custom-call(f32[4,16,16,128]{3,2,1,0:T(8,128)S(1)} %grid_from_boxes.1.grid, f32[2,8,128]{2,1,0:T(8,128)S(1)} %collective-permute-done.7.odd_pairs, ...), custom_call_target="tpu_custom_call" | custom-call | tf_op jit(solution)/shard_map/faces_and_rows/pallas_call | solution.py:318
  35.2 0.1 collective-permute-start.10
  35.3 0.5 %collective-permute-start.11 = (f32[152,128]{1,0:T(8,128)S(1)}, f32[152,128]{1,0:T(8,128)S(1)}, u32[]{:S(2)}, u32[]{:S(2)}) collective-permute-start(f32[152,128]{1,0:T(8,128)S(1)} %get-tuple-element.49), channel_id=1, source_target_pairs={{0,4},{4,8},{8,12},{12,0},{1,5},{5,9},{9,13},{13,1},{2,6},{6,10},{... | collective-permute-start | bytes 233480 | tf_op jit(solution)/shard_map/ppermute | solution.py:667
  35.8 1.5 %collective-permute-start.12 = (f32[16,128]{1,0:T(8,128)S(1)}, f32[16,128]{1,0:T(8,128)S(1)}, u32[]{:S(2)}, u32[]{:S(2)}) collective-permute-start(f32[16,128]{1,0:T(8,128)S(1)} %get-tuple-element.50), channel_id=1, source_target_pairs={{0,16},{16,0},{1,17},{17,1},{2,18},{18,2},{3,19},{19,3},{4,20},{20... | collective-permute-start | bytes 24584 | tf_op jit(solution)/shard_map/ppermute | solution.py:655
  37.3 1.9 %first_inside.1 = (f32[4,20,16,128]{3,2,1,0:T(8,128)S(1)}, f32[20,16,128]{2,1,0:T(8,128)S(1)}, f32[4,16,16,128]{3,2,1,0:T(8,128)S(1)}, f32[4,16,16,128]{3,2,1,0:...) custom-call(f32[4,16,16,128]{3,2,1,0:T(8,128)S(1)} %grid_from_boxes.1.grid, ...), custom_call_target="tpu_custom_call" | custom-call | flops 4194304 | bytes 2097152 | tf_op jit(solution)/shard_map/first_inside/pallas_call | solution.py:433
  39.2 0.3 collective-permute-done.12.refs_0_
  39.4 0.0 collective-permute-done.10.above
  39.4 0.5 %collective-permute-done.11.below = f32[152,128]{1,0:T(8,128)S(1)} collective-permute-done((f32[152,128]{1,0:T(8,128)S(1)}, f32[152,128]{1,0:T(8,128)S(1)}, u32[]{:S(2)}, u32[]{:S(2)}) %collective-permute-start.11) | collective-permute-done | bytes 77856 | tf_op jit(solution)/shard_map/ppermute | solution.py:667
  40.0 1.9 %last_sections.1 = f32[4,16,16,128]{3,2,1,0:T(8,128)} custom-call(f32[4,20,16,128]{3,2,1,0:T(8,128)S(1)} %get-tuple-element.42.wide, f32[20,16,128]{2,1,0:T(8,128)S(1)} %get-tuple-element.43.halves, f32[4,16,16,128]{3,2,1,0:T(8,128)S(1)} %get-tuple-element.44.first_in, f32[4,16,16,128]{3,2,1,0:T(8,128)S(1)} %get-tuple-element.45.beyond_in, ...), custom_call_target="tpu_custom_call" | custom-call | tf_op jit(solution)/shard_map/last_sections/pallas_call | solution.py:605
Async XLA Ops:
  1.4 9.5 %collective-permute-start = (f32[16,2,8,128]{3,2,1,0:T(8,128)S(1)}, f32[16,2,8,128]{3,2,1,0:T(8,128)S(1)}, u32[]{:S(2)}, u32[]{:S(2)}) collective-permute-start(f32[16,2,8,128]{3,2,1,0:T(8,128)S(1)} %get-tuple-element.28), channel_id=1, source_target_pairs={{0,3},{1,2},{2,1},{3,0},{16,19},{17,18},{18,17},{19,16},{4,7},{5,6... | collective-permute-start | bytes 393224 | tf_op jit(solution)/shard_map/ppermute | solution.py:639
  6.5 9.0 %collective-permute-start.1 = (f32[16,2,8,128]{3,2,1,0:T(8,128)S(1)}, f32[16,2,8,128]{3,2,1,0:T(8,128)S(1)}, u32[]{:S(2)}, u32[]{:S(2)}) collective-permute-start(f32[16,2,8,128]{3,2,1,0:T(8,128)S(1)} %get-tuple-element.29), channel_id=1, source_target_pairs={{0,1},{1,0},{2,3},{3,2},{16,17},{17,16},{18,19},{19,18},{4,5},{5,4... | collective-permute-start | bytes 393224 | tf_op jit(solution)/shard_map/ppermute | solution.py:639
  6.5 15.3 %collective-permute-start.2 = (f32[16,2,8,128]{3,2,1,0:T(8,128)S(1)}, f32[16,2,8,128]{3,2,1,0:T(8,128)S(1)}, u32[]{:S(2)}, u32[]{:S(2)}) collective-permute-start(f32[16,2,8,128]{3,2,1,0:T(8,128)S(1)} %get-tuple-element.30), channel_id=1, source_target_pairs={{0,2},{1,3},{2,0},{3,1},{16,18},{17,19},{18,16},{19,17},{4,6},{5,7... | collective-permute-start | bytes 393224 | tf_op jit(solution)/shard_map/ppermute | solution.py:639
  7.1 14.7 %collective-permute-start.3 = (f32[16,2,8,128]{3,2,1,0:T(8,128)S(1)}, f32[16,2,8,128]{3,2,1,0:T(8,128)S(1)}, u32[]{:S(2)}, u32[]{:S(2)}) collective-permute-start(f32[16,2,8,128]{3,2,1,0:T(8,128)S(1)} %get-tuple-element.31), channel_id=1, source_target_pairs={{0,16},{1,17},{2,18},{3,19},{16,0},{17,1},{18,2},{19,3},{4,20},{5,... | collective-permute-start | bytes 393224 | tf_op jit(solution)/shard_map/ppermute | solution.py:639
  8.8 19.1 %collective-permute-start.4 = (f32[16,2,8,128]{3,2,1,0:T(8,128)S(1)}, f32[16,2,8,128]{3,2,1,0:T(8,128)S(1)}, u32[]{:S(2)}, u32[]{:S(2)}) collective-permute-start(f32[16,2,8,128]{3,2,1,0:T(8,128)S(1)} %get-tuple-element.32), channel_id=1, source_target_pairs={{0,18},{1,19},{2,16},{3,17},{16,2},{17,3},{18,0},{19,1},{4,22},{5,... | collective-permute-start | bytes 393224 | tf_op jit(solution)/shard_map/ppermute | solution.py:639
  10.9 6.1 %copy-start = (s32[64]{0:T(128)S(1)}, s32[64]{0:T(128)}, u32[]{:S(2)}) copy-start(s32[64]{0:T(128)} %owner.1) | copy-start | bytes 772
  10.9 17.0 %collective-permute-start.5 = (f32[16,2,8,128]{3,2,1,0:T(8,128)S(1)}, f32[16,2,8,128]{3,2,1,0:T(8,128)S(1)}, u32[]{:S(2)}, u32[]{:S(2)}) collective-permute-start(f32[16,2,8,128]{3,2,1,0:T(8,128)S(1)} %get-tuple-element.33), channel_id=1, source_target_pairs={{0,17},{1,16},{2,19},{3,18},{16,1},{17,0},{18,3},{19,2},{4,21},{5,... | collective-permute-start | bytes 393224 | tf_op jit(solution)/shard_map/ppermute | solution.py:639
  15.5 12.4 %collective-permute-start.6 = (f32[16,2,8,128]{3,2,1,0:T(8,128)S(1)}, f32[16,2,8,128]{3,2,1,0:T(8,128)S(1)}, u32[]{:S(2)}, u32[]{:S(2)}) collective-permute-start(f32[16,2,8,128]{3,2,1,0:T(8,128)S(1)} %get-tuple-element.34), channel_id=1, source_target_pairs={{0,19},{1,18},{2,17},{3,16},{16,3},{17,2},{18,1},{19,0},{4,23},{5,... | collective-permute-start | bytes 393224 | tf_op jit(solution)/shard_map/ppermute | solution.py:639
  28.2 6.5 %collective-permute-start.9 = (f32[2,16,8,128]{3,2,1,0:T(8,128)S(1)}, f32[2,16,8,128]{3,2,1,0:T(8,128)S(1)}, u32[]{:S(2)}, u32[]{:S(2)}) collective-permute-start(f32[2,16,8,128]{3,2,1,0:T(8,128)S(1)} %get-tuple-element.39), channel_id=1, source_target_pairs={{0,16},{16,0},{1,17},{17,1},{2,18},{18,2},{3,19},{19,3},{4,20},{20... | collective-permute-start | bytes 393224 | tf_op jit(solution)/shard_map/ppermute | solution.py:655
  28.8 5.4 %collective-permute-start.7 = (f32[2,8,128]{2,1,0:T(8,128)S(1)}, f32[2,8,128]{2,1,0:T(8,128)S(1)}, u32[]{:S(2)}, u32[]{:S(2)}) collective-permute-start(f32[2,8,128]{2,1,0:T(8,128)S(1)} %get-tuple-element.37), channel_id=1, source_target_pairs={{1,2},{2,1},{3,0},{0,3},{5,6},{6,5},{7,4},{4,7},{9,10},{10,9},{11,... | collective-permute-start | bytes 24584 | tf_op jit(solution)/shard_map/ppermute | solution.py:659
  31.1 3.7 %collective-permute-start.8 = (f32[2,8,128]{2,1,0:T(8,128)S(1)}, f32[2,8,128]{2,1,0:T(8,128)S(1)}, u32[]{:S(2)}, u32[]{:S(2)}) collective-permute-start(f32[2,8,128]{2,1,0:T(8,128)S(1)} %get-tuple-element.38), channel_id=1, source_target_pairs={{0,1},{1,0},{2,3},{3,2},{4,5},{5,4},{6,7},{7,6},{8,9},{9,8},{10,11... | collective-permute-start | bytes 24584 | tf_op jit(solution)/shard_map/ppermute | solution.py:660
  35.2 4.2 %collective-permute-start.10 = (f32[152,128]{1,0:T(8,128)S(1)}, f32[152,128]{1,0:T(8,128)S(1)}, u32[]{:S(2)}, u32[]{:S(2)}) collective-permute-start(f32[152,128]{1,0:T(8,128)S(1)} %get-tuple-element.48), channel_id=1, source_target_pairs={{0,12},{4,0},{8,4},{12,8},{1,13},{5,1},{9,5},{13,9},{2,14},{6,2},{... | collective-permute-start | bytes 233480 | tf_op jit(solution)/shard_map/ppermute | solution.py:666
  35.3 4.7 %collective-permute-start.11 = (f32[152,128]{1,0:T(8,128)S(1)}, f32[152,128]{1,0:T(8,128)S(1)}, u32[]{:S(2)}, u32[]{:S(2)}) collective-permute-start(f32[152,128]{1,0:T(8,128)S(1)} %get-tuple-element.49), channel_id=1, source_target_pairs={{0,4},{4,8},{8,12},{12,0},{1,5},{5,9},{9,13},{13,1},{2,6},{6,10},{... | collective-permute-start | bytes 233480 | tf_op jit(solution)/shard_map/ppermute | solution.py:667
  35.8 3.7 %collective-permute-start.12 = (f32[16,128]{1,0:T(8,128)S(1)}, f32[16,128]{1,0:T(8,128)S(1)}, u32[]{:S(2)}, u32[]{:S(2)}) collective-permute-start(f32[16,128]{1,0:T(8,128)S(1)} %get-tuple-element.50), channel_id=1, source_target_pairs={{0,16},{16,0},{1,17},{17,1},{2,18},{18,2},{3,19},{19,3},{4,20},{20... | collective-permute-start | bytes 24584 | tf_op jit(solution)/shard_map/ppermute | solution.py:655

commit v13 on v12

--- a/solution.py
+++ b/solution.py
@@ -634,7 +634,7 @@
     departing = pack_boxes(old_fields, new_owner, group_size, capacity, split)
     table = position_table(old_owner, group_size, capacity)
     if split:
-        order = (3, 1, 2, 4, 6, 5, 7, 0)
+        order = (3, 1, 4, 2, 6, 5, 7, 0)
         arrived = [
             lax.ppermute(departing[k], ("gx", "gz"), [(i, i ^ k) for i in range(group_size)])
             if k

time: 42 us -> 42 us (level)
  no operation moved by 1% of the time
where the time goes in v13:
time: 42 us; the launch traced here: 41.8 us
  starting transfers between devices  22.2 us (53%)
  waiting for transfers between devices  11.3 us (27%)
  Pallas kernels  8.27 us (20%)
    ppermute x7, starting transfers between devices, body(): lax.ppermute(departing[k], ('gx', 'gz'), [(i, i ^ k) for i in range(group...  15.5 us
    ppermute x7, waiting for transfers between devices, body(): lax.ppermute(departing[k], ('gx', 'gz'), [(i, i ^ k) for i in range(group...  9.98 us
    ppermute x1, starting transfers between devices, body(): odd_pairs = lax.ppermute(odd_pairs, 'gz', pairs(along, 1))  2.24 us
    ppermute x2, starting transfers between devices, along_x(): return [lax.ppermute(sides[0], 'gx', ring(across, 1))]  2.1 us
    pallas_call x1, Pallas kernels, last_sections(): pl.pallas_call(kernel, out_shape=jax.ShapeDtypeStruct((FIELDS, NX, NY, LA...  1.91 us
    pallas_call x1, Pallas kernels, first_inside(): pl.pallas_call(kernel, out_shape=[shape(FIELDS, WIDE_X), shape(WIDE_X), s...  1.85 us
    ppermute x1, starting transfers between devices, body(): even_pairs = lax.ppermute(even_pairs, 'gz', pairs(along, 0))  1.73 us
    pallas_call x1, Pallas kernels, grid_from_boxes(): pl.pallas_call(kernel, out_shape=jax.ShapeDtypeStruct((FIELDS, NX, NY, LA...  1.38 us
  transfers between devices with their start and end apart: 13, of which 6 were waited for; matrix products, arithmetic and copies ran while one was open for 0% of the time, Pallas kernels for 10%

profile of v13, /device:TPU:0, one launch (start us, length us, event | category | flops | bytes accessed | tf_op | source)
XLA Modules:
  0.0 41.8 jit_solution(6497482351915504038)
XLA Ops:
  0.0 1.4 %pack_boxes.1 = (f32[16,2,8,128]{3,2,1,0:T(8,128)S(1)}, f32[16,2,8,128]{3,2,1,0:T(8,128)S(1)}, f32[16,2,8,128]{3,2,1,0:T(8,128)S(1)}, f32[16,2,8,128]{3,2,1,0:T(...) custom-call(s32[64]{0:T(128)} %owner_hbm.1, ...), custom_call_target="tpu_custom_call" | custom-call | tf_op jit(solution)/shard_map/pack_boxes/pallas_call | solution.py:82
  1.4 5.1 %collective-permute-start = (f32[16,2,8,128]{3,2,1,0:T(8,128)S(1)}, f32[16,2,8,128]{3,2,1,0:T(8,128)S(1)}, u32[]{:S(2)}, u32[]{:S(2)}) collective-permute-start(f32[16,2,8,128]{3,2,1,0:T(8,128)S(1)} %get-tuple-element.28), channel_id=1, source_target_pairs={{0,3},{1,2},{2,1},{3,0},{16,19},{17,18},{18,17},{19,16},{4,7},{5,6... | collective-permute-start | bytes 393224 | tf_op jit(solution)/shard_map/ppermute | solution.py:639
  6.5 0.0 collective-permute-start.1
  6.5 1.5 %collective-permute-start.2 = (f32[16,2,8,128]{3,2,1,0:T(8,128)S(1)}, f32[16,2,8,128]{3,2,1,0:T(8,128)S(1)}, u32[]{:S(2)}, u32[]{:S(2)}) collective-permute-start(f32[16,2,8,128]{3,2,1,0:T(8,128)S(1)} %get-tuple-element.30), channel_id=1, source_target_pairs={{0,16},{1,17},{2,18},{3,19},{16,0},{17,1},{18,2},{19,3},{4,20},{5,... | collective-permute-start | bytes 393224 | tf_op jit(solution)/shard_map/ppermute | solution.py:639
  8.0 0.8 %collective-permute-start.3 = (f32[16,2,8,128]{3,2,1,0:T(8,128)S(1)}, f32[16,2,8,128]{3,2,1,0:T(8,128)S(1)}, u32[]{:S(2)}, u32[]{:S(2)}) collective-permute-start(f32[16,2,8,128]{3,2,1,0:T(8,128)S(1)} %get-tuple-element.31), channel_id=1, source_target_pairs={{0,2},{1,3},{2,0},{3,1},{16,18},{17,19},{18,16},{19,17},{4,6},{5,7... | collective-permute-start | bytes 393224 | tf_op jit(solution)/shard_map/ppermute | solution.py:639
  8.8 2.1 %collective-permute-start.4 = (f32[16,2,8,128]{3,2,1,0:T(8,128)S(1)}, f32[16,2,8,128]{3,2,1,0:T(8,128)S(1)}, u32[]{:S(2)}, u32[]{:S(2)}) collective-permute-start(f32[16,2,8,128]{3,2,1,0:T(8,128)S(1)} %get-tuple-element.32), channel_id=1, source_target_pairs={{0,18},{1,19},{2,16},{3,17},{16,2},{17,3},{18,0},{19,1},{4,22},{5,... | collective-permute-start | bytes 393224 | tf_op jit(solution)/shard_map/ppermute | solution.py:639
  10.9 0.0 collective-permute-done.refs_0_
  10.9 0.0 copy-start
  10.9 4.6 %collective-permute-start.5 = (f32[16,2,8,128]{3,2,1,0:T(8,128)S(1)}, f32[16,2,8,128]{3,2,1,0:T(8,128)S(1)}, u32[]{:S(2)}, u32[]{:S(2)}) collective-permute-start(f32[16,2,8,128]{3,2,1,0:T(8,128)S(1)} %get-tuple-element.33), channel_id=1, source_target_pairs={{0,17},{1,16},{2,19},{3,18},{16,1},{17,0},{18,3},{19,2},{4,21},{5,... | collective-permute-start | bytes 393224 | tf_op jit(solution)/shard_map/ppermute | solution.py:639
  15.5 0.0 collective-permute-done.1.refs_1_
  15.5 1.5 %collective-permute-start.6 = (f32[16,2,8,128]{3,2,1,0:T(8,128)S(1)}, f32[16,2,8,128]{3,2,1,0:T(8,128)S(1)}, u32[]{:S(2)}, u32[]{:S(2)}) collective-permute-start(f32[16,2,8,128]{3,2,1,0:T(8,128)S(1)} %get-tuple-element.34), channel_id=1, source_target_pairs={{0,19},{1,18},{2,17},{3,16},{16,3},{17,2},{18,1},{19,0},{4,23},{5,... | collective-permute-start | bytes 393224 | tf_op jit(solution)/shard_map/ppermute | solution.py:639
  16.9 0.0 copy-done
  16.9 1.0 %position_table.1.table = s32[128]{0:T(128)S(4)} custom-call(s32[64]{0:T(128)S(1)} %copy-done), custom_call_target="tpu_custom_call" | custom-call | bytes 4194304 | tf_op jit(solution)/shard_map/position_table/pallas_call | solution.py:105
  17.9 0.0 collective-permute-done.2.refs_2_
  17.9 4.6 %collective-permute-done.3.refs_3_ = f32[16,2,8,128]{3,2,1,0:T(8,128)S(1)} collective-permute-done((f32[16,2,8,128]{3,2,1,0:T(8,128)S(1)}, f32[16,2,8,128]{3,2,1,0:T(8,128)S(1)}, u32[]{:S(2)}, u32[]{:S(2)}) %collective-permute-start.3) | collective-permute-done | bytes 131104 | tf_op jit(solution)/shard_map/ppermute | solution.py:639
  22.5 5.4 %collective-permute-done.4.refs_4_ = f32[16,2,8,128]{3,2,1,0:T(8,128)S(1)} collective-permute-done((f32[16,2,8,128]{3,2,1,0:T(8,128)S(1)}, f32[16,2,8,128]{3,2,1,0:T(8,128)S(1)}, u32[]{:S(2)}, u32[]{:S(2)}) %collective-permute-start.4) | collective-permute-done | bytes 131104 | tf_op jit(solution)/shard_map/ppermute | solution.py:639
  27.9 0.0 collective-permute-done.5.refs_5_
  27.9 0.0 collective-permute-done.6.refs_6_
  27.9 0.3 boxes_in_place.1
  28.2 0.6 %collective-permute-start.9 = (f32[2,16,8,128]{3,2,1,0:T(8,128)S(1)}, f32[2,16,8,128]{3,2,1,0:T(8,128)S(1)}, u32[]{:S(2)}, u32[]{:S(2)}) collective-permute-start(f32[2,16,8,128]{3,2,1,0:T(8,128)S(1)} %get-tuple-element.39), channel_id=1, source_target_pairs={{0,16},{16,0},{1,17},{17,1},{2,18},{18,2},{3,19},{19,3},{4,20},{20... | collective-permute-start | bytes 393224 | tf_op jit(solution)/shard_map/ppermute | solution.py:655
  28.8 2.2 %collective-permute-start.7 = (f32[2,8,128]{2,1,0:T(8,128)S(1)}, f32[2,8,128]{2,1,0:T(8,128)S(1)}, u32[]{:S(2)}, u32[]{:S(2)}) collective-permute-start(f32[2,8,128]{2,1,0:T(8,128)S(1)} %get-tuple-element.37), channel_id=1, source_target_pairs={{1,2},{2,1},{3,0},{0,3},{5,6},{6,5},{7,4},{4,7},{9,10},{10,9},{11,... | collective-permute-start | bytes 24584 | tf_op jit(solution)/shard_map/ppermute | solution.py:659
  31.0 1.7 %collective-permute-start.8 = (f32[2,8,128]{2,1,0:T(8,128)S(1)}, f32[2,8,128]{2,1,0:T(8,128)S(1)}, u32[]{:S(2)}, u32[]{:S(2)}) collective-permute-start(f32[2,8,128]{2,1,0:T(8,128)S(1)} %get-tuple-element.38), channel_id=1, source_target_pairs={{0,1},{1,0},{2,3},{3,2},{4,5},{5,4},{6,7},{7,6},{8,9},{9,8},{10,11... | collective-permute-start | bytes 24584 | tf_op jit(solution)/shard_map/ppermute | solution.py:660
  32.8 1.4 %grid_from_boxes.1.grid = f32[4,16,16,128]{3,2,1,0:T(8,128)S(1)} custom-call(f32[65,2,8,128]{3,2,1,0:T(8,128)S(1)} %get-tuple-element.36.held), custom_call_target="tpu_custom_call" | custom-call | flops 4194304 | bytes 2097152 | tf_op jit(solution)/shard_map/grid_from_boxes/pallas_call | solution.py:224
  34.2 0.1 collective-permute-done.7.odd_pairs
  34.2 0.4 %collective-permute-done.8.even_pairs = f32[2,8,128]{2,1,0:T(8,128)S(1)} collective-permute-done((f32[2,8,128]{2,1,0:T(8,128)S(1)}, f32[2,8,128]{2,1,0:T(8,128)S(1)}, u32[]{:S(2)}, u32[]{:S(2)}) %collective-permute-start.8) | collective-permute-done | bytes 8224 | tf_op jit(solution)/shard_map/ppermute | solution.py:660
  34.7 0.0 collective-permute-done.9.refs_0_
  34.7 0.5 %faces_and_rows.1 = (f32[4,4,16,128]{3,2,1,0:T(8,128)S(1)}, f32[2,2,8,128]{3,2,1,0:T(8,128)S(1)}, f32[152,128]{1,0:T(8,128)S(1)}, f32[152,128]{1,0:T(8,128)S(1)}, f32[16,128]{1,0:T(8,128)S(1)}) custom-call(f32[4,16,16,128]{3,2,1,0:T(8,128)S(1)} %grid_from_boxes.1.grid, f32[2,8,128]{2,1,0:T(8,128)S(1)} %collective-permute-done.7.odd_pairs, ...), custom_call_target="tpu_custom_call" | custom-call | tf_op jit(solution)/shard_map/faces_and_rows/pallas_call | solution.py:318
  35.2 0.1 collective-permute-start.10
  35.2 0.5 %collective-permute-start.11 = (f32[152,128]{1,0:T(8,128)S(1)}, f32[152,128]{1,0:T(8,128)S(1)}, u32[]{:S(2)}, u32[]{:S(2)}) collective-permute-start(f32[152,128]{1,0:T(8,128)S(1)} %get-tuple-element.49), channel_id=1, source_target_pairs={{0,4},{4,8},{8,12},{12,0},{1,5},{5,9},{9,13},{13,1},{2,6},{6,10},{... | collective-permute-start | bytes 233480 | tf_op jit(solution)/shard_map/ppermute | solution.py:667
  35.7 1.5 %collective-permute-start.12 = (f32[16,128]{1,0:T(8,128)S(1)}, f32[16,128]{1,0:T(8,128)S(1)}, u32[]{:S(2)}, u32[]{:S(2)}) collective-permute-start(f32[16,128]{1,0:T(8,128)S(1)} %get-tuple-element.50), channel_id=1, source_target_pairs={{0,16},{16,0},{1,17},{17,1},{2,18},{18,2},{3,19},{19,3},{4,20},{20... | collective-permute-start | bytes 24584 | tf_op jit(solution)/shard_map/ppermute | solution.py:655
  37.3 1.9 %first_inside.1 = (f32[4,20,16,128]{3,2,1,0:T(8,128)S(1)}, f32[20,16,128]{2,1,0:T(8,128)S(1)}, f32[4,16,16,128]{3,2,1,0:T(8,128)S(1)}, f32[4,16,16,128]{3,2,1,0:...) custom-call(f32[4,16,16,128]{3,2,1,0:T(8,128)S(1)} %grid_from_boxes.1.grid, ...), custom_call_target="tpu_custom_call" | custom-call | flops 4194304 | bytes 2097152 | tf_op jit(solution)/shard_map/first_inside/pallas_call | solution.py:433
  39.1 0.2 collective-permute-done.12.refs_0_
  39.4 0.0 collective-permute-done.10.above
  39.4 0.5 %collective-permute-done.11.below = f32[152,128]{1,0:T(8,128)S(1)} collective-permute-done((f32[152,128]{1,0:T(8,128)S(1)}, f32[152,128]{1,0:T(8,128)S(1)}, u32[]{:S(2)}, u32[]{:S(2)}) %collective-permute-start.11) | collective-permute-done | bytes 77856 | tf_op jit(solution)/shard_map/ppermute | solution.py:667
  39.9 1.9 %last_sections.1 = f32[4,16,16,128]{3,2,1,0:T(8,128)} custom-call(f32[4,20,16,128]{3,2,1,0:T(8,128)S(1)} %get-tuple-element.42.wide, f32[20,16,128]{2,1,0:T(8,128)S(1)} %get-tuple-element.43.halves, f32[4,16,16,128]{3,2,1,0:T(8,128)S(1)} %get-tuple-element.44.first_in, f32[4,16,16,128]{3,2,1,0:T(8,128)S(1)} %get-tuple-element.45.beyond_in, ...), custom_call_target="tpu_custom_call" | custom-call | tf_op jit(solution)/shard_map/last_sections/pallas_call | solution.py:605
Async XLA Ops:
  1.4 9.5 %collective-permute-start = (f32[16,2,8,128]{3,2,1,0:T(8,128)S(1)}, f32[16,2,8,128]{3,2,1,0:T(8,128)S(1)}, u32[]{:S(2)}, u32[]{:S(2)}) collective-permute-start(f32[16,2,8,128]{3,2,1,0:T(8,128)S(1)} %get-tuple-element.28), channel_id=1, source_target_pairs={{0,3},{1,2},{2,1},{3,0},{16,19},{17,18},{18,17},{19,16},{4,7},{5,6... | collective-permute-start | bytes 393224 | tf_op jit(solution)/shard_map/ppermute | solution.py:639
  6.5 9.0 %collective-permute-start.1 = (f32[16,2,8,128]{3,2,1,0:T(8,128)S(1)}, f32[16,2,8,128]{3,2,1,0:T(8,128)S(1)}, u32[]{:S(2)}, u32[]{:S(2)}) collective-permute-start(f32[16,2,8,128]{3,2,1,0:T(8,128)S(1)} %get-tuple-element.29), channel_id=1, source_target_pairs={{0,1},{1,0},{2,3},{3,2},{16,17},{17,16},{18,19},{19,18},{4,5},{5,4... | collective-permute-start | bytes 393224 | tf_op jit(solution)/shard_map/ppermute | solution.py:639
  6.5 11.4 %collective-permute-start.2 = (f32[16,2,8,128]{3,2,1,0:T(8,128)S(1)}, f32[16,2,8,128]{3,2,1,0:T(8,128)S(1)}, u32[]{:S(2)}, u32[]{:S(2)}) collective-permute-start(f32[16,2,8,128]{3,2,1,0:T(8,128)S(1)} %get-tuple-element.30), channel_id=1, source_target_pairs={{0,16},{1,17},{2,18},{3,19},{16,0},{17,1},{18,2},{19,3},{4,20},{5,... | collective-permute-start | bytes 393224 | tf_op jit(solution)/shard_map/ppermute | solution.py:639
  8.0 14.5 %collective-permute-start.3 = (f32[16,2,8,128]{3,2,1,0:T(8,128)S(1)}, f32[16,2,8,128]{3,2,1,0:T(8,128)S(1)}, u32[]{:S(2)}, u32[]{:S(2)}) collective-permute-start(f32[16,2,8,128]{3,2,1,0:T(8,128)S(1)} %get-tuple-element.31), channel_id=1, source_target_pairs={{0,2},{1,3},{2,0},{3,1},{16,18},{17,19},{18,16},{19,17},{4,6},{5,7... | collective-permute-start | bytes 393224 | tf_op jit(solution)/shard_map/ppermute | solution.py:639
  8.8 19.1 %collective-permute-start.4 = (f32[16,2,8,128]{3,2,1,0:T(8,128)S(1)}, f32[16,2,8,128]{3,2,1,0:T(8,128)S(1)}, u32[]{:S(2)}, u32[]{:S(2)}) collective-permute-start(f32[16,2,8,128]{3,2,1,0:T(8,128)S(1)} %get-tuple-element.32), channel_id=1, source_target_pairs={{0,18},{1,19},{2,16},{3,17},{16,2},{17,3},{18,0},{19,1},{4,22},{5,... | collective-permute-start | bytes 393224 | tf_op jit(solution)/shard_map/ppermute | solution.py:639
  10.9 6.0 %copy-start = (s32[64]{0:T(128)S(1)}, s32[64]{0:T(128)}, u32[]{:S(2)}) copy-start(s32[64]{0:T(128)} %owner.1) | copy-start | bytes 772
  10.9 17.0 %collective-permute-start.5 = (f32[16,2,8,128]{3,2,1,0:T(8,128)S(1)}, f32[16,2,8,128]{3,2,1,0:T(8,128)S(1)}, u32[]{:S(2)}, u32[]{:S(2)}) collective-permute-start(f32[16,2,8,128]{3,2,1,0:T(8,128)S(1)} %get-tuple-element.33), channel_id=1, source_target_pairs={{0,17},{1,16},{2,19},{3,18},{16,1},{17,0},{18,3},{19,2},{4,21},{5,... | collective-permute-start | bytes 393224 | tf_op jit(solution)/shard_map/ppermute | solution.py:639
  15.5 12.4 %collective-permute-start.6 = (f32[16,2,8,128]{3,2,1,0:T(8,128)S(1)}, f32[16,2,8,128]{3,2,1,0:T(8,128)S(1)}, u32[]{:S(2)}, u32[]{:S(2)}) collective-permute-start(f32[16,2,8,128]{3,2,1,0:T(8,128)S(1)} %get-tuple-element.34), channel_id=1, source_target_pairs={{0,19},{1,18},{2,17},{3,16},{16,3},{17,2},{18,1},{19,0},{4,23},{5,... | collective-permute-start | bytes 393224 | tf_op jit(solution)/shard_map/ppermute | solution.py:639
  28.2 6.5 %collective-permute-start.9 = (f32[2,16,8,128]{3,2,1,0:T(8,128)S(1)}, f32[2,16,8,128]{3,2,1,0:T(8,128)S(1)}, u32[]{:S(2)}, u32[]{:S(2)}) collective-permute-start(f32[2,16,8,128]{3,2,1,0:T(8,128)S(1)} %get-tuple-element.39), channel_id=1, source_target_pairs={{0,16},{16,0},{1,17},{17,1},{2,18},{18,2},{3,19},{19,3},{4,20},{20... | collective-permute-start | bytes 393224 | tf_op jit(solution)/shard_map/ppermute | solution.py:655
  28.8 5.4 %collective-permute-start.7 = (f32[2,8,128]{2,1,0:T(8,128)S(1)}, f32[2,8,128]{2,1,0:T(8,128)S(1)}, u32[]{:S(2)}, u32[]{:S(2)}) collective-permute-start(f32[2,8,128]{2,1,0:T(8,128)S(1)} %get-tuple-element.37), channel_id=1, source_target_pairs={{1,2},{2,1},{3,0},{0,3},{5,6},{6,5},{7,4},{4,7},{9,10},{10,9},{11,... | collective-permute-start | bytes 24584 | tf_op jit(solution)/shard_map/ppermute | solution.py:659
  31.0 3.7 %collective-permute-start.8 = (f32[2,8,128]{2,1,0:T(8,128)S(1)}, f32[2,8,128]{2,1,0:T(8,128)S(1)}, u32[]{:S(2)}, u32[]{:S(2)}) collective-permute-start(f32[2,8,128]{2,1,0:T(8,128)S(1)} %get-tuple-element.38), channel_id=1, source_target_pairs={{0,1},{1,0},{2,3},{3,2},{4,5},{5,4},{6,7},{7,6},{8,9},{9,8},{10,11... | collective-permute-start | bytes 24584 | tf_op jit(solution)/shard_map/ppermute | solution.py:660
  35.2 4.2 %collective-permute-start.10 = (f32[152,128]{1,0:T(8,128)S(1)}, f32[152,128]{1,0:T(8,128)S(1)}, u32[]{:S(2)}, u32[]{:S(2)}) collective-permute-start(f32[152,128]{1,0:T(8,128)S(1)} %get-tuple-element.48), channel_id=1, source_target_pairs={{0,12},{4,0},{8,4},{12,8},{1,13},{5,1},{9,5},{13,9},{2,14},{6,2},{... | collective-permute-start | bytes 233480 | tf_op jit(solution)/shard_map/ppermute | solution.py:666
  35.2 4.7 %collective-permute-start.11 = (f32[152,128]{1,0:T(8,128)S(1)}, f32[152,128]{1,0:T(8,128)S(1)}, u32[]{:S(2)}, u32[]{:S(2)}) collective-permute-start(f32[152,128]{1,0:T(8,128)S(1)} %get-tuple-element.49), channel_id=1, source_target_pairs={{0,4},{4,8},{8,12},{12,0},{1,5},{5,9},{9,13},{13,1},{2,6},{6,10},{... | collective-permute-start | bytes 233480 | tf_op jit(solution)/shard_map/ppermute | solution.py:667
  35.7 3.7 %collective-permute-start.12 = (f32[16,128]{1,0:T(8,128)S(1)}, f32[16,128]{1,0:T(8,128)S(1)}, u32[]{:S(2)}, u32[]{:S(2)}) collective-permute-start(f32[16,128]{1,0:T(8,128)S(1)} %get-tuple-element.50), channel_id=1, source_target_pairs={{0,16},{16,0},{1,17},{17,1},{2,18},{18,2},{3,19},{19,3},{4,20},{20... | collective-permute-start | bytes 24584 | tf_op jit(solution)/shard_map/ppermute | solution.py:655

commit v14 on v13

--- a/solution.py
+++ b/solution.py
@@ -77,7 +77,7 @@
                     ]
                 return carry
 
-            lax.fori_loop(0, rows, copy, 0, unroll=8)
+            lax.fori_loop(0, rows, copy, 0, unroll=16)
 
     return pl.pallas_call(
         kernel,
@@ -158,7 +158,7 @@
                 held[table[base + r]] = rows_in[r]
                 return carry
 
-            lax.fori_loop(0, rows, scatter, 0, unroll=8)
+            lax.fori_loop(0, rows, scatter, 0, unroll=16)
         for side in range(2):
             out = outs[0].at[side] if joined else outs[side]
             for by in range(BRICK_Y):

time: 42 us -> 41.8 us (level)
  no operation moved by 1% of the time
where the time goes in v14:
time: 41.8 us; the launch traced here: 41.7 us
  starting transfers between devices  22.2 us (53%)
  waiting for transfers between devices  11.3 us (27%)
  Pallas kernels  8.1 us (19%)
    ppermute x7, starting transfers between devices, body(): lax.ppermute(departing[k], ('gx', 'gz'), [(i, i ^ k) for i in range(group...  15.5 us
    ppermute x7, waiting for transfers between devices, body(): lax.ppermute(departing[k], ('gx', 'gz'), [(i, i ^ k) for i in range(group...  9.98 us
    ppermute x1, starting transfers between devices, body(): odd_pairs = lax.ppermute(odd_pairs, 'gz', pairs(along, 1))  2.24 us
    ppermute x2, starting transfers between devices, along_x(): return [lax.ppermute(sides[0], 'gx', ring(across, 1))]  2.11 us
    pallas_call x1, Pallas kernels, last_sections(): pl.pallas_call(kernel, out_shape=jax.ShapeDtypeStruct((FIELDS, NX, NY, LA...  1.91 us
    pallas_call x1, Pallas kernels, first_inside(): pl.pallas_call(kernel, out_shape=[shape(FIELDS, WIDE_X), shape(WIDE_X), s...  1.85 us
    ppermute x1, starting transfers between devices, body(): even_pairs = lax.ppermute(even_pairs, 'gz', pairs(along, 0))  1.74 us
    pallas_call x1, Pallas kernels, grid_from_boxes(): pl.pallas_call(kernel, out_shape=jax.ShapeDtypeStruct((FIELDS, NX, NY, LA...  1.38 us
  transfers between devices with their start and end apart: 13, of which 6 were waited for; matrix products, arithmetic and copies ran while one was open for 0% of the time, Pallas kernels for 10%

profile of v14, /device:TPU:0, one launch (start us, length us, event | category | flops | bytes accessed | tf_op | source)
XLA Modules:
  0.0 41.7 jit_solution(11876968132678468249)
XLA Ops:
  0.0 1.3 %pack_boxes.1 = (f32[16,2,8,128]{3,2,1,0:T(8,128)S(1)}, f32[16,2,8,128]{3,2,1,0:T(8,128)S(1)}, f32[16,2,8,128]{3,2,1,0:T(8,128)S(1)}, f32[16,2,8,128]{3,2,1,0:T(...) custom-call(s32[64]{0:T(128)} %owner_hbm.1, ...), custom_call_target="tpu_custom_call" | custom-call | tf_op jit(solution)/shard_map/pack_boxes/pallas_call | solution.py:82
  1.3 5.1 %collective-permute-start = (f32[16,2,8,128]{3,2,1,0:T(8,128)S(1)}, f32[16,2,8,128]{3,2,1,0:T(8,128)S(1)}, u32[]{:S(2)}, u32[]{:S(2)}) collective-permute-start(f32[16,2,8,128]{3,2,1,0:T(8,128)S(1)} %get-tuple-element.28), channel_id=1, source_target_pairs={{0,3},{1,2},{2,1},{3,0},{16,19},{17,18},{18,17},{19,16},{4,7},{5,6... | collective-permute-start | bytes 393224 | tf_op jit(solution)/shard_map/ppermute | solution.py:639
  6.4 0.0 collective-permute-start.1
  6.4 1.5 %collective-permute-start.2 = (f32[16,2,8,128]{3,2,1,0:T(8,128)S(1)}, f32[16,2,8,128]{3,2,1,0:T(8,128)S(1)}, u32[]{:S(2)}, u32[]{:S(2)}) collective-permute-start(f32[16,2,8,128]{3,2,1,0:T(8,128)S(1)} %get-tuple-element.30), channel_id=1, source_target_pairs={{0,16},{1,17},{2,18},{3,19},{16,0},{17,1},{18,2},{19,3},{4,20},{5,... | collective-permute-start | bytes 393224 | tf_op jit(solution)/shard_map/ppermute | solution.py:639
  7.9 0.8 %collective-permute-start.3 = (f32[16,2,8,128]{3,2,1,0:T(8,128)S(1)}, f32[16,2,8,128]{3,2,1,0:T(8,128)S(1)}, u32[]{:S(2)}, u32[]{:S(2)}) collective-permute-start(f32[16,2,8,128]{3,2,1,0:T(8,128)S(1)} %get-tuple-element.31), channel_id=1, source_target_pairs={{0,2},{1,3},{2,0},{3,1},{16,18},{17,19},{18,16},{19,17},{4,6},{5,7... | collective-permute-start | bytes 393224 | tf_op jit(solution)/shard_map/ppermute | solution.py:639
  8.7 2.1 %collective-permute-start.4 = (f32[16,2,8,128]{3,2,1,0:T(8,128)S(1)}, f32[16,2,8,128]{3,2,1,0:T(8,128)S(1)}, u32[]{:S(2)}, u32[]{:S(2)}) collective-permute-start(f32[16,2,8,128]{3,2,1,0:T(8,128)S(1)} %get-tuple-element.32), channel_id=1, source_target_pairs={{0,18},{1,19},{2,16},{3,17},{16,2},{17,3},{18,0},{19,1},{4,22},{5,... | collective-permute-start | bytes 393224 | tf_op jit(solution)/shard_map/ppermute | solution.py:639
  10.8 0.0 collective-permute-done.refs_0_
  10.8 0.0 copy-start
  10.8 4.6 %collective-permute-start.5 = (f32[16,2,8,128]{3,2,1,0:T(8,128)S(1)}, f32[16,2,8,128]{3,2,1,0:T(8,128)S(1)}, u32[]{:S(2)}, u32[]{:S(2)}) collective-permute-start(f32[16,2,8,128]{3,2,1,0:T(8,128)S(1)} %get-tuple-element.33), channel_id=1, source_target_pairs={{0,17},{1,16},{2,19},{3,18},{16,1},{17,0},{18,3},{19,2},{4,21},{5,... | collective-permute-start | bytes 393224 | tf_op jit(solution)/shard_map/ppermute | solution.py:639
  15.4 0.0 collective-permute-done.1.refs_1_
  15.4 1.5 %collective-permute-start.6 = (f32[16,2,8,128]{3,2,1,0:T(8,128)S(1)}, f32[16,2,8,128]{3,2,1,0:T(8,128)S(1)}, u32[]{:S(2)}, u32[]{:S(2)}) collective-permute-start(f32[16,2,8,128]{3,2,1,0:T(8,128)S(1)} %get-tuple-element.34), channel_id=1, source_target_pairs={{0,19},{1,18},{2,17},{3,16},{16,3},{17,2},{18,1},{19,0},{4,23},{5,... | collective-permute-start | bytes 393224 | tf_op jit(solution)/shard_map/ppermute | solution.py:639
  16.8 0.0 copy-done
  16.8 1.0 %position_table.1.table = s32[128]{0:T(128)S(4)} custom-call(s32[64]{0:T(128)S(1)} %copy-done), custom_call_target="tpu_custom_call" | custom-call | bytes 4194304 | tf_op jit(solution)/shard_map/position_table/pallas_call | solution.py:105
  17.8 0.0 collective-permute-done.2.refs_2_
  17.8 4.6 %collective-permute-done.3.refs_3_ = f32[16,2,8,128]{3,2,1,0:T(8,128)S(1)} collective-permute-done((f32[16,2,8,128]{3,2,1,0:T(8,128)S(1)}, f32[16,2,8,128]{3,2,1,0:T(8,128)S(1)}, u32[]{:S(2)}, u32[]{:S(2)}) %collective-permute-start.3) | collective-permute-done | bytes 131104 | tf_op jit(solution)/shard_map/ppermute | solution.py:639
  22.4 5.4 %collective-permute-done.4.refs_4_ = f32[16,2,8,128]{3,2,1,0:T(8,128)S(1)} collective-permute-done((f32[16,2,8,128]{3,2,1,0:T(8,128)S(1)}, f32[16,2,8,128]{3,2,1,0:T(8,128)S(1)}, u32[]{:S(2)}, u32[]{:S(2)}) %collective-permute-start.4) | collective-permute-done | bytes 131104 | tf_op jit(solution)/shard_map/ppermute | solution.py:639
  27.8 0.0 collective-permute-done.5.refs_5_
  27.8 0.0 collective-permute-done.6.refs_6_
  27.8 0.2 boxes_in_place.1
  28.1 0.6 %collective-permute-start.9 = (f32[2,16,8,128]{3,2,1,0:T(8,128)S(1)}, f32[2,16,8,128]{3,2,1,0:T(8,128)S(1)}, u32[]{:S(2)}, u32[]{:S(2)}) collective-permute-start(f32[2,16,8,128]{3,2,1,0:T(8,128)S(1)} %get-tuple-element.39), channel_id=1, source_target_pairs={{0,16},{16,0},{1,17},{17,1},{2,18},{18,2},{3,19},{19,3},{4,20},{20... | collective-permute-start | bytes 393224 | tf_op jit(solution)/shard_map/ppermute | solution.py:655
  28.6 2.2 %collective-permute-start.7 = (f32[2,8,128]{2,1,0:T(8,128)S(1)}, f32[2,8,128]{2,1,0:T(8,128)S(1)}, u32[]{:S(2)}, u32[]{:S(2)}) collective-permute-start(f32[2,8,128]{2,1,0:T(8,128)S(1)} %get-tuple-element.37), channel_id=1, source_target_pairs={{1,2},{2,1},{3,0},{0,3},{5,6},{6,5},{7,4},{4,7},{9,10},{10,9},{11,... | collective-permute-start | bytes 24584 | tf_op jit(solution)/shard_map/ppermute | solution.py:659
  30.9 1.7 %collective-permute-start.8 = (f32[2,8,128]{2,1,0:T(8,128)S(1)}, f32[2,8,128]{2,1,0:T(8,128)S(1)}, u32[]{:S(2)}, u32[]{:S(2)}) collective-permute-start(f32[2,8,128]{2,1,0:T(8,128)S(1)} %get-tuple-element.38), channel_id=1, source_target_pairs={{0,1},{1,0},{2,3},{3,2},{4,5},{5,4},{6,7},{7,6},{8,9},{9,8},{10,11... | collective-permute-start | bytes 24584 | tf_op jit(solution)/shard_map/ppermute | solution.py:660
  32.6 1.4 %grid_from_boxes.1.grid = f32[4,16,16,128]{3,2,1,0:T(8,128)S(1)} custom-call(f32[65,2,8,128]{3,2,1,0:T(8,128)S(1)} %get-tuple-element.36.held), custom_call_target="tpu_custom_call" | custom-call | flops 4194304 | bytes 2097152 | tf_op jit(solution)/shard_map/grid_from_boxes/pallas_call | solution.py:224
  34.0 0.1 collective-permute-done.7.odd_pairs
  34.1 0.4 %collective-permute-done.8.even_pairs = f32[2,8,128]{2,1,0:T(8,128)S(1)} collective-permute-done((f32[2,8,128]{2,1,0:T(8,128)S(1)}, f32[2,8,128]{2,1,0:T(8,128)S(1)}, u32[]{:S(2)}, u32[]{:S(2)}) %collective-permute-start.8) | collective-permute-done | bytes 8224 | tf_op jit(solution)/shard_map/ppermute | solution.py:660
  34.5 0.0 collective-permute-done.9.refs_0_
  34.5 0.5 %faces_and_rows.1 = (f32[4,4,16,128]{3,2,1,0:T(8,128)S(1)}, f32[2,2,8,128]{3,2,1,0:T(8,128)S(1)}, f32[152,128]{1,0:T(8,128)S(1)}, f32[152,128]{1,0:T(8,128)S(1)}, f32[16,128]{1,0:T(8,128)S(1)}) custom-call(f32[4,16,16,128]{3,2,1,0:T(8,128)S(1)} %grid_from_boxes.1.grid, f32[2,8,128]{2,1,0:T(8,128)S(1)} %collective-permute-done.7.odd_pairs, ...), custom_call_target="tpu_custom_call" | custom-call | tf_op jit(solution)/shard_map/faces_and_rows/pallas_call | solution.py:318
  35.0 0.1 collective-permute-start.10
  35.1 0.5 %collective-permute-start.11 = (f32[152,128]{1,0:T(8,128)S(1)}, f32[152,128]{1,0:T(8,128)S(1)}, u32[]{:S(2)}, u32[]{:S(2)}) collective-permute-start(f32[152,128]{1,0:T(8,128)S(1)} %get-tuple-element.49), channel_id=1, source_target_pairs={{0,4},{4,8},{8,12},{12,0},{1,5},{5,9},{9,13},{13,1},{2,6},{6,10},{... | collective-permute-start | bytes 233480 | tf_op jit(solution)/shard_map/ppermute | solution.py:667
  35.6 1.5 %collective-permute-start.12 = (f32[16,128]{1,0:T(8,128)S(1)}, f32[16,128]{1,0:T(8,128)S(1)}, u32[]{:S(2)}, u32[]{:S(2)}) collective-permute-start(f32[16,128]{1,0:T(8,128)S(1)} %get-tuple-element.50), channel_id=1, source_target_pairs={{0,16},{16,0},{1,17},{17,1},{2,18},{18,2},{3,19},{19,3},{4,20},{20... | collective-permute-start | bytes 24584 | tf_op jit(solution)/shard_map/ppermute | solution.py:655
  37.1 1.9 %first_inside.1 = (f32[4,20,16,128]{3,2,1,0:T(8,128)S(1)}, f32[20,16,128]{2,1,0:T(8,128)S(1)}, f32[4,16,16,128]{3,2,1,0:T(8,128)S(1)}, f32[4,16,16,128]{3,2,1,0:...) custom-call(f32[4,16,16,128]{3,2,1,0:T(8,128)S(1)} %grid_from_boxes.1.grid, ...), custom_call_target="tpu_custom_call" | custom-call | flops 4194304 | bytes 2097152 | tf_op jit(solution)/shard_map/first_inside/pallas_call | solution.py:433
  39.0 0.2 collective-permute-done.12.refs_0_
  39.2 0.0 collective-permute-done.10.above
  39.2 0.5 %collective-permute-done.11.below = f32[152,128]{1,0:T(8,128)S(1)} collective-permute-done((f32[152,128]{1,0:T(8,128)S(1)}, f32[152,128]{1,0:T(8,128)S(1)}, u32[]{:S(2)}, u32[]{:S(2)}) %collective-permute-start.11) | collective-permute-done | bytes 77856 | tf_op jit(solution)/shard_map/ppermute | solution.py:667
  39.7 1.9 %last_sections.1 = f32[4,16,16,128]{3,2,1,0:T(8,128)} custom-call(f32[4,20,16,128]{3,2,1,0:T(8,128)S(1)} %get-tuple-element.42.wide, f32[20,16,128]{2,1,0:T(8,128)S(1)} %get-tuple-element.43.halves, f32[4,16,16,128]{3,2,1,0:T(8,128)S(1)} %get-tuple-element.44.first_in, f32[4,16,16,128]{3,2,1,0:T(8,128)S(1)} %get-tuple-element.45.beyond_in, ...), custom_call_target="tpu_custom_call" | custom-call | tf_op jit(solution)/shard_map/last_sections/pallas_call | solution.py:605
Async XLA Ops:
  1.3 9.5 %collective-permute-start = (f32[16,2,8,128]{3,2,1,0:T(8,128)S(1)}, f32[16,2,8,128]{3,2,1,0:T(8,128)S(1)}, u32[]{:S(2)}, u32[]{:S(2)}) collective-permute-start(f32[16,2,8,128]{3,2,1,0:T(8,128)S(1)} %get-tuple-element.28), channel_id=1, source_target_pairs={{0,3},{1,2},{2,1},{3,0},{16,19},{17,18},{18,17},{19,16},{4,7},{5,6... | collective-permute-start | bytes 393224 | tf_op jit(solution)/shard_map/ppermute | solution.py:639
  6.4 9.0 %collective-permute-start.1 = (f32[16,2,8,128]{3,2,1,0:T(8,128)S(1)}, f32[16,2,8,128]{3,2,1,0:T(8,128)S(1)}, u32[]{:S(2)}, u32[]{:S(2)}) collective-permute-start(f32[16,2,8,128]{3,2,1,0:T(8,128)S(1)} %get-tuple-element.29), channel_id=1, source_target_pairs={{0,1},{1,0},{2,3},{3,2},{16,17},{17,16},{18,19},{19,18},{4,5},{5,4... | collective-permute-start | bytes 393224 | tf_op jit(solution)/shard_map/ppermute | solution.py:639
  6.4 11.4 %collective-permute-start.2 = (f32[16,2,8,128]{3,2,1,0:T(8,128)S(1)}, f32[16,2,8,128]{3,2,1,0:T(8,128)S(1)}, u32[]{:S(2)}, u32[]{:S(2)}) collective-permute-start(f32[16,2,8,128]{3,2,1,0:T(8,128)S(1)} %get-tuple-element.30), channel_id=1, source_target_pairs={{0,16},{1,17},{2,18},{3,19},{16,0},{17,1},{18,2},{19,3},{4,20},{5,... | collective-permute-start | bytes 393224 | tf_op jit(solution)/shard_map/ppermute | solution.py:639
  7.9 14.5 %collective-permute-start.3 = (f32[16,2,8,128]{3,2,1,0:T(8,128)S(1)}, f32[16,2,8,128]{3,2,1,0:T(8,128)S(1)}, u32[]{:S(2)}, u32[]{:S(2)}) collective-permute-start(f32[16,2,8,128]{3,2,1,0:T(8,128)S(1)} %get-tuple-element.31), channel_id=1, source_target_pairs={{0,2},{1,3},{2,0},{3,1},{16,18},{17,19},{18,16},{19,17},{4,6},{5,7... | collective-permute-start | bytes 393224 | tf_op jit(solution)/shard_map/ppermute | solution.py:639
  8.7 19.1 %collective-permute-start.4 = (f32[16,2,8,128]{3,2,1,0:T(8,128)S(1)}, f32[16,2,8,128]{3,2,1,0:T(8,128)S(1)}, u32[]{:S(2)}, u32[]{:S(2)}) collective-permute-start(f32[16,2,8,128]{3,2,1,0:T(8,128)S(1)} %get-tuple-element.32), channel_id=1, source_target_pairs={{0,18},{1,19},{2,16},{3,17},{16,2},{17,3},{18,0},{19,1},{4,22},{5,... | collective-permute-start | bytes 393224 | tf_op jit(solution)/shard_map/ppermute | solution.py:639
  10.8 6.0 %copy-start = (s32[64]{0:T(128)S(1)}, s32[64]{0:T(128)}, u32[]{:S(2)}) copy-start(s32[64]{0:T(128)} %owner.1) | copy-start | bytes 772
  10.8 17.0 %collective-permute-start.5 = (f32[16,2,8,128]{3,2,1,0:T(8,128)S(1)}, f32[16,2,8,128]{3,2,1,0:T(8,128)S(1)}, u32[]{:S(2)}, u32[]{:S(2)}) collective-permute-start(f32[16,2,8,128]{3,2,1,0:T(8,128)S(1)} %get-tuple-element.33), channel_id=1, source_target_pairs={{0,17},{1,16},{2,19},{3,18},{16,1},{17,0},{18,3},{19,2},{4,21},{5,... | collective-permute-start | bytes 393224 | tf_op jit(solution)/shard_map/ppermute | solution.py:639
  15.4 12.4 %collective-permute-start.6 = (f32[16,2,8,128]{3,2,1,0:T(8,128)S(1)}, f32[16,2,8,128]{3,2,1,0:T(8,128)S(1)}, u32[]{:S(2)}, u32[]{:S(2)}) collective-permute-start(f32[16,2,8,128]{3,2,1,0:T(8,128)S(1)} %get-tuple-element.34), channel_id=1, source_target_pairs={{0,19},{1,18},{2,17},{3,16},{16,3},{17,2},{18,1},{19,0},{4,23},{5,... | collective-permute-start | bytes 393224 | tf_op jit(solution)/shard_map/ppermute | solution.py:639
  28.1 6.5 %collective-permute-start.9 = (f32[2,16,8,128]{3,2,1,0:T(8,128)S(1)}, f32[2,16,8,128]{3,2,1,0:T(8,128)S(1)}, u32[]{:S(2)}, u32[]{:S(2)}) collective-permute-start(f32[2,16,8,128]{3,2,1,0:T(8,128)S(1)} %get-tuple-element.39), channel_id=1, source_target_pairs={{0,16},{16,0},{1,17},{17,1},{2,18},{18,2},{3,19},{19,3},{4,20},{20... | collective-permute-start | bytes 393224 | tf_op jit(solution)/shard_map/ppermute | solution.py:655
  28.6 5.4 %collective-permute-start.7 = (f32[2,8,128]{2,1,0:T(8,128)S(1)}, f32[2,8,128]{2,1,0:T(8,128)S(1)}, u32[]{:S(2)}, u32[]{:S(2)}) collective-permute-start(f32[2,8,128]{2,1,0:T(8,128)S(1)} %get-tuple-element.37), channel_id=1, source_target_pairs={{1,2},{2,1},{3,0},{0,3},{5,6},{6,5},{7,4},{4,7},{9,10},{10,9},{11,... | collective-permute-start | bytes 24584 | tf_op jit(solution)/shard_map/ppermute | solution.py:659
  30.9 3.7 %collective-permute-start.8 = (f32[2,8,128]{2,1,0:T(8,128)S(1)}, f32[2,8,128]{2,1,0:T(8,128)S(1)}, u32[]{:S(2)}, u32[]{:S(2)}) collective-permute-start(f32[2,8,128]{2,1,0:T(8,128)S(1)} %get-tuple-element.38), channel_id=1, source_target_pairs={{0,1},{1,0},{2,3},{3,2},{4,5},{5,4},{6,7},{7,6},{8,9},{9,8},{10,11... | collective-permute-start | bytes 24584 | tf_op jit(solution)/shard_map/ppermute | solution.py:660
  35.0 4.2 %collective-permute-start.10 = (f32[152,128]{1,0:T(8,128)S(1)}, f32[152,128]{1,0:T(8,128)S(1)}, u32[]{:S(2)}, u32[]{:S(2)}) collective-permute-start(f32[152,128]{1,0:T(8,128)S(1)} %get-tuple-element.48), channel_id=1, source_target_pairs={{0,12},{4,0},{8,4},{12,8},{1,13},{5,1},{9,5},{13,9},{2,14},{6,2},{... | collective-permute-start | bytes 233480 | tf_op jit(solution)/shard_map/ppermute | solution.py:666
  35.1 4.7 %collective-permute-start.11 = (f32[152,128]{1,0:T(8,128)S(1)}, f32[152,128]{1,0:T(8,128)S(1)}, u32[]{:S(2)}, u32[]{:S(2)}) collective-permute-start(f32[152,128]{1,0:T(8,128)S(1)} %get-tuple-element.49), channel_id=1, source_target_pairs={{0,4},{4,8},{8,12},{12,0},{1,5},{5,9},{9,13},{13,1},{2,6},{6,10},{... | collective-permute-start | bytes 233480 | tf_op jit(solution)/shard_map/ppermute | solution.py:667
  35.6 3.7 %collective-permute-start.12 = (f32[16,128]{1,0:T(8,128)S(1)}, f32[16,128]{1,0:T(8,128)S(1)}, u32[]{:S(2)}, u32[]{:S(2)}) collective-permute-start(f32[16,128]{1,0:T(8,128)S(1)} %get-tuple-element.50), channel_id=1, source_target_pairs={{0,16},{16,0},{1,17},{17,1},{2,18},{18,2},{3,19},{19,3},{4,20},{20... | collective-permute-start | bytes 24584 | tf_op jit(solution)/shard_map/ppermute | solution.py:655
